TPU v7x, 32 devices: a whole 2x2x4 slice. The times are simulated.
32 devices in a mesh: organ: 4 (over x, core), sub: 8 (over z, y).
Axes of the slice: x: 2, y: 2, z: 4, core: 2. Of those that a mesh axis runs over, the one named last changes fastest.
Arguments:
- dual_rhs: float32 [16, 4, 8, 5, 640], P(None, 'organ', 'sub')
- warm_start: float32 [16, 4, 8, 5, 640], P(None, 'organ', 'sub'), may hold values from -4 to 4
- inverse_blocks: float32 [4, 8, 5, 640, 640], P('organ', 'sub'), as said below
- coarse_basis: float32 [6, 4, 8, 5, 640], P(None, 'organ', 'sub')
- mortar_rows: float32 [4, 8, 128, 640], P('organ', 'sub'), may hold values from -0.25 to 0.25
- match_rounds: int32 [4, 8, 5], P('organ', 'sub'), may hold values from 0 to 4, each once within a row
- slave_owner: int32 [4, 8, 128, 1], P('organ', 'sub'), may hold values from 0 to 31; in each aligned block of 128 rows (0 to 127, 128 to 255, ..., all dimensions but the last counted through in order) at most 8 rows name the same one
- slave_dofs: int32 [4, 8, 128], P('organ', 'sub'), may hold values from 0 to 639
- active_set: int32 [4, 8, 128], P('organ', 'sub'), may hold values 0 or 1
- row_counts: int32 [4, 8, 1], P('organ', 'sub'), may hold values from 96 to 128, as said below
Outputs:
- solution: float32 [16, 4, 8, 5, 640], P(None, 'organ', 'sub')
Inputs may be any that keep to these rules, and one draw needn't show every extreme that they name: `match_rounds`: each device's row lists every round's face once. `slave_owner`: in the rows of one device no owner is named more than 8 times; in some device one owner is named exactly 8 times. `row_counts`: some device has all 128 rows live. `inverse_blocks`: each face block is symmetric positive definite.
All inputs are finite; a program needn't handle non-finite values. No bound on the sum of `active_set` on one device may be relied on, other than what follows from the above.
Results may differ from a plain program's by a relative error of at most 0.0001.
Values sent between devices are 32-bit elements; how exact they have to be, the bound alone decides.
No kernel may reach another device: no remote copies, remote signals or barrier semaphores. Data moves between devices by JAX's collectives and lax.ppermute only.
A program may use at most 128 MiB of HBM per device.

v0:
```python
import jax
import jax.numpy as jnp
from jax import lax
from jax.sharding import PartitionSpec as P

ITERS = 3
CAP = 8


def from_partner(value, axis, apart):
    mask = 2**apart
    pairs = [(source, source ^ mask) for source in range(lax.axis_size(axis))]
    return lax.ppermute(value, axis, pairs)


def local(
    dual_rhs,
    warm_start,
    inverse_blocks,
    coarse_basis,
    mortar_rows,
    match_rounds,
    slave_owner,
    slave_dofs,
    active_set,
    row_counts,
):
    directions = dual_rhs.shape[0]
    block_count = dual_rhs.shape[3]
    block_len = dual_rhs.shape[4]
    row_total = mortar_rows.shape[2]
    modes = coarse_basis.shape[0]
    right_side = dual_rhs.reshape(directions, block_count, block_len)
    starting = warm_start.reshape(directions, block_count, block_len)
    matrices = inverse_blocks.reshape(block_count, block_len, block_len)
    mode_basis = coarse_basis.reshape(modes, block_count, block_len)
    mortar = mortar_rows.reshape(row_total, block_len)
    rounds = match_rounds.reshape(-1)
    owner = slave_owner.reshape(-1)
    slave = slave_dofs.reshape(-1)
    live_rows = active_set.reshape(-1) * (
        jnp.arange(row_total, dtype=jnp.int32) < row_counts.reshape(())
    ).astype(jnp.int32)
    n_sub = lax.axis_size("sub")
    n_org = lax.axis_size("organ")
    devices = n_sub * n_org
    width = devices * CAP
    targets = (owner[:, None] == jnp.arange(devices, dtype=jnp.int32)[None, :]).astype(
        jnp.int32
    ) * live_rows[:, None]
    earlier = jnp.cumsum(targets, axis=0) - targets
    rank_row = jnp.sum(earlier * targets, axis=1)
    send_slot = jnp.where(live_rows > 0, owner * CAP + rank_row, width)
    outgoing_slave = jnp.full((width,), -1, jnp.int32).at[send_slot].set(slave, mode="drop")
    incoming_slave = lax.all_to_all(
        outgoing_slave, ("organ", "sub"), split_axis=0, concat_axis=0, tiled=True
    )
    incoming_ok = incoming_slave >= 0
    incoming_index = jnp.where(incoming_ok, incoming_slave, 0)

    def route(outgoing, backward):
        if backward:
            return lax.all_to_all(
                outgoing, ("organ", "sub"), split_axis=1, concat_axis=1, tiled=True
            )
        return lax.all_to_all(outgoing, ("organ", "sub"), split_axis=1, concat_axis=1, tiled=True)

    def contact_term(surface):
        row_vals = lax.dot_general(
            surface, mortar, (((1,), (1,)), ((), ())), precision=lax.Precision.HIGHEST
        )
        outgoing = (
            jnp.zeros((directions, width), jnp.float32).at[:, send_slot].set(row_vals, mode="drop")
        )
        received = route(outgoing, False)
        slave_vals = jnp.take(surface, incoming_index, axis=1)
        gap_vals = jnp.where(incoming_ok[None, :], received - slave_vals, 0.0)
        returned = route(gap_vals, True)
        row_gaps = jnp.take(returned, send_slot, axis=1, mode="fill", fill_value=0.0)
        master_part = jnp.dot(row_gaps, mortar, precision=lax.Precision.HIGHEST)
        slave_part = (
            jnp.zeros((directions, block_len), jnp.float32).at[:, incoming_index].add(gap_vals)
        )
        return master_part - slave_part

    block_ids = jnp.arange(block_count, dtype=jnp.int32)

    def jump(field):
        result = field
        for bit_index in range(3):
            selector = (rounds[bit_index] == block_ids).astype(jnp.float32)
            face_vals = lax.dynamic_index_in_dim(field, rounds[bit_index], 1, keepdims=False)
            remote = from_partner(face_vals, "sub", bit_index)
            result = result - selector[None, :, None] * remote[:, None, :]
        for bit_index in range(2):
            selector = (rounds[3 + bit_index] == block_ids).astype(jnp.float32)
            face_vals = lax.dynamic_index_in_dim(field, rounds[3 + bit_index], 1, keepdims=False)
            remote = from_partner(face_vals, "organ", bit_index)
            result = result - selector[None, :, None] * remote[:, None, :]
        return result.at[:, 0, :].add(contact_term(field[:, 0, :]))

    def operator(field):
        inner = jump(field)
        smoothed = jnp.einsum("kbn,bnm->kbm", inner, matrices, precision=lax.Precision.HIGHEST)
        return jump(smoothed)

    gram_local = jnp.einsum("mbn,lbn->ml", mode_basis, mode_basis, precision=lax.Precision.HIGHEST)
    gram_matrix = lax.psum(gram_local, "sub")
    factor = jnp.linalg.cholesky(gram_matrix)

    def project(resid):
        coeff_local = jnp.einsum("kbn,mbn->km", resid, mode_basis, precision=lax.Precision.HIGHEST)
        coeffs = lax.psum(coeff_local, "sub")
        solved = jax.scipy.linalg.cho_solve((factor, True), coeffs.T).T
        projected = resid - jnp.einsum(
            "km,mbn->kbn", solved, mode_basis, precision=lax.Precision.HIGHEST
        )
        rho_value = lax.psum(jnp.sum(resid * projected, axis=(1, 2)), ("organ", "sub"))
        return (projected, rho_value)

    solution = starting
    resid = right_side - operator(starting)
    projected, rho_now = project(resid)
    direction = projected
    for iteration in range(ITERS):
        image = operator(direction)
        curvature_sum = lax.psum(jnp.sum(direction * image, axis=(1, 2)), ("organ", "sub"))
        step_size = rho_now / curvature_sum
        solution = solution + step_size[:, None, None] * direction
        if iteration < ITERS - 1:
            resid = resid - step_size[:, None, None] * image
            projected, rho_new = project(resid)
            direction = projected + (rho_new / rho_now)[:, None, None] * direction
            rho_now = rho_new
    out_shape = (directions, 1, 1, block_count, block_len)
    return solution.reshape(out_shape)


def solution(mesh):
    in_specs = (
        P(None, "organ", "sub", None, None),
        P(None, "organ", "sub", None, None),
        P("organ", "sub", None, None, None),
        P(None, "organ", "sub", None, None),
        P("organ", "sub", None, None),
        P("organ", "sub", None),
        P("organ", "sub", None, None),
        P("organ", "sub", None),
        P("organ", "sub", None),
        P("organ", "sub", None),
    )
    out_specs = P(None, "organ", "sub", None, None)
    return jax.shard_map(local, mesh=mesh, in_specs=in_specs, out_specs=out_specs, check_vma=False)
```

profile of v0, /device:TPU:0, one launch (start us, length us, event | category | flops | bytes accessed | tf_op | source)
XLA Modules:
  0.0 551.5 jit_solution(9008600324721689535)
XLA Ops:
  5.6 7.3 %all-to-all-start = ((s32[32,8,1]{1,2,0:T(1,128)}), s32[32,8,1]{1,2,0:T(1,128)S(1)}, u32[]{:S(2)}, u32[]{:S(2)}) async-start(s32[32,8,1]{1,2,0:T(1,128)} %bitcast.15), calls=%async_computation | async-start | bytes 32768 | tf_op jit(solution)/shard_map/all_to_all | solution.py:55
  40.2 2.6 all-to-all-start.1
  44.9 5.0 all-to-all-done.1
  52.2 2.5 all-to-all-start.2
  58.1 3.7 all-to-all-done.2
  63.7 7.2 %fusion.6 = f32[5,16,640]{2,1,0:T(8,128)S(1)} fusion(f32[16,5,640]{2,0,1:T(8,128)S(1)} %fusion.120, f32[1,1,5,640,640]{4,3,2,1,0:T(8,128)} %param.34), kind=kOutput, calls=%fused_computation.39 | convolution fusion | flops 393216000 | bytes 8601600 | tf_op jit(solution)/shard_map/kbn,bnm->kbm/dot_general | solution.py:104
  87.6 2.5 all-to-all-start.4
  90.5 6.7 %all-to-all-done.4 = f32[32,1,128]{2,1,0:T(1,128)S(1)} async-done(((f32[32,1,128]{2,1,0:T(1,128)}), f32[32,1,128]{2,1,0:T(1,128)S(1)}, u32[]{:S(2)}, u32[]{:S(2)}) %all-to-all-start.4) | async-done | bytes 16416 | tf_op jit(solution)/shard_map/all_to_all | solution.py:63
  99.5 18.2 %all-reduce.1 = (f32[6,16]{1,0:T(8,128)S(1)}, f32[6,6]{0,1:T(8,128)S(1)}) all-reduce(f32[6,16]{1,0:T(8,128)S(1)} %convolution_bitcast_fusion.12, f32[6,6]{0,1:T(8,128)S(1)} %convolution_bitcast_fusion.13), channel_id=1, replica_groups=mesh['organ'=4,'sub'=8] {'sub'}, use_global_device_ids=true, to_apply=%region_10.13 | all-reduce | flops 132 | bytes 1056 | tf_op jit(solution)/shard_map/psum | solution.py:113
  123.1 2.5 all-to-all-start.5
  137.6 2.5 all-to-all-start.6
  140.5 6.7 %all-to-all-done.6 = f32[32,1,128]{2,1,0:T(1,128)S(1)} async-done(((f32[32,1,128]{2,1,0:T(1,128)}), f32[32,1,128]{2,1,0:T(1,128)S(1)}, u32[]{:S(2)}, u32[]{:S(2)}) %all-to-all-start.6) | async-done | bytes 16416 | tf_op jit(solution)/shard_map/all_to_all | solution.py:63
  149.0 7.3 %fusion.4 = f32[5,16,640]{2,1,0:T(8,128)S(1)} fusion(f32[16,5,640]{2,0,1:T(8,128)S(1)} %fusion.118, f32[1,1,5,640,640]{4,3,2,1,0:T(8,128)} %param.34), kind=kOutput, calls=%fused_computation.37 | convolution fusion | flops 393216000 | bytes 8601600 | tf_op jit(solution)/shard_map/kbn,bnm->kbm/dot_general | solution.py:104
  158.5 2.5 all-to-all-start.7
  176.0 6.7 %all-to-all-done.8 = f32[32,1,128]{2,1,0:T(1,128)S(1)} async-done(((f32[32,1,128]{2,1,0:T(1,128)}), f32[32,1,128]{2,1,0:T(1,128)S(1)}, u32[]{:S(2)}, u32[]{:S(2)}) %all-to-all-start.8) | async-done | bytes 16416 | tf_op jit(solution)/shard_map/all_to_all | solution.py:63
  184.7 38.3 %all-reduce = (f32[16]{0:T(128)S(1)}, f32[16]{0:T(128)S(1)}) all-reduce(f32[16]{0:T(128)S(1)} %get-tuple-element.105, f32[16]{0:T(128)S(1)} %get-tuple-element.104), channel_id=1, replica_groups=mesh['organ'=4,'sub'=8] {'organ','sub'}, use_global_device_ids=true, to_apply=%region_12.16 | all-reduce | flops 32 | bytes 256 | tf_op jit(solution)/shard_map/psum | solution.py:118
  223.4 20.4 %psum.74 = f32[6,16]{1,0:T(8,128)S(1)} all-reduce(f32[6,16]{1,0:T(8,128)S(1)} %convolution_bitcast_fusion.10), channel_id=1, replica_groups=mesh['organ'=4,'sub'=8] {'sub'}, use_global_device_ids=true, to_apply=%region_19.23 | all-reduce | flops 96 | bytes 768 | tf_op jit(solution)/shard_map/psum | solution.py:113
  244.7 37.1 %psum.75 = f32[16]{0:T(128)S(1)} all-reduce(f32[16]{0:T(128)S(1)} %get-tuple-element.163), channel_id=1, replica_groups=mesh['organ'=4,'sub'=8] {'organ','sub'}, use_global_device_ids=true, to_apply=%region_21.25 | all-reduce | flops 16 | bytes 128 | tf_op jit(solution)/shard_map/psum | solution.py:118
  284.1 5.1 all-to-all-start.9
  301.2 2.5 all-to-all-start.10
  304.1 6.7 %all-to-all-done.10 = f32[32,1,128]{2,1,0:T(1,128)S(1)} async-done(((f32[32,1,128]{2,1,0:T(1,128)}), f32[32,1,128]{2,1,0:T(1,128)S(1)}, u32[]{:S(2)}, u32[]{:S(2)}) %all-to-all-start.10) | async-done | bytes 16416 | tf_op jit(solution)/shard_map/all_to_all | solution.py:63
  312.6 7.3 %fusion.2 = f32[5,16,640]{2,1,0:T(8,128)S(1)} fusion(f32[16,5,640]{2,0,1:T(8,128)S(1)} %fusion.116, f32[1,1,5,640,640]{4,3,2,1,0:T(8,128)} %param.34), kind=kOutput, calls=%fused_computation.35 | convolution fusion | flops 393216000 | bytes 8601600 | tf_op jit(solution)/shard_map/kbn,bnm->kbm/dot_general | solution.py:104
  322.1 2.5 all-to-all-start.11
  339.5 6.7 %all-to-all-done.12 = f32[32,1,128]{2,1,0:T(1,128)S(1)} async-done(((f32[32,1,128]{2,1,0:T(1,128)}), f32[32,1,128]{2,1,0:T(1,128)S(1)}, u32[]{:S(2)}, u32[]{:S(2)}) %all-to-all-start.12) | async-done | bytes 16416 | tf_op jit(solution)/shard_map/all_to_all | solution.py:63
  348.3 38.3 %psum.76 = f32[16]{0:T(128)S(1)} all-reduce(f32[16]{0:T(128)S(1)} %multiply_reduce_fusion.2), channel_id=1, replica_groups=mesh['organ'=4,'sub'=8] {'organ','sub'}, use_global_device_ids=true, to_apply=%region_27.31 | all-reduce | flops 16 | bytes 128 | tf_op jit(solution)/shard_map/psum | solution.py:127
  386.9 20.4 %psum.77 = f32[6,16]{1,0:T(8,128)S(1)} all-reduce(f32[6,16]{1,0:T(8,128)S(1)} %convolution_bitcast_fusion.8), channel_id=1, replica_groups=mesh['organ'=4,'sub'=8] {'sub'}, use_global_device_ids=true, to_apply=%region_28.32 | all-reduce | flops 96 | bytes 768 | tf_op jit(solution)/shard_map/psum | solution.py:113
  408.2 37.1 %psum.78 = f32[16]{0:T(128)S(1)} all-reduce(f32[16]{0:T(128)S(1)} %get-tuple-element.165), channel_id=1, replica_groups=mesh['organ'=4,'sub'=8] {'organ','sub'}, use_global_device_ids=true, to_apply=%region_30.34 | all-reduce | flops 16 | bytes 128 | tf_op jit(solution)/shard_map/psum | solution.py:118
  447.7 5.1 all-to-all-start.13
  467.7 6.7 %all-to-all-done.14 = f32[32,1,128]{2,1,0:T(1,128)S(1)} async-done(((f32[32,1,128]{2,1,0:T(1,128)}), f32[32,1,128]{2,1,0:T(1,128)S(1)}, u32[]{:S(2)}, u32[]{:S(2)}) %all-to-all-start.14) | async-done | bytes 16416 | tf_op jit(solution)/shard_map/all_to_all | solution.py:63
  476.2 7.2 %fusion = f32[5,16,640]{2,1,0:T(8,128)S(1)} fusion(f32[16,5,640]{2,0,1:T(8,128)S(1)} %fusion.114, f32[1,1,5,640,640]{4,3,2,1,0:T(8,128)} %param.34), kind=kOutput, calls=%fused_computation.33 | convolution fusion | flops 393216000 | bytes 8601600 | tf_op jit(solution)/shard_map/kbn,bnm->kbm/dot_general | solution.py:104
  503.1 6.7 %all-to-all-done.16 = f32[32,1,128]{2,1,0:T(1,128)S(1)} async-done(((f32[32,1,128]{2,1,0:T(1,128)}), f32[32,1,128]{2,1,0:T(1,128)S(1)}, u32[]{:S(2)}, u32[]{:S(2)}) %all-to-all-start.16) | async-done | bytes 16416 | tf_op jit(solution)/shard_map/all_to_all | solution.py:63
  511.8 38.3 %psum.79 = f32[16]{0:T(128)S(1)} all-reduce(f32[16]{0:T(128)S(1)} %multiply_reduce_fusion), channel_id=1, replica_groups=mesh['organ'=4,'sub'=8] {'organ','sub'}, use_global_device_ids=true, to_apply=%region_36.40 | all-reduce | flops 16 | bytes 128 | tf_op jit(solution)/shard_map/psum | solution.py:127
  (328 shorter events, 169.2 us)
Async XLA Ops:
  5.6 34.6 %all-to-all-start = ((s32[32,8,1]{1,2,0:T(1,128)}), s32[32,8,1]{1,2,0:T(1,128)S(1)}, u32[]{:S(2)}, u32[]{:S(2)}) async-start(s32[32,8,1]{1,2,0:T(1,128)} %bitcast.15), calls=%async_computation | async-start | bytes 32768 | tf_op jit(solution)/shard_map/all_to_all | solution.py:55
  24.5 32.4 %collective-permute-start.3 = (f32[16,640]{1,0:T(8,128)S(1)}, f32[16,640]{1,0:T(8,128)S(1)}, u32[]{:S(2)}, u32[]{:S(2)}) collective-permute-start(f32[16,640]{1,0:T(8,128)S(1)} %bitcast.773), channel_id=1, source_target_pairs={{0,8},{8,0},{16,24},{24,16},{1,9},{9,1},{17,25},{25,17},{2,10},{10... | collective-permute-start | bytes 122888 | tf_op jit(solution)/shard_map/ppermute | solution.py:13
  24.8 32.1 %collective-permute-start.4 = (f32[16,640]{1,0:T(8,128)S(1)}, f32[16,640]{1,0:T(8,128)S(1)}, u32[]{:S(2)}, u32[]{:S(2)}) collective-permute-start(f32[16,640]{1,0:T(8,128)S(1)} %bitcast.774), channel_id=1, source_target_pairs={{0,16},{8,24},{16,0},{24,8},{1,17},{9,25},{17,1},{25,9},{2,18},{10... | collective-permute-start | bytes 122888 | tf_op jit(solution)/shard_map/ppermute | solution.py:13
  26.5 30.5 %collective-permute-start.1 = (f32[16,640]{1,0:T(8,128)S(1)}, f32[16,640]{1,0:T(8,128)S(1)}, u32[]{:S(2)}, u32[]{:S(2)}) collective-permute-start(f32[16,640]{1,0:T(8,128)S(1)} %bitcast.775), channel_id=1, source_target_pairs={{0,2},{1,3},{2,0},{3,1},{4,6},{5,7},{6,4},{7,5},{8,10},{9,11},{10,... | collective-permute-start | bytes 122888 | tf_op jit(solution)/shard_map/ppermute | solution.py:13
  28.0 29.0 %collective-permute-start.2 = (f32[16,640]{1,0:T(8,128)S(1)}, f32[16,640]{1,0:T(8,128)S(1)}, u32[]{:S(2)}, u32[]{:S(2)}) collective-permute-start(f32[16,640]{1,0:T(8,128)S(1)} %bitcast.776), channel_id=1, source_target_pairs={{0,4},{1,5},{2,6},{3,7},{4,0},{5,1},{6,2},{7,3},{8,12},{9,13},{10,... | collective-permute-start | bytes 122888 | tf_op jit(solution)/shard_map/ppermute | solution.py:13
  30.4 26.6 %collective-permute-start = (f32[16,640]{1,0:T(8,128)S(1)}, f32[16,640]{1,0:T(8,128)S(1)}, u32[]{:S(2)}, u32[]{:S(2)}) collective-permute-start(f32[16,640]{1,0:T(8,128)S(1)} %bitcast.777), channel_id=1, source_target_pairs={{0,1},{1,0},{2,3},{3,2},{4,5},{5,4},{6,7},{7,6},{8,9},{9,8},{10,11... | collective-permute-start | bytes 122888 | tf_op jit(solution)/shard_map/ppermute | solution.py:13
  75.7 14.6 %collective-permute-start.5 = (f32[16,640]{1,0:T(8,128)S(1)}, f32[16,640]{1,0:T(8,128)S(1)}, u32[]{:S(2)}, u32[]{:S(2)}) collective-permute-start(f32[16,640]{1,0:T(8,128)S(1)} %get-tuple-element.147), channel_id=1, source_target_pairs={{0,1},{1,0},{2,3},{3,2},{4,5},{5,4},{6,7},{7,6},{8,9},{9,8},{10,11... | collective-permute-start | bytes 122888 | tf_op jit(solution)/shard_map/ppermute | solution.py:13
  77.4 12.9 %collective-permute-start.9 = (f32[16,640]{1,0:T(8,128)S(1)}, f32[16,640]{1,0:T(8,128)S(1)}, u32[]{:S(2)}, u32[]{:S(2)}) collective-permute-start(f32[16,640]{1,0:T(8,128)S(1)} %get-tuple-element.148), channel_id=1, source_target_pairs={{0,16},{8,24},{16,0},{24,8},{1,17},{9,25},{17,1},{25,9},{2,18},{10... | collective-permute-start | bytes 122888 | tf_op jit(solution)/shard_map/ppermute | solution.py:13
  78.9 11.4 %collective-permute-start.8 = (f32[16,640]{1,0:T(8,128)S(1)}, f32[16,640]{1,0:T(8,128)S(1)}, u32[]{:S(2)}, u32[]{:S(2)}) collective-permute-start(f32[16,640]{1,0:T(8,128)S(1)} %get-tuple-element.149), channel_id=1, source_target_pairs={{0,8},{8,0},{16,24},{24,16},{1,9},{9,1},{17,25},{25,17},{2,10},{10... | collective-permute-start | bytes 122888 | tf_op jit(solution)/shard_map/ppermute | solution.py:13
  78.9 11.4 %collective-permute-start.7 = (f32[16,640]{1,0:T(8,128)S(1)}, f32[16,640]{1,0:T(8,128)S(1)}, u32[]{:S(2)}, u32[]{:S(2)}) collective-permute-start(f32[16,640]{1,0:T(8,128)S(1)} %get-tuple-element.150), channel_id=1, source_target_pairs={{0,4},{1,5},{2,6},{3,7},{4,0},{5,1},{6,2},{7,3},{8,12},{9,13},{10,... | collective-permute-start | bytes 122888 | tf_op jit(solution)/shard_map/ppermute | solution.py:13
  125.7 14.6 %collective-permute-start.14 = (f32[16,640]{1,0:T(8,128)S(1)}, f32[16,640]{1,0:T(8,128)S(1)}, u32[]{:S(2)}, u32[]{:S(2)}) collective-permute-start(f32[16,640]{1,0:T(8,128)S(1)} %get-tuple-element.142), channel_id=1, source_target_pairs={{0,16},{8,24},{16,0},{24,8},{1,17},{9,25},{17,1},{25,9},{2,18},{10... | collective-permute-start | bytes 122888 | tf_op jit(solution)/shard_map/ppermute | solution.py:13
  127.4 12.9 %collective-permute-start.13 = (f32[16,640]{1,0:T(8,128)S(1)}, f32[16,640]{1,0:T(8,128)S(1)}, u32[]{:S(2)}, u32[]{:S(2)}) collective-permute-start(f32[16,640]{1,0:T(8,128)S(1)} %get-tuple-element.143), channel_id=1, source_target_pairs={{0,8},{8,0},{16,24},{24,16},{1,9},{9,1},{17,25},{25,17},{2,10},{10... | collective-permute-start | bytes 122888 | tf_op jit(solution)/shard_map/ppermute | solution.py:13
  127.4 12.9 %collective-permute-start.12 = (f32[16,640]{1,0:T(8,128)S(1)}, f32[16,640]{1,0:T(8,128)S(1)}, u32[]{:S(2)}, u32[]{:S(2)}) collective-permute-start(f32[16,640]{1,0:T(8,128)S(1)} %get-tuple-element.144), channel_id=1, source_target_pairs={{0,4},{1,5},{2,6},{3,7},{4,0},{5,1},{6,2},{7,3},{8,12},{9,13},{10,... | collective-permute-start | bytes 122888 | tf_op jit(solution)/shard_map/ppermute | solution.py:13
  161.1 14.6 %collective-permute-start.15 = (f32[16,640]{1,0:T(8,128)S(1)}, f32[16,640]{1,0:T(8,128)S(1)}, u32[]{:S(2)}, u32[]{:S(2)}) collective-permute-start(f32[16,640]{1,0:T(8,128)S(1)} %get-tuple-element.136), channel_id=1, source_target_pairs={{0,1},{1,0},{2,3},{3,2},{4,5},{5,4},{6,7},{7,6},{8,9},{9,8},{10,11... | collective-permute-start | bytes 122888 | tf_op jit(solution)/shard_map/ppermute | solution.py:13
  162.9 12.9 %collective-permute-start.19 = (f32[16,640]{1,0:T(8,128)S(1)}, f32[16,640]{1,0:T(8,128)S(1)}, u32[]{:S(2)}, u32[]{:S(2)}) collective-permute-start(f32[16,640]{1,0:T(8,128)S(1)} %get-tuple-element.137), channel_id=1, source_target_pairs={{0,16},{8,24},{16,0},{24,8},{1,17},{9,25},{17,1},{25,9},{2,18},{10... | collective-permute-start | bytes 122888 | tf_op jit(solution)/shard_map/ppermute | solution.py:13
  164.3 11.4 %collective-permute-start.18 = (f32[16,640]{1,0:T(8,128)S(1)}, f32[16,640]{1,0:T(8,128)S(1)}, u32[]{:S(2)}, u32[]{:S(2)}) collective-permute-start(f32[16,640]{1,0:T(8,128)S(1)} %get-tuple-element.138), channel_id=1, source_target_pairs={{0,8},{8,0},{16,24},{24,16},{1,9},{9,1},{17,25},{25,17},{2,10},{10... | collective-permute-start | bytes 122888 | tf_op jit(solution)/shard_map/ppermute | solution.py:13
  164.3 11.4 %collective-permute-start.17 = (f32[16,640]{1,0:T(8,128)S(1)}, f32[16,640]{1,0:T(8,128)S(1)}, u32[]{:S(2)}, u32[]{:S(2)}) collective-permute-start(f32[16,640]{1,0:T(8,128)S(1)} %get-tuple-element.139), channel_id=1, source_target_pairs={{0,4},{1,5},{2,6},{3,7},{4,0},{5,1},{6,2},{7,3},{8,12},{9,13},{10,... | collective-permute-start | bytes 122888 | tf_op jit(solution)/shard_map/ppermute | solution.py:13
  284.1 13.3 %all-to-all-start.9 = ((f32[32,1,128]{2,1,0:T(1,128)}), f32[32,1,128]{2,1,0:T(1,128)S(1)}, u32[]{:S(2)}, u32[]{:S(2)}) async-start(f32[32,1,128]{2,1,0:T(1,128)} %reshape.941), calls=%async_computation.9 | async-start | bytes 32768 | tf_op jit(solution)/shard_map/all_to_all | solution.py:66
  289.2 14.6 %collective-permute-start.24 = (f32[16,640]{1,0:T(8,128)S(1)}, f32[16,640]{1,0:T(8,128)S(1)}, u32[]{:S(2)}, u32[]{:S(2)}) collective-permute-start(f32[16,640]{1,0:T(8,128)S(1)} %get-tuple-element.131), channel_id=1, source_target_pairs={{0,16},{8,24},{16,0},{24,8},{1,17},{9,25},{17,1},{25,9},{2,18},{10... | collective-permute-start | bytes 122888 | tf_op jit(solution)/shard_map/ppermute | solution.py:13
  291.1 12.8 %collective-permute-start.23 = (f32[16,640]{1,0:T(8,128)S(1)}, f32[16,640]{1,0:T(8,128)S(1)}, u32[]{:S(2)}, u32[]{:S(2)}) collective-permute-start(f32[16,640]{1,0:T(8,128)S(1)} %get-tuple-element.132), channel_id=1, source_target_pairs={{0,8},{8,0},{16,24},{24,16},{1,9},{9,1},{17,25},{25,17},{2,10},{10... | collective-permute-start | bytes 122888 | tf_op jit(solution)/shard_map/ppermute | solution.py:13
  291.1 12.8 %collective-permute-start.22 = (f32[16,640]{1,0:T(8,128)S(1)}, f32[16,640]{1,0:T(8,128)S(1)}, u32[]{:S(2)}, u32[]{:S(2)}) collective-permute-start(f32[16,640]{1,0:T(8,128)S(1)} %get-tuple-element.133), channel_id=1, source_target_pairs={{0,4},{1,5},{2,6},{3,7},{4,0},{5,1},{6,2},{7,3},{8,12},{9,13},{10,... | collective-permute-start | bytes 122888 | tf_op jit(solution)/shard_map/ppermute | solution.py:13
  324.7 14.6 %collective-permute-start.25 = (f32[16,640]{1,0:T(8,128)S(1)}, f32[16,640]{1,0:T(8,128)S(1)}, u32[]{:S(2)}, u32[]{:S(2)}) collective-permute-start(f32[16,640]{1,0:T(8,128)S(1)} %get-tuple-element.125), channel_id=1, source_target_pairs={{0,1},{1,0},{2,3},{3,2},{4,5},{5,4},{6,7},{7,6},{8,9},{9,8},{10,11... | collective-permute-start | bytes 122888 | tf_op jit(solution)/shard_map/ppermute | solution.py:13
  326.4 12.9 %collective-permute-start.29 = (f32[16,640]{1,0:T(8,128)S(1)}, f32[16,640]{1,0:T(8,128)S(1)}, u32[]{:S(2)}, u32[]{:S(2)}) collective-permute-start(f32[16,640]{1,0:T(8,128)S(1)} %get-tuple-element.126), channel_id=1, source_target_pairs={{0,16},{8,24},{16,0},{24,8},{1,17},{9,25},{17,1},{25,9},{2,18},{10... | collective-permute-start | bytes 122888 | tf_op jit(solution)/shard_map/ppermute | solution.py:13
  327.9 11.4 %collective-permute-start.27 = (f32[16,640]{1,0:T(8,128)S(1)}, f32[16,640]{1,0:T(8,128)S(1)}, u32[]{:S(2)}, u32[]{:S(2)}) collective-permute-start(f32[16,640]{1,0:T(8,128)S(1)} %get-tuple-element.128), channel_id=1, source_target_pairs={{0,4},{1,5},{2,6},{3,7},{4,0},{5,1},{6,2},{7,3},{8,12},{9,13},{10,... | collective-permute-start | bytes 122888 | tf_op jit(solution)/shard_map/ppermute | solution.py:13
  447.7 13.3 %all-to-all-start.13 = ((f32[32,1,128]{2,1,0:T(1,128)}), f32[32,1,128]{2,1,0:T(1,128)S(1)}, u32[]{:S(2)}, u32[]{:S(2)}) async-start(f32[32,1,128]{2,1,0:T(1,128)} %reshape.949), calls=%async_computation.13 | async-start | bytes 32768 | tf_op jit(solution)/shard_map/all_to_all | solution.py:66
  452.8 14.6 %collective-permute-start.34 = (f32[16,640]{1,0:T(8,128)S(1)}, f32[16,640]{1,0:T(8,128)S(1)}, u32[]{:S(2)}, u32[]{:S(2)}) collective-permute-start(f32[16,640]{1,0:T(8,128)S(1)} %get-tuple-element.120), channel_id=1, source_target_pairs={{0,16},{8,24},{16,0},{24,8},{1,17},{9,25},{17,1},{25,9},{2,18},{10... | collective-permute-start | bytes 122888 | tf_op jit(solution)/shard_map/ppermute | solution.py:13
  454.7 12.8 %collective-permute-start.33 = (f32[16,640]{1,0:T(8,128)S(1)}, f32[16,640]{1,0:T(8,128)S(1)}, u32[]{:S(2)}, u32[]{:S(2)}) collective-permute-start(f32[16,640]{1,0:T(8,128)S(1)} %get-tuple-element.121), channel_id=1, source_target_pairs={{0,8},{8,0},{16,24},{24,16},{1,9},{9,1},{17,25},{25,17},{2,10},{10... | collective-permute-start | bytes 122888 | tf_op jit(solution)/shard_map/ppermute | solution.py:13
  454.7 12.8 %collective-permute-start.32 = (f32[16,640]{1,0:T(8,128)S(1)}, f32[16,640]{1,0:T(8,128)S(1)}, u32[]{:S(2)}, u32[]{:S(2)}) collective-permute-start(f32[16,640]{1,0:T(8,128)S(1)} %get-tuple-element.122), channel_id=1, source_target_pairs={{0,4},{1,5},{2,6},{3,7},{4,0},{5,1},{6,2},{7,3},{8,12},{9,13},{10,... | collective-permute-start | bytes 122888 | tf_op jit(solution)/shard_map/ppermute | solution.py:13
  488.3 14.6 %collective-permute-start.35 = (f32[16,640]{1,0:T(8,128)S(1)}, f32[16,640]{1,0:T(8,128)S(1)}, u32[]{:S(2)}, u32[]{:S(2)}) collective-permute-start(f32[16,640]{1,0:T(8,128)S(1)} %get-tuple-element.114), channel_id=1, source_target_pairs={{0,1},{1,0},{2,3},{3,2},{4,5},{5,4},{6,7},{7,6},{8,9},{9,8},{10,11... | collective-permute-start | bytes 122888 | tf_op jit(solution)/shard_map/ppermute | solution.py:13
  490.0 12.9 %collective-permute-start.39 = (f32[16,640]{1,0:T(8,128)S(1)}, f32[16,640]{1,0:T(8,128)S(1)}, u32[]{:S(2)}, u32[]{:S(2)}) collective-permute-start(f32[16,640]{1,0:T(8,128)S(1)} %get-tuple-element.115), channel_id=1, source_target_pairs={{0,16},{8,24},{16,0},{24,8},{1,17},{9,25},{17,1},{25,9},{2,18},{10... | collective-permute-start | bytes 122888 | tf_op jit(solution)/shard_map/ppermute | solution.py:13
  491.5 11.4 %collective-permute-start.38 = (f32[16,640]{1,0:T(8,128)S(1)}, f32[16,640]{1,0:T(8,128)S(1)}, u32[]{:S(2)}, u32[]{:S(2)}) collective-permute-start(f32[16,640]{1,0:T(8,128)S(1)} %get-tuple-element.116), channel_id=1, source_target_pairs={{0,8},{8,0},{16,24},{24,16},{1,9},{9,1},{17,25},{25,17},{2,10},{10... | collective-permute-start | bytes 122888 | tf_op jit(solution)/shard_map/ppermute | solution.py:13
  491.5 11.4 %collective-permute-start.37 = (f32[16,640]{1,0:T(8,128)S(1)}, f32[16,640]{1,0:T(8,128)S(1)}, u32[]{:S(2)}, u32[]{:S(2)}) collective-permute-start(f32[16,640]{1,0:T(8,128)S(1)} %get-tuple-element.117), channel_id=1, source_target_pairs={{0,4},{1,5},{2,6},{3,7},{4,0},{5,1},{6,2},{7,3},{8,12},{9,13},{10,... | collective-permute-start | bytes 122888 | tf_op jit(solution)/shard_map/ppermute | solution.py:13
  (29 other events, 451.8 us)
where the time goes:
time: 561 us; the launch traced here: 552 us
  blocking collectives  248 us (44%)
  starting transfers between devices  111 us (20%)
  waiting for transfers between devices  55.7 us (10%)
  other arithmetic  42.5 us (8%)
  local copies, waits for them, and re-layouts  42.1 us (8%)
  matrix products  40.1 us (7%)
  between operations  11.8 us (2%)
    psum x3, blocking collectives, project(): lax.psum(jnp.sum(resid * projected, axis=(1, 2)), ('organ', 'sub'))  112 us
    psum x2, blocking collectives, local(): lax.psum(jnp.sum(direction * image, axis=(1, 2)), ('organ', 'sub'))  76.5 us
    psum x3, blocking collectives, project(): coeffs = lax.psum(coeff_local, 'sub')  59.1 us
    ppermute x40, starting transfers between devices, from_partner(): return lax.ppermute(value, axis, pairs)  58 us
    all_to_all x16, waiting for transfers between devices, route(): lax.all_to_all(outgoing, ('organ', 'sub'), split_axis=1, concat_axis=1, t...  55.4 us
    all_to_all x16, starting transfers between devices, route(): lax.all_to_all(outgoing, ('organ', 'sub'), split_axis=1, concat_axis=1, t...  45.9 us
    dot_general x4, matrix products, operator(): jnp.einsum('kbn,bnm->kbm', inner, matrices, precision=lax.Precision.HIGHEST)  29.1 us
    scatter-add x8, other arithmetic, contact_term(): jnp.zeros((directions, block_len), jnp.float32).at[:, incoming_index]  16.6 us
  transfers between devices with their start and end apart: 57, of which 9 were waited for; matrix products, arithmetic and copies ran while one was open for 10% of the time, Pallas kernels for 0%

commit v1 on v0

v1 whole, which is shorter than its diff:
```python
import functools

import jax
import jax.numpy as jnp
from jax import lax
from jax.experimental import pallas as pl
from jax.experimental.pallas import tpu as pltpu
from jax.sharding import PartitionSpec as P

ITERS = 3
CAP = 8
SUB_ROUNDS = 3
AXES = ("organ", "sub")
LANES = 128
F32 = jnp.float32
BF16 = jnp.bfloat16
VMEM_LIMIT = 16 * 2**20


def iota(shape, dim):
    return lax.broadcasted_iota(jnp.int32, shape, dim)


def halves(x):
    high = x.astype(BF16)
    return high, (x - high.astype(F32)).astype(BF16)


def thirds(x):
    high = x.astype(BF16)
    rest = x - high.astype(F32)
    middle = rest.astype(BF16)
    return high, middle, (rest - middle.astype(F32)).astype(BF16)


def bdot(a, b):
    return jnp.dot(a, b, preferred_element_type=F32)


def times(x, w_high, w_low):
    rows = x.shape[0]
    a, b, c = thirds(x)
    full = bdot(jnp.concatenate([a, b, c], axis=0), w_high)
    part = bdot(jnp.concatenate([a, b], axis=0), w_low)
    low = full[2 * rows :] + part[rows:]
    return full[:rows] + (full[rows : 2 * rows] + part[:rows] + low)


def times_split(x, w):
    rows = x.shape[0]
    a, b = halves(x)
    w_high, w_low = halves(w)
    full = bdot(jnp.concatenate([a, b], axis=0), w_high)
    return full[:rows] + (full[rows:] + bdot(a, w_low))


def square(x):
    rows, cols = x.shape
    if rows < LANES:
        x = jnp.concatenate([x, jnp.zeros((LANES - rows, cols), F32)], axis=0)
    if cols < LANES:
        x = jnp.concatenate([x, jnp.zeros((x.shape[0], LANES - cols), F32)], axis=1)
    return x.T


def pack(values, ends):
    pieces = [values[:, k * ends : (k + 1) * ends] for k in range(CAP)]
    return square(jnp.concatenate(pieces, axis=0))[:ends]


def unpack(lines, rows):
    ends = lines.shape[0]
    turned = square(lines)
    pieces = [turned[k * rows : (k + 1) * rows, :ends] for k in range(CAP)]
    return jnp.concatenate(pieces, axis=1)


def put(ref, per, line, value):
    ref[pl.ds(line, value.shape[0], stride=per), :] = value


def get(ref, per, line):
    return ref[pl.ds(line, ref.shape[0] // per, stride=per), :]


def to_column(row, base, rows):
    spread = jnp.broadcast_to(row, (rows, LANES))
    here = iota((rows, LANES), 1) == iota((rows, LANES), 0) + base
    return jnp.sum(jnp.where(here, spread, 0.0), axis=1, keepdims=True)


def at_lanes(column, base):
    rows = column.shape[0]
    here = iota((rows, LANES), 1) == iota((rows, LANES), 0) + base
    return jnp.where(here, column, 0.0)


def fold(x):
    return sum(x[:, i : i + LANES] for i in range(0, x.shape[1], LANES))


def dots_row(pairs, base=0):
    total = 0.0
    for place, (left, right) in enumerate(pairs):
        acc = sum(fold(left[f] * right[f]) for f in range(left.shape[0]))
        column = jnp.sum(acc, axis=1, keepdims=True)
        total = total + at_lanes(column, base + place * column.shape[0])
    return jnp.sum(total, axis=0, keepdims=True)


def coefficients_row(field, basis):
    total = 0.0
    blocks, directions = field.shape[0], field.shape[1]
    for m in range(basis.shape[0]):
        acc = sum(fold(field[f] * basis[m, f : f + 1, :]) for f in range(blocks))
        total = total + at_lanes(jnp.sum(acc, axis=1, keepdims=True), m * directions)
    return jnp.sum(total, axis=0, keepdims=True)


def contact(mine, theirs, per_mine, per_theirs, b_high, b_low):
    own = [get(mine, per_mine, i) for i in range(2)]
    other = [get(theirs, per_theirs, i) for i in range(2)]
    gaps = jnp.concatenate([own[0] + other[1], own[1] + other[0]], axis=0)
    directions = LANES // CAP
    return times(unpack(gaps, directions), b_high[...], b_low[...])


def send_contact(message, per, surface, t_high, t_low):
    devices = message.shape[0] // per
    lines = pack(times(surface, t_high[...], t_low[...]), 2 * devices)
    put(message, per, 0, lines[:devices])
    put(message, per, 1, lines[devices:])


def spread_rows(message, per, line, row):
    put(message, per, line, jnp.broadcast_to(row, (message.shape[0] // per, LANES)))


def ranks(owner_row, active_row, count):
    rows = owner_row.shape[1]
    up, across = iota((rows, rows), 0), iota((rows, rows), 1)
    diagonal = up == across

    def column(row):
        return jnp.sum(jnp.where(diagonal, row, 0), axis=1, keepdims=True)

    live_row = jnp.where(iota((1, rows), 1) < count, active_row, 0)
    owner_col, live_col = column(owner_row), column(live_row)
    same = owner_col == owner_row
    rank_col = jnp.sum(jnp.where(same & (across < up), live_row, 0), axis=1, keepdims=True)
    rank_row = jnp.sum(jnp.where(same & (up < across), live_col, 0), axis=0, keepdims=True)
    return column, live_row, live_col, owner_col, rank_row, rank_col


def setup_kernel(count, owner, dofs, active, basis, message):
    devices = message.shape[0]
    rows = owner.shape[1]
    column, live_row, _, _, _, rank_col = ranks(owner[...], active[...], count[0])
    named = (iota((devices, rows), 0) == owner[...]) & (live_row > 0)
    slots = jnp.where(iota((rows, LANES), 1) == rank_col, column(dofs[...]) + 1, 0)
    lines = jnp.dot(
        jnp.where(named, 1.0, 0.0),
        slots.astype(F32),
        precision=lax.Precision.HIGHEST,
        preferred_element_type=F32,
    )
    modes = basis.shape[0]
    lane = iota((1, LANES), 1)
    gram = jnp.zeros((1, LANES), F32)
    for i in range(modes):
        for j in range(i + 1):
            value = jnp.sum(fold(basis[i] * basis[j]), axis=0, keepdims=True)
            value = jnp.sum(value, axis=1, keepdims=True)
            gram = jnp.where(lane == LANES // 2 + 8 * i + j, value, gram)
    message[...] = jnp.where(iota((devices, LANES), 1) < CAP, lines, gram)


def slots_kernel(devices, count, owner, active, mortar, a_high, a_low, t_high, t_low):
    rows = owner.shape[1]
    ends = 2 * devices
    width = CAP * ends
    _, live_row, live_col, owner_col, rank_row, rank_col = ranks(
        owner[...], active[...], count[0]
    )
    slot_row = jnp.where(live_row > 0, rank_row * ends + owner[...], -1)
    slot_col = jnp.where(live_col > 0, rank_col * ends + owner_col, -1)
    pick = jnp.where(iota((width, rows), 0) == slot_row, 1.0, 0.0).astype(BF16)
    pick_t = jnp.where(iota((rows, width), 1) == slot_col, 1.0, 0.0).astype(BF16)
    for part, straight, turned in zip(
        halves(mortar[...]), (a_high, a_low), (t_high, t_low), strict=True
    ):
        straight[...] = bdot(pick, part).astype(BF16)
        turned[...] = bdot(part.astype(F32).T.astype(BF16), pick_t).astype(BF16)


def first_kernel(
    organs,
    matches,
    arrived,
    a_high,
    a_low,
    at_high,
    at_low,
    basis,
    start,
    right,
    message,
    b_high,
    t_high,
    modes_ref,
    *sends,
):
    devices = arrived.shape[0]
    subs = devices // organs
    ends = 2 * devices
    length = basis.shape[2]
    modes, blocks = basis.shape[0], basis.shape[1]
    directions = start.shape[1]
    dofs = arrived[...]
    place = iota((devices, length), 1).astype(F32) + 1.0
    for k in range(CAP):
        base = k * ends
        b_high[base : base + devices, :] = a_high[base : base + devices, :]
        unit = jnp.where(place == dofs[:, k : k + 1], -1.0, 0.0).astype(BF16)
        b_high[base + devices : base + ends, :] = unit
    turned = square(dofs)[:CAP, :devices]
    empty = jnp.zeros((1, devices), F32)
    pieces = []
    for k in range(CAP):
        pieces += [empty, turned[k : k + 1, :]]
    dof_row = jnp.concatenate(pieces, axis=1)
    place_t = iota((length, CAP * ends), 0).astype(F32) + 1.0
    unit_t = jnp.where(place_t == dof_row, -1.0, 0.0).astype(BF16)
    t_high[...] = at_high[...] + unit_t
    mine = lax.axis_index("organ") * subs
    total = jnp.sum(arrived[pl.ds(pl.multiple_of(mine, 8), subs), :], axis=0, keepdims=True)
    lane = iota((1, LANES), 1)

    def entry(i, j):
        here = lane == LANES // 2 + 8 * i + j
        return jnp.sum(jnp.where(here, total, 0.0), axis=1, keepdims=True)

    low, inverse = {}, {}
    for j in range(modes):
        pivot = entry(j, j) - sum(low[j, k] * low[j, k] for k in range(j))
        inverse[j, j] = 1.0 / jnp.sqrt(pivot)
        for i in range(j + 1, modes):
            value = entry(i, j) - sum(low[i, k] * low[j, k] for k in range(j))
            low[i, j] = value * inverse[j, j]
    for j in range(modes):
        for i in range(j + 1, modes):
            value = sum(low[i, k] * inverse[k, j] for k in range(j, i))
            inverse[i, j] = -inverse[i, i] * value
    for i in range(modes):
        modes_ref[i] = sum(inverse[i, j] * basis[j] for j in range(i + 1))
    for r in range(blocks):
        face = matches[r]
        sends[r][0:directions, :] = start[face]
        for m in range(modes):
            sends[r][directions + m : directions + m + 1, :] = modes_ref[m, pl.ds(face, 1), :]
        for m in range(modes, 8):
            sends[r][directions + m : directions + m + 1, :] = jnp.zeros((1, length), F32)
    first = [modes_ref[m, 0:1, :] for m in range(modes)]
    extra = jnp.zeros((2 * 16 - directions - modes, length), F32)
    both = jnp.concatenate([start[0]] + first + [extra], axis=0)
    values = times(both, t_high[...], at_low[...])
    lines = pack(values[:directions], ends)
    put(message, 4, 0, lines[:devices])
    put(message, 4, 1, lines[devices:])
    lines = pack(values[directions : directions + 8], ends)
    half = LANES // 2
    put(message, 4, 2, jnp.concatenate([lines[:devices, :half], lines[devices:, :half]], axis=1))
    spread_rows(message, 4, 3, coefficients_row(right, modes_ref))


def smooth(inner, matrices, smoothed):
    for f in range(inner.shape[0]):
        smoothed[f] = times_split(inner[f], matrices[f])


def jump_faces(matches, field, faces, result):
    rows = field.shape[1]
    for r, face in enumerate(faces):
        result[matches[r]] = field[matches[r]] - face[0:rows, :]


def start_kernel(
    organs, matches, sent, arrived, f0, f1, f2, f3, f4, start, modes_ref, b_high, b_low, t_high,
    t_low, matrices, message, smoothed, jump_modes, s0, s1, s2, s3, s4, inner,
):
    faces = (f0, f1, f2, f3, f4)
    devices = sent.shape[0] // 4
    subs = devices // organs
    directions = start.shape[1]
    modes, blocks = modes_ref.shape[0], modes_ref.shape[1]
    jump_faces(matches, start, faces, inner)
    inner[0] += contact(sent, arrived, 4, 4, b_high, b_low)
    smooth(inner, matrices, smoothed)
    send_contact(message, 2, smoothed[0], t_high, t_low)
    for r, out in enumerate((s0, s1, s2, s3, s4)):
        out[...] = smoothed[matches[r]]
    organ = lax.axis_index("organ")
    jump_modes[...] = jnp.zeros(jump_modes.shape, F32)
    for r in range(blocks):
        face = matches[r]
        for m in range(modes):
            own = modes_ref[m, pl.ds(face, 1), :]
            other = faces[r][directions + m : directions + m + 1, :]
            if r < SUB_ROUNDS:
                own = own - other
            else:
                partner = organ ^ (1 << (r - SUB_ROUNDS))
                jump_modes[face, pl.ds(m * organs + partner, 1), :] = -other
            jump_modes[face, pl.ds(m * organs + organ, 1), :] = own
    mine = get(sent, 4, 2)
    other = get(arrived, 4, 2)
    half = LANES // 2

    def lines(x):
        return jnp.concatenate([x[:, :half], x[:, half:]], axis=0)

    def swapped(x):
        return jnp.concatenate([x[:, half:], x[:, :half]], axis=0)

    own_rows = unpack(lines(mine), 8)
    other_rows = unpack(swapped(other), 8)
    source = lax.rem(iota(other_rows.shape, 1), devices) // subs
    stack = []
    for o in range(organs):
        owns = jnp.where(organ == o, 1.0, 0.0)
        stack.append(jnp.where(source == o, other_rows, 0.0) + owns * own_rows)
    added = times(jnp.concatenate(stack, axis=0), b_high[...], b_low[...])
    for o in range(organs):
        for m in range(modes):
            row = pl.ds(m * organs + o, 1)
            jump_modes[0, row, :] = jump_modes[0, row, :] + added[8 * o + m : 8 * o + m + 1]


def subtract_modes(field, columns, basis, f):
    value = field
    for m, column in enumerate(columns):
        value = value - column * basis[m, f : f + 1, :]
    return value


def residual_kernel(
    organs, matches, sent, arrived, first, f0, f1, f2, f3, f4, smoothed, right, modes_ref, b_high,
    b_low, t_high, t_low, message, resid, s0, s1, s2, s3, s4, image,
):
    devices = sent.shape[0] // 2
    subs = devices // organs
    blocks, directions = right.shape[0], right.shape[1]
    jump_faces(matches, smoothed, (f0, f1, f2, f3, f4), image)
    image[0] += contact(sent, arrived, 2, 2, b_high, b_low)
    mine = pl.multiple_of(lax.axis_index("organ") * subs * 4, 8)
    block = first[pl.ds(mine, subs * 4), :]
    here = lax.rem(iota(block.shape, 0), 4) == 3
    row = jnp.sum(jnp.where(here, block, 0.0), axis=0, keepdims=True)
    columns = [to_column(row, m * directions, directions) for m in range(modes_ref.shape[0])]
    for f in range(blocks):
        resid[f] = subtract_modes(right[f], columns, modes_ref, f) - image[f]
    send_residual(matches, resid, modes_ref, t_high, t_low, message, (s0, s1, s2, s3, s4))


def send_residual(matches, resid, modes_ref, t_high, t_low, message, sends):
    for r, out in enumerate(sends):
        out[...] = resid[matches[r]]
    send_contact(message, 3, resid[0], t_high, t_low)
    spread_rows(message, 3, 2, coefficients_row(resid, modes_ref))


def inner_kernel(organs, last, older, matches, *refs):
    sent, arrived, f0, f1, f2, f3, f4, resid, modes_ref, jump_modes = refs[:10]
    b_high, b_low, t_high, t_low, matrices = refs[10:15]
    rest = list(refs[15:])
    previous = rest.pop(0) if older else None
    message, projected, inner = rest[:3]
    smoothed = rest[3]
    sends = rest[4:]
    devices = sent.shape[0] // 3
    subs = devices // organs
    blocks, directions = resid.shape[0], resid.shape[1]
    modes = modes_ref.shape[0]
    parts = get(arrived, 3, 2)
    sums = [
        jnp.sum(parts[o * subs : (o + 1) * subs], axis=0, keepdims=True) for o in range(organs)
    ]
    organ = lax.axis_index("organ")
    own = sum(jnp.where(organ == o, 1.0, 0.0) * sums[o] for o in range(organs))
    columns = [to_column(own, m * directions, directions) for m in range(modes)]
    for f in range(blocks):
        projected[f] = subtract_modes(resid[f], columns, modes_ref, f)
    turned = square(jnp.concatenate(sums, axis=0))
    left = jnp.concatenate(
        [turned[m * directions : (m + 1) * directions, :organs] for m in range(8)], axis=1
    )
    jump_faces(matches, resid, (f0, f1, f2, f3, f4), inner)
    inner[0] += contact(sent, arrived, 3, 3, b_high, b_low)
    for f in range(blocks):
        inner[f] = inner[f] - times_split(left, jump_modes[f])
    smooth(inner, matrices, smoothed)
    pairs = [(projected, projected), (inner, smoothed)]
    if older:
        pairs.append((previous, smoothed))
    row = dots_row(pairs)
    if last:
        message[...] = jnp.broadcast_to(row, message.shape)
        return
    for r, out in enumerate(sends):
        out[...] = smoothed[matches[r]]
    send_contact(message, 3, smoothed[0], t_high, t_low)
    spread_rows(message, 3, 2, row)


def step_sizes(row, older, scalars, directions):
    rho = to_column(row, 0, directions)
    curvature = to_column(row, directions, directions)
    if not older:
        return rho, None, curvature, rho / curvature
    cross = to_column(row, 2 * directions, directions)
    beta = rho / scalars[0, :, 0:1]
    curvature = curvature + beta * (2.0 * cross + beta * scalars[1, :, 0:1])
    return rho, beta, curvature, rho / curvature


def outer_kernel(older, matches, *refs):
    sent, arrived, f0, f1, f2, f3, f4, projected, inner, smoothed, total, modes_ref = refs[:12]
    b_high, b_low, t_high, t_low = refs[12:16]
    rest = list(refs[16:])
    old_direction = old_inner = old_image = scalars = None
    if older:
        old_direction, old_inner, old_image, scalars = rest[:4]
        rest = rest[4:]
    message, resid, new_total, new_scalars, image = rest[:5]
    rest = rest[5:]
    if older:
        direction, new_inner = rest[:2]
        rest = rest[2:]
    blocks, directions = projected.shape[0], projected.shape[1]
    row = jnp.sum(get(arrived, 3, 2), axis=0, keepdims=True)
    rho, beta, curvature, step = step_sizes(row, older, scalars, directions)
    new_scalars[0] = jnp.broadcast_to(rho, (directions, LANES))
    new_scalars[1] = jnp.broadcast_to(curvature, (directions, LANES))
    jump_faces(matches, smoothed, (f0, f1, f2, f3, f4), image)
    image[0] += contact(sent, arrived, 3, 3, b_high, b_low)
    for f in range(blocks):
        if older:
            image[f] = image[f] + beta * old_image[f]
            direction[f] = projected[f] + beta * old_direction[f]
            new_inner[f] = inner[f] + beta * old_inner[f]
            new_total[f] = total[f] + step * direction[f]
        else:
            new_total[f] = total[f] + step * projected[f]
        resid[f] = projected[f] - step * image[f]
    send_residual(matches, resid, modes_ref, t_high, t_low, message, rest)


def last_kernel(arrived, projected, old_direction, total, scalars, out):
    blocks, directions = projected.shape[0], projected.shape[1]
    row = jnp.sum(arrived[...], axis=0, keepdims=True)
    _, beta, _, step = step_sizes(row, True, scalars, directions)
    for f in range(blocks):
        out[:, f, :] = total[f] + step * (projected[f] + beta * old_direction[f])


def call(kernel, outs, args, smem=0, scratch=(), cost=1_000_000):
    in_specs = [pl.BlockSpec(memory_space=pltpu.SMEM)] * smem
    in_specs += [pl.BlockSpec(memory_space=pltpu.VMEM)] * (len(args) - smem)
    return pl.pallas_call(
        kernel,
        out_shape=[jax.ShapeDtypeStruct(shape, kind) for shape, kind in outs],
        in_specs=in_specs,
        out_specs=[pl.BlockSpec(memory_space=pltpu.VMEM)] * len(outs),
        scratch_shapes=list(scratch),
        compiler_params=pltpu.CompilerParams(vmem_limit_bytes=VMEM_LIMIT),
        cost_estimate=pl.CostEstimate(flops=cost, bytes_accessed=cost, transcendentals=0),
    )(*args)


def from_partner(value, axis, apart):
    mask = 2**apart
    pairs = [(source, source ^ mask) for source in range(lax.axis_size(axis))]
    return lax.ppermute(value, axis, pairs)


def exchange(message):
    return lax.all_to_all(message, AXES, split_axis=0, concat_axis=0, tiled=True)


def swap_faces(faces):
    swapped = []
    for r, face in enumerate(faces):
        axis, apart = ("sub", r) if r < SUB_ROUNDS else ("organ", r - SUB_ROUNDS)
        swapped.append(from_partner(face, axis, apart))
    return swapped


def local(
    dual_rhs, warm_start, inverse_blocks, coarse_basis, mortar_rows, match_rounds, slave_owner,
    slave_dofs, active_set, row_counts,
):
    directions, blocks, length = dual_rhs.shape[0], dual_rhs.shape[3], dual_rhs.shape[4]
    rows = mortar_rows.shape[2]
    modes = coarse_basis.shape[0]
    organs, subs = lax.axis_size("organ"), lax.axis_size("sub")
    devices = organs * subs
    width = CAP * 2 * devices
    field = (blocks, directions, length)
    right = dual_rhs.reshape(directions, blocks, length).transpose(1, 0, 2)
    start = warm_start.reshape(directions, blocks, length).transpose(1, 0, 2)
    matrices = inverse_blocks.reshape(blocks, length, length)
    basis = coarse_basis.reshape(modes, blocks, length)
    mortar = mortar_rows.reshape(rows, length)
    matches = match_rounds.reshape(-1)
    owner = slave_owner.reshape(1, rows)
    dofs = slave_dofs.reshape(1, rows)
    active = active_set.reshape(1, rows)
    count = row_counts.reshape(1)
    face = ((directions, length), F32)
    whole = (field, F32)

    (setup,) = call(
        setup_kernel, [((devices, LANES), F32)], (count, owner, dofs, active, basis), smem=1
    )
    arrived = exchange(setup)
    a_high, a_low, at_high, t_low = call(
        functools.partial(slots_kernel, devices),
        [((width, length), BF16)] * 2 + [((length, width), BF16)] * 2,
        (count, owner, active, mortar),
        smem=1,
    )
    b_low = a_low

    sent, b_high, t_high, modes_ref, *faces = call(
        functools.partial(first_kernel, organs),
        [
            ((4 * devices, LANES), F32),
            ((width, length), BF16),
            ((length, width), BF16),
            ((modes, blocks, length), F32),
        ]
        + [((directions + 8, length), F32)] * blocks,
        (matches, arrived, a_high, a_low, at_high, t_low, basis, start, right),
        smem=1,
    )
    maps = (b_high, b_low, t_high, t_low)
    first = exchange(sent)
    faces = swap_faces(faces)

    message, smoothed, jump_modes, *sends = call(
        functools.partial(start_kernel, organs),
        [((2 * devices, LANES), F32), whole, ((blocks, 8 * organs, length), F32)]
        + [face] * blocks,
        (matches, sent, first, *faces, start, modes_ref, *maps, matrices),
        smem=1,
        scratch=[pltpu.VMEM(field, F32)],
    )
    arrived = exchange(message)
    faces = swap_faces(sends)

    sent, resid, *sends = call(
        functools.partial(residual_kernel, organs),
        [((3 * devices, LANES), F32), whole] + [face] * blocks,
        (matches, message, arrived, first, *faces, smoothed, right, modes_ref, *maps),
        smem=1,
        scratch=[pltpu.VMEM(field, F32)],
    )
    total = start
    direction = inner = image = scalars = None
    for step in range(ITERS):
        older, last = step > 0, step == ITERS - 1
        arrived = exchange(sent)
        faces = swap_faces(sends)
        previous = (inner,) if older else ()
        lines = devices if last else 3 * devices
        message, projected, new_inner, smoothed, *sends = call(
            functools.partial(inner_kernel, organs, last, older),
            [((lines, LANES), F32), whole, whole, whole] + ([] if last else [face] * blocks),
            (matches, sent, arrived, *faces, resid, modes_ref, jump_modes, *maps, matrices)
            + previous,
            smem=1,
        )
        arrived = exchange(message)
        if last:
            break
        faces = swap_faces(sends)
        old = (direction, inner, image, scalars) if older else ()
        sent, resid, total, scalars, image, *more = call(
            functools.partial(outer_kernel, older),
            [((3 * devices, LANES), F32), whole, whole, ((2, directions, LANES), F32), whole]
            + ([whole] * 2 if older else [])
            + [face] * blocks,
            (matches, message, arrived, *faces, projected, new_inner, smoothed, total, modes_ref)
            + maps
            + old,
            smem=1,
        )
        if older:
            direction, inner, *sends = more
        else:
            direction, inner, sends = projected, new_inner, more
    (result,) = call(
        last_kernel,
        [((directions, blocks, length), F32)],
        (arrived, projected, direction, total, scalars),
    )
    return result.reshape(dual_rhs.shape)


def solution(mesh):
    in_specs = (
        P(None, "organ", "sub", None, None),
        P(None, "organ", "sub", None, None),
        P("organ", "sub", None, None, None),
        P(None, "organ", "sub", None, None),
        P("organ", "sub", None, None),
        P("organ", "sub", None),
        P("organ", "sub", None, None),
        P("organ", "sub", None),
        P("organ", "sub", None),
        P("organ", "sub", None),
    )
    out_specs = P(None, "organ", "sub", None, None)
    return jax.shard_map(local, mesh=mesh, in_specs=in_specs, out_specs=out_specs, check_vma=False)
```

time: 561 us -> 227 us (0.40); the launches traced: 552 us -> 225 us
  blocking collectives: 248 us -> 9.09 us
  local copies, waits for them, and re-layouts: 42.1 us -> 96.5 us
  waiting for transfers between devices: 55.7 us -> 11.3 us
  other arithmetic: 42.5 us -> 0 us
  matrix products: 40.1 us -> 0 us
  starting transfers between devices: 111 us -> 82.2 us
  Pallas kernels: 0 us -> 24.6 us
  between operations: 11.8 us -> 1.11 us
    psum x8 -> x0, blocking collectives: 248 us -> none  [the longest x3 112 us: project(): lax.psum(jnp.sum(resid * projected, axis=(1, 2)), ('organ', 'sub'))]
    unnamed x54 -> x224, local copies, waits for them, and re-layouts: 14 us -> 86.1 us
    all_to_all x17 -> x8, waiting for transfers between devices: 55.4 us -> 1.44 us  [exchange(): lax.all_to_all(message, AXES, split_axis=0, concat_axis=0, tiled=True)]
    dot_general x27 -> x0, matrix products: 39.1 us -> none  [the longest x4 29.1 us: operator(): jnp.einsum('kbn,bnm->kbm', inner, matrices, precision=lax.Precision.HIGHEST)]
    pallas_call x0 -> x11, Pallas kernels: none -> 24.6 us  [call(): pl.pallas_call(kernel, out_shape=[jax.ShapeDtypeStruct(shape, kind) for s...]
    all_to_all x17 -> x8, starting transfers between devices: 53.2 us -> 32.2 us  [exchange(): lax.all_to_all(message, AXES, split_axis=0, concat_axis=0, tiled=True)]
    scatter-add x8 -> x0, other arithmetic: 16.6 us -> none  [contact_term(): jnp.zeros((directions, block_len), jnp.float32).at[:, incoming_index]]
    all_to_all x17 -> x0, other arithmetic: 12.3 us -> none  [the longest x16 11.6 us: route(): lax.all_to_all(outgoing, ('organ', 'sub'), split_axis=1, concat_axis=1, t...]
  transfers between devices with their start and end apart: 57 -> 43, of which waited for: 9 -> 15; matrix products, arithmetic and copies ran while one was open for 10% -> 0% of each run, Pallas kernels for 0% -> 0%
where the time goes in v1:
time: 227 us; the launch traced here: 225 us
  local copies, waits for them, and re-layouts  96.5 us (43%)
  starting transfers between devices  82.2 us (36%)
  Pallas kernels  24.6 us (11%)
  waiting for transfers between devices  11.3 us (5%)
  blocking collectives  9.09 us (4%)
    unnamed x224, local copies, waits for them, and re-layouts  86.1 us
    ppermute x35, starting transfers between devices, from_partner(): return lax.ppermute(value, axis, pairs)  50.1 us
    all_to_all x8, starting transfers between devices, exchange(): lax.all_to_all(message, AXES, split_axis=0, concat_axis=0, tiled=True)  32.2 us
    pallas_call x11, Pallas kernels, call(): pl.pallas_call(kernel, out_shape=[jax.ShapeDtypeStruct(shape, kind) for s...  24.6 us
    ppermute x35, waiting for transfers between devices, from_partner(): return lax.ppermute(value, axis, pairs)  9.89 us
    all_to_all x1, blocking collectives, exchange(): lax.all_to_all(message, AXES, split_axis=0, concat_axis=0, tiled=True)  9.09 us
    all_to_all x10, local copies, waits for them, and re-layouts, exchange(): lax.all_to_all(message, AXES, split_axis=0, concat_axis=0, tiled=True)  7.53 us
  transfers between devices with their start and end apart: 43, of which 15 were waited for; matrix products, arithmetic and copies ran while one was open for 0% of the time, Pallas kernels for 0%

profile of v1, /device:TPU:0, one launch (start us, length us, event | category | flops | bytes accessed | tf_op | source)
XLA Modules:
  0.0 224.8 jit_solution(1837803799236058132)
XLA Ops:
  4.5 7.3 %all-to-all-start = ((f32[32,1,128]{2,1,0:T(1,128)}), f32[32,1,128]{2,1,0:T(1,128)S(1)}, u32[]{:S(2)}, u32[]{:S(2)}) async-start(f32[32,1,128]{2,1,0:T(1,128)} %bitcast.8), calls=%async_computation | async-start | bytes 32768 | tf_op jit(solution)/shard_map/all_to_all | solution.py:487
  21.7 2.3 %shard_map.102 = (f32[128,128]{1,0:T(8,128)}, bf16[512,640]{1,0:T(8,128)(2,1)S(1)}, bf16[640,512]{1,0:T(8,128)(2,1)S(1)}, f32[6,5,640]{2,1,0:T(8,128)S(1)}, f32[...) custom-call(s32[5]{0:T(128)S(1)} %bitcast.47, ...), custom_call_target="tpu_custom_call" | custom-call | flops 1000000 | bytes 1000000 | tf_op jit(solution)/shard_map/pallas_call | solution.py:469
  26.5 4.9 %all-to-all-start.1 = ((f32[32,4,128]{2,1,0:T(4,128)}), f32[32,4,128]{2,1,0:T(4,128)S(1)}, u32[]{:S(2)}, u32[]{:S(2)}) async-start(f32[32,4,128]{2,1,0:T(4,128)} %bitcast.15), calls=%async_computation.1 | async-start | bytes 131072 | tf_op jit(solution)/shard_map/all_to_all | solution.py:487
  31.5 1.8 collective-permute-start
  34.8 2.4 %collective-permute-start.2 = (f32[24,640]{1,0:T(8,128)}, f32[24,640]{1,0:T(8,128)S(1)}, u32[]{:S(2)}, u32[]{:S(2)}) collective-permute-start(f32[24,640]{1,0:T(8,128)} %copy-done.80), channel_id=1, source_target_pairs={{0,4},{1,5},{2,6},{3,7},{4,0},{5,1},{6,2},{7,3},{8,12},{9,13},{10,... | collective-permute-start | bytes 184328 | tf_op jit(solution)/shard_map/ppermute | solution.py:483
  38.7 2.1 collective-permute-done.2.f2
  42.6 3.3 %copy-done = f32[1,1,5,640,640]{4,3,2,1,0:T(8,128)S(1)} copy-done((f32[1,1,5,640,640]{4,3,2,1,0:T(8,128)S(1)}, f32[1,1,5,640,640]{4,3,2,1,0:T(8,128)}, u32[]{:S(2)}) %copy-start) | copy-done | bytes 8192024
  49.1 4.0 %shard_map.103 = (f32[64,128]{1,0:T(8,128)}, f32[5,16,640]{2,1,0:T(8,128)S(1)}, f32[5,32,640]{2,1,0:T(8,128)S(1)}, f32[16,640]{1,0:T(8,128)S(1)}, f32[16,640]{1,...) custom-call(s32[5]{0:T(128)S(1)} %bitcast.48, ...), custom_call_target="tpu_custom_call" | custom-call | flops 1000000 | bytes 1000000 | tf_op jit(solution)/shard_map/pallas_call | solution.py:469
  56.9 3.2 %all-to-all-start.2 = ((f32[32,2,128]{2,1,0:T(2,128)}), f32[32,2,128]{2,1,0:T(2,128)S(1)}, u32[]{:S(2)}, u32[]{:S(2)}) async-start(f32[32,2,128]{2,1,0:T(2,128)} %bitcast.18), calls=%async_computation.2 | async-start | bytes 65536 | tf_op jit(solution)/shard_map/all_to_all | solution.py:487
  60.1 1.8 collective-permute-start.5
  63.4 2.4 %collective-permute-start.7 = (f32[16,640]{1,0:T(8,128)}, f32[16,640]{1,0:T(8,128)S(1)}, u32[]{:S(2)}, u32[]{:S(2)}) collective-permute-start(f32[16,640]{1,0:T(8,128)} %copy-done.109), channel_id=1, source_target_pairs={{0,4},{1,5},{2,6},{3,7},{4,0},{5,1},{6,2},{7,3},{8,12},{9,13},{10,... | collective-permute-start | bytes 122888 | tf_op jit(solution)/shard_map/ppermute | solution.py:483
  75.8 1.7 shard_map.104
  81.9 3.4 %all-to-all-start.3 = ((f32[32,3,128]{2,1,0:T(4,128)}), f32[32,3,128]{2,1,0:T(4,128)}, u32[]{:S(2)}, u32[]{:S(2)}) async-start(f32[32,3,128]{2,1,0:T(4,128)} %all_to_all.72), calls=%async_computation.3 | async-start | bytes 131072 | tf_op jit(solution)/shard_map/all_to_all | solution.py:487
  85.3 1.8 collective-permute-start.10
  88.5 2.4 %collective-permute-start.12 = (f32[16,640]{1,0:T(8,128)}, f32[16,640]{1,0:T(8,128)}, u32[]{:S(2)}, u32[]{:S(2)}) collective-permute-start(f32[16,640]{1,0:T(8,128)} %copy-done.96), channel_id=1, source_target_pairs={{0,4},{1,5},{2,6},{3,7},{4,0},{5,1},{6,2},{7,3},{8,12},{9,13},{10,... | collective-permute-start | bytes 122888 | tf_op jit(solution)/shard_map/ppermute | solution.py:483
  95.3 3.3 %copy-done.1 = f32[1,1,5,640,640]{4,3,2,1,0:T(8,128)S(1)} copy-done((f32[1,1,5,640,640]{4,3,2,1,0:T(8,128)S(1)}, f32[1,1,5,640,640]{4,3,2,1,0:T(8,128)}, u32[]{:S(2)}) %copy-start.1) | copy-done | bytes 8192024
  100.3 3.3 %shard_map.105 = (f32[96,128]{1,0:T(8,128)S(1)}, f32[5,16,640]{2,1,0:T(8,128)S(1)}, f32[5,16,640]{2,1,0:T(8,128)S(1)}, f32[5,16,640]{2,1,0:T(8,128)S(1)}, f32[16...) custom-call(s32[5]{0:T(128)S(1)} %bitcast.50, ...), custom_call_target="tpu_custom_call" | custom-call | flops 1000000 | bytes 1000000 | tf_op jit(solution)/shard_map/pallas_call | solution.py:469
  109.4 3.3 %all-to-all-start.4 = ((f32[32,3,128]{2,1,0:T(4,128)}), f32[32,3,128]{2,1,0:T(4,128)}, u32[]{:S(2)}, u32[]{:S(2)}) async-start(f32[32,3,128]{2,1,0:T(4,128)} %all_to_all.75), calls=%async_computation.4 | async-start | bytes 131072 | tf_op jit(solution)/shard_map/all_to_all | solution.py:487
  115.8 2.5 %collective-permute-start.17 = (f32[16,640]{1,0:T(8,128)}, f32[16,640]{1,0:T(8,128)}, u32[]{:S(2)}, u32[]{:S(2)}) collective-permute-start(f32[16,640]{1,0:T(8,128)} %copy-done.97), channel_id=1, source_target_pairs={{0,4},{1,5},{2,6},{3,7},{4,0},{5,1},{6,2},{7,3},{8,12},{9,13},{10,... | collective-permute-start | bytes 122888 | tf_op jit(solution)/shard_map/ppermute | solution.py:483
  126.2 1.7 shard_map.106
  134.3 3.5 %all-to-all-start.5 = ((f32[32,3,128]{2,1,0:T(4,128)}), f32[32,3,128]{2,1,0:T(4,128)}, u32[]{:S(2)}, u32[]{:S(2)}) async-start(f32[32,3,128]{2,1,0:T(4,128)} %all_to_all.78), calls=%async_computation.5 | async-start | bytes 131072 | tf_op jit(solution)/shard_map/all_to_all | solution.py:487
  140.8 2.5 %collective-permute-start.22 = (f32[16,640]{1,0:T(8,128)}, f32[16,640]{1,0:T(8,128)}, u32[]{:S(2)}, u32[]{:S(2)}) collective-permute-start(f32[16,640]{1,0:T(8,128)} %copy-done.95), channel_id=1, source_target_pairs={{0,4},{1,5},{2,6},{3,7},{4,0},{5,1},{6,2},{7,3},{8,12},{9,13},{10,... | collective-permute-start | bytes 122888 | tf_op jit(solution)/shard_map/ppermute | solution.py:483
  147.6 3.3 %copy-done.2 = f32[1,1,5,640,640]{4,3,2,1,0:T(8,128)S(1)} copy-done((f32[1,1,5,640,640]{4,3,2,1,0:T(8,128)S(1)}, f32[1,1,5,640,640]{4,3,2,1,0:T(8,128)}, u32[]{:S(2)}) %copy-start.2) | copy-done | bytes 8192024
  153.6 3.3 %shard_map.107 = (f32[96,128]{1,0:T(8,128)S(1)}, f32[5,16,640]{2,1,0:T(8,128)S(1)}, f32[5,16,640]{2,1,0:T(8,128)S(1)}, f32[5,16,640]{2,1,0:T(8,128)S(1)}, f32[16...) custom-call(s32[5]{0:T(128)S(1)} %bitcast.52, ...), custom_call_target="tpu_custom_call" | custom-call | flops 1000000 | bytes 1000000 | tf_op jit(solution)/shard_map/pallas_call | solution.py:469
  162.6 3.3 %all-to-all-start.6 = ((f32[32,3,128]{2,1,0:T(4,128)}), f32[32,3,128]{2,1,0:T(4,128)}, u32[]{:S(2)}, u32[]{:S(2)}) async-start(f32[32,3,128]{2,1,0:T(4,128)} %all_to_all.81), calls=%async_computation.6 | async-start | bytes 131072 | tf_op jit(solution)/shard_map/all_to_all | solution.py:487
  169.1 2.5 %collective-permute-start.27 = (f32[16,640]{1,0:T(8,128)}, f32[16,640]{1,0:T(8,128)}, u32[]{:S(2)}, u32[]{:S(2)}) collective-permute-start(f32[16,640]{1,0:T(8,128)} %copy-done.98), channel_id=1, source_target_pairs={{0,4},{1,5},{2,6},{3,7},{4,0},{5,1},{6,2},{7,3},{8,12},{9,13},{10,... | collective-permute-start | bytes 122888 | tf_op jit(solution)/shard_map/ppermute | solution.py:483
  183.0 2.2 shard_map.108
  192.2 3.3 %all-to-all-start.7 = ((f32[32,3,128]{2,1,0:T(4,128)}), f32[32,3,128]{2,1,0:T(4,128)}, u32[]{:S(2)}, u32[]{:S(2)}) async-start(f32[32,3,128]{2,1,0:T(4,128)} %all_to_all.84), calls=%async_computation.7 | async-start | bytes 131072 | tf_op jit(solution)/shard_map/all_to_all | solution.py:487
  198.7 2.5 %collective-permute-start.32 = (f32[16,640]{1,0:T(8,128)}, f32[16,640]{1,0:T(8,128)}, u32[]{:S(2)}, u32[]{:S(2)}) collective-permute-start(f32[16,640]{1,0:T(8,128)} %copy-done.84), channel_id=1, source_target_pairs={{0,4},{1,5},{2,6},{3,7},{4,0},{5,1},{6,2},{7,3},{8,12},{9,13},{10,... | collective-permute-start | bytes 122888 | tf_op jit(solution)/shard_map/ppermute | solution.py:483
  205.5 3.3 %copy-done.3 = f32[1,1,5,640,640]{4,3,2,1,0:T(8,128)S(1)} copy-done((f32[1,1,5,640,640]{4,3,2,1,0:T(8,128)S(1)}, f32[1,1,5,640,640]{4,3,2,1,0:T(8,128)}, u32[]{:S(2)}) %copy-start.3) | copy-done | bytes 8192024
  210.7 3.8 %shard_map.109 = (f32[32,128]{1,0:T(8,128)S(1)}, f32[5,16,640]{2,1,0:T(8,128)S(1)}, f32[5,16,640]{2,1,0:T(8,128)}, f32[5,16,640]{2,1,0:T(8,128)}) custom-call(s32[5]{0:T(128)S(1)} %bitcast.54, f32[96,128]{1,0:T(8,128)S(1)} %get-tuple-element.130.refs_0_, f32[96,128]{1,0:T(8,128)S(1)} %all_to_all.86.refs_1_, f32[16,640]{1,0:T(8,128)S(1)} %collective-permute-done.30.refs_2_, ...), custom_call_target="tpu_custom_call" | custom-call | flops 1000000 | bytes 1000000 | tf_op jit(solution)/shard_map/pallas_call | solution.py:469
  214.5 9.1 %all_to_all.99 = f32[32,1,128]{2,1,0:T(1,128)S(1)} all-to-all(f32[32,1,128]{2,1,0:T(1,128)S(1)} %bitcast.55), channel_id=1, replica_groups=mesh['organ'=4,'sub'=8] {'organ','sub'}, dimensions={0} | all-to-all | bytes 32768 | tf_op jit(solution)/shard_map/all_to_all | solution.py:487
  (303 shorter events, 121.9 us)
Async XLA Ops:
  4.5 14.3 %all-to-all-start = ((f32[32,1,128]{2,1,0:T(1,128)}), f32[32,1,128]{2,1,0:T(1,128)S(1)}, u32[]{:S(2)}, u32[]{:S(2)}) async-start(f32[32,1,128]{2,1,0:T(1,128)} %bitcast.8), calls=%async_computation | async-start | bytes 32768 | tf_op jit(solution)/shard_map/all_to_all | solution.py:487
  26.5 16.1 %all-to-all-start.1 = ((f32[32,4,128]{2,1,0:T(4,128)}), f32[32,4,128]{2,1,0:T(4,128)S(1)}, u32[]{:S(2)}, u32[]{:S(2)}) async-start(f32[32,4,128]{2,1,0:T(4,128)} %bitcast.15), calls=%async_computation.1 | async-start | bytes 131072 | tf_op jit(solution)/shard_map/all_to_all | solution.py:487
  31.5 7.2 %collective-permute-start = (f32[24,640]{1,0:T(8,128)}, f32[24,640]{1,0:T(8,128)S(1)}, u32[]{:S(2)}, u32[]{:S(2)}) collective-permute-start(f32[24,640]{1,0:T(8,128)} %get-tuple-element.79), channel_id=1, source_target_pairs={{0,1},{1,0},{2,3},{3,2},{4,5},{5,4},{6,7},{7,6},{8,9},{9,8},{10,11... | collective-permute-start | bytes 184328 | tf_op jit(solution)/shard_map/ppermute | solution.py:483
  33.3 5.4 %collective-permute-start.1 = (f32[24,640]{1,0:T(8,128)}, f32[24,640]{1,0:T(8,128)S(1)}, u32[]{:S(2)}, u32[]{:S(2)}) collective-permute-start(f32[24,640]{1,0:T(8,128)} %copy-done.81), channel_id=1, source_target_pairs={{0,2},{1,3},{2,0},{3,1},{4,6},{5,7},{6,4},{7,5},{8,10},{9,11},{10,... | collective-permute-start | bytes 184328 | tf_op jit(solution)/shard_map/ppermute | solution.py:483
  34.8 6.0 %collective-permute-start.2 = (f32[24,640]{1,0:T(8,128)}, f32[24,640]{1,0:T(8,128)S(1)}, u32[]{:S(2)}, u32[]{:S(2)}) collective-permute-start(f32[24,640]{1,0:T(8,128)} %copy-done.80), channel_id=1, source_target_pairs={{0,4},{1,5},{2,6},{3,7},{4,0},{5,1},{6,2},{7,3},{8,12},{9,13},{10,... | collective-permute-start | bytes 184328 | tf_op jit(solution)/shard_map/ppermute | solution.py:483
  37.2 4.8 %collective-permute-start.4 = (f32[24,640]{1,0:T(8,128)}, f32[24,640]{1,0:T(8,128)S(1)}, u32[]{:S(2)}, u32[]{:S(2)}) collective-permute-start(f32[24,640]{1,0:T(8,128)} %copy-done.78), channel_id=1, source_target_pairs={{0,16},{8,24},{16,0},{24,8},{1,17},{9,25},{17,1},{25,9},{2,18},{10... | collective-permute-start | bytes 184328 | tf_op jit(solution)/shard_map/ppermute | solution.py:483
  56.9 13.9 %all-to-all-start.2 = ((f32[32,2,128]{2,1,0:T(2,128)}), f32[32,2,128]{2,1,0:T(2,128)S(1)}, u32[]{:S(2)}, u32[]{:S(2)}) async-start(f32[32,2,128]{2,1,0:T(2,128)} %bitcast.18), calls=%async_computation.2 | async-start | bytes 65536 | tf_op jit(solution)/shard_map/all_to_all | solution.py:487
  60.1 7.2 %collective-permute-start.5 = (f32[16,640]{1,0:T(8,128)}, f32[16,640]{1,0:T(8,128)S(1)}, u32[]{:S(2)}, u32[]{:S(2)}) collective-permute-start(f32[16,640]{1,0:T(8,128)} %copy-done.111), channel_id=1, source_target_pairs={{0,1},{1,0},{2,3},{3,2},{4,5},{5,4},{6,7},{7,6},{8,9},{9,8},{10,11... | collective-permute-start | bytes 122888 | tf_op jit(solution)/shard_map/ppermute | solution.py:483
  62.0 5.4 %collective-permute-start.6 = (f32[16,640]{1,0:T(8,128)}, f32[16,640]{1,0:T(8,128)S(1)}, u32[]{:S(2)}, u32[]{:S(2)}) collective-permute-start(f32[16,640]{1,0:T(8,128)} %copy-done.110), channel_id=1, source_target_pairs={{0,2},{1,3},{2,0},{3,1},{4,6},{5,7},{6,4},{7,5},{8,10},{9,11},{10,... | collective-permute-start | bytes 122888 | tf_op jit(solution)/shard_map/ppermute | solution.py:483
  63.4 5.5 %collective-permute-start.7 = (f32[16,640]{1,0:T(8,128)}, f32[16,640]{1,0:T(8,128)S(1)}, u32[]{:S(2)}, u32[]{:S(2)}) collective-permute-start(f32[16,640]{1,0:T(8,128)} %copy-done.109), channel_id=1, source_target_pairs={{0,4},{1,5},{2,6},{3,7},{4,0},{5,1},{6,2},{7,3},{8,12},{9,13},{10,... | collective-permute-start | bytes 122888 | tf_op jit(solution)/shard_map/ppermute | solution.py:483
  81.9 10.7 %all-to-all-start.3 = ((f32[32,3,128]{2,1,0:T(4,128)}), f32[32,3,128]{2,1,0:T(4,128)}, u32[]{:S(2)}, u32[]{:S(2)}) async-start(f32[32,3,128]{2,1,0:T(4,128)} %all_to_all.72), calls=%async_computation.3 | async-start | bytes 131072 | tf_op jit(solution)/shard_map/all_to_all | solution.py:487
  85.3 8.1 %collective-permute-start.10 = (f32[16,640]{1,0:T(8,128)}, f32[16,640]{1,0:T(8,128)S(1)}, u32[]{:S(2)}, u32[]{:S(2)}) collective-permute-start(f32[16,640]{1,0:T(8,128)} %copy-done.105), channel_id=1, source_target_pairs={{0,1},{1,0},{2,3},{3,2},{4,5},{5,4},{6,7},{7,6},{8,9},{9,8},{10,11... | collective-permute-start | bytes 122888 | tf_op jit(solution)/shard_map/ppermute | solution.py:483
  87.1 7.0 %collective-permute-start.11 = (f32[16,640]{1,0:T(8,128)}, f32[16,640]{1,0:T(8,128)}, u32[]{:S(2)}, u32[]{:S(2)}) collective-permute-start(f32[16,640]{1,0:T(8,128)} %copy-done.100), channel_id=1, source_target_pairs={{0,2},{1,3},{2,0},{3,1},{4,6},{5,7},{6,4},{7,5},{8,10},{9,11},{10,... | collective-permute-start | bytes 122888 | tf_op jit(solution)/shard_map/ppermute | solution.py:483
  88.5 5.7 %collective-permute-start.12 = (f32[16,640]{1,0:T(8,128)}, f32[16,640]{1,0:T(8,128)}, u32[]{:S(2)}, u32[]{:S(2)}) collective-permute-start(f32[16,640]{1,0:T(8,128)} %copy-done.96), channel_id=1, source_target_pairs={{0,4},{1,5},{2,6},{3,7},{4,0},{5,1},{6,2},{7,3},{8,12},{9,13},{10,... | collective-permute-start | bytes 122888 | tf_op jit(solution)/shard_map/ppermute | solution.py:483
  91.0 4.3 %collective-permute-start.14 = (f32[16,640]{1,0:T(8,128)}, f32[16,640]{1,0:T(8,128)}, u32[]{:S(2)}, u32[]{:S(2)}) collective-permute-start(f32[16,640]{1,0:T(8,128)} %copy-done.87), channel_id=1, source_target_pairs={{0,16},{8,24},{16,0},{24,8},{1,17},{9,25},{17,1},{25,9},{2,18},{10... | collective-permute-start | bytes 122888 | tf_op jit(solution)/shard_map/ppermute | solution.py:483
  109.4 10.5 %all-to-all-start.4 = ((f32[32,3,128]{2,1,0:T(4,128)}), f32[32,3,128]{2,1,0:T(4,128)}, u32[]{:S(2)}, u32[]{:S(2)}) async-start(f32[32,3,128]{2,1,0:T(4,128)} %all_to_all.75), calls=%async_computation.4 | async-start | bytes 131072 | tf_op jit(solution)/shard_map/all_to_all | solution.py:487
  112.6 8.1 %collective-permute-start.15 = (f32[16,640]{1,0:T(8,128)}, f32[16,640]{1,0:T(8,128)S(1)}, u32[]{:S(2)}, u32[]{:S(2)}) collective-permute-start(f32[16,640]{1,0:T(8,128)} %copy-done.106), channel_id=1, source_target_pairs={{0,1},{1,0},{2,3},{3,2},{4,5},{5,4},{6,7},{7,6},{8,9},{9,8},{10,11... | collective-permute-start | bytes 122888 | tf_op jit(solution)/shard_map/ppermute | solution.py:483
  114.3 6.5 %collective-permute-start.16 = (f32[16,640]{1,0:T(8,128)}, f32[16,640]{1,0:T(8,128)S(1)}, u32[]{:S(2)}, u32[]{:S(2)}) collective-permute-start(f32[16,640]{1,0:T(8,128)} %copy-done.101), channel_id=1, source_target_pairs={{0,2},{1,3},{2,0},{3,1},{4,6},{5,7},{6,4},{7,5},{8,10},{9,11},{10,... | collective-permute-start | bytes 122888 | tf_op jit(solution)/shard_map/ppermute | solution.py:483
  115.8 5.6 %collective-permute-start.17 = (f32[16,640]{1,0:T(8,128)}, f32[16,640]{1,0:T(8,128)}, u32[]{:S(2)}, u32[]{:S(2)}) collective-permute-start(f32[16,640]{1,0:T(8,128)} %copy-done.97), channel_id=1, source_target_pairs={{0,4},{1,5},{2,6},{3,7},{4,0},{5,1},{6,2},{7,3},{8,12},{9,13},{10,... | collective-permute-start | bytes 122888 | tf_op jit(solution)/shard_map/ppermute | solution.py:483
  118.3 4.3 %collective-permute-start.19 = (f32[16,640]{1,0:T(8,128)}, f32[16,640]{1,0:T(8,128)}, u32[]{:S(2)}, u32[]{:S(2)}) collective-permute-start(f32[16,640]{1,0:T(8,128)} %copy-done.88), channel_id=1, source_target_pairs={{0,16},{8,24},{16,0},{24,8},{1,17},{9,25},{17,1},{25,9},{2,18},{10... | collective-permute-start | bytes 122888 | tf_op jit(solution)/shard_map/ppermute | solution.py:483
  134.3 10.5 %all-to-all-start.5 = ((f32[32,3,128]{2,1,0:T(4,128)}), f32[32,3,128]{2,1,0:T(4,128)}, u32[]{:S(2)}, u32[]{:S(2)}) async-start(f32[32,3,128]{2,1,0:T(4,128)} %all_to_all.78), calls=%async_computation.5 | async-start | bytes 131072 | tf_op jit(solution)/shard_map/all_to_all | solution.py:487
  137.8 7.9 %collective-permute-start.20 = (f32[16,640]{1,0:T(8,128)}, f32[16,640]{1,0:T(8,128)S(1)}, u32[]{:S(2)}, u32[]{:S(2)}) collective-permute-start(f32[16,640]{1,0:T(8,128)} %copy-done.103), channel_id=1, source_target_pairs={{0,1},{1,0},{2,3},{3,2},{4,5},{5,4},{6,7},{7,6},{8,9},{9,8},{10,11... | collective-permute-start | bytes 122888 | tf_op jit(solution)/shard_map/ppermute | solution.py:483
  139.3 6.5 %collective-permute-start.21 = (f32[16,640]{1,0:T(8,128)}, f32[16,640]{1,0:T(8,128)S(1)}, u32[]{:S(2)}, u32[]{:S(2)}) collective-permute-start(f32[16,640]{1,0:T(8,128)} %copy-done.99), channel_id=1, source_target_pairs={{0,2},{1,3},{2,0},{3,1},{4,6},{5,7},{6,4},{7,5},{8,10},{9,11},{10,... | collective-permute-start | bytes 122888 | tf_op jit(solution)/shard_map/ppermute | solution.py:483
  140.8 5.6 %collective-permute-start.22 = (f32[16,640]{1,0:T(8,128)}, f32[16,640]{1,0:T(8,128)}, u32[]{:S(2)}, u32[]{:S(2)}) collective-permute-start(f32[16,640]{1,0:T(8,128)} %copy-done.95), channel_id=1, source_target_pairs={{0,4},{1,5},{2,6},{3,7},{4,0},{5,1},{6,2},{7,3},{8,12},{9,13},{10,... | collective-permute-start | bytes 122888 | tf_op jit(solution)/shard_map/ppermute | solution.py:483
  162.6 10.5 %all-to-all-start.6 = ((f32[32,3,128]{2,1,0:T(4,128)}), f32[32,3,128]{2,1,0:T(4,128)}, u32[]{:S(2)}, u32[]{:S(2)}) async-start(f32[32,3,128]{2,1,0:T(4,128)} %all_to_all.81), calls=%async_computation.6 | async-start | bytes 131072 | tf_op jit(solution)/shard_map/all_to_all | solution.py:487
  165.9 8.1 %collective-permute-start.25 = (f32[16,640]{1,0:T(8,128)}, f32[16,640]{1,0:T(8,128)S(1)}, u32[]{:S(2)}, u32[]{:S(2)}) collective-permute-start(f32[16,640]{1,0:T(8,128)} %copy-done.107), channel_id=1, source_target_pairs={{0,1},{1,0},{2,3},{3,2},{4,5},{5,4},{6,7},{7,6},{8,9},{9,8},{10,11... | collective-permute-start | bytes 122888 | tf_op jit(solution)/shard_map/ppermute | solution.py:483
  167.6 6.5 %collective-permute-start.26 = (f32[16,640]{1,0:T(8,128)}, f32[16,640]{1,0:T(8,128)S(1)}, u32[]{:S(2)}, u32[]{:S(2)}) collective-permute-start(f32[16,640]{1,0:T(8,128)} %copy-done.102), channel_id=1, source_target_pairs={{0,2},{1,3},{2,0},{3,1},{4,6},{5,7},{6,4},{7,5},{8,10},{9,11},{10,... | collective-permute-start | bytes 122888 | tf_op jit(solution)/shard_map/ppermute | solution.py:483
  169.1 5.6 %collective-permute-start.27 = (f32[16,640]{1,0:T(8,128)}, f32[16,640]{1,0:T(8,128)}, u32[]{:S(2)}, u32[]{:S(2)}) collective-permute-start(f32[16,640]{1,0:T(8,128)} %copy-done.98), channel_id=1, source_target_pairs={{0,4},{1,5},{2,6},{3,7},{4,0},{5,1},{6,2},{7,3},{8,12},{9,13},{10,... | collective-permute-start | bytes 122888 | tf_op jit(solution)/shard_map/ppermute | solution.py:483
  192.2 10.6 %all-to-all-start.7 = ((f32[32,3,128]{2,1,0:T(4,128)}), f32[32,3,128]{2,1,0:T(4,128)}, u32[]{:S(2)}, u32[]{:S(2)}) async-start(f32[32,3,128]{2,1,0:T(4,128)} %all_to_all.84), calls=%async_computation.7 | async-start | bytes 131072 | tf_op jit(solution)/shard_map/all_to_all | solution.py:487
  195.5 8.1 %collective-permute-start.30 = (f32[16,640]{1,0:T(8,128)}, f32[16,640]{1,0:T(8,128)S(1)}, u32[]{:S(2)}, u32[]{:S(2)}) collective-permute-start(f32[16,640]{1,0:T(8,128)} %copy-done.91), channel_id=1, source_target_pairs={{0,1},{1,0},{2,3},{3,2},{4,5},{5,4},{6,7},{7,6},{8,9},{9,8},{10,11... | collective-permute-start | bytes 122888 | tf_op jit(solution)/shard_map/ppermute | solution.py:483
  197.2 6.5 %collective-permute-start.31 = (f32[16,640]{1,0:T(8,128)}, f32[16,640]{1,0:T(8,128)S(1)}, u32[]{:S(2)}, u32[]{:S(2)}) collective-permute-start(f32[16,640]{1,0:T(8,128)} %copy-done.86), channel_id=1, source_target_pairs={{0,2},{1,3},{2,0},{3,1},{4,6},{5,7},{6,4},{7,5},{8,10},{9,11},{10,... | collective-permute-start | bytes 122888 | tf_op jit(solution)/shard_map/ppermute | solution.py:483
  198.7 5.6 %collective-permute-start.32 = (f32[16,640]{1,0:T(8,128)}, f32[16,640]{1,0:T(8,128)}, u32[]{:S(2)}, u32[]{:S(2)}) collective-permute-start(f32[16,640]{1,0:T(8,128)} %copy-done.84), channel_id=1, source_target_pairs={{0,4},{1,5},{2,6},{3,7},{4,0},{5,1},{6,2},{7,3},{8,12},{9,13},{10,... | collective-permute-start | bytes 122888 | tf_op jit(solution)/shard_map/ppermute | solution.py:483
  (123 other events, 326.0 us)

commit v2 on v1

v2 whole, which is shorter than its diff:
```python
import functools

import jax
import jax.numpy as jnp
from jax import lax
from jax.experimental import pallas as pl
from jax.experimental.pallas import tpu as pltpu
from jax.sharding import PartitionSpec as P

ITERS = 3
CAP = 8
SUB_ROUNDS = 3
ORDER = (2, 0, 1, 4, 3)
NEAR = 3
AXES = ("organ", "sub")
LANES = 128
F32 = jnp.float32
BF16 = jnp.bfloat16
VMEM_LIMIT = 24 * 2**20
COST = 2_000_000


def iota(shape, dim):
    return lax.broadcasted_iota(jnp.int32, shape, dim)


def halves(x):
    high = x.astype(BF16)
    return high, (x - high.astype(F32)).astype(BF16)


def thirds(x):
    high = x.astype(BF16)
    rest = x - high.astype(F32)
    middle = rest.astype(BF16)
    return high, middle, (rest - middle.astype(F32)).astype(BF16)


def bdot(a, b):
    return jnp.dot(a, b, preferred_element_type=F32)


def times(x, w_high, w_low):
    rows = x.shape[0]
    a, b, c = thirds(x)
    full = bdot(jnp.concatenate([a, b, c], axis=0), w_high)
    part = bdot(jnp.concatenate([a, b], axis=0), w_low)
    low = full[2 * rows :] + part[rows:]
    return full[:rows] + (full[rows : 2 * rows] + part[:rows] + low)


def times_split(x, w):
    rows = x.shape[0]
    a, b = halves(x)
    w_high, w_low = halves(w)
    full = bdot(jnp.concatenate([a, b], axis=0), w_high)
    return full[:rows] + (full[rows:] + bdot(a, w_low))


def square(x):
    rows, cols = x.shape
    if rows < LANES:
        x = jnp.concatenate([x, jnp.zeros((LANES - rows, cols), F32)], axis=0)
    if cols < LANES:
        x = jnp.concatenate([x, jnp.zeros((x.shape[0], LANES - cols), F32)], axis=1)
    return x.T


def pack(master, slave, devices):
    def stacked(x):
        pieces = [x[:, k * devices : (k + 1) * devices] for k in range(CAP)]
        return jnp.concatenate(pieces, axis=0)

    turned = square(jnp.concatenate([stacked(master), stacked(slave)], axis=1))
    return turned[:devices], turned[devices : 2 * devices]


def unpack(master, slave, rows):
    devices = master.shape[0]
    turned = square(jnp.concatenate([master, slave], axis=0))

    def laid(first):
        pieces = [
            turned[k * rows : (k + 1) * rows, first : first + devices] for k in range(CAP)
        ]
        return jnp.concatenate(pieces, axis=1)

    return laid(0), laid(devices)


def put(ref, per, line, value):
    ref[pl.ds(line, value.shape[0], stride=per), :] = value


def get(ref, per, line):
    return ref[pl.ds(line, ref.shape[0] // per, stride=per), :]


def to_column(row, base, rows):
    spread = jnp.broadcast_to(row, (rows, LANES))
    here = iota((rows, LANES), 1) == iota((rows, LANES), 0) + base
    return jnp.sum(jnp.where(here, spread, 0.0), axis=1, keepdims=True)


def at_lanes(column, base):
    rows = column.shape[0]
    here = iota((rows, LANES), 1) == iota((rows, LANES), 0) + base
    return jnp.where(here, column, 0.0)


def fold(x):
    return sum(x[:, i : i + LANES] for i in range(0, x.shape[1], LANES))


def dots_row(pairs, base=0):
    total = 0.0
    for place, (left, right) in enumerate(pairs):
        acc = sum(fold(left[f] * right[f]) for f in range(left.shape[0]))
        column = jnp.sum(acc, axis=1, keepdims=True)
        total = total + at_lanes(column, base + place * column.shape[0])
    return jnp.sum(total, axis=0, keepdims=True)


def coefficients_row(field, basis):
    total = 0.0
    blocks, directions = field.shape[0], field.shape[1]
    for m in range(basis.shape[0]):
        acc = sum(fold(field[f] * basis[m, f : f + 1, :]) for f in range(blocks))
        total = total + at_lanes(jnp.sum(acc, axis=1, keepdims=True), m * directions)
    return jnp.sum(total, axis=0, keepdims=True)


def exact(x, unit):
    rows = x.shape[0]
    full = bdot(jnp.concatenate(thirds(x), axis=0), unit)
    return full[:rows] + (full[rows : 2 * rows] + full[2 * rows :])


def contact(mine, theirs, per_mine, per_theirs, a_high, a_low, unit):
    own = [get(mine, per_mine, i) for i in range(2)]
    other = [get(theirs, per_theirs, i) for i in range(2)]
    master, slave = unpack(own[0] + other[1], own[1] + other[0], LANES // CAP)
    return times(master, a_high[...], a_low[...]) + exact(slave, unit[...])


def send_contact(message, per, surface, t_high, t_low, unit_t):
    devices = message.shape[0] // per
    master = times(surface, t_high[...], t_low[...])
    slave = exact(surface, unit_t[...])
    for line, value in enumerate(pack(master, slave, devices)):
        put(message, per, line, value)


def spread_rows(message, per, line, row):
    put(message, per, line, jnp.broadcast_to(row, (message.shape[0] // per, LANES)))


def ranks(owner_row, active_row, count):
    rows = owner_row.shape[1]
    up, across = iota((rows, rows), 0), iota((rows, rows), 1)
    diagonal = up == across

    def column(row):
        return jnp.sum(jnp.where(diagonal, row, 0), axis=1, keepdims=True)

    live_row = jnp.where(iota((1, rows), 1) < count, active_row, 0)
    owner_col, live_col = column(owner_row), column(live_row)
    same = owner_col == owner_row
    rank_col = jnp.sum(jnp.where(same & (across < up), live_row, 0), axis=1, keepdims=True)
    rank_row = jnp.sum(jnp.where(same & (up < across), live_col, 0), axis=0, keepdims=True)
    return column, live_row, live_col, owner_col, rank_row, rank_col


def load_modes(basis, modes, blocks):
    return [
        jnp.concatenate([basis[m * blocks + f] for f in range(blocks)], axis=0)
        for m in range(modes)
    ]


def setup_kernel(blocks, count, owner, dofs, active, basis, message):
    devices = message.ref.shape[0]
    rows = owner.shape[1]
    column, live_row, _, _, _, rank_col = ranks(owner[...], active[...], count[0])
    named = (iota((devices, rows), 0) == owner[...]) & (live_row > 0)
    slots = jnp.where(iota((rows, LANES), 1) == rank_col, column(dofs[...]) + 1, 0)
    lines = jnp.dot(
        jnp.where(named, 1.0, 0.0),
        slots.astype(F32),
        precision=lax.Precision.HIGHEST,
        preferred_element_type=F32,
    )
    modes = basis.shape[0] // blocks
    slabs = load_modes(basis, modes, blocks)
    lane = iota((1, LANES), 1)
    gram = jnp.zeros((1, LANES), F32)
    for i in range(modes):
        for j in range(i + 1):
            value = jnp.sum(fold(slabs[i] * slabs[j]), axis=0, keepdims=True)
            value = jnp.sum(value, axis=1, keepdims=True)
            gram = jnp.where(lane == LANES // 2 + 8 * i + j, value, gram)
    message.ref[...] = jnp.where(iota((devices, LANES), 1) < CAP, lines, gram)


def slots_kernel(
    devices, count, owner, active, mortar, start_rows, right_rows, a_high, a_low, t_high, t_low,
    start, right,
):
    rows = owner.shape[1]
    width = CAP * devices
    _, live_row, live_col, owner_col, rank_row, rank_col = ranks(
        owner[...], active[...], count[0]
    )
    slot_row = jnp.where(live_row > 0, rank_row * devices + owner[...], -1)
    slot_col = jnp.where(live_col > 0, rank_col * devices + owner_col, -1)
    pick = jnp.where(iota((width, rows), 0) == slot_row, 1.0, 0.0).astype(BF16)
    pick_t = jnp.where(iota((rows, width), 1) == slot_col, 1.0, 0.0).astype(BF16)
    blocks, directions = start.ref.shape[0], start.ref.shape[1]
    for source, target in ((start_rows(), start), (right_rows(), right)):
        for f in range(blocks):
            for c in range(directions):
                target.ref[f, c : c + 1, :] = source[c * blocks + f]
        target.flush()
    for part, straight, turned in zip(
        halves(mortar()[...]), (a_high, a_low), (t_high, t_low), strict=True
    ):
        straight.ref[...] = bdot(pick, part).astype(BF16)
        straight.flush()
        turned.ref[...] = bdot(part.astype(F32).T.astype(BF16), pick_t).astype(BF16)
        turned.flush()


def first_kernel(
    organs, matches, arrived, basis, start, t_high, t_low, right, message, unit_t, unit,
    modes_out, *sends,
):
    devices = arrived.shape[0]
    subs = devices // organs
    blocks = len(sends)
    modes = basis.shape[0] // blocks
    length = basis.shape[2]
    dofs = arrived[...]
    turned = square(dofs)[:CAP, :devices]
    dof_row = jnp.concatenate([turned[k : k + 1, :] for k in range(CAP)], axis=1)
    place_t = iota((length, CAP * devices), 0).astype(F32) + 1.0
    unit_t.ref[...] = jnp.where(place_t == dof_row, -1.0, 0.0).astype(BF16)
    unit_t.flush()
    mine = lax.axis_index("organ") * subs
    total = jnp.sum(arrived[pl.ds(pl.multiple_of(mine, 8), subs), :], axis=0, keepdims=True)
    lane = iota((1, LANES), 1)

    def entry(i, j):
        here = lane == LANES // 2 + 8 * i + j
        return jnp.sum(jnp.where(here, total, 0.0), axis=1, keepdims=True)

    low, inverse = {}, {}
    for j in range(modes):
        pivot = entry(j, j) - sum(low[j, k] * low[j, k] for k in range(j))
        inverse[j, j] = 1.0 / jnp.sqrt(pivot)
        for i in range(j + 1, modes):
            value = entry(i, j) - sum(low[i, k] * low[j, k] for k in range(j))
            low[i, j] = value * inverse[j, j]
    for j in range(modes):
        for i in range(j + 1, modes):
            value = sum(low[i, k] * inverse[k, j] for k in range(j, i))
            inverse[i, j] = -inverse[i, i] * value
    slabs = load_modes(basis, modes, blocks)
    modes_ref = modes_out.ref
    for i in range(modes):
        modes_ref[i] = sum(inverse[i, j] * slabs[j] for j in range(i + 1))
    modes_out.flush()
    start = start()
    directions = start.shape[1]
    for r in range(blocks):
        face = matches[r]
        send = sends[r].ref
        send[0:directions, :] = start[face]
        for m in range(modes):
            send[directions + m : directions + m + 1, :] = modes_ref[m, pl.ds(face, 1), :]
        for m in range(modes, 8):
            send[directions + m : directions + m + 1, :] = jnp.zeros((1, length), F32)
        sends[r].flush()
    first = [modes_ref[m, 0:1, :] for m in range(modes)]
    extra = jnp.zeros((2 * 16 - directions - modes, length), F32)
    both = jnp.concatenate([start[0]] + first + [extra], axis=0)
    master = times(both, t_high()[...], t_low()[...])
    slave = exact(both, unit_t.ref[...])
    for line, value in enumerate(pack(master[:directions], slave[:directions], devices)):
        put(message.ref, 4, line, value)
    rows = slice(directions, directions + 8)
    lines = pack(master[rows], slave[rows], devices)
    half = LANES // 2
    put(message.ref, 4, 2, jnp.concatenate([line[:, :half] for line in lines], axis=1))
    spread_rows(message.ref, 4, 3, coefficients_row(right(), modes_ref))
    message.flush()
    place = iota((devices, length), 1).astype(F32) + 1.0
    for k in range(CAP):
        block = jnp.where(place == dofs[:, k : k + 1], -1.0, 0.0).astype(BF16)
        unit.ref[k * devices : (k + 1) * devices, :] = block


def smooth(inner, near, far, smoothed, f):
    early = near.shape[0]
    matrix = near[f] if f < early else far(f - early)[...]
    smoothed[f] = times_split(inner[f], matrix)


def fetch(matrices, near, sems):
    copies = [
        pltpu.make_async_copy(matrices.at[f], near.at[f], sems.at[f])
        for f in range(near.shape[0])
    ]
    for copy in copies:
        copy.start()
    return copies


def subtract_modes(field, columns, basis, f):
    value = field
    for m, column in enumerate(columns):
        value = value - column * basis[m, f : f + 1, :]
    return value


def start_contact(
    organs, arrived, sent, start, a_high, a_low, unit, modes_ref, right, matrices, new_right,
    base, added, near, sems,
):
    sent, start, maps = sent(), start(), (a_high(), a_low(), unit())
    copies = fetch(matrices, near, sems)
    devices = sent.shape[0] // 4
    subs = devices // organs
    blocks, directions = start.shape[0], start.shape[1]
    base[...] = start[...]
    base[0] += contact(sent, arrived, 4, 4, *maps)
    modes_ref, right = modes_ref(), right()
    organ = lax.axis_index("organ")
    block = arrived[pl.ds(pl.multiple_of(organ * subs * 4, 8), subs * 4), :]
    here = lax.rem(iota(block.shape, 0), 4) == 3
    row = jnp.sum(jnp.where(here, block, 0.0), axis=0, keepdims=True)
    columns = [to_column(row, m * directions, directions) for m in range(modes_ref.shape[0])]
    for f in range(blocks):
        new_right.ref[f] = subtract_modes(right[f], columns, modes_ref, f)
    new_right.flush()
    half = LANES // 2
    mine, other = get(sent, 4, 2), get(arrived, 4, 2)
    own_rows = unpack(mine[:, :half], mine[:, half:], 8)
    other_rows = unpack(other[:, half:], other[:, :half], 8)
    source = lax.rem(iota(own_rows[0].shape, 1), devices) // subs
    stacks = []
    for own_half, other_half in zip(own_rows, other_rows, strict=True):
        stack = []
        for o in range(organs):
            owns = jnp.where(organ == o, 1.0, 0.0)
            stack.append(jnp.where(source == o, other_half, 0.0) + owns * own_half)
        stacks.append(jnp.concatenate(stack, axis=0))
    added[...] = times(stacks[0], maps[0][...], maps[1][...]) + exact(stacks[1], maps[2][...])
    for copy in copies:
        copy.wait()


def start_kernel(
    organs, matches, f0, f1, f2, f3, f4, base, added, near, t_high, t_low, unit_t, modes_ref, far,
    message, smoothed_out, jump_out, s0, s1, s2, s3, s4, inner,
):
    faces = (f0, f1, f2, f3, f4)
    smoothed = smoothed_out.ref
    blocks, directions = base.shape[0], base.shape[1]
    for r, face in zip(ORDER, faces, strict=True):
        inner[matches[r]] = base[matches[r]] - face[0:directions, :]
    for f in range(blocks):
        smooth(inner, near, far, smoothed, f)
    for r, send in enumerate((s0, s1, s2, s3, s4)):
        send(smoothed.at[matches[r]])
    smoothed_out.flush()
    send_contact(message.ref, 2, smoothed[0], t_high(), t_low(), unit_t())
    message.flush()
    modes_ref = modes_ref()
    modes = modes_ref.shape[0]
    jump_modes = jump_out.ref
    organ = lax.axis_index("organ")
    jump_modes[...] = jnp.zeros(jump_modes.shape, F32)
    for r, values in zip(ORDER, faces, strict=True):
        face = matches[r]
        for m in range(modes):
            own = modes_ref[m, pl.ds(face, 1), :]
            other = values[directions + m : directions + m + 1, :]
            if r < SUB_ROUNDS:
                own = own - other
            else:
                partner = organ ^ (1 << (r - SUB_ROUNDS))
                jump_modes[face, pl.ds(m * organs + partner, 1), :] = -other
            jump_modes[face, pl.ds(m * organs + organ, 1), :] = own
    for o in range(organs):
        for m in range(modes):
            row = pl.ds(m * organs + o, 1)
            jump_modes[0, row, :] = jump_modes[0, row, :] + added[8 * o + m : 8 * o + m + 1, :]


def residual_contact(arrived, sent, smoothed, a_high, a_low, unit, right, part):
    sent, smoothed, right = sent(), smoothed(), right()
    part[...] = right[...] - smoothed[...]
    part[0] -= contact(sent, arrived, 2, 2, a_high(), a_low(), unit())


def residual_kernel(
    matches, f0, f1, f2, f3, f4, part, t_high, t_low, unit_t, modes_ref, message, resid, *sends
):
    for r, face in zip(ORDER, (f0, f1, f2, f3, f4), strict=True):
        resid.ref[matches[r]] = part[matches[r]] + face[...]
    send_residual(matches, resid, modes_ref, (t_high, t_low, unit_t), message, sends)


def send_residual(matches, resid, modes_ref, maps, message, sends):
    for r, send in enumerate(sends):
        send(resid.ref.at[matches[r]])
    resid.flush()
    send_contact(message.ref, 4, resid.ref[0], *(late() for late in maps))
    spread_rows(message.ref, 4, 2, coefficients_row(resid.ref, modes_ref()))
    message.flush()


def inner_contact(
    organs, arrived, sent, resid, a_high, a_low, unit, modes_ref, jump_modes, matrices,
    projected_out, base, near, norms, sems,
):
    sent, resid, maps = sent(), resid(), (a_high(), a_low(), unit())
    modes_ref, jump_modes = modes_ref(), jump_modes()
    copies = fetch(matrices, near, sems)
    devices = sent.shape[0] // 4
    subs = devices // organs
    blocks, directions = resid.shape[0], resid.shape[1]
    parts = get(arrived, 4, 2)
    sums = [
        jnp.sum(parts[o * subs : (o + 1) * subs], axis=0, keepdims=True) for o in range(organs)
    ]
    added = contact(sent, arrived, 4, 4, *maps)
    turned = square(jnp.concatenate(sums, axis=0))
    left = jnp.concatenate(
        [turned[m * directions : (m + 1) * directions, :organs] for m in range(8)], axis=1
    )
    organ = lax.axis_index("organ")
    own = sum(jnp.where(organ == o, 1.0, 0.0) * sums[o] for o in range(organs))
    columns = [to_column(own, m * directions, directions) for m in range(modes_ref.shape[0])]
    projected = projected_out.ref
    for f in range(blocks):
        projected[f] = subtract_modes(resid[f], columns, modes_ref, f)
    projected_out.flush()
    for f in range(blocks):
        value = resid[f] - times_split(left, jump_modes[f])
        base[f] = value + added if f == 0 else value
    norms[...] = jnp.broadcast_to(dots_row([(projected, projected)]), norms.shape)
    for copy in copies:
        copy.wait()


def inner_kernel(last, older, matches, f0, f1, f2, f3, f4, base, near, norms, *refs):
    rest = list(refs)
    previous = rest.pop(0) if older else None
    maps = None if last else rest[:3]
    far, message = rest[0 if last else 3 :][:2]
    rest = rest[2 if last else 5 :]
    if last:
        inner, smoothed = rest
    else:
        inner_out, smoothed_out = rest[:2]
        inner, smoothed = inner_out.ref, smoothed_out.ref
    for r, face in zip(ORDER, (f0, f1, f2, f3, f4), strict=True):
        inner[matches[r]] = base[matches[r]] - face[...]
    for f in range(inner.shape[0]):
        smooth(inner, near, far, smoothed, f)
    if not last:
        for r, send in enumerate(rest[2:]):
            send(smoothed.at[matches[r]])
        inner_out.flush()
        smoothed_out.flush()
        send_contact(message.ref, 4, smoothed[0], *(late() for late in maps))
    directions = inner.shape[1]
    pairs = [(inner, smoothed)]
    if older:
        pairs.append((previous(), smoothed))
    row = dots_row(pairs, directions) + norms[0:1, :]
    if last:
        message.ref[...] = jnp.broadcast_to(row, message.ref.shape)
    else:
        spread_rows(message.ref, 4, 2, row)


def step_sizes(row, older, scalars, directions):
    rho = to_column(row, 0, directions)
    curvature = to_column(row, directions, directions)
    if not older:
        return rho, None, curvature, rho / curvature
    cross = to_column(row, 2 * directions, directions)
    beta = rho / scalars[0, :, 0:1]
    curvature = curvature + beta * (2.0 * cross + beta * scalars[1, :, 0:1])
    return rho, beta, curvature, rho / curvature


def outer_contact(older, arrived, sent, smoothed, a_high, a_low, unit, projected, *refs):
    rest = list(refs)
    old_image = scalars = None
    if older:
        old_image, scalars = rest[0](), rest[1]()
        rest = rest[2:]
    new_scalars, part, steps, image = rest
    sent, smoothed, projected = sent(), smoothed(), projected()
    blocks, directions = smoothed.shape[0], smoothed.shape[1]
    row = jnp.sum(get(arrived, 4, 2), axis=0, keepdims=True)
    rho, beta, curvature, step = step_sizes(row, older, scalars, directions)
    wide = (directions, LANES)
    for place, column in enumerate((rho, curvature, step) + ((beta,) if older else ())):
        new_scalars.ref[place] = jnp.broadcast_to(column, wide)
    new_scalars.flush()
    steps[...] = jnp.broadcast_to(step, wide)
    added = contact(sent, arrived, 4, 4, a_high(), a_low(), unit())
    for f in range(blocks):
        value = smoothed[f]
        if f == 0:
            value = value + added
        if older:
            value = value + beta * old_image[f]
        image[f] = value
        part[f] = projected[f] - step * value


def outer_kernel(older, matches, f0, f1, f2, f3, f4, part, steps, image, *refs):
    t_high, t_low, unit_t, modes_ref = refs[:4]
    rest = list(refs[4:])
    if older:
        message, resid = rest[:2]
        sends = rest[2:]
    else:
        message, resid, new_image = rest[:3]
        sends = rest[3:]
    step = steps[:, 0:1]
    for r, face in zip(ORDER, (f0, f1, f2, f3, f4), strict=True):
        resid.ref[matches[r]] = part[matches[r]] + step * face[...]
        if not older:
            new_image.ref[matches[r]] = image[matches[r]] - face[...]
    send_residual(matches, resid, modes_ref, (t_high, t_low, unit_t), message, sends)


def update_kernel(older, projected, inner, total, scalars, *refs):
    projected, inner, total, scalars = (late() for late in (projected, inner, total, scalars))
    rest = list(refs)
    step = scalars[2, :, 0:1]
    if not older:
        for f in range(total.shape[0]):
            rest[0].ref[f] = total[f] + step * projected[f]
        return
    old_direction, old_inner = rest[0](), rest[1]()
    new_total, direction, new_inner = (out.ref for out in rest[2:])
    beta = scalars[3, :, 0:1]
    for f in range(total.shape[0]):
        value = projected[f] + beta * old_direction[f]
        direction[f] = value
        new_total[f] = total[f] + step * value
        new_inner[f] = inner[f] + beta * old_inner[f]


def last_kernel(arrived, projected, old_direction, total, scalars, out):
    projected, old_direction, total, scalars = (
        late() for late in (projected, old_direction, total, scalars)
    )
    blocks, directions = projected.shape[0], projected.shape[1]
    row = jnp.sum(arrived[...], axis=0, keepdims=True)
    _, beta, _, step = step_sizes(row, True, scalars, directions)
    for f in range(blocks):
        value = total[f] + step * (projected[f] + beta * old_direction[f])
        for c in range(directions):
            out.ref[c * blocks + f] = value[c : c + 1]


class Late:
    def __init__(self, source, target, sems):
        self.target = target
        if sems.shape[0] == 1:
            self.copies = [pltpu.make_async_copy(source, target, sems.at[0])]
        else:
            self.copies = [
                pltpu.make_async_copy(source.at[i], target.at[i], sems.at[i])
                for i in range(sems.shape[0])
            ]
        self.waiting = [True] * len(self.copies)
        for copy in self.copies:
            copy.start()

    def __call__(self, part=None):
        for i, copy in enumerate(self.copies):
            if self.waiting[i] and part in (None, i):
                copy.wait()
                self.waiting[i] = False
        return self.target if part is None else self.target.at[part]


class Send:
    def __init__(self, target, sem):
        self.target, self.sem, self.copy = target, sem, None

    def __call__(self, source):
        self.copy = pltpu.make_async_copy(source, self.target, self.sem)
        self.copy.start()


class Out:
    def __init__(self, ref, target, sem):
        self.ref = ref
        self.copy = pltpu.make_async_copy(ref, target, sem)
        self.started = False

    def flush(self):
        if not self.started:
            self.copy.start()
            self.started = True


def call(kernel, outs, args, late=(), smem=0, near=(), sends=(), scratch=(), whole=(), far=()):
    n_late, n_out, n_arg, n_near = len(late), len(outs), len(args), len(near)

    def body(*refs):
        refs = list(refs)

        def take(n):
            taken = refs[:n]
            del refs[:n]
            return taken

        given, sources, lasting = take(n_arg), take(n_late), take(len(whole))
        remote = take(len(far))
        targets, ports, close = take(n_out), take(len(sends)), take(n_near)
        buffers, ahead, results = take(n_late), take(len(far)), take(n_out)
        extra = take(len(scratch))
        in_sems, far_sems, out_sem = take(n_late), take(len(far)), refs[0]
        lates = [Late(s, b, m) for s, b, m in zip(sources, buffers, in_sems, strict=True)]
        for source, buffer, sem in zip(remote, ahead, far_sems, strict=True):
            skip = source.shape[0] - buffer.shape[0]
            lates.append(Late(source.at[pl.ds(skip, buffer.shape[0])], buffer, sem))
        written = [Out(r, t, out_sem.at[i]) for i, (r, t) in enumerate(zip(results, targets))]
        posts = [Send(t, out_sem.at[n_out + i]) for i, t in enumerate(ports)]
        kernel(*given, *lates, *lasting, *written, *posts, *close, *extra)
        for item in lates:
            item()
        for item in written:
            item.flush()
        for item in written + posts:
            item.copy.wait()

    in_specs = [pl.BlockSpec(memory_space=pltpu.SMEM)] * smem
    in_specs += [pl.BlockSpec(memory_space=pltpu.VMEM)] * (n_arg - smem)
    remote = tuple(late) + tuple(whole) + tuple(a for a, _ in far)
    in_specs += [pl.BlockSpec(memory_space=pltpu.HBM)] * len(remote)
    out_specs = [pl.BlockSpec(memory_space=pltpu.HBM)] * (n_out + len(sends))
    out_specs += [pl.BlockSpec(memory_space=pltpu.VMEM)] * n_near
    scratch_shapes = [pltpu.VMEM(a.shape, a.dtype) for a in late]
    scratch_shapes += [pltpu.VMEM((n,) + a.shape[1:], a.dtype) for a, n in far]
    scratch_shapes += [pltpu.VMEM(shape, kind) for shape, kind in outs]
    scratch_shapes += list(scratch)
    scratch_shapes += [pltpu.SemaphoreType.DMA((1,))] * n_late
    scratch_shapes += [pltpu.SemaphoreType.DMA((n,)) for _, n in far]
    scratch_shapes += [pltpu.SemaphoreType.DMA((max(n_out + len(sends), 1),))]
    return pl.pallas_call(
        body,
        out_shape=[pltpu.HBM(shape, kind) for shape, kind in tuple(outs) + tuple(sends)]
        + [pltpu.VMEM(shape, kind) for shape, kind in near],
        in_specs=in_specs,
        out_specs=out_specs,
        scratch_shapes=scratch_shapes,
        compiler_params=pltpu.CompilerParams(vmem_limit_bytes=VMEM_LIMIT),
        cost_estimate=pl.CostEstimate(
            flops=COST, bytes_accessed=COST, transcendentals=0
        ),
    )(*args, *(pltpu.with_memory_space_constraint(a, pltpu.HBM) for a in remote))


def from_partner(value, axis, apart):
    mask = 2**apart
    pairs = [(source, source ^ mask) for source in range(lax.axis_size(axis))]
    return lax.ppermute(value, axis, pairs)


def exchange(message):
    return lax.all_to_all(message, AXES, split_axis=0, concat_axis=0, tiled=True)


def swap_faces(faces):
    swapped = []
    for r in ORDER:
        axis, apart = ("sub", r) if r < SUB_ROUNDS else ("organ", r - SUB_ROUNDS)
        swapped.append(from_partner(faces[r], axis, apart))
    return swapped


def local(
    dual_rhs, warm_start, inverse_blocks, coarse_basis, mortar_rows, match_rounds, slave_owner,
    slave_dofs, active_set, row_counts,
):
    directions, blocks, length = dual_rhs.shape[0], dual_rhs.shape[3], dual_rhs.shape[4]
    rows = mortar_rows.shape[2]
    modes = coarse_basis.shape[0]
    organs, subs = lax.axis_size("organ"), lax.axis_size("sub")
    devices = organs * subs
    width = CAP * devices
    field = (blocks, directions, length)
    right_rows = dual_rhs.reshape(directions * blocks, 1, length)
    start_rows = warm_start.reshape(directions * blocks, 1, length)
    matrices = inverse_blocks.reshape(blocks, length, length)
    basis = coarse_basis.reshape(modes * blocks, 1, length)
    mortar = mortar_rows.reshape(rows, length)
    matches = match_rounds.reshape(-1)
    owner = slave_owner.reshape(1, rows)
    dofs = slave_dofs.reshape(1, rows)
    active = active_set.reshape(1, rows)
    count = row_counts.reshape(1)
    face = ((directions, length), F32)
    whole = (field, F32)
    message_line = ((4 * devices, LANES), F32)

    sends = [face] * blocks
    near_shape = ((NEAR, length, length), F32)
    fetching = [pltpu.SemaphoreType.DMA((NEAR,))]
    far = ((matrices, blocks - NEAR),)

    (setup,) = call(
        functools.partial(setup_kernel, blocks),
        [((devices, LANES), F32)],
        (count, owner, dofs, active, basis),
        smem=1,
    )
    arrived = exchange(setup)
    a_high, a_low, t_high, t_low, start, right = call(
        functools.partial(slots_kernel, devices),
        [((width, length), BF16)] * 2 + [((length, width), BF16)] * 2 + [whole] * 2,
        (count, owner, active),
        (mortar, start_rows, right_rows),
        smem=1,
    )
    sent, unit_t, unit, modes_ref, *faces = call(
        functools.partial(first_kernel, organs),
        [
            message_line,
            ((length, width), BF16),
            ((width, length), BF16),
            ((modes, blocks, length), F32),
        ]
        + [((directions + 8, length), F32)] * blocks,
        (matches, arrived, basis),
        (start, t_high, t_low, right),
        smem=1,
    )
    forth = (a_high, a_low, unit)
    back = (t_high, t_low, unit_t)
    arrived = exchange(sent)
    faces = swap_faces(faces)
    right, base, added, near = call(
        functools.partial(start_contact, organs),
        [whole],
        (arrived,),
        (sent, start) + forth + (modes_ref, right),
        whole=(matrices,),
        near=[whole, ((8 * organs, length), F32), near_shape],
        scratch=fetching,
    )
    message, smoothed, jump_modes, *posts = call(
        functools.partial(start_kernel, organs),
        [((2 * devices, LANES), F32), whole, ((blocks, 8 * organs, length), F32)],
        (matches, *faces, base, added, near),
        back + (modes_ref,),
        far=far,
        smem=1,
        sends=sends,
        scratch=[pltpu.VMEM(field, F32)],
    )
    arrived = exchange(message)
    faces = swap_faces(posts)
    (part,) = call(
        residual_contact, [], (arrived,), (message, smoothed) + forth + (right,), near=[whole]
    )
    sent, resid, *posts = call(
        residual_kernel,
        [message_line, whole],
        (matches, *faces, part),
        back + (modes_ref,),
        smem=1,
        sends=sends,
    )
    total = start
    direction = inner = image = scalars = None
    for step in range(ITERS):
        older, last = step > 0, step == ITERS - 1
        arrived = exchange(sent)
        faces = swap_faces(posts)
        projected, base, near, norms = call(
            functools.partial(inner_contact, organs),
            [whole],
            (arrived,),
            (sent, resid) + forth + (modes_ref, jump_modes),
            whole=(matrices,),
            near=[whole, near_shape, ((8, LANES), F32)],
            scratch=fetching,
        )
        previous = (inner,) if older else ()
        if last:
            (message,) = call(
                functools.partial(inner_kernel, last, older),
                [((devices, LANES), F32)],
                (matches, *faces, base, near, norms),
                previous,
                far=far,
                smem=1,
                scratch=[pltpu.VMEM(field, F32)] * 2,
            )
            arrived = exchange(message)
            break
        message, new_inner, smoothed, *posts = call(
            functools.partial(inner_kernel, last, older),
            [message_line, whole, whole],
            (matches, *faces, base, near, norms),
            previous + back,
            far=far,
            smem=1,
            sends=sends,
        )
        arrived = exchange(message)
        faces = swap_faces(posts)
        new_scalars, part, steps, image_part = call(
            functools.partial(outer_contact, older),
            [((4, directions, LANES), F32)],
            (arrived,),
            (message, smoothed) + forth + (projected,) + ((image, scalars) if older else ()),
            near=[whole, ((directions, LANES), F32), whole],
        )
        sent, resid, *posts = call(
            functools.partial(outer_kernel, older),
            [message_line, whole] + ([] if older else [whole]),
            (matches, *faces, part, steps, image_part),
            back + (modes_ref,),
            smem=1,
            sends=sends,
        )
        if not older:
            image, *posts = posts
        scalars = new_scalars
        updated = call(
            functools.partial(update_kernel, older),
            [whole] * (3 if older else 1),
            (),
            (projected, new_inner, total, scalars) + ((direction, inner) if older else ()),
        )
        if older:
            total, direction, inner = updated
        else:
            (total,) = updated
            direction, inner = projected, new_inner
    (result,) = call(
        last_kernel,
        [((directions * blocks, 1, length), F32)],
        (arrived,),
        (projected, direction, total, scalars),
    )
    return result.reshape(dual_rhs.shape)


def solution(mesh):
    in_specs = (
        P(None, "organ", "sub", None, None),
        P(None, "organ", "sub", None, None),
        P("organ", "sub", None, None, None),
        P(None, "organ", "sub", None, None),
        P("organ", "sub", None, None),
        P("organ", "sub", None),
        P("organ", "sub", None, None),
        P("organ", "sub", None),
        P("organ", "sub", None),
        P("organ", "sub", None),
    )
    out_specs = P(None, "organ", "sub", None, None)
    return jax.shard_map(local, mesh=mesh, in_specs=in_specs, out_specs=out_specs, check_vma=False)
```

time: 227 us -> 166 us (0.73)
  local copies, waits for them, and re-layouts: 96.5 us -> 5.69 us
  Pallas kernels: 24.6 us -> 66.3 us
  starting transfers between devices: 82.2 us -> 76.1 us
  waiting for transfers between devices: 11.3 us -> 5.54 us
    unnamed x224 -> x18, local copies, waits for them, and re-layouts: 86.1 us -> 5.69 us
    pallas_call x11 -> x20, Pallas kernels: 24.6 us -> 66.3 us  [call(): pl.pallas_call(body, out_shape=[pltpu.HBM(shape, kind) for shape, kind in...]
    ppermute x35, waiting for transfers between devices: 9.89 us -> 1.54 us  [from_partner(): return lax.ppermute(value, axis, pairs)]
    all_to_all x10 -> x0, local copies, waits for them, and re-layouts: 7.53 us -> none  [exchange(): lax.all_to_all(message, AXES, split_axis=0, concat_axis=0, tiled=True)]
    all_to_all x8, starting transfers between devices: 32.2 us -> 25.6 us  [exchange(): lax.all_to_all(message, AXES, split_axis=0, concat_axis=0, tiled=True)]
    all_to_all x8, waiting for transfers between devices: 1.44 us -> 3.99 us  [exchange(): lax.all_to_all(message, AXES, split_axis=0, concat_axis=0, tiled=True)]
  transfers between devices with their start and end apart: 43 -> 43, of which waited for: 15 -> 9; matrix products, arithmetic and copies ran while one was open for 0% -> 0% of each run, Pallas kernels for 0% -> 18%
where the time goes in v2:
time: 166 us; the launch traced here: 165 us
  starting transfers between devices  76.1 us (46%)
  Pallas kernels  66.3 us (40%)
  blocking collectives  9.64 us (6%)
  local copies, waits for them, and re-layouts  5.69 us (3%)
  waiting for transfers between devices  5.54 us (3%)
    pallas_call x20, Pallas kernels, call(): pl.pallas_call(body, out_shape=[pltpu.HBM(shape, kind) for shape, kind in...  66.3 us
    ppermute x35, starting transfers between devices, from_partner(): return lax.ppermute(value, axis, pairs)  50.4 us
    all_to_all x8, starting transfers between devices, exchange(): lax.all_to_all(message, AXES, split_axis=0, concat_axis=0, tiled=True)  25.6 us
    all_to_all x1, blocking collectives, exchange(): lax.all_to_all(message, AXES, split_axis=0, concat_axis=0, tiled=True)  9.64 us
    unnamed x18, local copies, waits for them, and re-layouts  5.69 us
    all_to_all x8, waiting for transfers between devices, exchange(): lax.all_to_all(message, AXES, split_axis=0, concat_axis=0, tiled=True)  3.99 us
  transfers between devices with their start and end apart: 43, of which 9 were waited for; matrix products, arithmetic and copies ran while one was open for 0% of the time, Pallas kernels for 18%

profile of v2, /device:TPU:0, one launch (start us, length us, event | category | flops | bytes accessed | tf_op | source)
XLA Modules:
  0.0 164.6 jit_solution(9914384853386985697)
XLA Ops:
  4.5 7.3 %all-to-all-start = ((f32[32,1,128]{2,1,0:T(1,128)}), f32[32,1,128]{2,1,0:T(1,128)S(1)}, u32[]{:S(2)}, u32[]{:S(2)}) async-start(f32[32,1,128]{2,1,0:T(1,128)} %bitcast.80), calls=%async_computation | async-start | bytes 32768 | tf_op jit(solution)/shard_map/all_to_all | solution.py:683
  13.1 2.6 %shard_map.101 = (bf16[256,640]{1,0:T(8,128)(2,1)}, bf16[256,640]{1,0:T(8,128)(2,1)}, bf16[640,256]{1,0:T(8,128)(2,1)}, bf16[640,256]{1,0:T(8,128)(2,1)}, f32[5,16,640]{2,1,0:T(8,128)}, /*index=5*/f32[5,16,640]{2,1,0:T(8,128)}) custom-call(s32[1]{0:T(128)} %bitcast.36.refs_0_, s32[1,128]{1,0:T(1,128)S(1)} %bitcast.57, s32[1,128]{1,0:T(1,128)S(1)} %bitcast.59, ...), custom_call_target="tpu_custom_call" | custom-call | flops 2000000 | bytes 2000000 | tf_op jit(solution)/shard_map/pallas_call | solution.py:662
  15.7 3.2 %all-to-all-done = f32[32,1,128]{2,1,0:T(1,128)S(1)} async-done(((f32[32,1,128]{2,1,0:T(1,128)}), f32[32,1,128]{2,1,0:T(1,128)S(1)}, u32[]{:S(2)}, u32[]{:S(2)}) %all-to-all-start) | async-done | bytes 16416 | tf_op jit(solution)/shard_map/all_to_all | solution.py:683
  20.5 3.5 %shard_map.102 = (f32[128,128]{1,0:T(8,128)}, bf16[640,256]{1,0:T(8,128)(2,1)}, bf16[256,640]{1,0:T(8,128)(2,1)}, f32[6,5,640]{2,1,0:T(8,128)}, f32[24,640]{1,0:...) custom-call(s32[5]{0:T(128)S(1)} %bitcast.48, ...), custom_call_target="tpu_custom_call" | custom-call | flops 2000000 | bytes 2000000 | tf_op jit(solution)/shard_map/pallas_call | solution.py:662
  24.0 2.7 %all-to-all-start.1 = ((f32[32,4,128]{2,1,0:T(4,128)}), f32[32,4,128]{2,1,0:T(4,128)S(1)}, u32[]{:S(2)}, u32[]{:S(2)}) async-start(f32[32,4,128]{2,1,0:T(4,128)} %bitcast.73), calls=%async_computation.1 | async-start | bytes 131072 | tf_op jit(solution)/shard_map/all_to_all | solution.py:683
  26.7 2.7 %collective-permute-start = (f32[24,640]{1,0:T(8,128)}, f32[24,640]{1,0:T(8,128)S(1)}, u32[]{:S(2)}, u32[]{:S(2)}) collective-permute-start(f32[24,640]{1,0:T(8,128)} %get-tuple-element.97), channel_id=1, source_target_pairs={{0,4},{1,5},{2,6},{3,7},{4,0},{5,1},{6,2},{7,3},{8,12},{9,13},{10,... | collective-permute-start | bytes 184328 | tf_op jit(solution)/shard_map/ppermute | solution.py:679
  34.0 3.9 %shard_map.103 = (f32[5,16,640]{2,1,0:T(8,128)}, f32[5,16,640]{2,1,0:T(8,128)S(1)}, f32[32,640]{1,0:T(8,128)S(1)}, f32[3,640,640]{2,1,0:T(8,128)S(1)}) custom-call(f32[128,128]{1,0:T(8,128)S(1)} %bitcast.41, f32[128,128]{1,0:T(8,128)} %get-tuple-element.102.refs_1_, f32[5,16,640]{2,1,0:T(8,128)} %get-tuple-element.93.refs_3_.refs_2_, ...), custom_call_target="tpu_custom_call" | custom-call | flops 2000000 | bytes 2000000 | tf_op jit(solution)/shard_map/pallas_call | solution.py:662
  38.1 5.4 %shard_map.104 = (f32[64,128]{1,0:T(8,128)}, f32[5,16,640]{2,1,0:T(8,128)}, f32[5,32,640]{2,1,0:T(8,128)}, f32[16,640]{1,0:T(8,128)}, f32[16,640]{1,0:T(8,128)},...) custom-call(s32[5]{0:T(128)S(1)} %bitcast.49, f32[24,640]{1,0:T(8,128)S(1)} %collective-permute-done.refs_1_, ...), custom_call_target="tpu_custom_call" | custom-call | flops 2000000 | bytes 2000000 | tf_op jit(solution)/shard_map/pallas_call | solution.py:662
  43.4 2.6 %all-to-all-start.2 = ((f32[32,2,128]{2,1,0:T(2,128)}), f32[32,2,128]{2,1,0:T(2,128)S(1)}, u32[]{:S(2)}, u32[]{:S(2)}) async-start(f32[32,2,128]{2,1,0:T(2,128)} %bitcast.78), calls=%async_computation.2 | async-start | bytes 65536 | tf_op jit(solution)/shard_map/all_to_all | solution.py:683
  46.0 2.7 %collective-permute-start.5 = (f32[16,640]{1,0:T(8,128)}, f32[16,640]{1,0:T(8,128)S(1)}, u32[]{:S(2)}, u32[]{:S(2)}) collective-permute-start(f32[16,640]{1,0:T(8,128)} %get-tuple-element.111), channel_id=1, source_target_pairs={{0,4},{1,5},{2,6},{3,7},{4,0},{5,1},{6,2},{7,3},{8,12},{9,13},{10,... | collective-permute-start | bytes 122888 | tf_op jit(solution)/shard_map/ppermute | solution.py:679
  56.0 3.3 %shard_map.106 = (f32[128,128]{1,0:T(8,128)}, f32[5,16,640]{2,1,0:T(8,128)}, f32[16,640]{1,0:T(8,128)}, f32[16,640]{1,0:T(8,128)}, f32[16,640]{1,0:T(8,128)}, /*index=5*/f32[16,640]{1,0:T(8,128)}, f32[16,640]{1,0:T(8,128)}) custom-call(s32[5]{0:T(128)S(1)} %bitcast.50, f32[16,640]{1,0:T(8,128)S(1)} %collective-permute-done.5.refs_1_, ...), custom_call_target="tpu_custom_call" | custom-call | flops 2000000 | bytes 2000000 | tf_op jit(solution)/shard_map/pallas_call | solution.py:662
  59.3 2.6 %all-to-all-start.3 = ((f32[32,4,128]{2,1,0:T(4,128)}), f32[32,4,128]{2,1,0:T(4,128)S(1)}, u32[]{:S(2)}, u32[]{:S(2)}) async-start(f32[32,4,128]{2,1,0:T(4,128)} %bitcast.72), calls=%async_computation.3 | async-start | bytes 131072 | tf_op jit(solution)/shard_map/all_to_all | solution.py:683
  61.8 2.7 %collective-permute-start.10 = (f32[16,640]{1,0:T(8,128)}, f32[16,640]{1,0:T(8,128)S(1)}, u32[]{:S(2)}, u32[]{:S(2)}) collective-permute-start(f32[16,640]{1,0:T(8,128)} %get-tuple-element.119), channel_id=1, source_target_pairs={{0,4},{1,5},{2,6},{3,7},{4,0},{5,1},{6,2},{7,3},{8,12},{9,13},{10,... | collective-permute-start | bytes 122888 | tf_op jit(solution)/shard_map/ppermute | solution.py:679
  69.2 4.2 %shard_map.107 = (f32[5,16,640]{2,1,0:T(8,128)}, f32[5,16,640]{2,1,0:T(8,128)S(1)}, f32[3,640,640]{2,1,0:T(8,128)S(1)}, f32[8,128]{1,0:T(8,128)S(1)}) custom-call(f32[128,128]{1,0:T(8,128)S(1)} %bitcast.40, f32[128,128]{1,0:T(8,128)} %get-tuple-element.124.refs_1_, f32[5,16,640]{2,1,0:T(8,128)} %get-tuple-element.125.refs_2_, ...), custom_call_target="tpu_custom_call" | custom-call | flops 2000000 | bytes 2000000 | tf_op jit(solution)/shard_map/pallas_call | solution.py:662
  73.5 5.0 %shard_map.108 = (f32[128,128]{1,0:T(8,128)}, f32[5,16,640]{2,1,0:T(8,128)}, f32[5,16,640]{2,1,0:T(8,128)}, f32[16,640]{1,0:T(8,128)}, f32[16,640]{1,0:T(8,128)}...) custom-call(s32[5]{0:T(128)S(1)} %bitcast.51, f32[16,640]{1,0:T(8,128)S(1)} %collective-permute-done.10.refs_1_, ...), custom_call_target="tpu_custom_call" | custom-call | flops 2000000 | bytes 2000000 | tf_op jit(solution)/shard_map/pallas_call | solution.py:662
  78.5 2.6 %all-to-all-start.4 = ((f32[32,4,128]{2,1,0:T(4,128)}), f32[32,4,128]{2,1,0:T(4,128)S(1)}, u32[]{:S(2)}, u32[]{:S(2)}) async-start(f32[32,4,128]{2,1,0:T(4,128)} %bitcast.75), calls=%async_computation.4 | async-start | bytes 131072 | tf_op jit(solution)/shard_map/all_to_all | solution.py:683
  81.1 2.7 %collective-permute-start.15 = (f32[16,640]{1,0:T(8,128)}, f32[16,640]{1,0:T(8,128)S(1)}, u32[]{:S(2)}, u32[]{:S(2)}) collective-permute-start(f32[16,640]{1,0:T(8,128)} %get-tuple-element.130), channel_id=1, source_target_pairs={{0,4},{1,5},{2,6},{3,7},{4,0},{5,1},{6,2},{7,3},{8,12},{9,13},{10,... | collective-permute-start | bytes 122888 | tf_op jit(solution)/shard_map/ppermute | solution.py:679
  91.1 3.4 %shard_map.110 = (f32[128,128]{1,0:T(8,128)}, f32[5,16,640]{2,1,0:T(8,128)}, f32[5,16,640]{2,1,0:T(8,128)}, f32[16,640]{1,0:T(8,128)}, f32[16,640]{1,0:T(8,128)}...) custom-call(s32[5]{0:T(128)S(1)} %bitcast.52, f32[16,640]{1,0:T(8,128)S(1)} %collective-permute-done.15.refs_1_, ...), custom_call_target="tpu_custom_call" | custom-call | flops 2000000 | bytes 2000000 | tf_op jit(solution)/shard_map/pallas_call | solution.py:662
  94.5 2.8 %all-to-all-start.5 = ((f32[32,4,128]{2,1,0:T(4,128)}), f32[32,4,128]{2,1,0:T(4,128)S(1)}, u32[]{:S(2)}, u32[]{:S(2)}) async-start(f32[32,4,128]{2,1,0:T(4,128)} %bitcast.71), calls=%async_computation.5 | async-start | bytes 131072 | tf_op jit(solution)/shard_map/all_to_all | solution.py:683
  97.3 2.5 %collective-permute-start.20 = (f32[16,640]{1,0:T(8,128)}, f32[16,640]{1,0:T(8,128)S(1)}, u32[]{:S(2)}, u32[]{:S(2)}) collective-permute-start(f32[16,640]{1,0:T(8,128)} %get-tuple-element.141), channel_id=1, source_target_pairs={{0,4},{1,5},{2,6},{3,7},{4,0},{5,1},{6,2},{7,3},{8,12},{9,13},{10,... | collective-permute-start | bytes 122888 | tf_op jit(solution)/shard_map/ppermute | solution.py:679
  104.5 4.2 %shard_map.111 = (f32[5,16,640]{2,1,0:T(8,128)}, f32[5,16,640]{2,1,0:T(8,128)S(1)}, f32[3,640,640]{2,1,0:T(8,128)S(1)}, f32[8,128]{1,0:T(8,128)S(1)}) custom-call(f32[128,128]{1,0:T(8,128)S(1)} %bitcast.42, f32[128,128]{1,0:T(8,128)} %get-tuple-element.146.refs_1_, f32[5,16,640]{2,1,0:T(8,128)} %get-tuple-element.147.refs_2_, ...), custom_call_target="tpu_custom_call" | custom-call | flops 2000000 | bytes 2000000 | tf_op jit(solution)/shard_map/pallas_call | solution.py:662
  108.8 5.1 %shard_map.112 = (f32[128,128]{1,0:T(8,128)}, f32[5,16,640]{2,1,0:T(8,128)}, f32[5,16,640]{2,1,0:T(8,128)}, f32[16,640]{1,0:T(8,128)}, f32[16,640]{1,0:T(8,128)}...) custom-call(s32[5]{0:T(128)S(1)} %bitcast.53, f32[16,640]{1,0:T(8,128)S(1)} %collective-permute-done.20.refs_1_, ...), custom_call_target="tpu_custom_call" | custom-call | flops 2000000 | bytes 2000000 | tf_op jit(solution)/shard_map/pallas_call | solution.py:662
  113.9 2.6 %all-to-all-start.6 = ((f32[32,4,128]{2,1,0:T(4,128)}), f32[32,4,128]{2,1,0:T(4,128)S(1)}, u32[]{:S(2)}, u32[]{:S(2)}) async-start(f32[32,4,128]{2,1,0:T(4,128)} %bitcast.74), calls=%async_computation.6 | async-start | bytes 131072 | tf_op jit(solution)/shard_map/all_to_all | solution.py:683
  116.5 2.7 %collective-permute-start.25 = (f32[16,640]{1,0:T(8,128)}, f32[16,640]{1,0:T(8,128)S(1)}, u32[]{:S(2)}, u32[]{:S(2)}) collective-permute-start(f32[16,640]{1,0:T(8,128)} %get-tuple-element.152), channel_id=1, source_target_pairs={{0,4},{1,5},{2,6},{3,7},{4,0},{5,1},{6,2},{7,3},{8,12},{9,13},{10,... | collective-permute-start | bytes 122888 | tf_op jit(solution)/shard_map/ppermute | solution.py:679
  123.9 2.3 %shard_map.113 = (f32[4,16,128]{2,1,0:T(8,128)}, f32[5,16,640]{2,1,0:T(8,128)S(1)}, f32[16,128]{1,0:T(8,128)S(1)}, f32[5,16,640]{2,1,0:T(8,128)S(1)}) custom-call(f32[128,128]{1,0:T(8,128)S(1)} %bitcast.43, f32[128,128]{1,0:T(8,128)} %get-tuple-element.157.refs_1_, f32[5,16,640]{2,1,0:T(8,128)} %get-tuple-element.158.refs_2_, ...), custom_call_target="tpu_custom_call" | custom-call | flops 2000000 | bytes 2000000 | tf_op jit(solution)/shard_map/pallas_call | solution.py:662
  126.5 3.3 %shard_map.114 = (f32[128,128]{1,0:T(8,128)}, f32[5,16,640]{2,1,0:T(8,128)}, f32[16,640]{1,0:T(8,128)}, f32[16,640]{1,0:T(8,128)}, f32[16,640]{1,0:T(8,128)}, /*index=5*/f32[16,640]{1,0:T(8,128)}, f32[16,640]{1,0:T(8,128)}) custom-call(s32[5]{0:T(128)S(1)} %bitcast.54, f32[16,640]{1,0:T(8,128)S(1)} %collective-permute-done.25.refs_1_, ...), custom_call_target="tpu_custom_call" | custom-call | flops 2000000 | bytes 2000000 | tf_op jit(solution)/shard_map/pallas_call | solution.py:662
  129.7 2.6 %all-to-all-start.7 = ((f32[32,4,128]{2,1,0:T(4,128)}), f32[32,4,128]{2,1,0:T(4,128)S(1)}, u32[]{:S(2)}, u32[]{:S(2)}) async-start(f32[32,4,128]{2,1,0:T(4,128)} %bitcast.70), calls=%async_computation.7 | async-start | bytes 131072 | tf_op jit(solution)/shard_map/all_to_all | solution.py:683
  132.3 2.7 %collective-permute-start.30 = (f32[16,640]{1,0:T(8,128)}, f32[16,640]{1,0:T(8,128)S(1)}, u32[]{:S(2)}, u32[]{:S(2)}) collective-permute-start(f32[16,640]{1,0:T(8,128)} %get-tuple-element.165), channel_id=1, source_target_pairs={{0,4},{1,5},{2,6},{3,7},{4,0},{5,1},{6,2},{7,3},{8,12},{9,13},{10,... | collective-permute-start | bytes 122888 | tf_op jit(solution)/shard_map/ppermute | solution.py:679
  141.5 2.3 %shard_map.117 = (f32[5,16,640]{2,1,0:T(8,128)}, f32[5,16,640]{2,1,0:T(8,128)}, f32[5,16,640]{2,1,0:T(8,128)}) custom-call(f32[5,16,640]{2,1,0:T(8,128)} %get-tuple-element.159.refs_6_.refs_0_, f32[5,16,640]{2,1,0:T(8,128)} %get-tuple-element.175.refs_1_, f32[5,16,640]{2,1,0:T(8,128)} %shard_map.116.refs_2_, ...), custom_call_target="tpu_custom_call" | custom-call | flops 2000000 | bytes 2000000 | tf_op jit(solution)/shard_map/pallas_call | solution.py:662
  143.8 4.3 %shard_map.115 = (f32[5,16,640]{2,1,0:T(8,128)}, f32[5,16,640]{2,1,0:T(8,128)S(1)}, f32[3,640,640]{2,1,0:T(8,128)S(1)}, f32[8,128]{1,0:T(8,128)S(1)}) custom-call(f32[128,128]{1,0:T(8,128)S(1)} %bitcast.39, f32[128,128]{1,0:T(8,128)} %get-tuple-element.170.refs_1_, f32[5,16,640]{2,1,0:T(8,128)} %get-tuple-element.171.refs_2_, ...), custom_call_target="tpu_custom_call" | custom-call | flops 2000000 | bytes 2000000 | tf_op jit(solution)/shard_map/pallas_call | solution.py:662
  148.2 4.5 %shard_map.118 = f32[32,128]{1,0:T(8,128)} custom-call(s32[5]{0:T(128)S(1)} %bitcast.55, f32[16,640]{1,0:T(8,128)S(1)} %collective-permute-done.30.refs_1_, f32[16,640]{1,0:T(8,128)S(1)} %collective-permute-done.31.refs_2_, f32[16,640]{1,0:T(8,128)S(1)} %collective-permute-done.32.refs_3_, f32[16,640]{1,0:T(8,128)S(1)} %collective-permute-done.33.refs_4_, ...), custom_call_target="tpu_custom_call" | custom-call | flops 2000000 | bytes 2000000 | tf_op jit(solution)/shard_map/pallas_call | solution.py:662
  152.7 9.6 %all_to_all.99 = f32[32,1,128]{2,1,0:T(1,128)S(1)} all-to-all(f32[32,1,128]{2,1,0:T(1,128)} %bitcast.79), channel_id=1, replica_groups=mesh['organ'=4,'sub'=8] {'organ','sub'}, dimensions={0} | all-to-all | bytes 32768 | tf_op jit(solution)/shard_map/all_to_all | solution.py:683
  (93 shorter events, 48.5 us)
Async XLA Ops:
  4.5 14.4 %all-to-all-start = ((f32[32,1,128]{2,1,0:T(1,128)}), f32[32,1,128]{2,1,0:T(1,128)S(1)}, u32[]{:S(2)}, u32[]{:S(2)}) async-start(f32[32,1,128]{2,1,0:T(1,128)} %bitcast.80), calls=%async_computation | async-start | bytes 32768 | tf_op jit(solution)/shard_map/all_to_all | solution.py:683
  24.0 10.1 %all-to-all-start.1 = ((f32[32,4,128]{2,1,0:T(4,128)}), f32[32,4,128]{2,1,0:T(4,128)S(1)}, u32[]{:S(2)}, u32[]{:S(2)}) async-start(f32[32,4,128]{2,1,0:T(4,128)} %bitcast.73), calls=%async_computation.1 | async-start | bytes 131072 | tf_op jit(solution)/shard_map/all_to_all | solution.py:683
  26.7 11.3 %collective-permute-start = (f32[24,640]{1,0:T(8,128)}, f32[24,640]{1,0:T(8,128)S(1)}, u32[]{:S(2)}, u32[]{:S(2)}) collective-permute-start(f32[24,640]{1,0:T(8,128)} %get-tuple-element.97), channel_id=1, source_target_pairs={{0,4},{1,5},{2,6},{3,7},{4,0},{5,1},{6,2},{7,3},{8,12},{9,13},{10,... | collective-permute-start | bytes 184328 | tf_op jit(solution)/shard_map/ppermute | solution.py:679
  29.4 8.6 %collective-permute-start.1 = (f32[24,640]{1,0:T(8,128)}, f32[24,640]{1,0:T(8,128)S(1)}, u32[]{:S(2)}, u32[]{:S(2)}) collective-permute-start(f32[24,640]{1,0:T(8,128)} %get-tuple-element.98), channel_id=1, source_target_pairs={{0,1},{1,0},{2,3},{3,2},{4,5},{5,4},{6,7},{7,6},{8,9},{9,8},{10,11... | collective-permute-start | bytes 184328 | tf_op jit(solution)/shard_map/ppermute | solution.py:679
  30.9 7.1 %collective-permute-start.2 = (f32[24,640]{1,0:T(8,128)}, f32[24,640]{1,0:T(8,128)S(1)}, u32[]{:S(2)}, u32[]{:S(2)}) collective-permute-start(f32[24,640]{1,0:T(8,128)} %get-tuple-element.99), channel_id=1, source_target_pairs={{0,2},{1,3},{2,0},{3,1},{4,6},{5,7},{6,4},{7,5},{8,10},{9,11},{10,... | collective-permute-start | bytes 184328 | tf_op jit(solution)/shard_map/ppermute | solution.py:679
  32.4 5.6 %collective-permute-start.3 = (f32[24,640]{1,0:T(8,128)}, f32[24,640]{1,0:T(8,128)S(1)}, u32[]{:S(2)}, u32[]{:S(2)}) collective-permute-start(f32[24,640]{1,0:T(8,128)} %get-tuple-element.100), channel_id=1, source_target_pairs={{0,16},{8,24},{16,0},{24,8},{1,17},{9,25},{17,1},{25,9},{2,18},{10... | collective-permute-start | bytes 184328 | tf_op jit(solution)/shard_map/ppermute | solution.py:679
  43.4 9.9 %all-to-all-start.2 = ((f32[32,2,128]{2,1,0:T(2,128)}), f32[32,2,128]{2,1,0:T(2,128)S(1)}, u32[]{:S(2)}, u32[]{:S(2)}) async-start(f32[32,2,128]{2,1,0:T(2,128)} %bitcast.78), calls=%async_computation.2 | async-start | bytes 65536 | tf_op jit(solution)/shard_map/all_to_all | solution.py:683
  46.0 9.1 %collective-permute-start.5 = (f32[16,640]{1,0:T(8,128)}, f32[16,640]{1,0:T(8,128)S(1)}, u32[]{:S(2)}, u32[]{:S(2)}) collective-permute-start(f32[16,640]{1,0:T(8,128)} %get-tuple-element.111), channel_id=1, source_target_pairs={{0,4},{1,5},{2,6},{3,7},{4,0},{5,1},{6,2},{7,3},{8,12},{9,13},{10,... | collective-permute-start | bytes 122888 | tf_op jit(solution)/shard_map/ppermute | solution.py:679
  48.7 6.4 %collective-permute-start.6 = (f32[16,640]{1,0:T(8,128)}, f32[16,640]{1,0:T(8,128)S(1)}, u32[]{:S(2)}, u32[]{:S(2)}) collective-permute-start(f32[16,640]{1,0:T(8,128)} %get-tuple-element.112), channel_id=1, source_target_pairs={{0,1},{1,0},{2,3},{3,2},{4,5},{5,4},{6,7},{7,6},{8,9},{9,8},{10,11... | collective-permute-start | bytes 122888 | tf_op jit(solution)/shard_map/ppermute | solution.py:679
  59.3 10.0 %all-to-all-start.3 = ((f32[32,4,128]{2,1,0:T(4,128)}), f32[32,4,128]{2,1,0:T(4,128)S(1)}, u32[]{:S(2)}, u32[]{:S(2)}) async-start(f32[32,4,128]{2,1,0:T(4,128)} %bitcast.72), calls=%async_computation.3 | async-start | bytes 131072 | tf_op jit(solution)/shard_map/all_to_all | solution.py:683
  61.8 11.6 %collective-permute-start.10 = (f32[16,640]{1,0:T(8,128)}, f32[16,640]{1,0:T(8,128)S(1)}, u32[]{:S(2)}, u32[]{:S(2)}) collective-permute-start(f32[16,640]{1,0:T(8,128)} %get-tuple-element.119), channel_id=1, source_target_pairs={{0,4},{1,5},{2,6},{3,7},{4,0},{5,1},{6,2},{7,3},{8,12},{9,13},{10,... | collective-permute-start | bytes 122888 | tf_op jit(solution)/shard_map/ppermute | solution.py:679
  64.5 8.9 %collective-permute-start.11 = (f32[16,640]{1,0:T(8,128)}, f32[16,640]{1,0:T(8,128)S(1)}, u32[]{:S(2)}, u32[]{:S(2)}) collective-permute-start(f32[16,640]{1,0:T(8,128)} %get-tuple-element.120), channel_id=1, source_target_pairs={{0,1},{1,0},{2,3},{3,2},{4,5},{5,4},{6,7},{7,6},{8,9},{9,8},{10,11... | collective-permute-start | bytes 122888 | tf_op jit(solution)/shard_map/ppermute | solution.py:679
  66.0 7.5 %collective-permute-start.12 = (f32[16,640]{1,0:T(8,128)}, f32[16,640]{1,0:T(8,128)S(1)}, u32[]{:S(2)}, u32[]{:S(2)}) collective-permute-start(f32[16,640]{1,0:T(8,128)} %get-tuple-element.121), channel_id=1, source_target_pairs={{0,2},{1,3},{2,0},{3,1},{4,6},{5,7},{6,4},{7,5},{8,10},{9,11},{10,... | collective-permute-start | bytes 122888 | tf_op jit(solution)/shard_map/ppermute | solution.py:679
  67.6 5.9 %collective-permute-start.13 = (f32[16,640]{1,0:T(8,128)}, f32[16,640]{1,0:T(8,128)S(1)}, u32[]{:S(2)}, u32[]{:S(2)}) collective-permute-start(f32[16,640]{1,0:T(8,128)} %get-tuple-element.122), channel_id=1, source_target_pairs={{0,16},{8,24},{16,0},{24,8},{1,17},{9,25},{17,1},{25,9},{2,18},{10... | collective-permute-start | bytes 122888 | tf_op jit(solution)/shard_map/ppermute | solution.py:679
  78.5 10.0 %all-to-all-start.4 = ((f32[32,4,128]{2,1,0:T(4,128)}), f32[32,4,128]{2,1,0:T(4,128)S(1)}, u32[]{:S(2)}, u32[]{:S(2)}) async-start(f32[32,4,128]{2,1,0:T(4,128)} %bitcast.75), calls=%async_computation.4 | async-start | bytes 131072 | tf_op jit(solution)/shard_map/all_to_all | solution.py:683
  81.1 9.5 %collective-permute-start.15 = (f32[16,640]{1,0:T(8,128)}, f32[16,640]{1,0:T(8,128)S(1)}, u32[]{:S(2)}, u32[]{:S(2)}) collective-permute-start(f32[16,640]{1,0:T(8,128)} %get-tuple-element.130), channel_id=1, source_target_pairs={{0,4},{1,5},{2,6},{3,7},{4,0},{5,1},{6,2},{7,3},{8,12},{9,13},{10,... | collective-permute-start | bytes 122888 | tf_op jit(solution)/shard_map/ppermute | solution.py:679
  83.8 6.8 %collective-permute-start.16 = (f32[16,640]{1,0:T(8,128)}, f32[16,640]{1,0:T(8,128)S(1)}, u32[]{:S(2)}, u32[]{:S(2)}) collective-permute-start(f32[16,640]{1,0:T(8,128)} %get-tuple-element.131), channel_id=1, source_target_pairs={{0,1},{1,0},{2,3},{3,2},{4,5},{5,4},{6,7},{7,6},{8,9},{9,8},{10,11... | collective-permute-start | bytes 122888 | tf_op jit(solution)/shard_map/ppermute | solution.py:679
  94.5 10.0 %all-to-all-start.5 = ((f32[32,4,128]{2,1,0:T(4,128)}), f32[32,4,128]{2,1,0:T(4,128)S(1)}, u32[]{:S(2)}, u32[]{:S(2)}) async-start(f32[32,4,128]{2,1,0:T(4,128)} %bitcast.71), calls=%async_computation.5 | async-start | bytes 131072 | tf_op jit(solution)/shard_map/all_to_all | solution.py:683
  97.3 11.5 %collective-permute-start.20 = (f32[16,640]{1,0:T(8,128)}, f32[16,640]{1,0:T(8,128)S(1)}, u32[]{:S(2)}, u32[]{:S(2)}) collective-permute-start(f32[16,640]{1,0:T(8,128)} %get-tuple-element.141), channel_id=1, source_target_pairs={{0,4},{1,5},{2,6},{3,7},{4,0},{5,1},{6,2},{7,3},{8,12},{9,13},{10,... | collective-permute-start | bytes 122888 | tf_op jit(solution)/shard_map/ppermute | solution.py:679
  99.8 8.9 %collective-permute-start.21 = (f32[16,640]{1,0:T(8,128)}, f32[16,640]{1,0:T(8,128)S(1)}, u32[]{:S(2)}, u32[]{:S(2)}) collective-permute-start(f32[16,640]{1,0:T(8,128)} %get-tuple-element.142), channel_id=1, source_target_pairs={{0,1},{1,0},{2,3},{3,2},{4,5},{5,4},{6,7},{7,6},{8,9},{9,8},{10,11... | collective-permute-start | bytes 122888 | tf_op jit(solution)/shard_map/ppermute | solution.py:679
  101.3 7.4 %collective-permute-start.22 = (f32[16,640]{1,0:T(8,128)}, f32[16,640]{1,0:T(8,128)S(1)}, u32[]{:S(2)}, u32[]{:S(2)}) collective-permute-start(f32[16,640]{1,0:T(8,128)} %get-tuple-element.143), channel_id=1, source_target_pairs={{0,2},{1,3},{2,0},{3,1},{4,6},{5,7},{6,4},{7,5},{8,10},{9,11},{10,... | collective-permute-start | bytes 122888 | tf_op jit(solution)/shard_map/ppermute | solution.py:679
  102.8 5.9 %collective-permute-start.23 = (f32[16,640]{1,0:T(8,128)}, f32[16,640]{1,0:T(8,128)S(1)}, u32[]{:S(2)}, u32[]{:S(2)}) collective-permute-start(f32[16,640]{1,0:T(8,128)} %get-tuple-element.144), channel_id=1, source_target_pairs={{0,16},{8,24},{16,0},{24,8},{1,17},{9,25},{17,1},{25,9},{2,18},{10... | collective-permute-start | bytes 122888 | tf_op jit(solution)/shard_map/ppermute | solution.py:679
  113.9 10.0 %all-to-all-start.6 = ((f32[32,4,128]{2,1,0:T(4,128)}), f32[32,4,128]{2,1,0:T(4,128)S(1)}, u32[]{:S(2)}, u32[]{:S(2)}) async-start(f32[32,4,128]{2,1,0:T(4,128)} %bitcast.74), calls=%async_computation.6 | async-start | bytes 131072 | tf_op jit(solution)/shard_map/all_to_all | solution.py:683
  116.5 9.7 %collective-permute-start.25 = (f32[16,640]{1,0:T(8,128)}, f32[16,640]{1,0:T(8,128)S(1)}, u32[]{:S(2)}, u32[]{:S(2)}) collective-permute-start(f32[16,640]{1,0:T(8,128)} %get-tuple-element.152), channel_id=1, source_target_pairs={{0,4},{1,5},{2,6},{3,7},{4,0},{5,1},{6,2},{7,3},{8,12},{9,13},{10,... | collective-permute-start | bytes 122888 | tf_op jit(solution)/shard_map/ppermute | solution.py:679
  119.2 7.0 %collective-permute-start.26 = (f32[16,640]{1,0:T(8,128)}, f32[16,640]{1,0:T(8,128)S(1)}, u32[]{:S(2)}, u32[]{:S(2)}) collective-permute-start(f32[16,640]{1,0:T(8,128)} %get-tuple-element.153), channel_id=1, source_target_pairs={{0,1},{1,0},{2,3},{3,2},{4,5},{5,4},{6,7},{7,6},{8,9},{9,8},{10,11... | collective-permute-start | bytes 122888 | tf_op jit(solution)/shard_map/ppermute | solution.py:679
  120.7 5.5 %collective-permute-start.27 = (f32[16,640]{1,0:T(8,128)}, f32[16,640]{1,0:T(8,128)S(1)}, u32[]{:S(2)}, u32[]{:S(2)}) collective-permute-start(f32[16,640]{1,0:T(8,128)} %get-tuple-element.154), channel_id=1, source_target_pairs={{0,2},{1,3},{2,0},{3,1},{4,6},{5,7},{6,4},{7,5},{8,10},{9,11},{10,... | collective-permute-start | bytes 122888 | tf_op jit(solution)/shard_map/ppermute | solution.py:679
  129.7 14.1 %all-to-all-start.7 = ((f32[32,4,128]{2,1,0:T(4,128)}), f32[32,4,128]{2,1,0:T(4,128)S(1)}, u32[]{:S(2)}, u32[]{:S(2)}) async-start(f32[32,4,128]{2,1,0:T(4,128)} %bitcast.70), calls=%async_computation.7 | async-start | bytes 131072 | tf_op jit(solution)/shard_map/all_to_all | solution.py:683
  132.3 15.8 %collective-permute-start.30 = (f32[16,640]{1,0:T(8,128)}, f32[16,640]{1,0:T(8,128)S(1)}, u32[]{:S(2)}, u32[]{:S(2)}) collective-permute-start(f32[16,640]{1,0:T(8,128)} %get-tuple-element.165), channel_id=1, source_target_pairs={{0,4},{1,5},{2,6},{3,7},{4,0},{5,1},{6,2},{7,3},{8,12},{9,13},{10,... | collective-permute-start | bytes 122888 | tf_op jit(solution)/shard_map/ppermute | solution.py:679
  135.1 13.1 %collective-permute-start.31 = (f32[16,640]{1,0:T(8,128)}, f32[16,640]{1,0:T(8,128)S(1)}, u32[]{:S(2)}, u32[]{:S(2)}) collective-permute-start(f32[16,640]{1,0:T(8,128)} %get-tuple-element.166), channel_id=1, source_target_pairs={{0,1},{1,0},{2,3},{3,2},{4,5},{5,4},{6,7},{7,6},{8,9},{9,8},{10,11... | collective-permute-start | bytes 122888 | tf_op jit(solution)/shard_map/ppermute | solution.py:679
  136.6 11.6 %collective-permute-start.32 = (f32[16,640]{1,0:T(8,128)}, f32[16,640]{1,0:T(8,128)S(1)}, u32[]{:S(2)}, u32[]{:S(2)}) collective-permute-start(f32[16,640]{1,0:T(8,128)} %get-tuple-element.167), channel_id=1, source_target_pairs={{0,2},{1,3},{2,0},{3,1},{4,6},{5,7},{6,4},{7,5},{8,10},{9,11},{10,... | collective-permute-start | bytes 122888 | tf_op jit(solution)/shard_map/ppermute | solution.py:679
  138.1 10.1 %collective-permute-start.33 = (f32[16,640]{1,0:T(8,128)}, f32[16,640]{1,0:T(8,128)S(1)}, u32[]{:S(2)}, u32[]{:S(2)}) collective-permute-start(f32[16,640]{1,0:T(8,128)} %get-tuple-element.168), channel_id=1, source_target_pairs={{0,16},{8,24},{16,0},{24,8},{1,17},{9,25},{17,1},{25,9},{2,18},{10... | collective-permute-start | bytes 122888 | tf_op jit(solution)/shard_map/ppermute | solution.py:679
  139.6 8.6 %collective-permute-start.34 = (f32[16,640]{1,0:T(8,128)}, f32[16,640]{1,0:T(8,128)S(1)}, u32[]{:S(2)}, u32[]{:S(2)}) collective-permute-start(f32[16,640]{1,0:T(8,128)} %get-tuple-element.169), channel_id=1, source_target_pairs={{0,8},{8,0},{16,24},{24,16},{1,9},{9,1},{17,25},{25,17},{2,10},{10... | collective-permute-start | bytes 122888 | tf_op jit(solution)/shard_map/ppermute | solution.py:679
  (20 other events, 53.9 us)

commit v3 on v2

--- a/solution.py
+++ b/solution.py
@@ -11,13 +11,13 @@
 CAP = 8
 SUB_ROUNDS = 3
 ORDER = (2, 0, 1, 4, 3)
-NEAR = 3
 AXES = ("organ", "sub")
 LANES = 128
 F32 = jnp.float32
 BF16 = jnp.bfloat16
 VMEM_LIMIT = 24 * 2**20
 COST = 2_000_000
+BRING = 1
 
 
 def iota(shape, dim):
@@ -180,6 +180,7 @@
 
 def setup_kernel(blocks, count, owner, dofs, active, basis, message):
     devices = message.ref.shape[0]
+    owner, dofs, active, basis = owner(), dofs(), active(), basis()
     rows = owner.shape[1]
     column, live_row, _, _, _, rank_col = ranks(owner[...], active[...], count[0])
     named = (iota((devices, rows), 0) == owner[...]) & (live_row > 0)
@@ -206,6 +207,7 @@
     devices, count, owner, active, mortar, start_rows, right_rows, a_high, a_low, t_high, t_low,
     start, right,
 ):
+    owner, active = owner(), active()
     rows = owner.shape[1]
     width = CAP * devices
     _, live_row, live_col, owner_col, rank_row, rank_col = ranks(
@@ -237,6 +239,7 @@
     devices = arrived.shape[0]
     subs = devices // organs
     blocks = len(sends)
+    basis = basis()
     modes = basis.shape[0] // blocks
     length = basis.shape[2]
     dofs = arrived[...]
@@ -299,20 +302,8 @@
         unit.ref[k * devices : (k + 1) * devices, :] = block
 
 
-def smooth(inner, near, far, smoothed, f):
-    early = near.shape[0]
-    matrix = near[f] if f < early else far(f - early)[...]
-    smoothed[f] = times_split(inner[f], matrix)
-
-
-def fetch(matrices, near, sems):
-    copies = [
-        pltpu.make_async_copy(matrices.at[f], near.at[f], sems.at[f])
-        for f in range(near.shape[0])
-    ]
-    for copy in copies:
-        copy.start()
-    return copies
+def smooth(inner, near, smoothed, f):
+    smoothed[f] = times_split(inner[f], near[f])
 
 
 def subtract_modes(field, columns, basis, f):
@@ -323,11 +314,10 @@
 
 
 def start_contact(
-    organs, arrived, sent, start, a_high, a_low, unit, modes_ref, right, matrices, new_right,
-    base, added, near, sems,
+    organs, arrived, sent, start, a_high, a_low, unit, modes_ref, right, new_right,
+    base, added,
 ):
     sent, start, maps = sent(), start(), (a_high(), a_low(), unit())
-    copies = fetch(matrices, near, sems)
     devices = sent.shape[0] // 4
     subs = devices // organs
     blocks, directions = start.shape[0], start.shape[1]
@@ -355,12 +345,10 @@
             stack.append(jnp.where(source == o, other_half, 0.0) + owns * own_half)
         stacks.append(jnp.concatenate(stack, axis=0))
     added[...] = times(stacks[0], maps[0][...], maps[1][...]) + exact(stacks[1], maps[2][...])
-    for copy in copies:
-        copy.wait()
 
 
 def start_kernel(
-    organs, matches, f0, f1, f2, f3, f4, base, added, near, t_high, t_low, unit_t, modes_ref, far,
+    organs, matches, f0, f1, f2, f3, f4, base, added, t_high, t_low, unit_t, near, modes_ref,
     message, smoothed_out, jump_out, s0, s1, s2, s3, s4, inner,
 ):
     faces = (f0, f1, f2, f3, f4)
@@ -369,13 +357,12 @@
     for r, face in zip(ORDER, faces, strict=True):
         inner[matches[r]] = base[matches[r]] - face[0:directions, :]
     for f in range(blocks):
-        smooth(inner, near, far, smoothed, f)
+        smooth(inner, near, smoothed, f)
     for r, send in enumerate((s0, s1, s2, s3, s4)):
         send(smoothed.at[matches[r]])
     smoothed_out.flush()
-    send_contact(message.ref, 2, smoothed[0], t_high(), t_low(), unit_t())
+    send_contact(message.ref, 2, smoothed[0], t_high, t_low, unit_t)
     message.flush()
-    modes_ref = modes_ref()
     modes = modes_ref.shape[0]
     jump_modes = jump_out.ref
     organ = lax.axis_index("organ")
@@ -415,18 +402,17 @@
     for r, send in enumerate(sends):
         send(resid.ref.at[matches[r]])
     resid.flush()
-    send_contact(message.ref, 4, resid.ref[0], *(late() for late in maps))
-    spread_rows(message.ref, 4, 2, coefficients_row(resid.ref, modes_ref()))
+    send_contact(message.ref, 4, resid.ref[0], *maps)
+    spread_rows(message.ref, 4, 2, coefficients_row(resid.ref, modes_ref))
     message.flush()
 
 
 def inner_contact(
-    organs, arrived, sent, resid, a_high, a_low, unit, modes_ref, jump_modes, matrices,
-    projected_out, base, near, norms, sems,
+    organs, arrived, sent, resid, a_high, a_low, unit, modes_ref, jump_modes, projected_out, base,
+    norms,
 ):
     sent, resid, maps = sent(), resid(), (a_high(), a_low(), unit())
     modes_ref, jump_modes = modes_ref(), jump_modes()
-    copies = fetch(matrices, near, sems)
     devices = sent.shape[0] // 4
     subs = devices // organs
     blocks, directions = resid.shape[0], resid.shape[1]
@@ -450,16 +436,14 @@
         value = resid[f] - times_split(left, jump_modes[f])
         base[f] = value + added if f == 0 else value
     norms[...] = jnp.broadcast_to(dots_row([(projected, projected)]), norms.shape)
-    for copy in copies:
-        copy.wait()
-
-
-def inner_kernel(last, older, matches, f0, f1, f2, f3, f4, base, near, norms, *refs):
+
+
+def inner_kernel(last, older, matches, f0, f1, f2, f3, f4, base, norms, near, *refs):
     rest = list(refs)
     previous = rest.pop(0) if older else None
     maps = None if last else rest[:3]
-    far, message = rest[0 if last else 3 :][:2]
-    rest = rest[2 if last else 5 :]
+    message = rest[0 if last else 3]
+    rest = rest[1 if last else 4 :]
     if last:
         inner, smoothed = rest
     else:
@@ -468,17 +452,17 @@
     for r, face in zip(ORDER, (f0, f1, f2, f3, f4), strict=True):
         inner[matches[r]] = base[matches[r]] - face[...]
     for f in range(inner.shape[0]):
-        smooth(inner, near, far, smoothed, f)
+        smooth(inner, near, smoothed, f)
     if not last:
         for r, send in enumerate(rest[2:]):
             send(smoothed.at[matches[r]])
         inner_out.flush()
         smoothed_out.flush()
-        send_contact(message.ref, 4, smoothed[0], *(late() for late in maps))
+        send_contact(message.ref, 4, smoothed[0], *maps)
     directions = inner.shape[1]
     pairs = [(inner, smoothed)]
     if older:
-        pairs.append((previous(), smoothed))
+        pairs.append((previous, smoothed))
     row = dots_row(pairs, directions) + norms[0:1, :]
     if last:
         message.ref[...] = jnp.broadcast_to(row, message.ref.shape)
@@ -573,25 +557,16 @@
 
 
 class Late:
-    def __init__(self, source, target, sems):
-        self.target = target
-        if sems.shape[0] == 1:
-            self.copies = [pltpu.make_async_copy(source, target, sems.at[0])]
-        else:
-            self.copies = [
-                pltpu.make_async_copy(source.at[i], target.at[i], sems.at[i])
-                for i in range(sems.shape[0])
-            ]
-        self.waiting = [True] * len(self.copies)
-        for copy in self.copies:
-            copy.start()
-
-    def __call__(self, part=None):
-        for i, copy in enumerate(self.copies):
-            if self.waiting[i] and part in (None, i):
-                copy.wait()
-                self.waiting[i] = False
-        return self.target if part is None else self.target.at[part]
+    def __init__(self, source, target, sem):
+        self.target, self.waiting = target, True
+        self.copy = pltpu.make_async_copy(source, target, sem)
+        self.copy.start()
+
+    def __call__(self):
+        if self.waiting:
+            self.copy.wait()
+            self.waiting = False
+        return self.target
 
 
 class Send:
@@ -615,8 +590,9 @@
             self.started = True
 
 
-def call(kernel, outs, args, late=(), smem=0, near=(), sends=(), scratch=(), whole=(), far=()):
+def call(kernel, outs, args, late=(), smem=0, near=(), sends=(), scratch=(), bring=()):
     n_late, n_out, n_arg, n_near = len(late), len(outs), len(args), len(near)
+    brought = [(a.shape, a.dtype) for a in bring]
 
     def body(*refs):
         refs = list(refs)
@@ -626,21 +602,25 @@
             del refs[:n]
             return taken
 
-        given, sources, lasting = take(n_arg), take(n_late), take(len(whole))
-        remote = take(len(far))
+        given, sources, origins = take(n_arg), take(n_late), take(len(bring))
         targets, ports, close = take(n_out), take(len(sends)), take(n_near)
-        buffers, ahead, results = take(n_late), take(len(far)), take(n_out)
+        goals = take(len(bring))
+        buffers, results = take(n_late), take(n_out)
         extra = take(len(scratch))
-        in_sems, far_sems, out_sem = take(n_late), take(len(far)), refs[0]
-        lates = [Late(s, b, m) for s, b, m in zip(sources, buffers, in_sems, strict=True)]
-        for source, buffer, sem in zip(remote, ahead, far_sems, strict=True):
-            skip = source.shape[0] - buffer.shape[0]
-            lates.append(Late(source.at[pl.ds(skip, buffer.shape[0])], buffer, sem))
+        in_sem, bring_sem, out_sem = refs
+        lates = [Late(s, b, in_sem.at[i]) for i, (s, b) in enumerate(zip(sources, buffers))]
         written = [Out(r, t, out_sem.at[i]) for i, (r, t) in enumerate(zip(results, targets))]
         posts = [Send(t, out_sem.at[n_out + i]) for i, t in enumerate(ports)]
-        kernel(*given, *lates, *lasting, *written, *posts, *close, *extra)
+        copies = []
+        for i, (origin, goal) in enumerate(zip(origins, goals, strict=True)):
+            copies.append(pltpu.make_async_copy(origin, goal, bring_sem.at[i]))
+        for copy in copies:
+            copy.start(priority=BRING)
+        kernel(*given, *lates, *written, *posts, *close, *extra)
         for item in lates:
             item()
+        for copy in copies:
+            copy.wait()
         for item in written:
             item.flush()
         for item in written + posts:
@@ -648,28 +628,24 @@
 
     in_specs = [pl.BlockSpec(memory_space=pltpu.SMEM)] * smem
     in_specs += [pl.BlockSpec(memory_space=pltpu.VMEM)] * (n_arg - smem)
-    remote = tuple(late) + tuple(whole) + tuple(a for a, _ in far)
+    remote = tuple(late) + tuple(bring)
     in_specs += [pl.BlockSpec(memory_space=pltpu.HBM)] * len(remote)
     out_specs = [pl.BlockSpec(memory_space=pltpu.HBM)] * (n_out + len(sends))
-    out_specs += [pl.BlockSpec(memory_space=pltpu.VMEM)] * n_near
+    out_specs += [pl.BlockSpec(memory_space=pltpu.VMEM)] * (n_near + len(bring))
     scratch_shapes = [pltpu.VMEM(a.shape, a.dtype) for a in late]
-    scratch_shapes += [pltpu.VMEM((n,) + a.shape[1:], a.dtype) for a, n in far]
     scratch_shapes += [pltpu.VMEM(shape, kind) for shape, kind in outs]
     scratch_shapes += list(scratch)
-    scratch_shapes += [pltpu.SemaphoreType.DMA((1,))] * n_late
-    scratch_shapes += [pltpu.SemaphoreType.DMA((n,)) for _, n in far]
-    scratch_shapes += [pltpu.SemaphoreType.DMA((max(n_out + len(sends), 1),))]
+    counts = (n_late, len(bring), n_out + len(sends))
+    scratch_shapes += [pltpu.SemaphoreType.DMA((max(n, 1),)) for n in counts]
     return pl.pallas_call(
         body,
         out_shape=[pltpu.HBM(shape, kind) for shape, kind in tuple(outs) + tuple(sends)]
-        + [pltpu.VMEM(shape, kind) for shape, kind in near],
+        + [pltpu.VMEM(shape, kind) for shape, kind in list(near) + brought],
         in_specs=in_specs,
         out_specs=out_specs,
         scratch_shapes=scratch_shapes,
         compiler_params=pltpu.CompilerParams(vmem_limit_bytes=VMEM_LIMIT),
-        cost_estimate=pl.CostEstimate(
-            flops=COST, bytes_accessed=COST, transcendentals=0
-        ),
+        cost_estimate=pl.CostEstimate(flops=COST, bytes_accessed=COST, transcendentals=0),
     )(*args, *(pltpu.with_memory_space_constraint(a, pltpu.HBM) for a in remote))
 
 
@@ -717,22 +693,21 @@
     message_line = ((4 * devices, LANES), F32)
 
     sends = [face] * blocks
-    near_shape = ((NEAR, length, length), F32)
-    fetching = [pltpu.SemaphoreType.DMA((NEAR,))]
-    far = ((matrices, blocks - NEAR),)
+    near_matrices = (matrices,)
 
     (setup,) = call(
         functools.partial(setup_kernel, blocks),
         [((devices, LANES), F32)],
-        (count, owner, dofs, active, basis),
+        (count,),
+        (owner, dofs, active, basis),
         smem=1,
     )
     arrived = exchange(setup)
     a_high, a_low, t_high, t_low, start, right = call(
         functools.partial(slots_kernel, devices),
         [((width, length), BF16)] * 2 + [((length, width), BF16)] * 2 + [whole] * 2,
-        (count, owner, active),
-        (mortar, start_rows, right_rows),
+        (count,),
+        (owner, active, mortar, start_rows, right_rows),
         smem=1,
     )
     sent, unit_t, unit, modes_ref, *faces = call(
@@ -744,43 +719,45 @@
             ((modes, blocks, length), F32),
         ]
         + [((directions + 8, length), F32)] * blocks,
-        (matches, arrived, basis),
-        (start, t_high, t_low, right),
+        (matches, arrived),
+        (basis, start, t_high, t_low, right),
         smem=1,
     )
     forth = (a_high, a_low, unit)
     back = (t_high, t_low, unit_t)
+    back_modes = back + (modes_ref,)
     arrived = exchange(sent)
     faces = swap_faces(faces)
-    right, base, added, near = call(
+    right, base, added, *maps, modes_near, near = call(
         functools.partial(start_contact, organs),
         [whole],
         (arrived,),
         (sent, start) + forth + (modes_ref, right),
-        whole=(matrices,),
-        near=[whole, ((8 * organs, length), F32), near_shape],
-        scratch=fetching,
+        near=[whole, ((8 * organs, length), F32)],
+        bring=back_modes + near_matrices,
     )
     message, smoothed, jump_modes, *posts = call(
         functools.partial(start_kernel, organs),
         [((2 * devices, LANES), F32), whole, ((blocks, 8 * organs, length), F32)],
-        (matches, *faces, base, added, near),
-        back + (modes_ref,),
-        far=far,
+        (matches, *faces, base, added, *maps, near, modes_near),
         smem=1,
         sends=sends,
         scratch=[pltpu.VMEM(field, F32)],
     )
     arrived = exchange(message)
     faces = swap_faces(posts)
-    (part,) = call(
-        residual_contact, [], (arrived,), (message, smoothed) + forth + (right,), near=[whole]
+    part, *maps = call(
+        residual_contact,
+        [],
+        (arrived,),
+        (message, smoothed) + forth + (right,),
+        near=[whole],
+        bring=back_modes,
     )
     sent, resid, *posts = call(
         residual_kernel,
         [message_line, whole],
-        (matches, *faces, part),
-        back + (modes_ref,),
+        (matches, *faces, part, *maps),
         smem=1,
         sends=sends,
     )
@@ -790,24 +767,21 @@
         older, last = step > 0, step == ITERS - 1
         arrived = exchange(sent)
         faces = swap_faces(posts)
-        projected, base, near, norms = call(
+        ahead = near_matrices + ((inner,) if older else ()) + (() if last else back)
+        projected, base, norms, *ahead = call(
             functools.partial(inner_contact, organs),
             [whole],
             (arrived,),
             (sent, resid) + forth + (modes_ref, jump_modes),
-            whole=(matrices,),
-            near=[whole, near_shape, ((8, LANES), F32)],
-            scratch=fetching,
+            near=[whole, ((8, LANES), F32)],
+            bring=ahead,
         )
-        previous = (inner,) if older else ()
         if last:
             (message,) = call(
                 functools.partial(inner_kernel, last, older),
                 [((devices, LANES), F32)],
-                (matches, *faces, base, near, norms),
-                previous,
-                far=far,
-                smem=1,
+                (matches, *faces, base, norms, *ahead),
+                        smem=1,
                 scratch=[pltpu.VMEM(field, F32)] * 2,
             )
             arrived = exchange(message)
@@ -815,26 +789,24 @@
         message, new_inner, smoothed, *posts = call(
             functools.partial(inner_kernel, last, older),
             [message_line, whole, whole],
-            (matches, *faces, base, near, norms),
-            previous + back,
-            far=far,
-            smem=1,
+            (matches, *faces, base, norms, *ahead),
+                smem=1,
             sends=sends,
         )
         arrived = exchange(message)
         faces = swap_faces(posts)
-        new_scalars, part, steps, image_part = call(
+        new_scalars, part, steps, image_part, *maps = call(
             functools.partial(outer_contact, older),
             [((4, directions, LANES), F32)],
             (arrived,),
             (message, smoothed) + forth + (projected,) + ((image, scalars) if older else ()),
             near=[whole, ((directions, LANES), F32), whole],
+            bring=back_modes,
         )
         sent, resid, *posts = call(
             functools.partial(outer_kernel, older),
             [message_line, whole] + ([] if older else [whole]),
-            (matches, *faces, part, steps, image_part),
-            back + (modes_ref,),
+            (matches, *faces, part, steps, image_part, *maps),
             smem=1,
             sends=sends,
         )

time: 166 us -> 151 us (0.910)
  Pallas kernels: 66.3 us -> 56.5 us
  local copies, waits for them, and re-layouts: 5.69 us -> 0.66 us
    pallas_call x20, Pallas kernels: 66.3 us -> 56.5 us  [call(): pl.pallas_call(body, out_shape=[pltpu.HBM(shape, kind) for shape, kind in...]
    unnamed x18 -> x4, local copies, waits for them, and re-layouts: 5.69 us -> 0.66 us
  transfers between devices with their start and end apart: 43 -> 43, of which waited for: 9 -> 9; matrix products, arithmetic and copies ran while one was open for 0% -> 0% of each run, Pallas kernels for 18% -> 20%
where the time goes in v3:
time: 151 us; the launch traced here: 150 us
  starting transfers between devices  75.9 us (50%)
  Pallas kernels  56.5 us (37%)
  blocking collectives  9.6 us (6%)
  waiting for transfers between devices  6.49 us (4%)
    pallas_call x20, Pallas kernels, call(): pl.pallas_call(body, out_shape=[pltpu.HBM(shape, kind) for shape, kind in...  56.5 us
    ppermute x35, starting transfers between devices, from_partner(): return lax.ppermute(value, axis, pairs)  50.4 us
    all_to_all x8, starting transfers between devices, exchange(): lax.all_to_all(message, AXES, split_axis=0, concat_axis=0, tiled=True)  25.5 us
    all_to_all x1, blocking collectives, exchange(): lax.all_to_all(message, AXES, split_axis=0, concat_axis=0, tiled=True)  9.6 us
    all_to_all x8, waiting for transfers between devices, exchange(): lax.all_to_all(message, AXES, split_axis=0, concat_axis=0, tiled=True)  5.17 us
  transfers between devices with their start and end apart: 43, of which 9 were waited for; matrix products, arithmetic and copies ran while one was open for 0% of the time, Pallas kernels for 20%

profile of v3, /device:TPU:0, one launch (start us, length us, event | category | flops | bytes accessed | tf_op | source)
XLA Modules:
  0.0 150.5 jit_solution(9452634796642113470)
XLA Ops:
  2.6 7.3 %all-to-all-start = ((f32[32,1,128]{2,1,0:T(1,128)}), f32[32,1,128]{2,1,0:T(1,128)S(1)}, u32[]{:S(2)}, u32[]{:S(2)}) async-start(f32[32,1,128]{2,1,0:T(1,128)} %bitcast.71), calls=%async_computation | async-start | bytes 32768 | tf_op jit(solution)/shard_map/all_to_all | solution.py:659
  9.9 2.8 %shard_map.101 = (bf16[256,640]{1,0:T(8,128)(2,1)}, bf16[256,640]{1,0:T(8,128)(2,1)}, bf16[640,256]{1,0:T(8,128)(2,1)}, bf16[640,256]{1,0:T(8,128)(2,1)}, f32[5,16,640]{2,1,0:T(8,128)}, /*index=5*/f32[5,16,640]{2,1,0:T(8,128)}) custom-call(s32[1]{0:T(128)} %bitcast.36.refs_0_, s32[1,128]{1,0:T(1,128)} %bitcast.73, s32[1,128]{1,0:T(1,128)} %bitcast.75, ...), custom_call_target="tpu_custom_call" | custom-call | flops 2000000 | bytes 2000000 | tf_op jit(solution)/shard_map/pallas_call | solution.py:640
  12.7 4.3 %all-to-all-done = f32[32,1,128]{2,1,0:T(1,128)S(1)} async-done(((f32[32,1,128]{2,1,0:T(1,128)}), f32[32,1,128]{2,1,0:T(1,128)S(1)}, u32[]{:S(2)}, u32[]{:S(2)}) %all-to-all-start) | async-done | bytes 16416 | tf_op jit(solution)/shard_map/all_to_all | solution.py:659
  17.7 3.6 %shard_map.102 = (f32[128,128]{1,0:T(8,128)}, bf16[640,256]{1,0:T(8,128)(2,1)}, bf16[256,640]{1,0:T(8,128)(2,1)}, f32[6,5,640]{2,1,0:T(8,128)}, f32[24,640]{1,0:...) custom-call(s32[5]{0:T(128)S(1)} %bitcast.46, ...), custom_call_target="tpu_custom_call" | custom-call | flops 2000000 | bytes 2000000 | tf_op jit(solution)/shard_map/pallas_call | solution.py:640
  21.3 2.6 %all-to-all-start.1 = ((f32[32,4,128]{2,1,0:T(4,128)}), f32[32,4,128]{2,1,0:T(4,128)S(1)}, u32[]{:S(2)}, u32[]{:S(2)}) async-start(f32[32,4,128]{2,1,0:T(4,128)} %bitcast.64), calls=%async_computation.1 | async-start | bytes 131072 | tf_op jit(solution)/shard_map/all_to_all | solution.py:659
  23.9 2.7 %collective-permute-start = (f32[24,640]{1,0:T(8,128)}, f32[24,640]{1,0:T(8,128)S(1)}, u32[]{:S(2)}, u32[]{:S(2)}) collective-permute-start(f32[24,640]{1,0:T(8,128)} %get-tuple-element.122), channel_id=1, source_target_pairs={{0,4},{1,5},{2,6},{3,7},{4,0},{5,1},{6,2},{7,3},{8,12},{9,13},{10,... | collective-permute-start | bytes 184328 | tf_op jit(solution)/shard_map/ppermute | solution.py:655
  31.2 4.4 %shard_map.103 = (f32[5,16,640]{2,1,0:T(8,128)}, f32[5,16,640]{2,1,0:T(8,128)S(1)}, f32[32,640]{1,0:T(8,128)S(1)}, bf16[640,256]{1,0:T(8,128)(2,1)S(1)}, bf16[64...) custom-call(f32[128,128]{1,0:T(8,128)S(1)} %bitcast.38, ...), custom_call_target="tpu_custom_call" | custom-call | flops 2000000 | bytes 2000000 | tf_op jit(solution)/shard_map/pallas_call | solution.py:640
  35.7 3.4 %shard_map.104 = (f32[64,128]{1,0:T(8,128)}, f32[5,16,640]{2,1,0:T(8,128)}, f32[5,32,640]{2,1,0:T(8,128)}, f32[16,640]{1,0:T(8,128)}, f32[16,640]{1,0:T(8,128)},...) custom-call(s32[5]{0:T(128)S(1)} %bitcast.47, f32[24,640]{1,0:T(8,128)S(1)} %collective-permute-done.refs_1_, ...), custom_call_target="tpu_custom_call" | custom-call | flops 2000000 | bytes 2000000 | tf_op jit(solution)/shard_map/pallas_call | solution.py:640
  39.1 2.6 %all-to-all-start.2 = ((f32[32,2,128]{2,1,0:T(2,128)}), f32[32,2,128]{2,1,0:T(2,128)S(1)}, u32[]{:S(2)}, u32[]{:S(2)}) async-start(f32[32,2,128]{2,1,0:T(2,128)} %bitcast.69), calls=%async_computation.2 | async-start | bytes 65536 | tf_op jit(solution)/shard_map/all_to_all | solution.py:659
  41.6 2.7 %collective-permute-start.5 = (f32[16,640]{1,0:T(8,128)}, f32[16,640]{1,0:T(8,128)S(1)}, u32[]{:S(2)}, u32[]{:S(2)}) collective-permute-start(f32[16,640]{1,0:T(8,128)} %get-tuple-element.140), channel_id=1, source_target_pairs={{0,4},{1,5},{2,6},{3,7},{4,0},{5,1},{6,2},{7,3},{8,12},{9,13},{10,... | collective-permute-start | bytes 122888 | tf_op jit(solution)/shard_map/ppermute | solution.py:655
  53.4 2.6 %all-to-all-start.3 = ((f32[32,4,128]{2,1,0:T(4,128)}), f32[32,4,128]{2,1,0:T(4,128)S(1)}, u32[]{:S(2)}, u32[]{:S(2)}) async-start(f32[32,4,128]{2,1,0:T(4,128)} %bitcast.63), calls=%async_computation.3 | async-start | bytes 131072 | tf_op jit(solution)/shard_map/all_to_all | solution.py:659
  56.0 2.7 %collective-permute-start.10 = (f32[16,640]{1,0:T(8,128)}, f32[16,640]{1,0:T(8,128)S(1)}, u32[]{:S(2)}, u32[]{:S(2)}) collective-permute-start(f32[16,640]{1,0:T(8,128)} %get-tuple-element.153), channel_id=1, source_target_pairs={{0,4},{1,5},{2,6},{3,7},{4,0},{5,1},{6,2},{7,3},{8,12},{9,13},{10,... | collective-permute-start | bytes 122888 | tf_op jit(solution)/shard_map/ppermute | solution.py:655
  63.3 4.3 %shard_map.107 = (f32[5,16,640]{2,1,0:T(8,128)}, f32[5,16,640]{2,1,0:T(8,128)S(1)}, f32[8,128]{1,0:T(8,128)S(1)}, f32[5,640,640]{2,1,0:T(8,128)S(1)}, bf16[640,2...) custom-call(f32[128,128]{1,0:T(8,128)S(1)} %bitcast.39, ...), custom_call_target="tpu_custom_call" | custom-call | flops 2000000 | bytes 2000000 | tf_op jit(solution)/shard_map/pallas_call | solution.py:640
  67.7 3.2 %shard_map.108 = (f32[128,128]{1,0:T(8,128)}, f32[5,16,640]{2,1,0:T(8,128)}, f32[5,16,640]{2,1,0:T(8,128)}, f32[16,640]{1,0:T(8,128)}, f32[16,640]{1,0:T(8,128)}...) custom-call(s32[5]{0:T(128)S(1)} %bitcast.49, f32[16,640]{1,0:T(8,128)S(1)} %collective-permute-done.10.refs_1_, ...), custom_call_target="tpu_custom_call" | custom-call | flops 2000000 | bytes 2000000 | tf_op jit(solution)/shard_map/pallas_call | solution.py:640
  70.8 2.6 %all-to-all-start.4 = ((f32[32,4,128]{2,1,0:T(4,128)}), f32[32,4,128]{2,1,0:T(4,128)S(1)}, u32[]{:S(2)}, u32[]{:S(2)}) async-start(f32[32,4,128]{2,1,0:T(4,128)} %bitcast.66), calls=%async_computation.4 | async-start | bytes 131072 | tf_op jit(solution)/shard_map/all_to_all | solution.py:659
  73.4 2.7 %collective-permute-start.15 = (f32[16,640]{1,0:T(8,128)}, f32[16,640]{1,0:T(8,128)S(1)}, u32[]{:S(2)}, u32[]{:S(2)}) collective-permute-start(f32[16,640]{1,0:T(8,128)} %get-tuple-element.167), channel_id=1, source_target_pairs={{0,4},{1,5},{2,6},{3,7},{4,0},{5,1},{6,2},{7,3},{8,12},{9,13},{10,... | collective-permute-start | bytes 122888 | tf_op jit(solution)/shard_map/ppermute | solution.py:655
  80.8 2.2 %shard_map.109 = (f32[4,16,128]{2,1,0:T(8,128)}, f32[5,16,640]{2,1,0:T(8,128)S(1)}, f32[16,128]{1,0:T(8,128)S(1)}, f32[5,16,640]{2,1,0:T(8,128)S(1)}, bf16[640,2...) custom-call(f32[128,128]{1,0:T(8,128)S(1)} %bitcast.42, ...), custom_call_target="tpu_custom_call" | custom-call | flops 2000000 | bytes 2000000 | tf_op jit(solution)/shard_map/pallas_call | solution.py:640
  85.3 2.8 %all-to-all-start.5 = ((f32[32,4,128]{2,1,0:T(4,128)}), f32[32,4,128]{2,1,0:T(4,128)S(1)}, u32[]{:S(2)}, u32[]{:S(2)}) async-start(f32[32,4,128]{2,1,0:T(4,128)} %bitcast.62), calls=%async_computation.5 | async-start | bytes 131072 | tf_op jit(solution)/shard_map/all_to_all | solution.py:659
  88.1 2.5 %collective-permute-start.20 = (f32[16,640]{1,0:T(8,128)}, f32[16,640]{1,0:T(8,128)S(1)}, u32[]{:S(2)}, u32[]{:S(2)}) collective-permute-start(f32[16,640]{1,0:T(8,128)} %get-tuple-element.182), channel_id=1, source_target_pairs={{0,4},{1,5},{2,6},{3,7},{4,0},{5,1},{6,2},{7,3},{8,12},{9,13},{10,... | collective-permute-start | bytes 122888 | tf_op jit(solution)/shard_map/ppermute | solution.py:655
  95.3 4.3 %shard_map.111 = (f32[5,16,640]{2,1,0:T(8,128)}, f32[5,16,640]{2,1,0:T(8,128)S(1)}, f32[8,128]{1,0:T(8,128)S(1)}, f32[5,640,640]{2,1,0:T(8,128)S(1)}, f32[5,16,6...) custom-call(f32[128,128]{1,0:T(8,128)S(1)} %bitcast.40, ...), custom_call_target="tpu_custom_call" | custom-call | flops 2000000 | bytes 2000000 | tf_op jit(solution)/shard_map/pallas_call | solution.py:640
  99.7 3.3 %shard_map.112 = (f32[128,128]{1,0:T(8,128)}, f32[5,16,640]{2,1,0:T(8,128)}, f32[5,16,640]{2,1,0:T(8,128)}, f32[16,640]{1,0:T(8,128)}, f32[16,640]{1,0:T(8,128)}...) custom-call(s32[5]{0:T(128)S(1)} %bitcast.51, f32[16,640]{1,0:T(8,128)S(1)} %collective-permute-done.20.refs_1_, ...), custom_call_target="tpu_custom_call" | custom-call | flops 2000000 | bytes 2000000 | tf_op jit(solution)/shard_map/pallas_call | solution.py:640
  103.0 2.6 %all-to-all-start.6 = ((f32[32,4,128]{2,1,0:T(4,128)}), f32[32,4,128]{2,1,0:T(4,128)S(1)}, u32[]{:S(2)}, u32[]{:S(2)}) async-start(f32[32,4,128]{2,1,0:T(4,128)} %bitcast.65), calls=%async_computation.6 | async-start | bytes 131072 | tf_op jit(solution)/shard_map/all_to_all | solution.py:659
  105.5 2.7 %collective-permute-start.25 = (f32[16,640]{1,0:T(8,128)}, f32[16,640]{1,0:T(8,128)S(1)}, u32[]{:S(2)}, u32[]{:S(2)}) collective-permute-start(f32[16,640]{1,0:T(8,128)} %get-tuple-element.197), channel_id=1, source_target_pairs={{0,4},{1,5},{2,6},{3,7},{4,0},{5,1},{6,2},{7,3},{8,12},{9,13},{10,... | collective-permute-start | bytes 122888 | tf_op jit(solution)/shard_map/ppermute | solution.py:655
  112.9 2.4 %shard_map.113 = (f32[4,16,128]{2,1,0:T(8,128)}, f32[5,16,640]{2,1,0:T(8,128)S(1)}, f32[16,128]{1,0:T(8,128)S(1)}, f32[5,16,640]{2,1,0:T(8,128)S(1)}, bf16[640,2...) custom-call(f32[128,128]{1,0:T(8,128)S(1)} %bitcast.41, ...), custom_call_target="tpu_custom_call" | custom-call | flops 2000000 | bytes 2000000 | tf_op jit(solution)/shard_map/pallas_call | solution.py:640
  117.3 2.6 %all-to-all-start.7 = ((f32[32,4,128]{2,1,0:T(4,128)}), f32[32,4,128]{2,1,0:T(4,128)S(1)}, u32[]{:S(2)}, u32[]{:S(2)}) async-start(f32[32,4,128]{2,1,0:T(4,128)} %bitcast.61), calls=%async_computation.7 | async-start | bytes 131072 | tf_op jit(solution)/shard_map/all_to_all | solution.py:659
  119.9 2.7 %collective-permute-start.30 = (f32[16,640]{1,0:T(8,128)}, f32[16,640]{1,0:T(8,128)S(1)}, u32[]{:S(2)}, u32[]{:S(2)}) collective-permute-start(f32[16,640]{1,0:T(8,128)} %get-tuple-element.214), channel_id=1, source_target_pairs={{0,4},{1,5},{2,6},{3,7},{4,0},{5,1},{6,2},{7,3},{8,12},{9,13},{10,... | collective-permute-start | bytes 122888 | tf_op jit(solution)/shard_map/ppermute | solution.py:655
  127.2 1.9 %shard_map.115.refs_2_ = f32[5,16,640]{2,1,0:T(8,128)} custom-call(f32[5,16,640]{2,1,0:T(8,128)} %get-tuple-element.174.refs_6_.refs_0_.refs_4_, f32[5,16,640]{2,1,0:T(8,128)} %get-tuple-element.189.refs_9_.refs_1_.refs_5_, f32[5,16,640]{2,1,0:T(8,128)} %get-tuple-element.118.refs_3_.refs_2_, f32[4,16,128]{2,1,0:T(8,128)} %get-tuple-element.206.refs_8_.refs_3_), custom_call_target="tpu_custom_call" | custom-call | flops 2000000 | bytes 2000000 | tf_op jit(solution)/shard_map/pallas_call | solution.py:640
  129.1 2.3 %shard_map.116 = (f32[5,16,640]{2,1,0:T(8,128)}, f32[5,16,640]{2,1,0:T(8,128)}, f32[5,16,640]{2,1,0:T(8,128)}) custom-call(f32[5,16,640]{2,1,0:T(8,128)} %get-tuple-element.204.refs_6_.refs_0_, f32[5,16,640]{2,1,0:T(8,128)} %get-tuple-element.221.refs_1_, f32[5,16,640]{2,1,0:T(8,128)} %shard_map.115.refs_2_, ...), custom_call_target="tpu_custom_call" | custom-call | flops 2000000 | bytes 2000000 | tf_op jit(solution)/shard_map/pallas_call | solution.py:640
  131.5 4.1 %shard_map.117 = (f32[5,16,640]{2,1,0:T(8,128)}, f32[5,16,640]{2,1,0:T(8,128)S(1)}, f32[8,128]{1,0:T(8,128)S(1)}, f32[5,640,640]{2,1,0:T(8,128)S(1)}, f32[5,16,640]{2,1,0:T(8,128)S(1)}) custom-call(f32[128,128]{1,0:T(8,128)S(1)} %bitcast.37, f32[128,128]{1,0:T(8,128)} %get-tuple-element.219.refs_1_, f32[5,16,640]{2,1,0:T(8,128)} %get-tuple-element.220.refs_2_, ...), custom_call_target="tpu_custom_call" | custom-call | flops 2000000 | bytes 2000000 | tf_op jit(solution)/shard_map/pallas_call | solution.py:640
  135.6 3.0 %shard_map.118 = f32[32,128]{1,0:T(8,128)} custom-call(s32[5]{0:T(128)S(1)} %bitcast.53, f32[16,640]{1,0:T(8,128)S(1)} %collective-permute-done.30.refs_1_, f32[16,640]{1,0:T(8,128)S(1)} %collective-permute-done.31.refs_2_, f32[16,640]{1,0:T(8,128)S(1)} %collective-permute-done.32.refs_3_, f32[16,640]{1,0:T(8,128)S(1)} %collective-permute-done.33.refs_4_, ...), custom_call_target="tpu_custom_call" | custom-call | flops 2000000 | bytes 2000000 | tf_op jit(solution)/shard_map/pallas_call | solution.py:640
  138.6 9.6 %all_to_all.99 = f32[32,1,128]{2,1,0:T(1,128)S(1)} all-to-all(f32[32,1,128]{2,1,0:T(1,128)} %bitcast.70), channel_id=1, replica_groups=mesh['organ'=4,'sub'=8] {'organ','sub'}, dimensions={0} | all-to-all | bytes 32768 | tf_op jit(solution)/shard_map/all_to_all | solution.py:659
  148.2 2.1 %shard_map.119 = f32[80,1,640]{2,1,0:T(1,128)} custom-call(f32[32,128]{1,0:T(8,128)S(1)} %bitcast.45, f32[5,16,640]{2,1,0:T(8,128)} %get-tuple-element.228.refs_1_, f32[5,16,640]{2,1,0:T(8,128)} %get-tuple-element.229.refs_2_, f32[5,16,640]{2,1,0:T(8,128)} %get-tuple-element.230.refs_3_, f32[4,16,128]{2,1,0:T(8,128)} %get-tuple-element.222.refs_3_.refs_4_), custom_call_target="tpu_custom_call" | custom-call | flops 2000000 | bytes 2000000 | tf_op jit(solution)/shard_map/pallas_call | solution.py:640
  (79 shorter events, 43.8 us)
Async XLA Ops:
  2.6 14.4 %all-to-all-start = ((f32[32,1,128]{2,1,0:T(1,128)}), f32[32,1,128]{2,1,0:T(1,128)S(1)}, u32[]{:S(2)}, u32[]{:S(2)}) async-start(f32[32,1,128]{2,1,0:T(1,128)} %bitcast.71), calls=%async_computation | async-start | bytes 32768 | tf_op jit(solution)/shard_map/all_to_all | solution.py:659
  21.3 10.0 %all-to-all-start.1 = ((f32[32,4,128]{2,1,0:T(4,128)}), f32[32,4,128]{2,1,0:T(4,128)S(1)}, u32[]{:S(2)}, u32[]{:S(2)}) async-start(f32[32,4,128]{2,1,0:T(4,128)} %bitcast.64), calls=%async_computation.1 | async-start | bytes 131072 | tf_op jit(solution)/shard_map/all_to_all | solution.py:659
  23.9 11.8 %collective-permute-start = (f32[24,640]{1,0:T(8,128)}, f32[24,640]{1,0:T(8,128)S(1)}, u32[]{:S(2)}, u32[]{:S(2)}) collective-permute-start(f32[24,640]{1,0:T(8,128)} %get-tuple-element.122), channel_id=1, source_target_pairs={{0,4},{1,5},{2,6},{3,7},{4,0},{5,1},{6,2},{7,3},{8,12},{9,13},{10,... | collective-permute-start | bytes 184328 | tf_op jit(solution)/shard_map/ppermute | solution.py:655
  26.6 9.1 %collective-permute-start.1 = (f32[24,640]{1,0:T(8,128)}, f32[24,640]{1,0:T(8,128)S(1)}, u32[]{:S(2)}, u32[]{:S(2)}) collective-permute-start(f32[24,640]{1,0:T(8,128)} %get-tuple-element.123), channel_id=1, source_target_pairs={{0,1},{1,0},{2,3},{3,2},{4,5},{5,4},{6,7},{7,6},{8,9},{9,8},{10,11... | collective-permute-start | bytes 184328 | tf_op jit(solution)/shard_map/ppermute | solution.py:655
  28.1 7.6 %collective-permute-start.2 = (f32[24,640]{1,0:T(8,128)}, f32[24,640]{1,0:T(8,128)S(1)}, u32[]{:S(2)}, u32[]{:S(2)}) collective-permute-start(f32[24,640]{1,0:T(8,128)} %get-tuple-element.124), channel_id=1, source_target_pairs={{0,2},{1,3},{2,0},{3,1},{4,6},{5,7},{6,4},{7,5},{8,10},{9,11},{10,... | collective-permute-start | bytes 184328 | tf_op jit(solution)/shard_map/ppermute | solution.py:655
  29.6 6.1 %collective-permute-start.3 = (f32[24,640]{1,0:T(8,128)}, f32[24,640]{1,0:T(8,128)S(1)}, u32[]{:S(2)}, u32[]{:S(2)}) collective-permute-start(f32[24,640]{1,0:T(8,128)} %get-tuple-element.125), channel_id=1, source_target_pairs={{0,16},{8,24},{16,0},{24,8},{1,17},{9,25},{17,1},{25,9},{2,18},{10... | collective-permute-start | bytes 184328 | tf_op jit(solution)/shard_map/ppermute | solution.py:655
  39.1 9.8 %all-to-all-start.2 = ((f32[32,2,128]{2,1,0:T(2,128)}), f32[32,2,128]{2,1,0:T(2,128)S(1)}, u32[]{:S(2)}, u32[]{:S(2)}) async-start(f32[32,2,128]{2,1,0:T(2,128)} %bitcast.69), calls=%async_computation.2 | async-start | bytes 65536 | tf_op jit(solution)/shard_map/all_to_all | solution.py:659
  41.6 9.2 %collective-permute-start.5 = (f32[16,640]{1,0:T(8,128)}, f32[16,640]{1,0:T(8,128)S(1)}, u32[]{:S(2)}, u32[]{:S(2)}) collective-permute-start(f32[16,640]{1,0:T(8,128)} %get-tuple-element.140), channel_id=1, source_target_pairs={{0,4},{1,5},{2,6},{3,7},{4,0},{5,1},{6,2},{7,3},{8,12},{9,13},{10,... | collective-permute-start | bytes 122888 | tf_op jit(solution)/shard_map/ppermute | solution.py:655
  44.3 6.5 %collective-permute-start.6 = (f32[16,640]{1,0:T(8,128)}, f32[16,640]{1,0:T(8,128)S(1)}, u32[]{:S(2)}, u32[]{:S(2)}) collective-permute-start(f32[16,640]{1,0:T(8,128)} %get-tuple-element.141), channel_id=1, source_target_pairs={{0,1},{1,0},{2,3},{3,2},{4,5},{5,4},{6,7},{7,6},{8,9},{9,8},{10,11... | collective-permute-start | bytes 122888 | tf_op jit(solution)/shard_map/ppermute | solution.py:655
  53.4 10.0 %all-to-all-start.3 = ((f32[32,4,128]{2,1,0:T(4,128)}), f32[32,4,128]{2,1,0:T(4,128)S(1)}, u32[]{:S(2)}, u32[]{:S(2)}) async-start(f32[32,4,128]{2,1,0:T(4,128)} %bitcast.63), calls=%async_computation.3 | async-start | bytes 131072 | tf_op jit(solution)/shard_map/all_to_all | solution.py:659
  56.0 11.7 %collective-permute-start.10 = (f32[16,640]{1,0:T(8,128)}, f32[16,640]{1,0:T(8,128)S(1)}, u32[]{:S(2)}, u32[]{:S(2)}) collective-permute-start(f32[16,640]{1,0:T(8,128)} %get-tuple-element.153), channel_id=1, source_target_pairs={{0,4},{1,5},{2,6},{3,7},{4,0},{5,1},{6,2},{7,3},{8,12},{9,13},{10,... | collective-permute-start | bytes 122888 | tf_op jit(solution)/shard_map/ppermute | solution.py:655
  58.7 8.9 %collective-permute-start.11 = (f32[16,640]{1,0:T(8,128)}, f32[16,640]{1,0:T(8,128)S(1)}, u32[]{:S(2)}, u32[]{:S(2)}) collective-permute-start(f32[16,640]{1,0:T(8,128)} %get-tuple-element.154), channel_id=1, source_target_pairs={{0,1},{1,0},{2,3},{3,2},{4,5},{5,4},{6,7},{7,6},{8,9},{9,8},{10,11... | collective-permute-start | bytes 122888 | tf_op jit(solution)/shard_map/ppermute | solution.py:655
  60.2 7.5 %collective-permute-start.12 = (f32[16,640]{1,0:T(8,128)}, f32[16,640]{1,0:T(8,128)S(1)}, u32[]{:S(2)}, u32[]{:S(2)}) collective-permute-start(f32[16,640]{1,0:T(8,128)} %get-tuple-element.155), channel_id=1, source_target_pairs={{0,2},{1,3},{2,0},{3,1},{4,6},{5,7},{6,4},{7,5},{8,10},{9,11},{10,... | collective-permute-start | bytes 122888 | tf_op jit(solution)/shard_map/ppermute | solution.py:655
  61.7 5.9 %collective-permute-start.13 = (f32[16,640]{1,0:T(8,128)}, f32[16,640]{1,0:T(8,128)S(1)}, u32[]{:S(2)}, u32[]{:S(2)}) collective-permute-start(f32[16,640]{1,0:T(8,128)} %get-tuple-element.156), channel_id=1, source_target_pairs={{0,16},{8,24},{16,0},{24,8},{1,17},{9,25},{17,1},{25,9},{2,18},{10... | collective-permute-start | bytes 122888 | tf_op jit(solution)/shard_map/ppermute | solution.py:655
  70.8 10.0 %all-to-all-start.4 = ((f32[32,4,128]{2,1,0:T(4,128)}), f32[32,4,128]{2,1,0:T(4,128)S(1)}, u32[]{:S(2)}, u32[]{:S(2)}) async-start(f32[32,4,128]{2,1,0:T(4,128)} %bitcast.66), calls=%async_computation.4 | async-start | bytes 131072 | tf_op jit(solution)/shard_map/all_to_all | solution.py:659
  73.4 9.6 %collective-permute-start.15 = (f32[16,640]{1,0:T(8,128)}, f32[16,640]{1,0:T(8,128)S(1)}, u32[]{:S(2)}, u32[]{:S(2)}) collective-permute-start(f32[16,640]{1,0:T(8,128)} %get-tuple-element.167), channel_id=1, source_target_pairs={{0,4},{1,5},{2,6},{3,7},{4,0},{5,1},{6,2},{7,3},{8,12},{9,13},{10,... | collective-permute-start | bytes 122888 | tf_op jit(solution)/shard_map/ppermute | solution.py:655
  76.1 6.9 %collective-permute-start.16 = (f32[16,640]{1,0:T(8,128)}, f32[16,640]{1,0:T(8,128)S(1)}, u32[]{:S(2)}, u32[]{:S(2)}) collective-permute-start(f32[16,640]{1,0:T(8,128)} %get-tuple-element.168), channel_id=1, source_target_pairs={{0,1},{1,0},{2,3},{3,2},{4,5},{5,4},{6,7},{7,6},{8,9},{9,8},{10,11... | collective-permute-start | bytes 122888 | tf_op jit(solution)/shard_map/ppermute | solution.py:655
  85.3 10.0 %all-to-all-start.5 = ((f32[32,4,128]{2,1,0:T(4,128)}), f32[32,4,128]{2,1,0:T(4,128)S(1)}, u32[]{:S(2)}, u32[]{:S(2)}) async-start(f32[32,4,128]{2,1,0:T(4,128)} %bitcast.62), calls=%async_computation.5 | async-start | bytes 131072 | tf_op jit(solution)/shard_map/all_to_all | solution.py:659
  88.1 11.5 %collective-permute-start.20 = (f32[16,640]{1,0:T(8,128)}, f32[16,640]{1,0:T(8,128)S(1)}, u32[]{:S(2)}, u32[]{:S(2)}) collective-permute-start(f32[16,640]{1,0:T(8,128)} %get-tuple-element.182), channel_id=1, source_target_pairs={{0,4},{1,5},{2,6},{3,7},{4,0},{5,1},{6,2},{7,3},{8,12},{9,13},{10,... | collective-permute-start | bytes 122888 | tf_op jit(solution)/shard_map/ppermute | solution.py:655
  90.7 9.0 %collective-permute-start.21 = (f32[16,640]{1,0:T(8,128)}, f32[16,640]{1,0:T(8,128)S(1)}, u32[]{:S(2)}, u32[]{:S(2)}) collective-permute-start(f32[16,640]{1,0:T(8,128)} %get-tuple-element.183), channel_id=1, source_target_pairs={{0,1},{1,0},{2,3},{3,2},{4,5},{5,4},{6,7},{7,6},{8,9},{9,8},{10,11... | collective-permute-start | bytes 122888 | tf_op jit(solution)/shard_map/ppermute | solution.py:655
  92.2 7.5 %collective-permute-start.22 = (f32[16,640]{1,0:T(8,128)}, f32[16,640]{1,0:T(8,128)S(1)}, u32[]{:S(2)}, u32[]{:S(2)}) collective-permute-start(f32[16,640]{1,0:T(8,128)} %get-tuple-element.184), channel_id=1, source_target_pairs={{0,2},{1,3},{2,0},{3,1},{4,6},{5,7},{6,4},{7,5},{8,10},{9,11},{10,... | collective-permute-start | bytes 122888 | tf_op jit(solution)/shard_map/ppermute | solution.py:655
  93.7 6.0 %collective-permute-start.23 = (f32[16,640]{1,0:T(8,128)}, f32[16,640]{1,0:T(8,128)S(1)}, u32[]{:S(2)}, u32[]{:S(2)}) collective-permute-start(f32[16,640]{1,0:T(8,128)} %get-tuple-element.185), channel_id=1, source_target_pairs={{0,16},{8,24},{16,0},{24,8},{1,17},{9,25},{17,1},{25,9},{2,18},{10... | collective-permute-start | bytes 122888 | tf_op jit(solution)/shard_map/ppermute | solution.py:655
  103.0 10.0 %all-to-all-start.6 = ((f32[32,4,128]{2,1,0:T(4,128)}), f32[32,4,128]{2,1,0:T(4,128)S(1)}, u32[]{:S(2)}, u32[]{:S(2)}) async-start(f32[32,4,128]{2,1,0:T(4,128)} %bitcast.65), calls=%async_computation.6 | async-start | bytes 131072 | tf_op jit(solution)/shard_map/all_to_all | solution.py:659
  105.5 9.8 %collective-permute-start.25 = (f32[16,640]{1,0:T(8,128)}, f32[16,640]{1,0:T(8,128)S(1)}, u32[]{:S(2)}, u32[]{:S(2)}) collective-permute-start(f32[16,640]{1,0:T(8,128)} %get-tuple-element.197), channel_id=1, source_target_pairs={{0,4},{1,5},{2,6},{3,7},{4,0},{5,1},{6,2},{7,3},{8,12},{9,13},{10,... | collective-permute-start | bytes 122888 | tf_op jit(solution)/shard_map/ppermute | solution.py:655
  108.3 7.1 %collective-permute-start.26 = (f32[16,640]{1,0:T(8,128)}, f32[16,640]{1,0:T(8,128)S(1)}, u32[]{:S(2)}, u32[]{:S(2)}) collective-permute-start(f32[16,640]{1,0:T(8,128)} %get-tuple-element.198), channel_id=1, source_target_pairs={{0,1},{1,0},{2,3},{3,2},{4,5},{5,4},{6,7},{7,6},{8,9},{9,8},{10,11... | collective-permute-start | bytes 122888 | tf_op jit(solution)/shard_map/ppermute | solution.py:655
  109.8 5.6 %collective-permute-start.27 = (f32[16,640]{1,0:T(8,128)}, f32[16,640]{1,0:T(8,128)S(1)}, u32[]{:S(2)}, u32[]{:S(2)}) collective-permute-start(f32[16,640]{1,0:T(8,128)} %get-tuple-element.199), channel_id=1, source_target_pairs={{0,2},{1,3},{2,0},{3,1},{4,6},{5,7},{6,4},{7,5},{8,10},{9,11},{10,... | collective-permute-start | bytes 122888 | tf_op jit(solution)/shard_map/ppermute | solution.py:655
  117.3 14.1 %all-to-all-start.7 = ((f32[32,4,128]{2,1,0:T(4,128)}), f32[32,4,128]{2,1,0:T(4,128)S(1)}, u32[]{:S(2)}, u32[]{:S(2)}) async-start(f32[32,4,128]{2,1,0:T(4,128)} %bitcast.61), calls=%async_computation.7 | async-start | bytes 131072 | tf_op jit(solution)/shard_map/all_to_all | solution.py:659
  119.9 15.6 %collective-permute-start.30 = (f32[16,640]{1,0:T(8,128)}, f32[16,640]{1,0:T(8,128)S(1)}, u32[]{:S(2)}, u32[]{:S(2)}) collective-permute-start(f32[16,640]{1,0:T(8,128)} %get-tuple-element.214), channel_id=1, source_target_pairs={{0,4},{1,5},{2,6},{3,7},{4,0},{5,1},{6,2},{7,3},{8,12},{9,13},{10,... | collective-permute-start | bytes 122888 | tf_op jit(solution)/shard_map/ppermute | solution.py:655
  122.7 12.9 %collective-permute-start.31 = (f32[16,640]{1,0:T(8,128)}, f32[16,640]{1,0:T(8,128)S(1)}, u32[]{:S(2)}, u32[]{:S(2)}) collective-permute-start(f32[16,640]{1,0:T(8,128)} %get-tuple-element.215), channel_id=1, source_target_pairs={{0,1},{1,0},{2,3},{3,2},{4,5},{5,4},{6,7},{7,6},{8,9},{9,8},{10,11... | collective-permute-start | bytes 122888 | tf_op jit(solution)/shard_map/ppermute | solution.py:655
  124.2 11.4 %collective-permute-start.32 = (f32[16,640]{1,0:T(8,128)}, f32[16,640]{1,0:T(8,128)S(1)}, u32[]{:S(2)}, u32[]{:S(2)}) collective-permute-start(f32[16,640]{1,0:T(8,128)} %get-tuple-element.216), channel_id=1, source_target_pairs={{0,2},{1,3},{2,0},{3,1},{4,6},{5,7},{6,4},{7,5},{8,10},{9,11},{10,... | collective-permute-start | bytes 122888 | tf_op jit(solution)/shard_map/ppermute | solution.py:655
  125.7 9.9 %collective-permute-start.33 = (f32[16,640]{1,0:T(8,128)}, f32[16,640]{1,0:T(8,128)S(1)}, u32[]{:S(2)}, u32[]{:S(2)}) collective-permute-start(f32[16,640]{1,0:T(8,128)} %get-tuple-element.217), channel_id=1, source_target_pairs={{0,16},{8,24},{16,0},{24,8},{1,17},{9,25},{17,1},{25,9},{2,18},{10... | collective-permute-start | bytes 122888 | tf_op jit(solution)/shard_map/ppermute | solution.py:655
  127.2 8.4 %collective-permute-start.34 = (f32[16,640]{1,0:T(8,128)}, f32[16,640]{1,0:T(8,128)S(1)}, u32[]{:S(2)}, u32[]{:S(2)}) collective-permute-start(f32[16,640]{1,0:T(8,128)} %get-tuple-element.218), channel_id=1, source_target_pairs={{0,8},{8,0},{16,24},{24,16},{1,9},{9,1},{17,25},{25,17},{2,10},{10... | collective-permute-start | bytes 122888 | tf_op jit(solution)/shard_map/ppermute | solution.py:655
  (13 other events, 81.2 us)

commit v4 on v3

--- a/solution.py
+++ b/solution.py
@@ -18,6 +18,7 @@
 VMEM_LIMIT = 24 * 2**20
 COST = 2_000_000
 BRING = 1
+BAND = 256
 
 
 def iota(shape, dim):
@@ -233,7 +234,7 @@
 
 
 def first_kernel(
-    organs, matches, arrived, basis, start, t_high, t_low, right, message, unit_t, unit,
+    organs, arrived, matches, basis, start, t_high, t_low, right, message, unit_t, unit,
     modes_out, *sends,
 ):
     devices = arrived.shape[0]
@@ -272,7 +273,7 @@
     for i in range(modes):
         modes_ref[i] = sum(inverse[i, j] * slabs[j] for j in range(i + 1))
     modes_out.flush()
-    start = start()
+    start, matches = start(), matches()
     directions = start.shape[1]
     for r in range(blocks):
         face = matches[r]
@@ -302,8 +303,44 @@
         unit.ref[k * devices : (k + 1) * devices, :] = block
 
 
+def turned_dot(a, b):
+    return lax.dot_general(a, b, (((1,), (1,)), ((), ())), preferred_element_type=F32)
+
+
+def times_symmetric(x, parts, f):
+    rows = x.shape[0]
+    a, b = halves(x)
+    stacked = jnp.concatenate([a, b], axis=0)
+    pieces = []
+    first = 0
+    for part in parts:
+        w_high, w_low = halves(part[f])
+        depth, width = w_high.shape
+        here = slice(first, first + depth)
+        after = slice(first + depth, first + width)
+        high, low = bdot(stacked[:, here], w_high), bdot(a[:, here], w_low)
+        value = high[:rows] + (high[rows:] + low)
+        pieces.append((first, value))
+        if width > depth:
+            high = turned_dot(stacked[:, after], w_high[:, depth:])
+            low = turned_dot(a[:, after], w_low[:, depth:])
+            pieces.append((first, high[:rows] + (high[rows:] + low)))
+        first += depth
+    bands = []
+    edges = [0]
+    for part in parts:
+        edges.append(edges[-1] + part.shape[1])
+    for start, stop in zip(edges[:-1], edges[1:], strict=True):
+        total = 0.0
+        for begin, value in pieces:
+            if begin <= start and stop <= begin + value.shape[1]:
+                total = total + value[:, start - begin : stop - begin]
+        bands.append(total)
+    return jnp.concatenate(bands, axis=1)
+
+
 def smooth(inner, near, smoothed, f):
-    smoothed[f] = times_split(inner[f], near[f])
+    smoothed[f] = times_symmetric(inner[f], near, f)
 
 
 def subtract_modes(field, columns, basis, f):
@@ -348,9 +385,11 @@
 
 
 def start_kernel(
-    organs, matches, f0, f1, f2, f3, f4, base, added, t_high, t_low, unit_t, near, modes_ref,
-    message, smoothed_out, jump_out, s0, s1, s2, s3, s4, inner,
+    organs, bands, matches, f0, f1, f2, f3, f4, base, added, *refs
 ):
+    near, rest = refs[:bands], refs[bands:]
+    t_high, t_low, unit_t, modes_ref, message, smoothed_out, jump_out = rest[:7]
+    s0, s1, s2, s3, s4, inner = rest[7:]
     faces = (f0, f1, f2, f3, f4)
     smoothed = smoothed_out.ref
     blocks, directions = base.shape[0], base.shape[1]
@@ -358,11 +397,12 @@
         inner[matches[r]] = base[matches[r]] - face[0:directions, :]
     for f in range(blocks):
         smooth(inner, near, smoothed, f)
+        if f == 0:
+            send_contact(message.ref, 2, smoothed[0], t_high, t_low, unit_t)
+            message.flush()
     for r, send in enumerate((s0, s1, s2, s3, s4)):
         send(smoothed.at[matches[r]])
     smoothed_out.flush()
-    send_contact(message.ref, 2, smoothed[0], t_high, t_low, unit_t)
-    message.flush()
     modes = modes_ref.shape[0]
     jump_modes = jump_out.ref
     organ = lax.axis_index("organ")
@@ -408,9 +448,18 @@
 
 
 def inner_contact(
-    organs, arrived, sent, resid, a_high, a_low, unit, modes_ref, jump_modes, projected_out, base,
-    norms,
+    organs, steps, arrived, sent, resid, a_high, a_low, unit, modes_ref, jump_modes, *refs
 ):
+    rest = list(refs)
+    if steps:
+        start, behind, jumps, sizes = (
+            rest[0],
+            *(rest[1 + i * steps : 1 + (i + 1) * steps] for i in range(3)),
+        )
+        projected, total, direction, jumped, last_size, base, norms = rest[1 + 3 * steps :]
+    else:
+        projected_out, base, norms = rest
+        projected = projected_out.ref
     sent, resid, maps = sent(), resid(), (a_high(), a_low(), unit())
     modes_ref, jump_modes = modes_ref(), jump_modes()
     devices = sent.shape[0] // 4
@@ -428,18 +477,34 @@
     organ = lax.axis_index("organ")
     own = sum(jnp.where(organ == o, 1.0, 0.0) * sums[o] for o in range(organs))
     columns = [to_column(own, m * directions, directions) for m in range(modes_ref.shape[0])]
-    projected = projected_out.ref
     for f in range(blocks):
         projected[f] = subtract_modes(resid[f], columns, modes_ref, f)
-    projected_out.flush()
+    if not steps:
+        projected_out.flush()
     for f in range(blocks):
         value = resid[f] - times_split(left, jump_modes[f])
         base[f] = value + added if f == 0 else value
     norms[...] = jnp.broadcast_to(dots_row([(projected, projected)]), norms.shape)
-
-
-def inner_kernel(last, older, matches, f0, f1, f2, f3, f4, base, norms, near, *refs):
-    rest = list(refs)
+    if steps:
+        start = start()
+        behind, jumps, sizes = ([late() for late in group] for group in (behind, jumps, sizes))
+        last_size[...] = sizes[-1][...]
+        for f in range(blocks):
+            value = behind[0][f]
+            sum_up = start[f] + sizes[0][2, :, 0:1] * value
+            for field, size in zip(behind[1:], sizes[1:], strict=True):
+                value = field[f] + size[3, :, 0:1] * value
+                sum_up = sum_up + size[2, :, 0:1] * value
+            total[f] = sum_up
+            direction[f] = value
+            value = jumps[0][f]
+            for field, size in zip(jumps[1:], sizes[1:], strict=True):
+                value = field[f] + size[3, :, 0:1] * value
+            jumped[f] = value
+
+
+def inner_kernel(bands, last, older, matches, f0, f1, f2, f3, f4, base, norms, *refs):
+    near, rest = refs[:bands], list(refs[bands:])
     previous = rest.pop(0) if older else None
     maps = None if last else rest[:3]
     message = rest[0 if last else 3]
@@ -451,14 +516,16 @@
         inner, smoothed = inner_out.ref, smoothed_out.ref
     for r, face in zip(ORDER, (f0, f1, f2, f3, f4), strict=True):
         inner[matches[r]] = base[matches[r]] - face[...]
+    if not last:
+        inner_out.flush()
     for f in range(inner.shape[0]):
         smooth(inner, near, smoothed, f)
+        if f == 0 and not last:
+            send_contact(message.ref, 4, smoothed[0], *maps)
     if not last:
         for r, send in enumerate(rest[2:]):
             send(smoothed.at[matches[r]])
-        inner_out.flush()
         smoothed_out.flush()
-        send_contact(message.ref, 4, smoothed[0], *maps)
     directions = inner.shape[1]
     pairs = [(inner, smoothed)]
     if older:
@@ -485,9 +552,10 @@
     rest = list(refs)
     old_image = scalars = None
     if older:
-        old_image, scalars = rest[0](), rest[1]()
-        rest = rest[2:]
-    new_scalars, part, steps, image = rest
+        old_image, scalars, new_scalars, part, steps, image = rest
+        old_image, scalars = old_image(), scalars()
+    else:
+        new_scalars, part, steps, image = rest
     sent, smoothed, projected = sent(), smoothed(), projected()
     blocks, directions = smoothed.shape[0], smoothed.shape[1]
     row = jnp.sum(get(arrived, 4, 2), axis=0, keepdims=True)
@@ -525,28 +593,7 @@
     send_residual(matches, resid, modes_ref, (t_high, t_low, unit_t), message, sends)
 
 
-def update_kernel(older, projected, inner, total, scalars, *refs):
-    projected, inner, total, scalars = (late() for late in (projected, inner, total, scalars))
-    rest = list(refs)
-    step = scalars[2, :, 0:1]
-    if not older:
-        for f in range(total.shape[0]):
-            rest[0].ref[f] = total[f] + step * projected[f]
-        return
-    old_direction, old_inner = rest[0](), rest[1]()
-    new_total, direction, new_inner = (out.ref for out in rest[2:])
-    beta = scalars[3, :, 0:1]
-    for f in range(total.shape[0]):
-        value = projected[f] + beta * old_direction[f]
-        direction[f] = value
-        new_total[f] = total[f] + step * value
-        new_inner[f] = inner[f] + beta * old_inner[f]
-
-
 def last_kernel(arrived, projected, old_direction, total, scalars, out):
-    projected, old_direction, total, scalars = (
-        late() for late in (projected, old_direction, total, scalars)
-    )
     blocks, directions = projected.shape[0], projected.shape[1]
     row = jnp.sum(arrived[...], axis=0, keepdims=True)
     _, beta, _, step = step_sizes(row, True, scalars, directions)
@@ -590,9 +637,10 @@
             self.started = True
 
 
-def call(kernel, outs, args, late=(), smem=0, near=(), sends=(), scratch=(), bring=()):
+def call(kernel, outs, args, late=(), smem=0, near=(), sends=(), scratch=(), bring=(), held=0):
     n_late, n_out, n_arg, n_near = len(late), len(outs), len(args), len(near)
-    brought = [(a.shape, a.dtype) for a in bring]
+    bring = [item if isinstance(item, tuple) else (item, item.shape, None) for item in bring]
+    brought = [(shape, a.dtype) for a, shape, _ in bring]
 
     def body(*refs):
         refs = list(refs)
@@ -613,6 +661,10 @@
         posts = [Send(t, out_sem.at[n_out + i]) for i, t in enumerate(ports)]
         copies = []
         for i, (origin, goal) in enumerate(zip(origins, goals, strict=True)):
+            first = bring[i][2]
+            if first is not None:
+                rows, columns = goal.shape[1], goal.shape[2]
+                origin = origin.at[:, pl.ds(first, rows), pl.ds(first, columns)]
             copies.append(pltpu.make_async_copy(origin, goal, bring_sem.at[i]))
         for copy in copies:
             copy.start(priority=BRING)
@@ -628,11 +680,12 @@
 
     in_specs = [pl.BlockSpec(memory_space=pltpu.SMEM)] * smem
     in_specs += [pl.BlockSpec(memory_space=pltpu.VMEM)] * (n_arg - smem)
-    remote = tuple(late) + tuple(bring)
+    remote = tuple(late) + tuple(a for a, _, _ in bring)
     in_specs += [pl.BlockSpec(memory_space=pltpu.HBM)] * len(remote)
     out_specs = [pl.BlockSpec(memory_space=pltpu.HBM)] * (n_out + len(sends))
     out_specs += [pl.BlockSpec(memory_space=pltpu.VMEM)] * (n_near + len(bring))
-    scratch_shapes = [pltpu.VMEM(a.shape, a.dtype) for a in late]
+    scratch_shapes = [pltpu.SMEM(a.shape, a.dtype) for a in late[:held]]
+    scratch_shapes += [pltpu.VMEM(a.shape, a.dtype) for a in late[held:]]
     scratch_shapes += [pltpu.VMEM(shape, kind) for shape, kind in outs]
     scratch_shapes += list(scratch)
     counts = (n_late, len(bring), n_out + len(sends))
@@ -693,7 +746,13 @@
     message_line = ((4 * devices, LANES), F32)
 
     sends = [face] * blocks
-    near_matrices = (matrices,)
+    near_matrices, first = [], 0
+    while first < length:
+        rows = min(BAND, length - first)
+        near_matrices.append((matrices, (blocks, rows, length - first), first))
+        first += rows
+    near_matrices = tuple(near_matrices)
+    bands = len(near_matrices)
 
     (setup,) = call(
         functools.partial(setup_kernel, blocks),
@@ -719,27 +778,27 @@
             ((modes, blocks, length), F32),
         ]
         + [((directions + 8, length), F32)] * blocks,
-        (matches, arrived),
-        (basis, start, t_high, t_low, right),
-        smem=1,
+        (arrived,),
+        (matches, basis, start, t_high, t_low, right),
+        held=1,
     )
     forth = (a_high, a_low, unit)
     back = (t_high, t_low, unit_t)
     back_modes = back + (modes_ref,)
     arrived = exchange(sent)
     faces = swap_faces(faces)
-    right, base, added, *maps, modes_near, near = call(
+    right, base, added, *more = call(
         functools.partial(start_contact, organs),
         [whole],
         (arrived,),
         (sent, start) + forth + (modes_ref, right),
         near=[whole, ((8 * organs, length), F32)],
-        bring=back_modes + near_matrices,
+        bring=near_matrices + back_modes,
     )
     message, smoothed, jump_modes, *posts = call(
-        functools.partial(start_kernel, organs),
+        functools.partial(start_kernel, organs, bands),
         [((2 * devices, LANES), F32), whole, ((blocks, 8 * organs, length), F32)],
-        (matches, *faces, base, added, *maps, near, modes_near),
+        (matches, *faces, base, added, *more),
         smem=1,
         sends=sends,
         scratch=[pltpu.VMEM(field, F32)],
@@ -761,74 +820,71 @@
         smem=1,
         sends=sends,
     )
-    total = start
-    direction = inner = image = scalars = None
+    image = None
+    size = (4, directions, LANES)
+    fields, jumps, scalars = [], [], []
     for step in range(ITERS):
         older, last = step > 0, step == ITERS - 1
         arrived = exchange(sent)
         faces = swap_faces(posts)
-        ahead = near_matrices + ((inner,) if older else ()) + (() if last else back)
-        projected, base, norms, *ahead = call(
-            functools.partial(inner_contact, organs),
-            [whole],
+        history = (start, *fields, *jumps, *scalars) if last else ()
+        more_near = [whole] * 3 + [(size, F32)] if last else []
+        ahead = () if last else back
+        if older and not last:
+            ahead = (jumps[-1],) + ahead
+        projected, *more = call(
+            functools.partial(inner_contact, organs, step if last else 0),
+            [] if last else [whole],
             (arrived,),
-            (sent, resid) + forth + (modes_ref, jump_modes),
-            near=[whole, ((8, LANES), F32)],
-            bring=ahead,
+            (sent, resid) + forth + (modes_ref, jump_modes) + history,
+            near=([whole] + more_near if last else []) + [whole, ((8, LANES), F32)],
+            bring=near_matrices + ahead,
         )
         if last:
+            total, direction, jumped, last_size, base, norms, *near = more
             (message,) = call(
-                functools.partial(inner_kernel, last, older),
+                functools.partial(inner_kernel, bands, last, older),
                 [((devices, LANES), F32)],
-                (matches, *faces, base, norms, *ahead),
-                        smem=1,
+                (matches, *faces, base, norms, *near, jumped),
+                smem=1,
                 scratch=[pltpu.VMEM(field, F32)] * 2,
             )
             arrived = exchange(message)
             break
-        message, new_inner, smoothed, *posts = call(
-            functools.partial(inner_kernel, last, older),
+        message, inner, smoothed, *posts = call(
+            functools.partial(inner_kernel, bands, last, older),
             [message_line, whole, whole],
-            (matches, *faces, base, norms, *ahead),
-                smem=1,
+            (matches, *faces, *more),
+            smem=1,
             sends=sends,
         )
         arrived = exchange(message)
         faces = swap_faces(posts)
-        new_scalars, part, steps, image_part, *maps = call(
+        old = (image, scalars[-1]) if older else ()
+        new_scalars, *more = call(
             functools.partial(outer_contact, older),
-            [((4, directions, LANES), F32)],
+            [(size, F32)],
             (arrived,),
-            (message, smoothed) + forth + (projected,) + ((image, scalars) if older else ()),
+            (message, smoothed) + forth + (projected,) + old,
             near=[whole, ((directions, LANES), F32), whole],
             bring=back_modes,
         )
         sent, resid, *posts = call(
             functools.partial(outer_kernel, older),
             [message_line, whole] + ([] if older else [whole]),
-            (matches, *faces, part, steps, image_part, *maps),
+            (matches, *faces, *more),
             smem=1,
             sends=sends,
         )
         if not older:
             image, *posts = posts
-        scalars = new_scalars
-        updated = call(
-            functools.partial(update_kernel, older),
-            [whole] * (3 if older else 1),
-            (),
-            (projected, new_inner, total, scalars) + ((direction, inner) if older else ()),
-        )
-        if older:
-            total, direction, inner = updated
-        else:
-            (total,) = updated
-            direction, inner = projected, new_inner
+        fields.append(projected)
+        jumps.append(inner)
+        scalars.append(new_scalars)
     (result,) = call(
         last_kernel,
         [((directions * blocks, 1, length), F32)],
-        (arrived,),
-        (projected, direction, total, scalars),
+        (arrived, projected, direction, total, last_size),
     )
     return result.reshape(dual_rhs.shape)
 

time: 151 us -> 143 us (0.947)
  Pallas kernels: 56.5 us -> 49 us
    pallas_call x20 -> x18, Pallas kernels: 56.5 us -> 49 us  [call(): pl.pallas_call(body, out_shape=[pltpu.HBM(shape, kind) for shape, kind in...]
  transfers between devices with their start and end apart: 43 -> 43, of which waited for: 9 -> 10; matrix products, arithmetic and copies ran while one was open for 0% -> 0% of each run, Pallas kernels for 20% -> 17%
where the time goes in v4:
time: 143 us; the launch traced here: 142 us
  starting transfers between devices  75.9 us (53%)
  Pallas kernels  49 us (34%)
  blocking collectives  9.6 us (7%)
  waiting for transfers between devices  6.66 us (5%)
    ppermute x35, starting transfers between devices, from_partner(): return lax.ppermute(value, axis, pairs)  50.4 us
    pallas_call x18, Pallas kernels, call(): pl.pallas_call(body, out_shape=[pltpu.HBM(shape, kind) for shape, kind in...  49 us
    all_to_all x8, starting transfers between devices, exchange(): lax.all_to_all(message, AXES, split_axis=0, concat_axis=0, tiled=True)  25.5 us
    all_to_all x1, blocking collectives, exchange(): lax.all_to_all(message, AXES, split_axis=0, concat_axis=0, tiled=True)  9.6 us
    all_to_all x8, waiting for transfers between devices, exchange(): lax.all_to_all(message, AXES, split_axis=0, concat_axis=0, tiled=True)  5.33 us
  transfers between devices with their start and end apart: 43, of which 10 were waited for; matrix products, arithmetic and copies ran while one was open for 0% of the time, Pallas kernels for 17%

profile of v4, /device:TPU:0, one launch (start us, length us, event | category | flops | bytes accessed | tf_op | source)
XLA Modules:
  0.0 142.5 jit_solution(11891985534040071073)
XLA Ops:
  0.7 1.9 %shard_map.100 = f32[32,128]{1,0:T(8,128)} custom-call(s32[1]{0:T(128)} %bitcast.35.refs_0_, s32[1,128]{1,0:T(1,128)} %bitcast.80, s32[1,128]{1,0:T(1,128)} %bitcast.84, s32[1,128]{1,0:T(1,128)} %bitcast.82, f32[30,1,640]{2,1,0:T(1,128)} %bitcast.67), custom_call_target="tpu_custom_call" | custom-call | flops 2000000 | bytes 2000000 | tf_op jit(solution)/shard_map/pallas_call | solution.py:693
  2.6 7.3 %all-to-all-start = ((f32[32,1,128]{2,1,0:T(1,128)}), f32[32,1,128]{2,1,0:T(1,128)S(1)}, u32[]{:S(2)}, u32[]{:S(2)}) async-start(f32[32,1,128]{2,1,0:T(1,128)} %bitcast.79), calls=%async_computation | async-start | bytes 32768 | tf_op jit(solution)/shard_map/all_to_all | solution.py:712
  9.9 2.8 %shard_map.101 = (bf16[256,640]{1,0:T(8,128)(2,1)}, bf16[256,640]{1,0:T(8,128)(2,1)}, bf16[640,256]{1,0:T(8,128)(2,1)}, bf16[640,256]{1,0:T(8,128)(2,1)}, f32[5,16,640]{2,1,0:T(8,128)}, /*index=5*/f32[5,16,640]{2,1,0:T(8,128)}) custom-call(s32[1]{0:T(128)} %bitcast.36.refs_0_, s32[1,128]{1,0:T(1,128)} %bitcast.81, s32[1,128]{1,0:T(1,128)} %bitcast.83, ...), custom_call_target="tpu_custom_call" | custom-call | flops 2000000 | bytes 2000000 | tf_op jit(solution)/shard_map/pallas_call | solution.py:693
  12.7 4.3 %all-to-all-done = f32[32,1,128]{2,1,0:T(1,128)S(1)} async-done(((f32[32,1,128]{2,1,0:T(1,128)}), f32[32,1,128]{2,1,0:T(1,128)S(1)}, u32[]{:S(2)}, u32[]{:S(2)}) %all-to-all-start) | async-done | bytes 16416 | tf_op jit(solution)/shard_map/all_to_all | solution.py:712
  17.0 3.1 %shard_map.102 = (f32[128,128]{1,0:T(8,128)}, bf16[640,256]{1,0:T(8,128)(2,1)}, bf16[256,640]{1,0:T(8,128)(2,1)}, f32[6,5,640]{2,1,0:T(8,128)}, f32[24,640]{1,0:...) custom-call(f32[32,128]{1,0:T(8,128)S(1)} %bitcast.44, s32[5]{0:T(128)} %bitcast.46, ...), custom_call_target="tpu_custom_call" | custom-call | flops 2000000 | bytes 2000000 | tf_op jit(solution)/shard_map/pallas_call | solution.py:693
  20.1 2.6 %all-to-all-start.1 = ((f32[32,4,128]{2,1,0:T(4,128)}), f32[32,4,128]{2,1,0:T(4,128)S(1)}, u32[]{:S(2)}, u32[]{:S(2)}) async-start(f32[32,4,128]{2,1,0:T(4,128)} %bitcast.72), calls=%async_computation.1 | async-start | bytes 131072 | tf_op jit(solution)/shard_map/all_to_all | solution.py:712
  22.7 2.7 %collective-permute-start = (f32[24,640]{1,0:T(8,128)}, f32[24,640]{1,0:T(8,128)S(1)}, u32[]{:S(2)}, u32[]{:S(2)}) collective-permute-start(f32[24,640]{1,0:T(8,128)} %get-tuple-element.130), channel_id=1, source_target_pairs={{0,4},{1,5},{2,6},{3,7},{4,0},{5,1},{6,2},{7,3},{8,12},{9,13},{10,... | collective-permute-start | bytes 184328 | tf_op jit(solution)/shard_map/ppermute | solution.py:708
  30.1 3.6 %shard_map.103 = (f32[5,16,640]{2,1,0:T(8,128)}, f32[5,16,640]{2,1,0:T(8,128)S(1)}, f32[32,640]{1,0:T(8,128)S(1)}, f32[5,256,640]{2,1,0:T(8,128)S(1)}, f32[5,256...) custom-call(f32[128,128]{1,0:T(8,128)S(1)} %bitcast.38, ...), custom_call_target="tpu_custom_call" | custom-call | flops 2000000 | bytes 2000000 | tf_op jit(solution)/shard_map/pallas_call | solution.py:693
  33.8 3.6 %shard_map.104 = (f32[64,128]{1,0:T(8,128)}, f32[5,16,640]{2,1,0:T(8,128)}, f32[5,32,640]{2,1,0:T(8,128)}, f32[16,640]{1,0:T(8,128)}, f32[16,640]{1,0:T(8,128)},...) custom-call(s32[5]{0:T(128)S(1)} %bitcast.47, f32[24,640]{1,0:T(8,128)S(1)} %collective-permute-done.refs_1_, ...), custom_call_target="tpu_custom_call" | custom-call | flops 2000000 | bytes 2000000 | tf_op jit(solution)/shard_map/pallas_call | solution.py:693
  37.4 2.6 %all-to-all-start.2 = ((f32[32,2,128]{2,1,0:T(2,128)}), f32[32,2,128]{2,1,0:T(2,128)S(1)}, u32[]{:S(2)}, u32[]{:S(2)}) async-start(f32[32,2,128]{2,1,0:T(2,128)} %bitcast.77), calls=%async_computation.2 | async-start | bytes 65536 | tf_op jit(solution)/shard_map/all_to_all | solution.py:712
  39.9 2.7 %collective-permute-start.5 = (f32[16,640]{1,0:T(8,128)}, f32[16,640]{1,0:T(8,128)S(1)}, u32[]{:S(2)}, u32[]{:S(2)}) collective-permute-start(f32[16,640]{1,0:T(8,128)} %get-tuple-element.150), channel_id=1, source_target_pairs={{0,4},{1,5},{2,6},{3,7},{4,0},{5,1},{6,2},{7,3},{8,12},{9,13},{10,... | collective-permute-start | bytes 122888 | tf_op jit(solution)/shard_map/ppermute | solution.py:708
  47.2 1.9 %shard_map.105 = (f32[5,16,640]{2,1,0:T(8,128)S(1)}, bf16[640,256]{1,0:T(8,128)(2,1)S(1)}, bf16[640,256]{1,0:T(8,128)(2,1)S(1)}, bf16[640,256]{1,0:T(8,128)(2,1)S(1)}, f32[6,5,640]{2,1,0:T(8,128)S(1)}) custom-call(f32[64,128]{1,0:T(8,128)S(1)} %bitcast.43, f32[64,128]{1,0:T(8,128)} %get-tuple-element.155.refs_1_, f32[5,16,640]{2,1,0:T(8,128)} %get-tuple-element.156.refs_2_, ...), custom_call_target="tpu_custom_call" | custom-call | flops 2000000 | bytes 2000000 | tf_op jit(solution)/shard_map/pallas_call | solution.py:693
  51.7 2.6 %all-to-all-start.3 = ((f32[32,4,128]{2,1,0:T(4,128)}), f32[32,4,128]{2,1,0:T(4,128)S(1)}, u32[]{:S(2)}, u32[]{:S(2)}) async-start(f32[32,4,128]{2,1,0:T(4,128)} %bitcast.71), calls=%async_computation.3 | async-start | bytes 131072 | tf_op jit(solution)/shard_map/all_to_all | solution.py:712
  54.3 2.7 %collective-permute-start.10 = (f32[16,640]{1,0:T(8,128)}, f32[16,640]{1,0:T(8,128)S(1)}, u32[]{:S(2)}, u32[]{:S(2)}) collective-permute-start(f32[16,640]{1,0:T(8,128)} %get-tuple-element.163), channel_id=1, source_target_pairs={{0,4},{1,5},{2,6},{3,7},{4,0},{5,1},{6,2},{7,3},{8,12},{9,13},{10,... | collective-permute-start | bytes 122888 | tf_op jit(solution)/shard_map/ppermute | solution.py:708
  61.7 3.6 %shard_map.107 = (f32[5,16,640]{2,1,0:T(8,128)}, f32[5,16,640]{2,1,0:T(8,128)S(1)}, f32[8,128]{1,0:T(8,128)S(1)}, f32[5,256,640]{2,1,0:T(8,128)S(1)}, f32[5,256,...) custom-call(f32[128,128]{1,0:T(8,128)S(1)} %bitcast.39, ...), custom_call_target="tpu_custom_call" | custom-call | flops 2000000 | bytes 2000000 | tf_op jit(solution)/shard_map/pallas_call | solution.py:693
  65.4 3.5 %shard_map.108 = (f32[128,128]{1,0:T(8,128)}, f32[5,16,640]{2,1,0:T(8,128)}, f32[5,16,640]{2,1,0:T(8,128)}, f32[16,640]{1,0:T(8,128)}, f32[16,640]{1,0:T(8,128)}...) custom-call(s32[5]{0:T(128)S(1)} %bitcast.49, f32[16,640]{1,0:T(8,128)S(1)} %collective-permute-done.10.refs_1_, ...), custom_call_target="tpu_custom_call" | custom-call | flops 2000000 | bytes 2000000 | tf_op jit(solution)/shard_map/pallas_call | solution.py:693
  68.8 2.6 %all-to-all-start.4 = ((f32[32,4,128]{2,1,0:T(4,128)}), f32[32,4,128]{2,1,0:T(4,128)S(1)}, u32[]{:S(2)}, u32[]{:S(2)}) async-start(f32[32,4,128]{2,1,0:T(4,128)} %bitcast.74), calls=%async_computation.4 | async-start | bytes 131072 | tf_op jit(solution)/shard_map/all_to_all | solution.py:712
  71.4 2.7 %collective-permute-start.15 = (f32[16,640]{1,0:T(8,128)}, f32[16,640]{1,0:T(8,128)S(1)}, u32[]{:S(2)}, u32[]{:S(2)}) collective-permute-start(f32[16,640]{1,0:T(8,128)} %get-tuple-element.179), channel_id=1, source_target_pairs={{0,4},{1,5},{2,6},{3,7},{4,0},{5,1},{6,2},{7,3},{8,12},{9,13},{10,... | collective-permute-start | bytes 122888 | tf_op jit(solution)/shard_map/ppermute | solution.py:708
  78.8 2.2 %shard_map.109 = (f32[4,16,128]{2,1,0:T(8,128)}, f32[5,16,640]{2,1,0:T(8,128)S(1)}, f32[16,128]{1,0:T(8,128)S(1)}, f32[5,16,640]{2,1,0:T(8,128)S(1)}, bf16[640,2...) custom-call(f32[128,128]{1,0:T(8,128)S(1)} %bitcast.42, ...), custom_call_target="tpu_custom_call" | custom-call | flops 2000000 | bytes 2000000 | tf_op jit(solution)/shard_map/pallas_call | solution.py:693
  81.4 1.9 %shard_map.110 = (f32[128,128]{1,0:T(8,128)}, f32[5,16,640]{2,1,0:T(8,128)}, f32[5,16,640]{2,1,0:T(8,128)}, f32[16,640]{1,0:T(8,128)}, f32[16,640]{1,0:T(8,128)}...) custom-call(s32[5]{0:T(128)S(1)} %bitcast.50, f32[16,640]{1,0:T(8,128)S(1)} %collective-permute-done.15.refs_1_, ...), custom_call_target="tpu_custom_call" | custom-call | flops 2000000 | bytes 2000000 | tf_op jit(solution)/shard_map/pallas_call | solution.py:693
  83.3 2.8 %all-to-all-start.5 = ((f32[32,4,128]{2,1,0:T(4,128)}), f32[32,4,128]{2,1,0:T(4,128)S(1)}, u32[]{:S(2)}, u32[]{:S(2)}) async-start(f32[32,4,128]{2,1,0:T(4,128)} %bitcast.70), calls=%async_computation.5 | async-start | bytes 131072 | tf_op jit(solution)/shard_map/all_to_all | solution.py:712
  86.1 2.5 %collective-permute-start.20 = (f32[16,640]{1,0:T(8,128)}, f32[16,640]{1,0:T(8,128)S(1)}, u32[]{:S(2)}, u32[]{:S(2)}) collective-permute-start(f32[16,640]{1,0:T(8,128)} %get-tuple-element.194), channel_id=1, source_target_pairs={{0,4},{1,5},{2,6},{3,7},{4,0},{5,1},{6,2},{7,3},{8,12},{9,13},{10,... | collective-permute-start | bytes 122888 | tf_op jit(solution)/shard_map/ppermute | solution.py:708
  93.3 3.7 %shard_map.111 = (f32[5,16,640]{2,1,0:T(8,128)}, f32[5,16,640]{2,1,0:T(8,128)S(1)}, f32[8,128]{1,0:T(8,128)S(1)}, f32[5,256,640]{2,1,0:T(8,128)S(1)}, f32[5,256,...) custom-call(f32[128,128]{1,0:T(8,128)S(1)} %bitcast.40, ...), custom_call_target="tpu_custom_call" | custom-call | flops 2000000 | bytes 2000000 | tf_op jit(solution)/shard_map/pallas_call | solution.py:693
  97.1 3.5 %shard_map.112 = (f32[128,128]{1,0:T(8,128)}, f32[5,16,640]{2,1,0:T(8,128)}, f32[5,16,640]{2,1,0:T(8,128)}, f32[16,640]{1,0:T(8,128)}, f32[16,640]{1,0:T(8,128)}...) custom-call(s32[5]{0:T(128)S(1)} %bitcast.51, f32[16,640]{1,0:T(8,128)S(1)} %collective-permute-done.20.refs_1_, ...), custom_call_target="tpu_custom_call" | custom-call | flops 2000000 | bytes 2000000 | tf_op jit(solution)/shard_map/pallas_call | solution.py:693
  100.6 2.5 %all-to-all-start.6 = ((f32[32,4,128]{2,1,0:T(4,128)}), f32[32,4,128]{2,1,0:T(4,128)S(1)}, u32[]{:S(2)}, u32[]{:S(2)}) async-start(f32[32,4,128]{2,1,0:T(4,128)} %bitcast.73), calls=%async_computation.6 | async-start | bytes 131072 | tf_op jit(solution)/shard_map/all_to_all | solution.py:712
  103.1 2.7 %collective-permute-start.25 = (f32[16,640]{1,0:T(8,128)}, f32[16,640]{1,0:T(8,128)S(1)}, u32[]{:S(2)}, u32[]{:S(2)}) collective-permute-start(f32[16,640]{1,0:T(8,128)} %get-tuple-element.211), channel_id=1, source_target_pairs={{0,4},{1,5},{2,6},{3,7},{4,0},{5,1},{6,2},{7,3},{8,12},{9,13},{10,... | collective-permute-start | bytes 122888 | tf_op jit(solution)/shard_map/ppermute | solution.py:708
  110.5 2.4 %shard_map.113 = (f32[4,16,128]{2,1,0:T(8,128)}, f32[5,16,640]{2,1,0:T(8,128)S(1)}, f32[16,128]{1,0:T(8,128)S(1)}, f32[5,16,640]{2,1,0:T(8,128)S(1)}, bf16[640,2...) custom-call(f32[128,128]{1,0:T(8,128)S(1)} %bitcast.41, ...), custom_call_target="tpu_custom_call" | custom-call | flops 2000000 | bytes 2000000 | tf_op jit(solution)/shard_map/pallas_call | solution.py:693
  115.0 2.6 %all-to-all-start.7 = ((f32[32,4,128]{2,1,0:T(4,128)}), f32[32,4,128]{2,1,0:T(4,128)S(1)}, u32[]{:S(2)}, u32[]{:S(2)}) async-start(f32[32,4,128]{2,1,0:T(4,128)} %bitcast.69), calls=%async_computation.7 | async-start | bytes 131072 | tf_op jit(solution)/shard_map/all_to_all | solution.py:712
  117.6 2.7 %collective-permute-start.30 = (f32[16,640]{1,0:T(8,128)}, f32[16,640]{1,0:T(8,128)S(1)}, u32[]{:S(2)}, u32[]{:S(2)}) collective-permute-start(f32[16,640]{1,0:T(8,128)} %get-tuple-element.228), channel_id=1, source_target_pairs={{0,4},{1,5},{2,6},{3,7},{4,0},{5,1},{6,2},{7,3},{8,12},{9,13},{10,... | collective-permute-start | bytes 122888 | tf_op jit(solution)/shard_map/ppermute | solution.py:708
  124.9 3.7 %shard_map.115 = (f32[5,16,640]{2,1,0:T(8,128)S(1)}, f32[5,16,640]{2,1,0:T(8,128)S(1)}, f32[5,16,640]{2,1,0:T(8,128)S(1)}, f32[5,16,640]{2,1,0:T(8,128)S(1)}, f3...) custom-call(f32[128,128]{1,0:T(8,128)S(1)} %bitcast.37, ...), custom_call_target="tpu_custom_call" | custom-call | flops 2000000 | bytes 2000000 | tf_op jit(solution)/shard_map/pallas_call | solution.py:693
  128.7 3.0 %shard_map.116 = f32[32,128]{1,0:T(8,128)} custom-call(s32[5]{0:T(128)S(1)} %bitcast.53, f32[16,640]{1,0:T(8,128)S(1)} %collective-permute-done.30.refs_1_, f32[16,640]{1,0:T(8,128)S(1)} %collective-permute-done.31.refs_2_, f32[16,640]{1,0:T(8,128)S(1)} %collective-permute-done.32.refs_3_, f32[16,640]{1,0:T(8,128)S(1)} %collective-permute-done.33.refs_4_, ...), custom_call_target="tpu_custom_call" | custom-call | flops 2000000 | bytes 2000000 | tf_op jit(solution)/shard_map/pallas_call | solution.py:693
  131.7 9.6 %all_to_all.99 = f32[32,1,128]{2,1,0:T(1,128)S(1)} all-to-all(f32[32,1,128]{2,1,0:T(1,128)} %bitcast.78), channel_id=1, replica_groups=mesh['organ'=4,'sub'=8] {'organ','sub'}, dimensions={0} | all-to-all | bytes 32768 | tf_op jit(solution)/shard_map/all_to_all | solution.py:712
  (75 shorter events, 38.4 us)
Async XLA Ops:
  2.6 14.4 %all-to-all-start = ((f32[32,1,128]{2,1,0:T(1,128)}), f32[32,1,128]{2,1,0:T(1,128)S(1)}, u32[]{:S(2)}, u32[]{:S(2)}) async-start(f32[32,1,128]{2,1,0:T(1,128)} %bitcast.79), calls=%async_computation | async-start | bytes 32768 | tf_op jit(solution)/shard_map/all_to_all | solution.py:712
  20.1 10.0 %all-to-all-start.1 = ((f32[32,4,128]{2,1,0:T(4,128)}), f32[32,4,128]{2,1,0:T(4,128)S(1)}, u32[]{:S(2)}, u32[]{:S(2)}) async-start(f32[32,4,128]{2,1,0:T(4,128)} %bitcast.72), calls=%async_computation.1 | async-start | bytes 131072 | tf_op jit(solution)/shard_map/all_to_all | solution.py:712
  22.7 11.0 %collective-permute-start = (f32[24,640]{1,0:T(8,128)}, f32[24,640]{1,0:T(8,128)S(1)}, u32[]{:S(2)}, u32[]{:S(2)}) collective-permute-start(f32[24,640]{1,0:T(8,128)} %get-tuple-element.130), channel_id=1, source_target_pairs={{0,4},{1,5},{2,6},{3,7},{4,0},{5,1},{6,2},{7,3},{8,12},{9,13},{10,... | collective-permute-start | bytes 184328 | tf_op jit(solution)/shard_map/ppermute | solution.py:708
  25.4 8.3 %collective-permute-start.1 = (f32[24,640]{1,0:T(8,128)}, f32[24,640]{1,0:T(8,128)S(1)}, u32[]{:S(2)}, u32[]{:S(2)}) collective-permute-start(f32[24,640]{1,0:T(8,128)} %get-tuple-element.131), channel_id=1, source_target_pairs={{0,1},{1,0},{2,3},{3,2},{4,5},{5,4},{6,7},{7,6},{8,9},{9,8},{10,11... | collective-permute-start | bytes 184328 | tf_op jit(solution)/shard_map/ppermute | solution.py:708
  26.9 6.8 %collective-permute-start.2 = (f32[24,640]{1,0:T(8,128)}, f32[24,640]{1,0:T(8,128)S(1)}, u32[]{:S(2)}, u32[]{:S(2)}) collective-permute-start(f32[24,640]{1,0:T(8,128)} %get-tuple-element.132), channel_id=1, source_target_pairs={{0,2},{1,3},{2,0},{3,1},{4,6},{5,7},{6,4},{7,5},{8,10},{9,11},{10,... | collective-permute-start | bytes 184328 | tf_op jit(solution)/shard_map/ppermute | solution.py:708
  28.4 5.3 %collective-permute-start.3 = (f32[24,640]{1,0:T(8,128)}, f32[24,640]{1,0:T(8,128)S(1)}, u32[]{:S(2)}, u32[]{:S(2)}) collective-permute-start(f32[24,640]{1,0:T(8,128)} %get-tuple-element.133), channel_id=1, source_target_pairs={{0,16},{8,24},{16,0},{24,8},{1,17},{9,25},{17,1},{25,9},{2,18},{10... | collective-permute-start | bytes 184328 | tf_op jit(solution)/shard_map/ppermute | solution.py:708
  37.4 9.8 %all-to-all-start.2 = ((f32[32,2,128]{2,1,0:T(2,128)}), f32[32,2,128]{2,1,0:T(2,128)S(1)}, u32[]{:S(2)}, u32[]{:S(2)}) async-start(f32[32,2,128]{2,1,0:T(2,128)} %bitcast.77), calls=%async_computation.2 | async-start | bytes 65536 | tf_op jit(solution)/shard_map/all_to_all | solution.py:712
  39.9 9.2 %collective-permute-start.5 = (f32[16,640]{1,0:T(8,128)}, f32[16,640]{1,0:T(8,128)S(1)}, u32[]{:S(2)}, u32[]{:S(2)}) collective-permute-start(f32[16,640]{1,0:T(8,128)} %get-tuple-element.150), channel_id=1, source_target_pairs={{0,4},{1,5},{2,6},{3,7},{4,0},{5,1},{6,2},{7,3},{8,12},{9,13},{10,... | collective-permute-start | bytes 122888 | tf_op jit(solution)/shard_map/ppermute | solution.py:708
  42.7 6.5 %collective-permute-start.6 = (f32[16,640]{1,0:T(8,128)}, f32[16,640]{1,0:T(8,128)S(1)}, u32[]{:S(2)}, u32[]{:S(2)}) collective-permute-start(f32[16,640]{1,0:T(8,128)} %get-tuple-element.151), channel_id=1, source_target_pairs={{0,1},{1,0},{2,3},{3,2},{4,5},{5,4},{6,7},{7,6},{8,9},{9,8},{10,11... | collective-permute-start | bytes 122888 | tf_op jit(solution)/shard_map/ppermute | solution.py:708
  51.7 10.0 %all-to-all-start.3 = ((f32[32,4,128]{2,1,0:T(4,128)}), f32[32,4,128]{2,1,0:T(4,128)S(1)}, u32[]{:S(2)}, u32[]{:S(2)}) async-start(f32[32,4,128]{2,1,0:T(4,128)} %bitcast.71), calls=%async_computation.3 | async-start | bytes 131072 | tf_op jit(solution)/shard_map/all_to_all | solution.py:712
  54.3 11.0 %collective-permute-start.10 = (f32[16,640]{1,0:T(8,128)}, f32[16,640]{1,0:T(8,128)S(1)}, u32[]{:S(2)}, u32[]{:S(2)}) collective-permute-start(f32[16,640]{1,0:T(8,128)} %get-tuple-element.163), channel_id=1, source_target_pairs={{0,4},{1,5},{2,6},{3,7},{4,0},{5,1},{6,2},{7,3},{8,12},{9,13},{10,... | collective-permute-start | bytes 122888 | tf_op jit(solution)/shard_map/ppermute | solution.py:708
  57.0 8.3 %collective-permute-start.11 = (f32[16,640]{1,0:T(8,128)}, f32[16,640]{1,0:T(8,128)S(1)}, u32[]{:S(2)}, u32[]{:S(2)}) collective-permute-start(f32[16,640]{1,0:T(8,128)} %get-tuple-element.164), channel_id=1, source_target_pairs={{0,1},{1,0},{2,3},{3,2},{4,5},{5,4},{6,7},{7,6},{8,9},{9,8},{10,11... | collective-permute-start | bytes 122888 | tf_op jit(solution)/shard_map/ppermute | solution.py:708
  58.5 6.8 %collective-permute-start.12 = (f32[16,640]{1,0:T(8,128)}, f32[16,640]{1,0:T(8,128)S(1)}, u32[]{:S(2)}, u32[]{:S(2)}) collective-permute-start(f32[16,640]{1,0:T(8,128)} %get-tuple-element.165), channel_id=1, source_target_pairs={{0,2},{1,3},{2,0},{3,1},{4,6},{5,7},{6,4},{7,5},{8,10},{9,11},{10,... | collective-permute-start | bytes 122888 | tf_op jit(solution)/shard_map/ppermute | solution.py:708
  60.0 5.3 %collective-permute-start.13 = (f32[16,640]{1,0:T(8,128)}, f32[16,640]{1,0:T(8,128)S(1)}, u32[]{:S(2)}, u32[]{:S(2)}) collective-permute-start(f32[16,640]{1,0:T(8,128)} %get-tuple-element.166), channel_id=1, source_target_pairs={{0,16},{8,24},{16,0},{24,8},{1,17},{9,25},{17,1},{25,9},{2,18},{10... | collective-permute-start | bytes 122888 | tf_op jit(solution)/shard_map/ppermute | solution.py:708
  68.8 10.0 %all-to-all-start.4 = ((f32[32,4,128]{2,1,0:T(4,128)}), f32[32,4,128]{2,1,0:T(4,128)S(1)}, u32[]{:S(2)}, u32[]{:S(2)}) async-start(f32[32,4,128]{2,1,0:T(4,128)} %bitcast.74), calls=%async_computation.4 | async-start | bytes 131072 | tf_op jit(solution)/shard_map/all_to_all | solution.py:712
  71.4 9.6 %collective-permute-start.15 = (f32[16,640]{1,0:T(8,128)}, f32[16,640]{1,0:T(8,128)S(1)}, u32[]{:S(2)}, u32[]{:S(2)}) collective-permute-start(f32[16,640]{1,0:T(8,128)} %get-tuple-element.179), channel_id=1, source_target_pairs={{0,4},{1,5},{2,6},{3,7},{4,0},{5,1},{6,2},{7,3},{8,12},{9,13},{10,... | collective-permute-start | bytes 122888 | tf_op jit(solution)/shard_map/ppermute | solution.py:708
  74.2 6.9 %collective-permute-start.16 = (f32[16,640]{1,0:T(8,128)}, f32[16,640]{1,0:T(8,128)S(1)}, u32[]{:S(2)}, u32[]{:S(2)}) collective-permute-start(f32[16,640]{1,0:T(8,128)} %get-tuple-element.180), channel_id=1, source_target_pairs={{0,1},{1,0},{2,3},{3,2},{4,5},{5,4},{6,7},{7,6},{8,9},{9,8},{10,11... | collective-permute-start | bytes 122888 | tf_op jit(solution)/shard_map/ppermute | solution.py:708
  75.7 5.4 %collective-permute-start.17 = (f32[16,640]{1,0:T(8,128)}, f32[16,640]{1,0:T(8,128)S(1)}, u32[]{:S(2)}, u32[]{:S(2)}) collective-permute-start(f32[16,640]{1,0:T(8,128)} %get-tuple-element.181), channel_id=1, source_target_pairs={{0,2},{1,3},{2,0},{3,1},{4,6},{5,7},{6,4},{7,5},{8,10},{9,11},{10,... | collective-permute-start | bytes 122888 | tf_op jit(solution)/shard_map/ppermute | solution.py:708
  83.3 10.0 %all-to-all-start.5 = ((f32[32,4,128]{2,1,0:T(4,128)}), f32[32,4,128]{2,1,0:T(4,128)S(1)}, u32[]{:S(2)}, u32[]{:S(2)}) async-start(f32[32,4,128]{2,1,0:T(4,128)} %bitcast.70), calls=%async_computation.5 | async-start | bytes 131072 | tf_op jit(solution)/shard_map/all_to_all | solution.py:712
  86.1 10.9 %collective-permute-start.20 = (f32[16,640]{1,0:T(8,128)}, f32[16,640]{1,0:T(8,128)S(1)}, u32[]{:S(2)}, u32[]{:S(2)}) collective-permute-start(f32[16,640]{1,0:T(8,128)} %get-tuple-element.194), channel_id=1, source_target_pairs={{0,4},{1,5},{2,6},{3,7},{4,0},{5,1},{6,2},{7,3},{8,12},{9,13},{10,... | collective-permute-start | bytes 122888 | tf_op jit(solution)/shard_map/ppermute | solution.py:708
  88.6 8.4 %collective-permute-start.21 = (f32[16,640]{1,0:T(8,128)}, f32[16,640]{1,0:T(8,128)S(1)}, u32[]{:S(2)}, u32[]{:S(2)}) collective-permute-start(f32[16,640]{1,0:T(8,128)} %get-tuple-element.195), channel_id=1, source_target_pairs={{0,1},{1,0},{2,3},{3,2},{4,5},{5,4},{6,7},{7,6},{8,9},{9,8},{10,11... | collective-permute-start | bytes 122888 | tf_op jit(solution)/shard_map/ppermute | solution.py:708
  90.1 6.9 %collective-permute-start.22 = (f32[16,640]{1,0:T(8,128)}, f32[16,640]{1,0:T(8,128)S(1)}, u32[]{:S(2)}, u32[]{:S(2)}) collective-permute-start(f32[16,640]{1,0:T(8,128)} %get-tuple-element.196), channel_id=1, source_target_pairs={{0,2},{1,3},{2,0},{3,1},{4,6},{5,7},{6,4},{7,5},{8,10},{9,11},{10,... | collective-permute-start | bytes 122888 | tf_op jit(solution)/shard_map/ppermute | solution.py:708
  91.7 5.4 %collective-permute-start.23 = (f32[16,640]{1,0:T(8,128)}, f32[16,640]{1,0:T(8,128)S(1)}, u32[]{:S(2)}, u32[]{:S(2)}) collective-permute-start(f32[16,640]{1,0:T(8,128)} %get-tuple-element.197), channel_id=1, source_target_pairs={{0,16},{8,24},{16,0},{24,8},{1,17},{9,25},{17,1},{25,9},{2,18},{10... | collective-permute-start | bytes 122888 | tf_op jit(solution)/shard_map/ppermute | solution.py:708
  100.6 9.9 %all-to-all-start.6 = ((f32[32,4,128]{2,1,0:T(4,128)}), f32[32,4,128]{2,1,0:T(4,128)S(1)}, u32[]{:S(2)}, u32[]{:S(2)}) async-start(f32[32,4,128]{2,1,0:T(4,128)} %bitcast.73), calls=%async_computation.6 | async-start | bytes 131072 | tf_op jit(solution)/shard_map/all_to_all | solution.py:712
  103.1 9.8 %collective-permute-start.25 = (f32[16,640]{1,0:T(8,128)}, f32[16,640]{1,0:T(8,128)S(1)}, u32[]{:S(2)}, u32[]{:S(2)}) collective-permute-start(f32[16,640]{1,0:T(8,128)} %get-tuple-element.211), channel_id=1, source_target_pairs={{0,4},{1,5},{2,6},{3,7},{4,0},{5,1},{6,2},{7,3},{8,12},{9,13},{10,... | collective-permute-start | bytes 122888 | tf_op jit(solution)/shard_map/ppermute | solution.py:708
  105.9 7.1 %collective-permute-start.26 = (f32[16,640]{1,0:T(8,128)}, f32[16,640]{1,0:T(8,128)S(1)}, u32[]{:S(2)}, u32[]{:S(2)}) collective-permute-start(f32[16,640]{1,0:T(8,128)} %get-tuple-element.212), channel_id=1, source_target_pairs={{0,1},{1,0},{2,3},{3,2},{4,5},{5,4},{6,7},{7,6},{8,9},{9,8},{10,11... | collective-permute-start | bytes 122888 | tf_op jit(solution)/shard_map/ppermute | solution.py:708
  107.4 5.6 %collective-permute-start.27 = (f32[16,640]{1,0:T(8,128)}, f32[16,640]{1,0:T(8,128)S(1)}, u32[]{:S(2)}, u32[]{:S(2)}) collective-permute-start(f32[16,640]{1,0:T(8,128)} %get-tuple-element.213), channel_id=1, source_target_pairs={{0,2},{1,3},{2,0},{3,1},{4,6},{5,7},{6,4},{7,5},{8,10},{9,11},{10,... | collective-permute-start | bytes 122888 | tf_op jit(solution)/shard_map/ppermute | solution.py:708
  115.0 10.0 %all-to-all-start.7 = ((f32[32,4,128]{2,1,0:T(4,128)}), f32[32,4,128]{2,1,0:T(4,128)S(1)}, u32[]{:S(2)}, u32[]{:S(2)}) async-start(f32[32,4,128]{2,1,0:T(4,128)} %bitcast.69), calls=%async_computation.7 | async-start | bytes 131072 | tf_op jit(solution)/shard_map/all_to_all | solution.py:712
  117.6 11.1 %collective-permute-start.30 = (f32[16,640]{1,0:T(8,128)}, f32[16,640]{1,0:T(8,128)S(1)}, u32[]{:S(2)}, u32[]{:S(2)}) collective-permute-start(f32[16,640]{1,0:T(8,128)} %get-tuple-element.228), channel_id=1, source_target_pairs={{0,4},{1,5},{2,6},{3,7},{4,0},{5,1},{6,2},{7,3},{8,12},{9,13},{10,... | collective-permute-start | bytes 122888 | tf_op jit(solution)/shard_map/ppermute | solution.py:708
  120.3 8.4 %collective-permute-start.31 = (f32[16,640]{1,0:T(8,128)}, f32[16,640]{1,0:T(8,128)S(1)}, u32[]{:S(2)}, u32[]{:S(2)}) collective-permute-start(f32[16,640]{1,0:T(8,128)} %get-tuple-element.229), channel_id=1, source_target_pairs={{0,1},{1,0},{2,3},{3,2},{4,5},{5,4},{6,7},{7,6},{8,9},{9,8},{10,11... | collective-permute-start | bytes 122888 | tf_op jit(solution)/shard_map/ppermute | solution.py:708
  121.8 6.9 %collective-permute-start.32 = (f32[16,640]{1,0:T(8,128)}, f32[16,640]{1,0:T(8,128)S(1)}, u32[]{:S(2)}, u32[]{:S(2)}) collective-permute-start(f32[16,640]{1,0:T(8,128)} %get-tuple-element.230), channel_id=1, source_target_pairs={{0,2},{1,3},{2,0},{3,1},{4,6},{5,7},{6,4},{7,5},{8,10},{9,11},{10,... | collective-permute-start | bytes 122888 | tf_op jit(solution)/shard_map/ppermute | solution.py:708
  123.3 5.4 %collective-permute-start.33 = (f32[16,640]{1,0:T(8,128)}, f32[16,640]{1,0:T(8,128)S(1)}, u32[]{:S(2)}, u32[]{:S(2)}) collective-permute-start(f32[16,640]{1,0:T(8,128)} %get-tuple-element.231), channel_id=1, source_target_pairs={{0,16},{8,24},{16,0},{24,8},{1,17},{9,25},{17,1},{25,9},{2,18},{10... | collective-permute-start | bytes 122888 | tf_op jit(solution)/shard_map/ppermute | solution.py:708
  (12 other events, 45.1 us)

commit v5 on v4

--- a/solution.py
+++ b/solution.py
@@ -17,7 +17,6 @@
 BF16 = jnp.bfloat16
 VMEM_LIMIT = 24 * 2**20
 COST = 2_000_000
-BRING = 1
 BAND = 256
 
 
@@ -41,11 +40,15 @@
     return jnp.dot(a, b, preferred_element_type=F32)
 
 
-def times(x, w_high, w_low):
+def turned_dot(a, b):
+    return lax.dot_general(a, b, (((1,), (1,)), ((), ())), preferred_element_type=F32)
+
+
+def times(x, w_high, w_low, dot=bdot):
     rows = x.shape[0]
     a, b, c = thirds(x)
-    full = bdot(jnp.concatenate([a, b, c], axis=0), w_high)
-    part = bdot(jnp.concatenate([a, b], axis=0), w_low)
+    full = dot(jnp.concatenate([a, b, c], axis=0), w_high)
+    part = dot(jnp.concatenate([a, b], axis=0), w_low)
     low = full[2 * rows :] + part[rows:]
     return full[:rows] + (full[rows : 2 * rows] + part[:rows] + low)
 
@@ -131,9 +134,9 @@
     return jnp.sum(total, axis=0, keepdims=True)
 
 
-def exact(x, unit):
+def exact(x, unit, dot=bdot):
     rows = x.shape[0]
-    full = bdot(jnp.concatenate(thirds(x), axis=0), unit)
+    full = dot(jnp.concatenate(thirds(x), axis=0), unit)
     return full[:rows] + (full[rows : 2 * rows] + full[2 * rows :])
 
 
@@ -144,10 +147,10 @@
     return times(master, a_high[...], a_low[...]) + exact(slave, unit[...])
 
 
-def send_contact(message, per, surface, t_high, t_low, unit_t):
+def send_contact(message, per, surface, a_high, a_low, unit):
     devices = message.shape[0] // per
-    master = times(surface, t_high[...], t_low[...])
-    slave = exact(surface, unit_t[...])
+    master = times(surface, a_high[...], a_low[...], turned_dot)
+    slave = exact(surface, unit[...], turned_dot)
     for line, value in enumerate(pack(master, slave, devices)):
         put(message, per, line, value)
 
@@ -169,7 +172,7 @@
     same = owner_col == owner_row
     rank_col = jnp.sum(jnp.where(same & (across < up), live_row, 0), axis=1, keepdims=True)
     rank_row = jnp.sum(jnp.where(same & (up < across), live_col, 0), axis=0, keepdims=True)
-    return column, live_row, live_col, owner_col, rank_row, rank_col
+    return column, live_row, rank_row, rank_col
 
 
 def load_modes(basis, modes, blocks):
@@ -183,7 +186,7 @@
     devices = message.ref.shape[0]
     owner, dofs, active, basis = owner(), dofs(), active(), basis()
     rows = owner.shape[1]
-    column, live_row, _, _, _, rank_col = ranks(owner[...], active[...], count[0])
+    column, live_row, _, rank_col = ranks(owner[...], active[...], count[0])
     named = (iota((devices, rows), 0) == owner[...]) & (live_row > 0)
     slots = jnp.where(iota((rows, LANES), 1) == rank_col, column(dofs[...]) + 1, 0)
     lines = jnp.dot(
@@ -205,37 +208,27 @@
 
 
 def slots_kernel(
-    devices, count, owner, active, mortar, start_rows, right_rows, a_high, a_low, t_high, t_low,
-    start, right,
+    devices, count, owner, active, mortar, start_rows, right_rows, a_high, a_low, start, right
 ):
     owner, active = owner(), active()
     rows = owner.shape[1]
     width = CAP * devices
-    _, live_row, live_col, owner_col, rank_row, rank_col = ranks(
-        owner[...], active[...], count[0]
-    )
+    _, live_row, rank_row, _ = ranks(owner[...], active[...], count[0])
     slot_row = jnp.where(live_row > 0, rank_row * devices + owner[...], -1)
-    slot_col = jnp.where(live_col > 0, rank_col * devices + owner_col, -1)
     pick = jnp.where(iota((width, rows), 0) == slot_row, 1.0, 0.0).astype(BF16)
-    pick_t = jnp.where(iota((rows, width), 1) == slot_col, 1.0, 0.0).astype(BF16)
     blocks, directions = start.ref.shape[0], start.ref.shape[1]
     for source, target in ((start_rows(), start), (right_rows(), right)):
         for f in range(blocks):
             for c in range(directions):
                 target.ref[f, c : c + 1, :] = source[c * blocks + f]
         target.flush()
-    for part, straight, turned in zip(
-        halves(mortar()[...]), (a_high, a_low), (t_high, t_low), strict=True
-    ):
-        straight.ref[...] = bdot(pick, part).astype(BF16)
-        straight.flush()
-        turned.ref[...] = bdot(part.astype(F32).T.astype(BF16), pick_t).astype(BF16)
-        turned.flush()
+    for part, target in zip(halves(mortar()[...]), (a_high, a_low), strict=True):
+        target.ref[...] = bdot(pick, part).astype(BF16)
+        target.flush()
 
 
 def first_kernel(
-    organs, arrived, matches, basis, start, t_high, t_low, right, message, unit_t, unit,
-    modes_out, *sends,
+    organs, arrived, matches, basis, start, a_high, a_low, right, message, unit, modes_out, *sends
 ):
     devices = arrived.shape[0]
     subs = devices // organs
@@ -244,11 +237,11 @@
     modes = basis.shape[0] // blocks
     length = basis.shape[2]
     dofs = arrived[...]
-    turned = square(dofs)[:CAP, :devices]
-    dof_row = jnp.concatenate([turned[k : k + 1, :] for k in range(CAP)], axis=1)
-    place_t = iota((length, CAP * devices), 0).astype(F32) + 1.0
-    unit_t.ref[...] = jnp.where(place_t == dof_row, -1.0, 0.0).astype(BF16)
-    unit_t.flush()
+    place = iota((devices, length), 1).astype(F32) + 1.0
+    for k in range(CAP):
+        block = jnp.where(place == dofs[:, k : k + 1], -1.0, 0.0).astype(BF16)
+        unit.ref[k * devices : (k + 1) * devices, :] = block
+    unit.flush()
     mine = lax.axis_index("organ") * subs
     total = jnp.sum(arrived[pl.ds(pl.multiple_of(mine, 8), subs), :], axis=0, keepdims=True)
     lane = iota((1, LANES), 1)
@@ -287,8 +280,8 @@
     first = [modes_ref[m, 0:1, :] for m in range(modes)]
     extra = jnp.zeros((2 * 16 - directions - modes, length), F32)
     both = jnp.concatenate([start[0]] + first + [extra], axis=0)
-    master = times(both, t_high()[...], t_low()[...])
-    slave = exact(both, unit_t.ref[...])
+    master = times(both, a_high()[...], a_low()[...], turned_dot)
+    slave = exact(both, unit.ref[...], turned_dot)
     for line, value in enumerate(pack(master[:directions], slave[:directions], devices)):
         put(message.ref, 4, line, value)
     rows = slice(directions, directions + 8)
@@ -297,14 +290,6 @@
     put(message.ref, 4, 2, jnp.concatenate([line[:, :half] for line in lines], axis=1))
     spread_rows(message.ref, 4, 3, coefficients_row(right(), modes_ref))
     message.flush()
-    place = iota((devices, length), 1).astype(F32) + 1.0
-    for k in range(CAP):
-        block = jnp.where(place == dofs[:, k : k + 1], -1.0, 0.0).astype(BF16)
-        unit.ref[k * devices : (k + 1) * devices, :] = block
-
-
-def turned_dot(a, b):
-    return lax.dot_general(a, b, (((1,), (1,)), ((), ())), preferred_element_type=F32)
 
 
 def times_symmetric(x, parts, f):
@@ -351,8 +336,7 @@
 
 
 def start_contact(
-    organs, arrived, sent, start, a_high, a_low, unit, modes_ref, right, new_right,
-    base, added,
+    organs, arrived, sent, start, right, a_high, a_low, unit, modes_ref, new_right, base, added
 ):
     sent, start, maps = sent(), start(), (a_high(), a_low(), unit())
     devices = sent.shape[0] // 4
@@ -385,11 +369,10 @@
 
 
 def start_kernel(
-    organs, bands, matches, f0, f1, f2, f3, f4, base, added, *refs
+    organs, bands, matches, f0, f1, f2, f3, f4, base, added, a_high, a_low, unit, modes_ref, *refs
 ):
     near, rest = refs[:bands], refs[bands:]
-    t_high, t_low, unit_t, modes_ref, message, smoothed_out, jump_out = rest[:7]
-    s0, s1, s2, s3, s4, inner = rest[7:]
+    message, smoothed_out, jump_out, s0, s1, s2, s3, s4, inner = rest
     faces = (f0, f1, f2, f3, f4)
     smoothed = smoothed_out.ref
     blocks, directions = base.shape[0], base.shape[1]
@@ -398,7 +381,7 @@
     for f in range(blocks):
         smooth(inner, near, smoothed, f)
         if f == 0:
-            send_contact(message.ref, 2, smoothed[0], t_high, t_low, unit_t)
+            send_contact(message.ref, 2, smoothed[0], a_high, a_low, unit)
             message.flush()
     for r, send in enumerate((s0, s1, s2, s3, s4)):
         send(smoothed.at[matches[r]])
@@ -424,18 +407,18 @@
             jump_modes[0, row, :] = jump_modes[0, row, :] + added[8 * o + m : 8 * o + m + 1, :]
 
 
-def residual_contact(arrived, sent, smoothed, a_high, a_low, unit, right, part):
+def residual_contact(arrived, sent, smoothed, right, a_high, a_low, unit, part):
     sent, smoothed, right = sent(), smoothed(), right()
     part[...] = right[...] - smoothed[...]
     part[0] -= contact(sent, arrived, 2, 2, a_high(), a_low(), unit())
 
 
 def residual_kernel(
-    matches, f0, f1, f2, f3, f4, part, t_high, t_low, unit_t, modes_ref, message, resid, *sends
+    matches, f0, f1, f2, f3, f4, part, a_high, a_low, unit, modes_ref, message, resid, *sends
 ):
     for r, face in zip(ORDER, (f0, f1, f2, f3, f4), strict=True):
         resid.ref[matches[r]] = part[matches[r]] + face[...]
-    send_residual(matches, resid, modes_ref, (t_high, t_low, unit_t), message, sends)
+    send_residual(matches, resid, modes_ref, (a_high, a_low, unit), message, sends)
 
 
 def send_residual(matches, resid, modes_ref, maps, message, sends):
@@ -448,9 +431,10 @@
 
 
 def inner_contact(
-    organs, steps, arrived, sent, resid, a_high, a_low, unit, modes_ref, jump_modes, *refs
+    organs, steps, arrived, sent, resid, modes_ref, jump_modes, *refs
 ):
     rest = list(refs)
+    a_high, a_low, unit = (rest.pop(0) for _ in range(3))
     if steps:
         start, behind, jumps, sizes = (
             rest[0],
@@ -504,11 +488,10 @@
 
 
 def inner_kernel(bands, last, older, matches, f0, f1, f2, f3, f4, base, norms, *refs):
-    near, rest = refs[:bands], list(refs[bands:])
+    maps, rest = (None, refs) if last else (refs[:3], refs[3:])
+    near, rest = rest[:bands], list(rest[bands:])
     previous = rest.pop(0) if older else None
-    maps = None if last else rest[:3]
-    message = rest[0 if last else 3]
-    rest = rest[1 if last else 4 :]
+    message = rest.pop(0)
     if last:
         inner, smoothed = rest
     else:
@@ -548,14 +531,13 @@
     return rho, beta, curvature, rho / curvature
 
 
-def outer_contact(older, arrived, sent, smoothed, a_high, a_low, unit, projected, *refs):
+def outer_contact(older, arrived, sent, smoothed, projected, *refs):
     rest = list(refs)
     old_image = scalars = None
     if older:
-        old_image, scalars, new_scalars, part, steps, image = rest
-        old_image, scalars = old_image(), scalars()
-    else:
-        new_scalars, part, steps, image = rest
+        old_image, scalars = rest[0](), rest[1]()
+        rest = rest[2:]
+    a_high, a_low, unit, new_scalars, part, steps, image = rest
     sent, smoothed, projected = sent(), smoothed(), projected()
     blocks, directions = smoothed.shape[0], smoothed.shape[1]
     row = jnp.sum(get(arrived, 4, 2), axis=0, keepdims=True)
@@ -577,7 +559,7 @@
 
 
 def outer_kernel(older, matches, f0, f1, f2, f3, f4, part, steps, image, *refs):
-    t_high, t_low, unit_t, modes_ref = refs[:4]
+    a_high, a_low, unit, modes_ref = refs[:4]
     rest = list(refs[4:])
     if older:
         message, resid = rest[:2]
@@ -590,7 +572,7 @@
         resid.ref[matches[r]] = part[matches[r]] + step * face[...]
         if not older:
             new_image.ref[matches[r]] = image[matches[r]] - face[...]
-    send_residual(matches, resid, modes_ref, (t_high, t_low, unit_t), message, sends)
+    send_residual(matches, resid, modes_ref, (a_high, a_low, unit), message, sends)
 
 
 def last_kernel(arrived, projected, old_direction, total, scalars, out):
@@ -604,10 +586,12 @@
 
 
 class Late:
-    def __init__(self, source, target, sem):
-        self.target, self.waiting = target, True
+    def __init__(self, source, target, sem, priority=0):
+        self.target, self.waiting, self.priority = target, True, priority
         self.copy = pltpu.make_async_copy(source, target, sem)
-        self.copy.start()
+
+    def start(self):
+        self.copy.start(priority=self.priority)
 
     def __call__(self):
         if self.waiting:
@@ -637,7 +621,7 @@
             self.started = True
 
 
-def call(kernel, outs, args, late=(), smem=0, near=(), sends=(), scratch=(), bring=(), held=0):
+def call(kernel, outs, args, late=(), smem=0, near=(), sends=(), scratch=(), bring=(), held=0, shared=0):
     n_late, n_out, n_arg, n_near = len(late), len(outs), len(args), len(near)
     bring = [item if isinstance(item, tuple) else (item, item.shape, None) for item in bring]
     brought = [(shape, a.dtype) for a, shape, _ in bring]
@@ -656,23 +640,21 @@
         buffers, results = take(n_late), take(n_out)
         extra = take(len(scratch))
         in_sem, bring_sem, out_sem = refs
-        lates = [Late(s, b, in_sem.at[i]) for i, (s, b) in enumerate(zip(sources, buffers))]
-        written = [Out(r, t, out_sem.at[i]) for i, (r, t) in enumerate(zip(results, targets))]
-        posts = [Send(t, out_sem.at[n_out + i]) for i, t in enumerate(ports)]
         copies = []
         for i, (origin, goal) in enumerate(zip(origins, goals, strict=True)):
             first = bring[i][2]
             if first is not None:
                 rows, columns = goal.shape[1], goal.shape[2]
                 origin = origin.at[:, pl.ds(first, rows), pl.ds(first, columns)]
-            copies.append(pltpu.make_async_copy(origin, goal, bring_sem.at[i]))
-        for copy in copies:
-            copy.start(priority=BRING)
-        kernel(*given, *lates, *written, *posts, *close, *extra)
-        for item in lates:
+            copies.append(Late(origin, goal, bring_sem.at[i], 0 if i < shared else 1))
+        lates = [Late(s, b, in_sem.at[i]) for i, (s, b) in enumerate(zip(sources, buffers))]
+        for item in copies[:shared] + lates + copies[shared:]:
+            item.start()
+        written = [Out(r, t, out_sem.at[i]) for i, (r, t) in enumerate(zip(results, targets))]
+        posts = [Send(t, out_sem.at[n_out + i]) for i, t in enumerate(ports)]
+        kernel(*given, *lates, *copies[:shared], *written, *posts, *close, *extra)
+        for item in lates + copies:
             item()
-        for copy in copies:
-            copy.wait()
         for item in written:
             item.flush()
         for item in written + posts:
@@ -762,38 +744,36 @@
         smem=1,
     )
     arrived = exchange(setup)
-    a_high, a_low, t_high, t_low, start, right = call(
+    a_high, a_low, start, right = call(
         functools.partial(slots_kernel, devices),
-        [((width, length), BF16)] * 2 + [((length, width), BF16)] * 2 + [whole] * 2,
+        [((width, length), BF16)] * 2 + [whole] * 2,
         (count,),
         (owner, active, mortar, start_rows, right_rows),
         smem=1,
     )
-    sent, unit_t, unit, modes_ref, *faces = call(
+    sent, unit, modes_ref, *faces = call(
         functools.partial(first_kernel, organs),
         [
             message_line,
-            ((length, width), BF16),
             ((width, length), BF16),
             ((modes, blocks, length), F32),
         ]
         + [((directions + 8, length), F32)] * blocks,
         (arrived,),
-        (matches, basis, start, t_high, t_low, right),
+        (matches, basis, start, a_high, a_low, right),
         held=1,
     )
-    forth = (a_high, a_low, unit)
-    back = (t_high, t_low, unit_t)
-    back_modes = back + (modes_ref,)
+    maps = (a_high, a_low, unit)
     arrived = exchange(sent)
     faces = swap_faces(faces)
     right, base, added, *more = call(
         functools.partial(start_contact, organs),
         [whole],
         (arrived,),
-        (sent, start) + forth + (modes_ref, right),
+        (sent, start, right),
         near=[whole, ((8 * organs, length), F32)],
-        bring=near_matrices + back_modes,
+        bring=maps + (modes_ref,) + near_matrices,
+        shared=4,
     )
     message, smoothed, jump_modes, *posts = call(
         functools.partial(start_kernel, organs, bands),
@@ -805,18 +785,19 @@
     )
     arrived = exchange(message)
     faces = swap_faces(posts)
-    part, *maps = call(
+    part, *more = call(
         residual_contact,
         [],
         (arrived,),
-        (message, smoothed) + forth + (right,),
+        (message, smoothed, right),
         near=[whole],
-        bring=back_modes,
+        bring=maps + (modes_ref,),
+        shared=3,
     )
     sent, resid, *posts = call(
         residual_kernel,
         [message_line, whole],
-        (matches, *faces, part, *maps),
+        (matches, *faces, part, *more),
         smem=1,
         sends=sends,
     )
@@ -829,16 +810,15 @@
         faces = swap_faces(posts)
         history = (start, *fields, *jumps, *scalars) if last else ()
         more_near = [whole] * 3 + [(size, F32)] if last else []
-        ahead = () if last else back
-        if older and not last:
-            ahead = (jumps[-1],) + ahead
+        ahead = (jumps[-1],) if older and not last else ()
         projected, *more = call(
             functools.partial(inner_contact, organs, step if last else 0),
             [] if last else [whole],
             (arrived,),
-            (sent, resid) + forth + (modes_ref, jump_modes) + history,
+            (sent, resid, modes_ref, jump_modes) + (maps if last else ()) + history,
             near=([whole] + more_near if last else []) + [whole, ((8, LANES), F32)],
-            bring=near_matrices + ahead,
+            bring=(() if last else maps) + near_matrices + ahead,
+            shared=0 if last else 3,
         )
         if last:
             total, direction, jumped, last_size, base, norms, *near = more
@@ -865,9 +845,10 @@
             functools.partial(outer_contact, older),
             [(size, F32)],
             (arrived,),
-            (message, smoothed) + forth + (projected,) + old,
+            (message, smoothed, projected) + old,
             near=[whole, ((directions, LANES), F32), whole],
-            bring=back_modes,
+            bring=maps + (modes_ref,),
+            shared=3,
         )
         sent, resid, *posts = call(
             functools.partial(outer_kernel, older),

time: 143 us -> 142 us (level)
  transfers between devices with their start and end apart: 43 -> 43, of which waited for: 10 -> 10; matrix products, arithmetic and copies ran while one was open for 0% -> 0% of each run, Pallas kernels for 17% -> 16%
where the time goes in v5:
time: 142 us
  starting transfers between devices  75.9 us (53%)
  Pallas kernels  47.6 us (34%)
  blocking collectives  9.6 us (7%)
  waiting for transfers between devices  7.28 us (5%)
    ppermute x35, starting transfers between devices, from_partner(): return lax.ppermute(value, axis, pairs)  50.4 us
    pallas_call x18, Pallas kernels, call(): pl.pallas_call(body, out_shape=[pltpu.HBM(shape, kind) for shape, kind in...  47.6 us
    all_to_all x8, starting transfers between devices, exchange(): lax.all_to_all(message, AXES, split_axis=0, concat_axis=0, tiled=True)  25.4 us
    all_to_all x1, blocking collectives, exchange(): lax.all_to_all(message, AXES, split_axis=0, concat_axis=0, tiled=True)  9.6 us
    all_to_all x8, waiting for transfers between devices, exchange(): lax.all_to_all(message, AXES, split_axis=0, concat_axis=0, tiled=True)  5.63 us
  transfers between devices with their start and end apart: 43, of which 10 were waited for; matrix products, arithmetic and copies ran while one was open for 0% of the time, Pallas kernels for 16%

profile of v5, /device:TPU:0, one launch (start us, length us, event | category | flops | bytes accessed | tf_op | source)
XLA Modules:
  0.0 141.6 jit_solution(13437842492813577762)
XLA Ops:
  0.7 1.9 %shard_map.100 = f32[32,128]{1,0:T(8,128)} custom-call(s32[1]{0:T(128)} %bitcast.35.refs_0_, s32[1,128]{1,0:T(1,128)} %bitcast.80, s32[1,128]{1,0:T(1,128)} %bitcast.84, s32[1,128]{1,0:T(1,128)} %bitcast.82, f32[30,1,640]{2,1,0:T(1,128)} %bitcast.67), custom_call_target="tpu_custom_call" | custom-call | flops 2000000 | bytes 2000000 | tf_op jit(solution)/shard_map/pallas_call | solution.py:675
  2.6 7.3 %all-to-all-start = ((f32[32,1,128]{2,1,0:T(1,128)}), f32[32,1,128]{2,1,0:T(1,128)S(1)}, u32[]{:S(2)}, u32[]{:S(2)}) async-start(f32[32,1,128]{2,1,0:T(1,128)} %bitcast.79), calls=%async_computation | async-start | bytes 32768 | tf_op jit(solution)/shard_map/all_to_all | solution.py:694
  9.9 2.5 %shard_map.101 = (bf16[256,640]{1,0:T(8,128)(2,1)}, bf16[256,640]{1,0:T(8,128)(2,1)}, f32[5,16,640]{2,1,0:T(8,128)}, f32[5,16,640]{2,1,0:T(8,128)}) custom-call(s32[1]{0:T(128)} %bitcast.36.refs_0_, s32[1,128]{1,0:T(1,128)} %bitcast.81, s32[1,128]{1,0:T(1,128)} %bitcast.83, f32[128,640]{1,0:T(8,128)} %bitcast.66, f32[80,1,640]{2,1,0:T(1,128)} %bitcast.75, ...), custom_call_target="tpu_custom_call" | custom-call | flops 2000000 | bytes 2000000 | tf_op jit(solution)/shard_map/pallas_call | solution.py:675
  12.4 4.6 %all-to-all-done = f32[32,1,128]{2,1,0:T(1,128)S(1)} async-done(((f32[32,1,128]{2,1,0:T(1,128)}), f32[32,1,128]{2,1,0:T(1,128)S(1)}, u32[]{:S(2)}, u32[]{:S(2)}) %all-to-all-start) | async-done | bytes 16416 | tf_op jit(solution)/shard_map/all_to_all | solution.py:694
  17.0 2.9 %shard_map.102 = (f32[128,128]{1,0:T(8,128)}, bf16[256,640]{1,0:T(8,128)(2,1)}, f32[6,5,640]{2,1,0:T(8,128)}, f32[24,640]{1,0:T(8,128)}, f32[24,640]{1,0:T(8,128...) custom-call(f32[32,128]{1,0:T(8,128)S(1)} %bitcast.44, s32[5]{0:T(128)} %bitcast.46, ...), custom_call_target="tpu_custom_call" | custom-call | flops 2000000 | bytes 2000000 | tf_op jit(solution)/shard_map/pallas_call | solution.py:675
  19.9 2.6 %all-to-all-start.1 = ((f32[32,4,128]{2,1,0:T(4,128)}), f32[32,4,128]{2,1,0:T(4,128)S(1)}, u32[]{:S(2)}, u32[]{:S(2)}) async-start(f32[32,4,128]{2,1,0:T(4,128)} %bitcast.72), calls=%async_computation.1 | async-start | bytes 131072 | tf_op jit(solution)/shard_map/all_to_all | solution.py:694
  22.5 2.7 %collective-permute-start = (f32[24,640]{1,0:T(8,128)}, f32[24,640]{1,0:T(8,128)S(1)}, u32[]{:S(2)}, u32[]{:S(2)}) collective-permute-start(f32[24,640]{1,0:T(8,128)} %get-tuple-element.127), channel_id=1, source_target_pairs={{0,4},{1,5},{2,6},{3,7},{4,0},{5,1},{6,2},{7,3},{8,12},{9,13},{10,... | collective-permute-start | bytes 184328 | tf_op jit(solution)/shard_map/ppermute | solution.py:690
  29.9 3.2 %shard_map.103 = (f32[5,16,640]{2,1,0:T(8,128)}, f32[5,16,640]{2,1,0:T(8,128)S(1)}, f32[32,640]{1,0:T(8,128)S(1)}, bf16[256,640]{1,0:T(8,128)(2,1)S(1)}, bf16[25...) custom-call(f32[128,128]{1,0:T(8,128)S(1)} %bitcast.38, ...), custom_call_target="tpu_custom_call" | custom-call | flops 2000000 | bytes 2000000 | tf_op jit(solution)/shard_map/pallas_call | solution.py:675
  33.2 3.7 %shard_map.104 = (f32[64,128]{1,0:T(8,128)}, f32[5,16,640]{2,1,0:T(8,128)}, f32[5,32,640]{2,1,0:T(8,128)}, f32[16,640]{1,0:T(8,128)}, f32[16,640]{1,0:T(8,128)},...) custom-call(s32[5]{0:T(128)S(1)} %bitcast.47, f32[24,640]{1,0:T(8,128)S(1)} %collective-permute-done.refs_1_, ...), custom_call_target="tpu_custom_call" | custom-call | flops 2000000 | bytes 2000000 | tf_op jit(solution)/shard_map/pallas_call | solution.py:675
  36.8 2.5 %all-to-all-start.2 = ((f32[32,2,128]{2,1,0:T(2,128)}), f32[32,2,128]{2,1,0:T(2,128)S(1)}, u32[]{:S(2)}, u32[]{:S(2)}) async-start(f32[32,2,128]{2,1,0:T(2,128)} %bitcast.77), calls=%async_computation.2 | async-start | bytes 65536 | tf_op jit(solution)/shard_map/all_to_all | solution.py:694
  39.4 2.7 %collective-permute-start.5 = (f32[16,640]{1,0:T(8,128)}, f32[16,640]{1,0:T(8,128)S(1)}, u32[]{:S(2)}, u32[]{:S(2)}) collective-permute-start(f32[16,640]{1,0:T(8,128)} %get-tuple-element.144), channel_id=1, source_target_pairs={{0,4},{1,5},{2,6},{3,7},{4,0},{5,1},{6,2},{7,3},{8,12},{9,13},{10,... | collective-permute-start | bytes 122888 | tf_op jit(solution)/shard_map/ppermute | solution.py:690
  51.2 2.6 %all-to-all-start.3 = ((f32[32,4,128]{2,1,0:T(4,128)}), f32[32,4,128]{2,1,0:T(4,128)S(1)}, u32[]{:S(2)}, u32[]{:S(2)}) async-start(f32[32,4,128]{2,1,0:T(4,128)} %bitcast.71), calls=%async_computation.3 | async-start | bytes 131072 | tf_op jit(solution)/shard_map/all_to_all | solution.py:694
  53.8 2.7 %collective-permute-start.10 = (f32[16,640]{1,0:T(8,128)}, f32[16,640]{1,0:T(8,128)S(1)}, u32[]{:S(2)}, u32[]{:S(2)}) collective-permute-start(f32[16,640]{1,0:T(8,128)} %get-tuple-element.157), channel_id=1, source_target_pairs={{0,4},{1,5},{2,6},{3,7},{4,0},{5,1},{6,2},{7,3},{8,12},{9,13},{10,... | collective-permute-start | bytes 122888 | tf_op jit(solution)/shard_map/ppermute | solution.py:690
  61.2 3.3 %shard_map.107 = (f32[5,16,640]{2,1,0:T(8,128)}, f32[5,16,640]{2,1,0:T(8,128)S(1)}, f32[8,128]{1,0:T(8,128)S(1)}, bf16[256,640]{1,0:T(8,128)(2,1)S(1)}, bf16[256...) custom-call(f32[128,128]{1,0:T(8,128)S(1)} %bitcast.39, ...), custom_call_target="tpu_custom_call" | custom-call | flops 2000000 | bytes 2000000 | tf_op jit(solution)/shard_map/pallas_call | solution.py:675
  64.6 3.6 %shard_map.108 = (f32[128,128]{1,0:T(8,128)}, f32[5,16,640]{2,1,0:T(8,128)}, f32[5,16,640]{2,1,0:T(8,128)}, f32[16,640]{1,0:T(8,128)}, f32[16,640]{1,0:T(8,128)}...) custom-call(s32[5]{0:T(128)S(1)} %bitcast.49, f32[16,640]{1,0:T(8,128)S(1)} %collective-permute-done.10.refs_1_, ...), custom_call_target="tpu_custom_call" | custom-call | flops 2000000 | bytes 2000000 | tf_op jit(solution)/shard_map/pallas_call | solution.py:675
  68.2 2.5 %all-to-all-start.4 = ((f32[32,4,128]{2,1,0:T(4,128)}), f32[32,4,128]{2,1,0:T(4,128)S(1)}, u32[]{:S(2)}, u32[]{:S(2)}) async-start(f32[32,4,128]{2,1,0:T(4,128)} %bitcast.74), calls=%async_computation.4 | async-start | bytes 131072 | tf_op jit(solution)/shard_map/all_to_all | solution.py:694
  70.7 2.7 %collective-permute-start.15 = (f32[16,640]{1,0:T(8,128)}, f32[16,640]{1,0:T(8,128)S(1)}, u32[]{:S(2)}, u32[]{:S(2)}) collective-permute-start(f32[16,640]{1,0:T(8,128)} %get-tuple-element.173), channel_id=1, source_target_pairs={{0,4},{1,5},{2,6},{3,7},{4,0},{5,1},{6,2},{7,3},{8,12},{9,13},{10,... | collective-permute-start | bytes 122888 | tf_op jit(solution)/shard_map/ppermute | solution.py:690
  78.1 2.1 %shard_map.109 = (f32[4,16,128]{2,1,0:T(8,128)}, f32[5,16,640]{2,1,0:T(8,128)S(1)}, f32[16,128]{1,0:T(8,128)S(1)}, f32[5,16,640]{2,1,0:T(8,128)S(1)}, bf16[256,6...) custom-call(f32[128,128]{1,0:T(8,128)S(1)} %bitcast.42, ...), custom_call_target="tpu_custom_call" | custom-call | flops 2000000 | bytes 2000000 | tf_op jit(solution)/shard_map/pallas_call | solution.py:675
  80.7 2.0 %shard_map.110 = (f32[128,128]{1,0:T(8,128)}, f32[5,16,640]{2,1,0:T(8,128)}, f32[5,16,640]{2,1,0:T(8,128)}, f32[16,640]{1,0:T(8,128)}, f32[16,640]{1,0:T(8,128)}...) custom-call(s32[5]{0:T(128)S(1)} %bitcast.50, f32[16,640]{1,0:T(8,128)S(1)} %collective-permute-done.15.refs_1_, ...), custom_call_target="tpu_custom_call" | custom-call | flops 2000000 | bytes 2000000 | tf_op jit(solution)/shard_map/pallas_call | solution.py:675
  82.7 2.8 %all-to-all-start.5 = ((f32[32,4,128]{2,1,0:T(4,128)}), f32[32,4,128]{2,1,0:T(4,128)S(1)}, u32[]{:S(2)}, u32[]{:S(2)}) async-start(f32[32,4,128]{2,1,0:T(4,128)} %bitcast.70), calls=%async_computation.5 | async-start | bytes 131072 | tf_op jit(solution)/shard_map/all_to_all | solution.py:694
  85.5 2.5 %collective-permute-start.20 = (f32[16,640]{1,0:T(8,128)}, f32[16,640]{1,0:T(8,128)S(1)}, u32[]{:S(2)}, u32[]{:S(2)}) collective-permute-start(f32[16,640]{1,0:T(8,128)} %get-tuple-element.188), channel_id=1, source_target_pairs={{0,4},{1,5},{2,6},{3,7},{4,0},{5,1},{6,2},{7,3},{8,12},{9,13},{10,... | collective-permute-start | bytes 122888 | tf_op jit(solution)/shard_map/ppermute | solution.py:690
  92.7 3.4 %shard_map.111 = (f32[5,16,640]{2,1,0:T(8,128)}, f32[5,16,640]{2,1,0:T(8,128)S(1)}, f32[8,128]{1,0:T(8,128)S(1)}, bf16[256,640]{1,0:T(8,128)(2,1)S(1)}, bf16[256...) custom-call(f32[128,128]{1,0:T(8,128)S(1)} %bitcast.40, ...), custom_call_target="tpu_custom_call" | custom-call | flops 2000000 | bytes 2000000 | tf_op jit(solution)/shard_map/pallas_call | solution.py:675
  96.1 3.5 %shard_map.112 = (f32[128,128]{1,0:T(8,128)}, f32[5,16,640]{2,1,0:T(8,128)}, f32[5,16,640]{2,1,0:T(8,128)}, f32[16,640]{1,0:T(8,128)}, f32[16,640]{1,0:T(8,128)}...) custom-call(s32[5]{0:T(128)S(1)} %bitcast.51, f32[16,640]{1,0:T(8,128)S(1)} %collective-permute-done.20.refs_1_, ...), custom_call_target="tpu_custom_call" | custom-call | flops 2000000 | bytes 2000000 | tf_op jit(solution)/shard_map/pallas_call | solution.py:675
  99.6 2.6 %all-to-all-start.6 = ((f32[32,4,128]{2,1,0:T(4,128)}), f32[32,4,128]{2,1,0:T(4,128)S(1)}, u32[]{:S(2)}, u32[]{:S(2)}) async-start(f32[32,4,128]{2,1,0:T(4,128)} %bitcast.73), calls=%async_computation.6 | async-start | bytes 131072 | tf_op jit(solution)/shard_map/all_to_all | solution.py:694
  102.2 2.7 %collective-permute-start.25 = (f32[16,640]{1,0:T(8,128)}, f32[16,640]{1,0:T(8,128)S(1)}, u32[]{:S(2)}, u32[]{:S(2)}) collective-permute-start(f32[16,640]{1,0:T(8,128)} %get-tuple-element.205), channel_id=1, source_target_pairs={{0,4},{1,5},{2,6},{3,7},{4,0},{5,1},{6,2},{7,3},{8,12},{9,13},{10,... | collective-permute-start | bytes 122888 | tf_op jit(solution)/shard_map/ppermute | solution.py:690
  109.6 2.2 %shard_map.113 = (f32[4,16,128]{2,1,0:T(8,128)}, f32[5,16,640]{2,1,0:T(8,128)S(1)}, f32[16,128]{1,0:T(8,128)S(1)}, f32[5,16,640]{2,1,0:T(8,128)S(1)}, bf16[256,6...) custom-call(f32[128,128]{1,0:T(8,128)S(1)} %bitcast.41, ...), custom_call_target="tpu_custom_call" | custom-call | flops 2000000 | bytes 2000000 | tf_op jit(solution)/shard_map/pallas_call | solution.py:675
  112.2 1.9 %shard_map.114 = (f32[128,128]{1,0:T(8,128)}, f32[5,16,640]{2,1,0:T(8,128)}, f32[16,640]{1,0:T(8,128)}, f32[16,640]{1,0:T(8,128)}, f32[16,640]{1,0:T(8,128)}, /*index=5*/f32[16,640]{1,0:T(8,128)}, f32[16,640]{1,0:T(8,128)}) custom-call(s32[5]{0:T(128)S(1)} %bitcast.52, f32[16,640]{1,0:T(8,128)S(1)} %collective-permute-done.25.refs_1_, ...), custom_call_target="tpu_custom_call" | custom-call | flops 2000000 | bytes 2000000 | tf_op jit(solution)/shard_map/pallas_call | solution.py:675
  114.1 2.6 %all-to-all-start.7 = ((f32[32,4,128]{2,1,0:T(4,128)}), f32[32,4,128]{2,1,0:T(4,128)S(1)}, u32[]{:S(2)}, u32[]{:S(2)}) async-start(f32[32,4,128]{2,1,0:T(4,128)} %bitcast.69), calls=%async_computation.7 | async-start | bytes 131072 | tf_op jit(solution)/shard_map/all_to_all | solution.py:694
  116.7 2.7 %collective-permute-start.30 = (f32[16,640]{1,0:T(8,128)}, f32[16,640]{1,0:T(8,128)S(1)}, u32[]{:S(2)}, u32[]{:S(2)}) collective-permute-start(f32[16,640]{1,0:T(8,128)} %get-tuple-element.222), channel_id=1, source_target_pairs={{0,4},{1,5},{2,6},{3,7},{4,0},{5,1},{6,2},{7,3},{8,12},{9,13},{10,... | collective-permute-start | bytes 122888 | tf_op jit(solution)/shard_map/ppermute | solution.py:690
  124.1 3.7 %shard_map.115 = (f32[5,16,640]{2,1,0:T(8,128)S(1)}, f32[5,16,640]{2,1,0:T(8,128)S(1)}, f32[5,16,640]{2,1,0:T(8,128)S(1)}, f32[5,16,640]{2,1,0:T(8,128)S(1)}, f3...) custom-call(f32[128,128]{1,0:T(8,128)S(1)} %bitcast.37, ...), custom_call_target="tpu_custom_call" | custom-call | flops 2000000 | bytes 2000000 | tf_op jit(solution)/shard_map/pallas_call | solution.py:675
  127.9 3.0 %shard_map.116 = f32[32,128]{1,0:T(8,128)} custom-call(s32[5]{0:T(128)S(1)} %bitcast.53, f32[16,640]{1,0:T(8,128)S(1)} %collective-permute-done.30.refs_1_, f32[16,640]{1,0:T(8,128)S(1)} %collective-permute-done.31.refs_2_, f32[16,640]{1,0:T(8,128)S(1)} %collective-permute-done.32.refs_3_, f32[16,640]{1,0:T(8,128)S(1)} %collective-permute-done.33.refs_4_, ...), custom_call_target="tpu_custom_call" | custom-call | flops 2000000 | bytes 2000000 | tf_op jit(solution)/shard_map/pallas_call | solution.py:675
  130.9 9.6 %all_to_all.99 = f32[32,1,128]{2,1,0:T(1,128)S(1)} all-to-all(f32[32,1,128]{2,1,0:T(1,128)} %bitcast.78), channel_id=1, replica_groups=mesh['organ'=4,'sub'=8] {'organ','sub'}, dimensions={0} | all-to-all | bytes 32768 | tf_op jit(solution)/shard_map/all_to_all | solution.py:694
  (75 shorter events, 38.9 us)
Async XLA Ops:
  2.6 14.4 %all-to-all-start = ((f32[32,1,128]{2,1,0:T(1,128)}), f32[32,1,128]{2,1,0:T(1,128)S(1)}, u32[]{:S(2)}, u32[]{:S(2)}) async-start(f32[32,1,128]{2,1,0:T(1,128)} %bitcast.79), calls=%async_computation | async-start | bytes 32768 | tf_op jit(solution)/shard_map/all_to_all | solution.py:694
  19.9 10.0 %all-to-all-start.1 = ((f32[32,4,128]{2,1,0:T(4,128)}), f32[32,4,128]{2,1,0:T(4,128)S(1)}, u32[]{:S(2)}, u32[]{:S(2)}) async-start(f32[32,4,128]{2,1,0:T(4,128)} %bitcast.72), calls=%async_computation.1 | async-start | bytes 131072 | tf_op jit(solution)/shard_map/all_to_all | solution.py:694
  22.5 10.6 %collective-permute-start = (f32[24,640]{1,0:T(8,128)}, f32[24,640]{1,0:T(8,128)S(1)}, u32[]{:S(2)}, u32[]{:S(2)}) collective-permute-start(f32[24,640]{1,0:T(8,128)} %get-tuple-element.127), channel_id=1, source_target_pairs={{0,4},{1,5},{2,6},{3,7},{4,0},{5,1},{6,2},{7,3},{8,12},{9,13},{10,... | collective-permute-start | bytes 184328 | tf_op jit(solution)/shard_map/ppermute | solution.py:690
  25.2 7.9 %collective-permute-start.1 = (f32[24,640]{1,0:T(8,128)}, f32[24,640]{1,0:T(8,128)S(1)}, u32[]{:S(2)}, u32[]{:S(2)}) collective-permute-start(f32[24,640]{1,0:T(8,128)} %get-tuple-element.128), channel_id=1, source_target_pairs={{0,1},{1,0},{2,3},{3,2},{4,5},{5,4},{6,7},{7,6},{8,9},{9,8},{10,11... | collective-permute-start | bytes 184328 | tf_op jit(solution)/shard_map/ppermute | solution.py:690
  26.7 6.4 %collective-permute-start.2 = (f32[24,640]{1,0:T(8,128)}, f32[24,640]{1,0:T(8,128)S(1)}, u32[]{:S(2)}, u32[]{:S(2)}) collective-permute-start(f32[24,640]{1,0:T(8,128)} %get-tuple-element.129), channel_id=1, source_target_pairs={{0,2},{1,3},{2,0},{3,1},{4,6},{5,7},{6,4},{7,5},{8,10},{9,11},{10,... | collective-permute-start | bytes 184328 | tf_op jit(solution)/shard_map/ppermute | solution.py:690
  28.2 4.9 %collective-permute-start.3 = (f32[24,640]{1,0:T(8,128)}, f32[24,640]{1,0:T(8,128)S(1)}, u32[]{:S(2)}, u32[]{:S(2)}) collective-permute-start(f32[24,640]{1,0:T(8,128)} %get-tuple-element.130), channel_id=1, source_target_pairs={{0,16},{8,24},{16,0},{24,8},{1,17},{9,25},{17,1},{25,9},{2,18},{10... | collective-permute-start | bytes 184328 | tf_op jit(solution)/shard_map/ppermute | solution.py:690
  36.8 9.8 %all-to-all-start.2 = ((f32[32,2,128]{2,1,0:T(2,128)}), f32[32,2,128]{2,1,0:T(2,128)S(1)}, u32[]{:S(2)}, u32[]{:S(2)}) async-start(f32[32,2,128]{2,1,0:T(2,128)} %bitcast.77), calls=%async_computation.2 | async-start | bytes 65536 | tf_op jit(solution)/shard_map/all_to_all | solution.py:694
  39.4 9.1 %collective-permute-start.5 = (f32[16,640]{1,0:T(8,128)}, f32[16,640]{1,0:T(8,128)S(1)}, u32[]{:S(2)}, u32[]{:S(2)}) collective-permute-start(f32[16,640]{1,0:T(8,128)} %get-tuple-element.144), channel_id=1, source_target_pairs={{0,4},{1,5},{2,6},{3,7},{4,0},{5,1},{6,2},{7,3},{8,12},{9,13},{10,... | collective-permute-start | bytes 122888 | tf_op jit(solution)/shard_map/ppermute | solution.py:690
  42.1 6.4 %collective-permute-start.6 = (f32[16,640]{1,0:T(8,128)}, f32[16,640]{1,0:T(8,128)S(1)}, u32[]{:S(2)}, u32[]{:S(2)}) collective-permute-start(f32[16,640]{1,0:T(8,128)} %get-tuple-element.145), channel_id=1, source_target_pairs={{0,1},{1,0},{2,3},{3,2},{4,5},{5,4},{6,7},{7,6},{8,9},{9,8},{10,11... | collective-permute-start | bytes 122888 | tf_op jit(solution)/shard_map/ppermute | solution.py:690
  51.2 10.0 %all-to-all-start.3 = ((f32[32,4,128]{2,1,0:T(4,128)}), f32[32,4,128]{2,1,0:T(4,128)S(1)}, u32[]{:S(2)}, u32[]{:S(2)}) async-start(f32[32,4,128]{2,1,0:T(4,128)} %bitcast.71), calls=%async_computation.3 | async-start | bytes 131072 | tf_op jit(solution)/shard_map/all_to_all | solution.py:694
  53.8 10.7 %collective-permute-start.10 = (f32[16,640]{1,0:T(8,128)}, f32[16,640]{1,0:T(8,128)S(1)}, u32[]{:S(2)}, u32[]{:S(2)}) collective-permute-start(f32[16,640]{1,0:T(8,128)} %get-tuple-element.157), channel_id=1, source_target_pairs={{0,4},{1,5},{2,6},{3,7},{4,0},{5,1},{6,2},{7,3},{8,12},{9,13},{10,... | collective-permute-start | bytes 122888 | tf_op jit(solution)/shard_map/ppermute | solution.py:690
  56.5 8.0 %collective-permute-start.11 = (f32[16,640]{1,0:T(8,128)}, f32[16,640]{1,0:T(8,128)S(1)}, u32[]{:S(2)}, u32[]{:S(2)}) collective-permute-start(f32[16,640]{1,0:T(8,128)} %get-tuple-element.158), channel_id=1, source_target_pairs={{0,1},{1,0},{2,3},{3,2},{4,5},{5,4},{6,7},{7,6},{8,9},{9,8},{10,11... | collective-permute-start | bytes 122888 | tf_op jit(solution)/shard_map/ppermute | solution.py:690
  58.0 6.5 %collective-permute-start.12 = (f32[16,640]{1,0:T(8,128)}, f32[16,640]{1,0:T(8,128)S(1)}, u32[]{:S(2)}, u32[]{:S(2)}) collective-permute-start(f32[16,640]{1,0:T(8,128)} %get-tuple-element.159), channel_id=1, source_target_pairs={{0,2},{1,3},{2,0},{3,1},{4,6},{5,7},{6,4},{7,5},{8,10},{9,11},{10,... | collective-permute-start | bytes 122888 | tf_op jit(solution)/shard_map/ppermute | solution.py:690
  59.6 5.0 %collective-permute-start.13 = (f32[16,640]{1,0:T(8,128)}, f32[16,640]{1,0:T(8,128)S(1)}, u32[]{:S(2)}, u32[]{:S(2)}) collective-permute-start(f32[16,640]{1,0:T(8,128)} %get-tuple-element.160), channel_id=1, source_target_pairs={{0,16},{8,24},{16,0},{24,8},{1,17},{9,25},{17,1},{25,9},{2,18},{10... | collective-permute-start | bytes 122888 | tf_op jit(solution)/shard_map/ppermute | solution.py:690
  68.2 9.9 %all-to-all-start.4 = ((f32[32,4,128]{2,1,0:T(4,128)}), f32[32,4,128]{2,1,0:T(4,128)S(1)}, u32[]{:S(2)}, u32[]{:S(2)}) async-start(f32[32,4,128]{2,1,0:T(4,128)} %bitcast.74), calls=%async_computation.4 | async-start | bytes 131072 | tf_op jit(solution)/shard_map/all_to_all | solution.py:694
  70.7 9.5 %collective-permute-start.15 = (f32[16,640]{1,0:T(8,128)}, f32[16,640]{1,0:T(8,128)S(1)}, u32[]{:S(2)}, u32[]{:S(2)}) collective-permute-start(f32[16,640]{1,0:T(8,128)} %get-tuple-element.173), channel_id=1, source_target_pairs={{0,4},{1,5},{2,6},{3,7},{4,0},{5,1},{6,2},{7,3},{8,12},{9,13},{10,... | collective-permute-start | bytes 122888 | tf_op jit(solution)/shard_map/ppermute | solution.py:690
  73.4 6.8 %collective-permute-start.16 = (f32[16,640]{1,0:T(8,128)}, f32[16,640]{1,0:T(8,128)S(1)}, u32[]{:S(2)}, u32[]{:S(2)}) collective-permute-start(f32[16,640]{1,0:T(8,128)} %get-tuple-element.174), channel_id=1, source_target_pairs={{0,1},{1,0},{2,3},{3,2},{4,5},{5,4},{6,7},{7,6},{8,9},{9,8},{10,11... | collective-permute-start | bytes 122888 | tf_op jit(solution)/shard_map/ppermute | solution.py:690
  74.9 5.3 %collective-permute-start.17 = (f32[16,640]{1,0:T(8,128)}, f32[16,640]{1,0:T(8,128)S(1)}, u32[]{:S(2)}, u32[]{:S(2)}) collective-permute-start(f32[16,640]{1,0:T(8,128)} %get-tuple-element.175), channel_id=1, source_target_pairs={{0,2},{1,3},{2,0},{3,1},{4,6},{5,7},{6,4},{7,5},{8,10},{9,11},{10,... | collective-permute-start | bytes 122888 | tf_op jit(solution)/shard_map/ppermute | solution.py:690
  82.7 10.0 %all-to-all-start.5 = ((f32[32,4,128]{2,1,0:T(4,128)}), f32[32,4,128]{2,1,0:T(4,128)S(1)}, u32[]{:S(2)}, u32[]{:S(2)}) async-start(f32[32,4,128]{2,1,0:T(4,128)} %bitcast.70), calls=%async_computation.5 | async-start | bytes 131072 | tf_op jit(solution)/shard_map/all_to_all | solution.py:694
  85.5 10.6 %collective-permute-start.20 = (f32[16,640]{1,0:T(8,128)}, f32[16,640]{1,0:T(8,128)S(1)}, u32[]{:S(2)}, u32[]{:S(2)}) collective-permute-start(f32[16,640]{1,0:T(8,128)} %get-tuple-element.188), channel_id=1, source_target_pairs={{0,4},{1,5},{2,6},{3,7},{4,0},{5,1},{6,2},{7,3},{8,12},{9,13},{10,... | collective-permute-start | bytes 122888 | tf_op jit(solution)/shard_map/ppermute | solution.py:690
  88.0 8.1 %collective-permute-start.21 = (f32[16,640]{1,0:T(8,128)}, f32[16,640]{1,0:T(8,128)S(1)}, u32[]{:S(2)}, u32[]{:S(2)}) collective-permute-start(f32[16,640]{1,0:T(8,128)} %get-tuple-element.189), channel_id=1, source_target_pairs={{0,1},{1,0},{2,3},{3,2},{4,5},{5,4},{6,7},{7,6},{8,9},{9,8},{10,11... | collective-permute-start | bytes 122888 | tf_op jit(solution)/shard_map/ppermute | solution.py:690
  89.5 6.6 %collective-permute-start.22 = (f32[16,640]{1,0:T(8,128)}, f32[16,640]{1,0:T(8,128)S(1)}, u32[]{:S(2)}, u32[]{:S(2)}) collective-permute-start(f32[16,640]{1,0:T(8,128)} %get-tuple-element.190), channel_id=1, source_target_pairs={{0,2},{1,3},{2,0},{3,1},{4,6},{5,7},{6,4},{7,5},{8,10},{9,11},{10,... | collective-permute-start | bytes 122888 | tf_op jit(solution)/shard_map/ppermute | solution.py:690
  91.1 5.0 %collective-permute-start.23 = (f32[16,640]{1,0:T(8,128)}, f32[16,640]{1,0:T(8,128)S(1)}, u32[]{:S(2)}, u32[]{:S(2)}) collective-permute-start(f32[16,640]{1,0:T(8,128)} %get-tuple-element.191), channel_id=1, source_target_pairs={{0,16},{8,24},{16,0},{24,8},{1,17},{9,25},{17,1},{25,9},{2,18},{10... | collective-permute-start | bytes 122888 | tf_op jit(solution)/shard_map/ppermute | solution.py:690
  99.6 10.0 %all-to-all-start.6 = ((f32[32,4,128]{2,1,0:T(4,128)}), f32[32,4,128]{2,1,0:T(4,128)S(1)}, u32[]{:S(2)}, u32[]{:S(2)}) async-start(f32[32,4,128]{2,1,0:T(4,128)} %bitcast.73), calls=%async_computation.6 | async-start | bytes 131072 | tf_op jit(solution)/shard_map/all_to_all | solution.py:694
  102.2 9.6 %collective-permute-start.25 = (f32[16,640]{1,0:T(8,128)}, f32[16,640]{1,0:T(8,128)S(1)}, u32[]{:S(2)}, u32[]{:S(2)}) collective-permute-start(f32[16,640]{1,0:T(8,128)} %get-tuple-element.205), channel_id=1, source_target_pairs={{0,4},{1,5},{2,6},{3,7},{4,0},{5,1},{6,2},{7,3},{8,12},{9,13},{10,... | collective-permute-start | bytes 122888 | tf_op jit(solution)/shard_map/ppermute | solution.py:690
  105.0 6.9 %collective-permute-start.26 = (f32[16,640]{1,0:T(8,128)}, f32[16,640]{1,0:T(8,128)S(1)}, u32[]{:S(2)}, u32[]{:S(2)}) collective-permute-start(f32[16,640]{1,0:T(8,128)} %get-tuple-element.206), channel_id=1, source_target_pairs={{0,1},{1,0},{2,3},{3,2},{4,5},{5,4},{6,7},{7,6},{8,9},{9,8},{10,11... | collective-permute-start | bytes 122888 | tf_op jit(solution)/shard_map/ppermute | solution.py:690
  106.5 5.4 %collective-permute-start.27 = (f32[16,640]{1,0:T(8,128)}, f32[16,640]{1,0:T(8,128)S(1)}, u32[]{:S(2)}, u32[]{:S(2)}) collective-permute-start(f32[16,640]{1,0:T(8,128)} %get-tuple-element.207), channel_id=1, source_target_pairs={{0,2},{1,3},{2,0},{3,1},{4,6},{5,7},{6,4},{7,5},{8,10},{9,11},{10,... | collective-permute-start | bytes 122888 | tf_op jit(solution)/shard_map/ppermute | solution.py:690
  114.1 10.0 %all-to-all-start.7 = ((f32[32,4,128]{2,1,0:T(4,128)}), f32[32,4,128]{2,1,0:T(4,128)S(1)}, u32[]{:S(2)}, u32[]{:S(2)}) async-start(f32[32,4,128]{2,1,0:T(4,128)} %bitcast.69), calls=%async_computation.7 | async-start | bytes 131072 | tf_op jit(solution)/shard_map/all_to_all | solution.py:694
  116.7 11.1 %collective-permute-start.30 = (f32[16,640]{1,0:T(8,128)}, f32[16,640]{1,0:T(8,128)S(1)}, u32[]{:S(2)}, u32[]{:S(2)}) collective-permute-start(f32[16,640]{1,0:T(8,128)} %get-tuple-element.222), channel_id=1, source_target_pairs={{0,4},{1,5},{2,6},{3,7},{4,0},{5,1},{6,2},{7,3},{8,12},{9,13},{10,... | collective-permute-start | bytes 122888 | tf_op jit(solution)/shard_map/ppermute | solution.py:690
  119.4 8.4 %collective-permute-start.31 = (f32[16,640]{1,0:T(8,128)}, f32[16,640]{1,0:T(8,128)S(1)}, u32[]{:S(2)}, u32[]{:S(2)}) collective-permute-start(f32[16,640]{1,0:T(8,128)} %get-tuple-element.223), channel_id=1, source_target_pairs={{0,1},{1,0},{2,3},{3,2},{4,5},{5,4},{6,7},{7,6},{8,9},{9,8},{10,11... | collective-permute-start | bytes 122888 | tf_op jit(solution)/shard_map/ppermute | solution.py:690
  120.9 6.9 %collective-permute-start.32 = (f32[16,640]{1,0:T(8,128)}, f32[16,640]{1,0:T(8,128)S(1)}, u32[]{:S(2)}, u32[]{:S(2)}) collective-permute-start(f32[16,640]{1,0:T(8,128)} %get-tuple-element.224), channel_id=1, source_target_pairs={{0,2},{1,3},{2,0},{3,1},{4,6},{5,7},{6,4},{7,5},{8,10},{9,11},{10,... | collective-permute-start | bytes 122888 | tf_op jit(solution)/shard_map/ppermute | solution.py:690
  122.5 5.4 %collective-permute-start.33 = (f32[16,640]{1,0:T(8,128)}, f32[16,640]{1,0:T(8,128)S(1)}, u32[]{:S(2)}, u32[]{:S(2)}) collective-permute-start(f32[16,640]{1,0:T(8,128)} %get-tuple-element.225), channel_id=1, source_target_pairs={{0,16},{8,24},{16,0},{24,8},{1,17},{9,25},{17,1},{25,9},{2,18},{10... | collective-permute-start | bytes 122888 | tf_op jit(solution)/shard_map/ppermute | solution.py:690
  (12 other events, 43.5 us)

commit v6 on v5

--- a/solution.py
+++ b/solution.py
@@ -208,7 +208,8 @@
 
 
 def slots_kernel(
-    devices, count, owner, active, mortar, start_rows, right_rows, a_high, a_low, start, right
+    devices, count, owner, active, mortar, start_rows, right_rows, basis, a_high, a_low, start,
+    right, products,
 ):
     owner, active = owner(), active()
     rows = owner.shape[1]
@@ -225,10 +226,16 @@
     for part, target in zip(halves(mortar()[...]), (a_high, a_low), strict=True):
         target.ref[...] = bdot(pick, part).astype(BF16)
         target.flush()
+    basis = basis()
+    modes, length = basis.shape[0] // blocks, basis.shape[2]
+    first = [basis[m * blocks] for m in range(modes)]
+    extra = jnp.zeros((2 * 16 - directions - modes, length), F32)
+    both = jnp.concatenate([start.ref[0]] + first + [extra], axis=0)
+    products.ref[...] = times(both, a_high.ref[...], a_low.ref[...], turned_dot)
 
 
 def first_kernel(
-    organs, arrived, matches, basis, start, a_high, a_low, right, message, unit, modes_out, *sends
+    organs, arrived, matches, basis, start, products, right, message, unit, modes_out, *sends
 ):
     devices = arrived.shape[0]
     subs = devices // organs
@@ -280,12 +287,18 @@
     first = [modes_ref[m, 0:1, :] for m in range(modes)]
     extra = jnp.zeros((2 * 16 - directions - modes, length), F32)
     both = jnp.concatenate([start[0]] + first + [extra], axis=0)
-    master = times(both, a_high()[...], a_low()[...], turned_dot)
+    products = products()
+    turned_modes = [
+        sum(inverse[i, j] * products[directions + j : directions + j + 1, :] for j in range(i + 1))
+        for i in range(modes)
+    ]
+    none = jnp.zeros((8 - modes, products.shape[1]), F32)
+    turned_modes = jnp.concatenate(turned_modes + [none], axis=0)
     slave = exact(both, unit.ref[...], turned_dot)
-    for line, value in enumerate(pack(master[:directions], slave[:directions], devices)):
+    for line, value in enumerate(pack(products[0:directions, :], slave[:directions], devices)):
         put(message.ref, 4, line, value)
     rows = slice(directions, directions + 8)
-    lines = pack(master[rows], slave[rows], devices)
+    lines = pack(turned_modes, slave[rows], devices)
     half = LANES // 2
     put(message.ref, 4, 2, jnp.concatenate([line[:, :half] for line in lines], axis=1))
     spread_rows(message.ref, 4, 3, coefficients_row(right(), modes_ref))
@@ -744,11 +757,11 @@
         smem=1,
     )
     arrived = exchange(setup)
-    a_high, a_low, start, right = call(
+    a_high, a_low, start, right, products = call(
         functools.partial(slots_kernel, devices),
-        [((width, length), BF16)] * 2 + [whole] * 2,
+        [((width, length), BF16)] * 2 + [whole] * 2 + [((32, width), F32)],
         (count,),
-        (owner, active, mortar, start_rows, right_rows),
+        (owner, active, mortar, start_rows, right_rows, basis),
         smem=1,
     )
     sent, unit, modes_ref, *faces = call(
@@ -760,7 +773,7 @@
         ]
         + [((directions + 8, length), F32)] * blocks,
         (arrived,),
-        (matches, basis, start, a_high, a_low, right),
+        (matches, basis, start, products, right),
         held=1,
     )
     maps = (a_high, a_low, unit)

time: 142 us -> 142 us (level)
  no operation moved by 1% of the time
where the time goes in v6:
time: 142 us; the launch traced here: 141 us
  starting transfers between devices  75.9 us (53%)
  Pallas kernels  47.8 us (34%)
  blocking collectives  9.6 us (7%)
  waiting for transfers between devices  6.93 us (5%)
    ppermute x35, starting transfers between devices, from_partner(): return lax.ppermute(value, axis, pairs)  50.4 us
    pallas_call x18, Pallas kernels, call(): pl.pallas_call(body, out_shape=[pltpu.HBM(shape, kind) for shape, kind in...  47.8 us
    all_to_all x8, starting transfers between devices, exchange(): lax.all_to_all(message, AXES, split_axis=0, concat_axis=0, tiled=True)  25.4 us
    all_to_all x1, blocking collectives, exchange(): lax.all_to_all(message, AXES, split_axis=0, concat_axis=0, tiled=True)  9.6 us
    all_to_all x8, waiting for transfers between devices, exchange(): lax.all_to_all(message, AXES, split_axis=0, concat_axis=0, tiled=True)  5.28 us
  transfers between devices with their start and end apart: 43, of which 10 were waited for; matrix products, arithmetic and copies ran while one was open for 0% of the time, Pallas kernels for 16%

profile of v6, /device:TPU:0, one launch (start us, length us, event | category | flops | bytes accessed | tf_op | source)
XLA Modules:
  0.0 141.4 jit_solution(12980400198821740371)
XLA Ops:
  0.7 1.9 %shard_map.100 = f32[32,128]{1,0:T(8,128)} custom-call(s32[1]{0:T(128)} %bitcast.35.refs_0_, s32[1,128]{1,0:T(1,128)} %bitcast.81, s32[1,128]{1,0:T(1,128)} %bitcast.85, s32[1,128]{1,0:T(1,128)} %bitcast.83, f32[30,1,640]{2,1,0:T(1,128)} %bitcast.66), custom_call_target="tpu_custom_call" | custom-call | flops 2000000 | bytes 2000000 | tf_op jit(solution)/shard_map/pallas_call | solution.py:688
  2.6 7.3 %all-to-all-start = ((f32[32,1,128]{2,1,0:T(1,128)}), f32[32,1,128]{2,1,0:T(1,128)S(1)}, u32[]{:S(2)}, u32[]{:S(2)}) async-start(f32[32,1,128]{2,1,0:T(1,128)} %bitcast.80), calls=%async_computation | async-start | bytes 32768 | tf_op jit(solution)/shard_map/all_to_all | solution.py:707
  9.9 2.8 %shard_map.101 = (bf16[256,640]{1,0:T(8,128)(2,1)}, bf16[256,640]{1,0:T(8,128)(2,1)}, f32[5,16,640]{2,1,0:T(8,128)}, f32[5,16,640]{2,1,0:T(8,128)}, f32[32,256]{1,0:T(8,128)}) custom-call(s32[1]{0:T(128)} %bitcast.36.refs_0_, s32[1,128]{1,0:T(1,128)} %bitcast.82, s32[1,128]{1,0:T(1,128)} %bitcast.84, f32[128,640]{1,0:T(8,128)} %bitcast.69, ...), custom_call_target="tpu_custom_call" | custom-call | flops 2000000 | bytes 2000000 | tf_op jit(solution)/shard_map/pallas_call | solution.py:688
  12.7 4.3 %all-to-all-done = f32[32,1,128]{2,1,0:T(1,128)S(1)} async-done(((f32[32,1,128]{2,1,0:T(1,128)}), f32[32,1,128]{2,1,0:T(1,128)S(1)}, u32[]{:S(2)}, u32[]{:S(2)}) %all-to-all-start) | async-done | bytes 16416 | tf_op jit(solution)/shard_map/all_to_all | solution.py:707
  17.0 2.7 %shard_map.102 = (f32[128,128]{1,0:T(8,128)}, bf16[256,640]{1,0:T(8,128)(2,1)}, f32[6,5,640]{2,1,0:T(8,128)}, f32[24,640]{1,0:T(8,128)}, f32[24,640]{1,0:T(8,128...) custom-call(f32[32,128]{1,0:T(8,128)S(1)} %bitcast.44, s32[5]{0:T(128)} %bitcast.46, ...), custom_call_target="tpu_custom_call" | custom-call | flops 2000000 | bytes 2000000 | tf_op jit(solution)/shard_map/pallas_call | solution.py:688
  19.7 2.6 %all-to-all-start.1 = ((f32[32,4,128]{2,1,0:T(4,128)}), f32[32,4,128]{2,1,0:T(4,128)S(1)}, u32[]{:S(2)}, u32[]{:S(2)}) async-start(f32[32,4,128]{2,1,0:T(4,128)} %bitcast.73), calls=%async_computation.1 | async-start | bytes 131072 | tf_op jit(solution)/shard_map/all_to_all | solution.py:707
  22.3 2.7 %collective-permute-start = (f32[24,640]{1,0:T(8,128)}, f32[24,640]{1,0:T(8,128)S(1)}, u32[]{:S(2)}, u32[]{:S(2)}) collective-permute-start(f32[24,640]{1,0:T(8,128)} %get-tuple-element.127), channel_id=1, source_target_pairs={{0,4},{1,5},{2,6},{3,7},{4,0},{5,1},{6,2},{7,3},{8,12},{9,13},{10,... | collective-permute-start | bytes 184328 | tf_op jit(solution)/shard_map/ppermute | solution.py:703
  29.7 3.2 %shard_map.103 = (f32[5,16,640]{2,1,0:T(8,128)}, f32[5,16,640]{2,1,0:T(8,128)S(1)}, f32[32,640]{1,0:T(8,128)S(1)}, bf16[256,640]{1,0:T(8,128)(2,1)S(1)}, bf16[25...) custom-call(f32[128,128]{1,0:T(8,128)S(1)} %bitcast.38, ...), custom_call_target="tpu_custom_call" | custom-call | flops 2000000 | bytes 2000000 | tf_op jit(solution)/shard_map/pallas_call | solution.py:688
  33.0 3.7 %shard_map.104 = (f32[64,128]{1,0:T(8,128)}, f32[5,16,640]{2,1,0:T(8,128)}, f32[5,32,640]{2,1,0:T(8,128)}, f32[16,640]{1,0:T(8,128)}, f32[16,640]{1,0:T(8,128)},...) custom-call(s32[5]{0:T(128)S(1)} %bitcast.47, f32[24,640]{1,0:T(8,128)S(1)} %collective-permute-done.refs_1_, ...), custom_call_target="tpu_custom_call" | custom-call | flops 2000000 | bytes 2000000 | tf_op jit(solution)/shard_map/pallas_call | solution.py:688
  36.6 2.5 %all-to-all-start.2 = ((f32[32,2,128]{2,1,0:T(2,128)}), f32[32,2,128]{2,1,0:T(2,128)S(1)}, u32[]{:S(2)}, u32[]{:S(2)}) async-start(f32[32,2,128]{2,1,0:T(2,128)} %bitcast.78), calls=%async_computation.2 | async-start | bytes 65536 | tf_op jit(solution)/shard_map/all_to_all | solution.py:707
  39.2 2.7 %collective-permute-start.5 = (f32[16,640]{1,0:T(8,128)}, f32[16,640]{1,0:T(8,128)S(1)}, u32[]{:S(2)}, u32[]{:S(2)}) collective-permute-start(f32[16,640]{1,0:T(8,128)} %get-tuple-element.146), channel_id=1, source_target_pairs={{0,4},{1,5},{2,6},{3,7},{4,0},{5,1},{6,2},{7,3},{8,12},{9,13},{10,... | collective-permute-start | bytes 122888 | tf_op jit(solution)/shard_map/ppermute | solution.py:703
  51.0 2.6 %all-to-all-start.3 = ((f32[32,4,128]{2,1,0:T(4,128)}), f32[32,4,128]{2,1,0:T(4,128)S(1)}, u32[]{:S(2)}, u32[]{:S(2)}) async-start(f32[32,4,128]{2,1,0:T(4,128)} %bitcast.72), calls=%async_computation.3 | async-start | bytes 131072 | tf_op jit(solution)/shard_map/all_to_all | solution.py:707
  53.6 2.7 %collective-permute-start.10 = (f32[16,640]{1,0:T(8,128)}, f32[16,640]{1,0:T(8,128)S(1)}, u32[]{:S(2)}, u32[]{:S(2)}) collective-permute-start(f32[16,640]{1,0:T(8,128)} %get-tuple-element.159), channel_id=1, source_target_pairs={{0,4},{1,5},{2,6},{3,7},{4,0},{5,1},{6,2},{7,3},{8,12},{9,13},{10,... | collective-permute-start | bytes 122888 | tf_op jit(solution)/shard_map/ppermute | solution.py:703
  61.0 3.3 %shard_map.107 = (f32[5,16,640]{2,1,0:T(8,128)}, f32[5,16,640]{2,1,0:T(8,128)S(1)}, f32[8,128]{1,0:T(8,128)S(1)}, bf16[256,640]{1,0:T(8,128)(2,1)S(1)}, bf16[256...) custom-call(f32[128,128]{1,0:T(8,128)S(1)} %bitcast.39, ...), custom_call_target="tpu_custom_call" | custom-call | flops 2000000 | bytes 2000000 | tf_op jit(solution)/shard_map/pallas_call | solution.py:688
  64.4 3.6 %shard_map.108 = (f32[128,128]{1,0:T(8,128)}, f32[5,16,640]{2,1,0:T(8,128)}, f32[5,16,640]{2,1,0:T(8,128)}, f32[16,640]{1,0:T(8,128)}, f32[16,640]{1,0:T(8,128)}...) custom-call(s32[5]{0:T(128)S(1)} %bitcast.49, f32[16,640]{1,0:T(8,128)S(1)} %collective-permute-done.10.refs_1_, ...), custom_call_target="tpu_custom_call" | custom-call | flops 2000000 | bytes 2000000 | tf_op jit(solution)/shard_map/pallas_call | solution.py:688
  68.0 2.5 %all-to-all-start.4 = ((f32[32,4,128]{2,1,0:T(4,128)}), f32[32,4,128]{2,1,0:T(4,128)S(1)}, u32[]{:S(2)}, u32[]{:S(2)}) async-start(f32[32,4,128]{2,1,0:T(4,128)} %bitcast.75), calls=%async_computation.4 | async-start | bytes 131072 | tf_op jit(solution)/shard_map/all_to_all | solution.py:707
  70.5 2.7 %collective-permute-start.15 = (f32[16,640]{1,0:T(8,128)}, f32[16,640]{1,0:T(8,128)S(1)}, u32[]{:S(2)}, u32[]{:S(2)}) collective-permute-start(f32[16,640]{1,0:T(8,128)} %get-tuple-element.175), channel_id=1, source_target_pairs={{0,4},{1,5},{2,6},{3,7},{4,0},{5,1},{6,2},{7,3},{8,12},{9,13},{10,... | collective-permute-start | bytes 122888 | tf_op jit(solution)/shard_map/ppermute | solution.py:703
  77.9 2.1 %shard_map.109 = (f32[4,16,128]{2,1,0:T(8,128)}, f32[5,16,640]{2,1,0:T(8,128)S(1)}, f32[16,128]{1,0:T(8,128)S(1)}, f32[5,16,640]{2,1,0:T(8,128)S(1)}, bf16[256,6...) custom-call(f32[128,128]{1,0:T(8,128)S(1)} %bitcast.42, ...), custom_call_target="tpu_custom_call" | custom-call | flops 2000000 | bytes 2000000 | tf_op jit(solution)/shard_map/pallas_call | solution.py:688
  80.5 2.0 %shard_map.110 = (f32[128,128]{1,0:T(8,128)}, f32[5,16,640]{2,1,0:T(8,128)}, f32[5,16,640]{2,1,0:T(8,128)}, f32[16,640]{1,0:T(8,128)}, f32[16,640]{1,0:T(8,128)}...) custom-call(s32[5]{0:T(128)S(1)} %bitcast.50, f32[16,640]{1,0:T(8,128)S(1)} %collective-permute-done.15.refs_1_, ...), custom_call_target="tpu_custom_call" | custom-call | flops 2000000 | bytes 2000000 | tf_op jit(solution)/shard_map/pallas_call | solution.py:688
  82.5 2.8 %all-to-all-start.5 = ((f32[32,4,128]{2,1,0:T(4,128)}), f32[32,4,128]{2,1,0:T(4,128)S(1)}, u32[]{:S(2)}, u32[]{:S(2)}) async-start(f32[32,4,128]{2,1,0:T(4,128)} %bitcast.71), calls=%async_computation.5 | async-start | bytes 131072 | tf_op jit(solution)/shard_map/all_to_all | solution.py:707
  85.3 2.5 %collective-permute-start.20 = (f32[16,640]{1,0:T(8,128)}, f32[16,640]{1,0:T(8,128)S(1)}, u32[]{:S(2)}, u32[]{:S(2)}) collective-permute-start(f32[16,640]{1,0:T(8,128)} %get-tuple-element.190), channel_id=1, source_target_pairs={{0,4},{1,5},{2,6},{3,7},{4,0},{5,1},{6,2},{7,3},{8,12},{9,13},{10,... | collective-permute-start | bytes 122888 | tf_op jit(solution)/shard_map/ppermute | solution.py:703
  92.5 3.4 %shard_map.111 = (f32[5,16,640]{2,1,0:T(8,128)}, f32[5,16,640]{2,1,0:T(8,128)S(1)}, f32[8,128]{1,0:T(8,128)S(1)}, bf16[256,640]{1,0:T(8,128)(2,1)S(1)}, bf16[256...) custom-call(f32[128,128]{1,0:T(8,128)S(1)} %bitcast.40, ...), custom_call_target="tpu_custom_call" | custom-call | flops 2000000 | bytes 2000000 | tf_op jit(solution)/shard_map/pallas_call | solution.py:688
  95.9 3.5 %shard_map.112 = (f32[128,128]{1,0:T(8,128)}, f32[5,16,640]{2,1,0:T(8,128)}, f32[5,16,640]{2,1,0:T(8,128)}, f32[16,640]{1,0:T(8,128)}, f32[16,640]{1,0:T(8,128)}...) custom-call(s32[5]{0:T(128)S(1)} %bitcast.51, f32[16,640]{1,0:T(8,128)S(1)} %collective-permute-done.20.refs_1_, ...), custom_call_target="tpu_custom_call" | custom-call | flops 2000000 | bytes 2000000 | tf_op jit(solution)/shard_map/pallas_call | solution.py:688
  99.4 2.6 %all-to-all-start.6 = ((f32[32,4,128]{2,1,0:T(4,128)}), f32[32,4,128]{2,1,0:T(4,128)S(1)}, u32[]{:S(2)}, u32[]{:S(2)}) async-start(f32[32,4,128]{2,1,0:T(4,128)} %bitcast.74), calls=%async_computation.6 | async-start | bytes 131072 | tf_op jit(solution)/shard_map/all_to_all | solution.py:707
  102.0 2.7 %collective-permute-start.25 = (f32[16,640]{1,0:T(8,128)}, f32[16,640]{1,0:T(8,128)S(1)}, u32[]{:S(2)}, u32[]{:S(2)}) collective-permute-start(f32[16,640]{1,0:T(8,128)} %get-tuple-element.207), channel_id=1, source_target_pairs={{0,4},{1,5},{2,6},{3,7},{4,0},{5,1},{6,2},{7,3},{8,12},{9,13},{10,... | collective-permute-start | bytes 122888 | tf_op jit(solution)/shard_map/ppermute | solution.py:703
  109.4 2.2 %shard_map.113 = (f32[4,16,128]{2,1,0:T(8,128)}, f32[5,16,640]{2,1,0:T(8,128)S(1)}, f32[16,128]{1,0:T(8,128)S(1)}, f32[5,16,640]{2,1,0:T(8,128)S(1)}, bf16[256,6...) custom-call(f32[128,128]{1,0:T(8,128)S(1)} %bitcast.41, ...), custom_call_target="tpu_custom_call" | custom-call | flops 2000000 | bytes 2000000 | tf_op jit(solution)/shard_map/pallas_call | solution.py:688
  112.0 1.9 %shard_map.114 = (f32[128,128]{1,0:T(8,128)}, f32[5,16,640]{2,1,0:T(8,128)}, f32[16,640]{1,0:T(8,128)}, f32[16,640]{1,0:T(8,128)}, f32[16,640]{1,0:T(8,128)}, /*index=5*/f32[16,640]{1,0:T(8,128)}, f32[16,640]{1,0:T(8,128)}) custom-call(s32[5]{0:T(128)S(1)} %bitcast.52, f32[16,640]{1,0:T(8,128)S(1)} %collective-permute-done.25.refs_1_, ...), custom_call_target="tpu_custom_call" | custom-call | flops 2000000 | bytes 2000000 | tf_op jit(solution)/shard_map/pallas_call | solution.py:688
  113.9 2.6 %all-to-all-start.7 = ((f32[32,4,128]{2,1,0:T(4,128)}), f32[32,4,128]{2,1,0:T(4,128)S(1)}, u32[]{:S(2)}, u32[]{:S(2)}) async-start(f32[32,4,128]{2,1,0:T(4,128)} %bitcast.70), calls=%async_computation.7 | async-start | bytes 131072 | tf_op jit(solution)/shard_map/all_to_all | solution.py:707
  116.5 2.7 %collective-permute-start.30 = (f32[16,640]{1,0:T(8,128)}, f32[16,640]{1,0:T(8,128)S(1)}, u32[]{:S(2)}, u32[]{:S(2)}) collective-permute-start(f32[16,640]{1,0:T(8,128)} %get-tuple-element.224), channel_id=1, source_target_pairs={{0,4},{1,5},{2,6},{3,7},{4,0},{5,1},{6,2},{7,3},{8,12},{9,13},{10,... | collective-permute-start | bytes 122888 | tf_op jit(solution)/shard_map/ppermute | solution.py:703
  123.9 3.7 %shard_map.115 = (f32[5,16,640]{2,1,0:T(8,128)S(1)}, f32[5,16,640]{2,1,0:T(8,128)S(1)}, f32[5,16,640]{2,1,0:T(8,128)S(1)}, f32[5,16,640]{2,1,0:T(8,128)S(1)}, f3...) custom-call(f32[128,128]{1,0:T(8,128)S(1)} %bitcast.37, ...), custom_call_target="tpu_custom_call" | custom-call | flops 2000000 | bytes 2000000 | tf_op jit(solution)/shard_map/pallas_call | solution.py:688
  127.7 3.0 %shard_map.116 = f32[32,128]{1,0:T(8,128)} custom-call(s32[5]{0:T(128)S(1)} %bitcast.53, f32[16,640]{1,0:T(8,128)S(1)} %collective-permute-done.30.refs_1_, f32[16,640]{1,0:T(8,128)S(1)} %collective-permute-done.31.refs_2_, f32[16,640]{1,0:T(8,128)S(1)} %collective-permute-done.32.refs_3_, f32[16,640]{1,0:T(8,128)S(1)} %collective-permute-done.33.refs_4_, ...), custom_call_target="tpu_custom_call" | custom-call | flops 2000000 | bytes 2000000 | tf_op jit(solution)/shard_map/pallas_call | solution.py:688
  130.7 9.6 %all_to_all.99 = f32[32,1,128]{2,1,0:T(1,128)S(1)} all-to-all(f32[32,1,128]{2,1,0:T(1,128)} %bitcast.79), channel_id=1, replica_groups=mesh['organ'=4,'sub'=8] {'organ','sub'}, dimensions={0} | all-to-all | bytes 32768 | tf_op jit(solution)/shard_map/all_to_all | solution.py:707
  (75 shorter events, 38.9 us)
Async XLA Ops:
  2.6 14.4 %all-to-all-start = ((f32[32,1,128]{2,1,0:T(1,128)}), f32[32,1,128]{2,1,0:T(1,128)S(1)}, u32[]{:S(2)}, u32[]{:S(2)}) async-start(f32[32,1,128]{2,1,0:T(1,128)} %bitcast.80), calls=%async_computation | async-start | bytes 32768 | tf_op jit(solution)/shard_map/all_to_all | solution.py:707
  19.7 10.0 %all-to-all-start.1 = ((f32[32,4,128]{2,1,0:T(4,128)}), f32[32,4,128]{2,1,0:T(4,128)S(1)}, u32[]{:S(2)}, u32[]{:S(2)}) async-start(f32[32,4,128]{2,1,0:T(4,128)} %bitcast.73), calls=%async_computation.1 | async-start | bytes 131072 | tf_op jit(solution)/shard_map/all_to_all | solution.py:707
  22.3 10.6 %collective-permute-start = (f32[24,640]{1,0:T(8,128)}, f32[24,640]{1,0:T(8,128)S(1)}, u32[]{:S(2)}, u32[]{:S(2)}) collective-permute-start(f32[24,640]{1,0:T(8,128)} %get-tuple-element.127), channel_id=1, source_target_pairs={{0,4},{1,5},{2,6},{3,7},{4,0},{5,1},{6,2},{7,3},{8,12},{9,13},{10,... | collective-permute-start | bytes 184328 | tf_op jit(solution)/shard_map/ppermute | solution.py:703
  25.0 7.9 %collective-permute-start.1 = (f32[24,640]{1,0:T(8,128)}, f32[24,640]{1,0:T(8,128)S(1)}, u32[]{:S(2)}, u32[]{:S(2)}) collective-permute-start(f32[24,640]{1,0:T(8,128)} %get-tuple-element.128), channel_id=1, source_target_pairs={{0,1},{1,0},{2,3},{3,2},{4,5},{5,4},{6,7},{7,6},{8,9},{9,8},{10,11... | collective-permute-start | bytes 184328 | tf_op jit(solution)/shard_map/ppermute | solution.py:703
  26.5 6.4 %collective-permute-start.2 = (f32[24,640]{1,0:T(8,128)}, f32[24,640]{1,0:T(8,128)S(1)}, u32[]{:S(2)}, u32[]{:S(2)}) collective-permute-start(f32[24,640]{1,0:T(8,128)} %get-tuple-element.129), channel_id=1, source_target_pairs={{0,2},{1,3},{2,0},{3,1},{4,6},{5,7},{6,4},{7,5},{8,10},{9,11},{10,... | collective-permute-start | bytes 184328 | tf_op jit(solution)/shard_map/ppermute | solution.py:703
  28.0 4.9 %collective-permute-start.3 = (f32[24,640]{1,0:T(8,128)}, f32[24,640]{1,0:T(8,128)S(1)}, u32[]{:S(2)}, u32[]{:S(2)}) collective-permute-start(f32[24,640]{1,0:T(8,128)} %get-tuple-element.130), channel_id=1, source_target_pairs={{0,16},{8,24},{16,0},{24,8},{1,17},{9,25},{17,1},{25,9},{2,18},{10... | collective-permute-start | bytes 184328 | tf_op jit(solution)/shard_map/ppermute | solution.py:703
  36.6 9.8 %all-to-all-start.2 = ((f32[32,2,128]{2,1,0:T(2,128)}), f32[32,2,128]{2,1,0:T(2,128)S(1)}, u32[]{:S(2)}, u32[]{:S(2)}) async-start(f32[32,2,128]{2,1,0:T(2,128)} %bitcast.78), calls=%async_computation.2 | async-start | bytes 65536 | tf_op jit(solution)/shard_map/all_to_all | solution.py:707
  39.2 9.1 %collective-permute-start.5 = (f32[16,640]{1,0:T(8,128)}, f32[16,640]{1,0:T(8,128)S(1)}, u32[]{:S(2)}, u32[]{:S(2)}) collective-permute-start(f32[16,640]{1,0:T(8,128)} %get-tuple-element.146), channel_id=1, source_target_pairs={{0,4},{1,5},{2,6},{3,7},{4,0},{5,1},{6,2},{7,3},{8,12},{9,13},{10,... | collective-permute-start | bytes 122888 | tf_op jit(solution)/shard_map/ppermute | solution.py:703
  41.9 6.4 %collective-permute-start.6 = (f32[16,640]{1,0:T(8,128)}, f32[16,640]{1,0:T(8,128)S(1)}, u32[]{:S(2)}, u32[]{:S(2)}) collective-permute-start(f32[16,640]{1,0:T(8,128)} %get-tuple-element.147), channel_id=1, source_target_pairs={{0,1},{1,0},{2,3},{3,2},{4,5},{5,4},{6,7},{7,6},{8,9},{9,8},{10,11... | collective-permute-start | bytes 122888 | tf_op jit(solution)/shard_map/ppermute | solution.py:703
  51.0 10.0 %all-to-all-start.3 = ((f32[32,4,128]{2,1,0:T(4,128)}), f32[32,4,128]{2,1,0:T(4,128)S(1)}, u32[]{:S(2)}, u32[]{:S(2)}) async-start(f32[32,4,128]{2,1,0:T(4,128)} %bitcast.72), calls=%async_computation.3 | async-start | bytes 131072 | tf_op jit(solution)/shard_map/all_to_all | solution.py:707
  53.6 10.7 %collective-permute-start.10 = (f32[16,640]{1,0:T(8,128)}, f32[16,640]{1,0:T(8,128)S(1)}, u32[]{:S(2)}, u32[]{:S(2)}) collective-permute-start(f32[16,640]{1,0:T(8,128)} %get-tuple-element.159), channel_id=1, source_target_pairs={{0,4},{1,5},{2,6},{3,7},{4,0},{5,1},{6,2},{7,3},{8,12},{9,13},{10,... | collective-permute-start | bytes 122888 | tf_op jit(solution)/shard_map/ppermute | solution.py:703
  56.3 8.0 %collective-permute-start.11 = (f32[16,640]{1,0:T(8,128)}, f32[16,640]{1,0:T(8,128)S(1)}, u32[]{:S(2)}, u32[]{:S(2)}) collective-permute-start(f32[16,640]{1,0:T(8,128)} %get-tuple-element.160), channel_id=1, source_target_pairs={{0,1},{1,0},{2,3},{3,2},{4,5},{5,4},{6,7},{7,6},{8,9},{9,8},{10,11... | collective-permute-start | bytes 122888 | tf_op jit(solution)/shard_map/ppermute | solution.py:703
  57.8 6.5 %collective-permute-start.12 = (f32[16,640]{1,0:T(8,128)}, f32[16,640]{1,0:T(8,128)S(1)}, u32[]{:S(2)}, u32[]{:S(2)}) collective-permute-start(f32[16,640]{1,0:T(8,128)} %get-tuple-element.161), channel_id=1, source_target_pairs={{0,2},{1,3},{2,0},{3,1},{4,6},{5,7},{6,4},{7,5},{8,10},{9,11},{10,... | collective-permute-start | bytes 122888 | tf_op jit(solution)/shard_map/ppermute | solution.py:703
  59.4 5.0 %collective-permute-start.13 = (f32[16,640]{1,0:T(8,128)}, f32[16,640]{1,0:T(8,128)S(1)}, u32[]{:S(2)}, u32[]{:S(2)}) collective-permute-start(f32[16,640]{1,0:T(8,128)} %get-tuple-element.162), channel_id=1, source_target_pairs={{0,16},{8,24},{16,0},{24,8},{1,17},{9,25},{17,1},{25,9},{2,18},{10... | collective-permute-start | bytes 122888 | tf_op jit(solution)/shard_map/ppermute | solution.py:703
  68.0 9.9 %all-to-all-start.4 = ((f32[32,4,128]{2,1,0:T(4,128)}), f32[32,4,128]{2,1,0:T(4,128)S(1)}, u32[]{:S(2)}, u32[]{:S(2)}) async-start(f32[32,4,128]{2,1,0:T(4,128)} %bitcast.75), calls=%async_computation.4 | async-start | bytes 131072 | tf_op jit(solution)/shard_map/all_to_all | solution.py:707
  70.5 9.5 %collective-permute-start.15 = (f32[16,640]{1,0:T(8,128)}, f32[16,640]{1,0:T(8,128)S(1)}, u32[]{:S(2)}, u32[]{:S(2)}) collective-permute-start(f32[16,640]{1,0:T(8,128)} %get-tuple-element.175), channel_id=1, source_target_pairs={{0,4},{1,5},{2,6},{3,7},{4,0},{5,1},{6,2},{7,3},{8,12},{9,13},{10,... | collective-permute-start | bytes 122888 | tf_op jit(solution)/shard_map/ppermute | solution.py:703
  73.2 6.8 %collective-permute-start.16 = (f32[16,640]{1,0:T(8,128)}, f32[16,640]{1,0:T(8,128)S(1)}, u32[]{:S(2)}, u32[]{:S(2)}) collective-permute-start(f32[16,640]{1,0:T(8,128)} %get-tuple-element.176), channel_id=1, source_target_pairs={{0,1},{1,0},{2,3},{3,2},{4,5},{5,4},{6,7},{7,6},{8,9},{9,8},{10,11... | collective-permute-start | bytes 122888 | tf_op jit(solution)/shard_map/ppermute | solution.py:703
  74.7 5.3 %collective-permute-start.17 = (f32[16,640]{1,0:T(8,128)}, f32[16,640]{1,0:T(8,128)S(1)}, u32[]{:S(2)}, u32[]{:S(2)}) collective-permute-start(f32[16,640]{1,0:T(8,128)} %get-tuple-element.177), channel_id=1, source_target_pairs={{0,2},{1,3},{2,0},{3,1},{4,6},{5,7},{6,4},{7,5},{8,10},{9,11},{10,... | collective-permute-start | bytes 122888 | tf_op jit(solution)/shard_map/ppermute | solution.py:703
  82.5 10.0 %all-to-all-start.5 = ((f32[32,4,128]{2,1,0:T(4,128)}), f32[32,4,128]{2,1,0:T(4,128)S(1)}, u32[]{:S(2)}, u32[]{:S(2)}) async-start(f32[32,4,128]{2,1,0:T(4,128)} %bitcast.71), calls=%async_computation.5 | async-start | bytes 131072 | tf_op jit(solution)/shard_map/all_to_all | solution.py:707
  85.3 10.6 %collective-permute-start.20 = (f32[16,640]{1,0:T(8,128)}, f32[16,640]{1,0:T(8,128)S(1)}, u32[]{:S(2)}, u32[]{:S(2)}) collective-permute-start(f32[16,640]{1,0:T(8,128)} %get-tuple-element.190), channel_id=1, source_target_pairs={{0,4},{1,5},{2,6},{3,7},{4,0},{5,1},{6,2},{7,3},{8,12},{9,13},{10,... | collective-permute-start | bytes 122888 | tf_op jit(solution)/shard_map/ppermute | solution.py:703
  87.8 8.1 %collective-permute-start.21 = (f32[16,640]{1,0:T(8,128)}, f32[16,640]{1,0:T(8,128)S(1)}, u32[]{:S(2)}, u32[]{:S(2)}) collective-permute-start(f32[16,640]{1,0:T(8,128)} %get-tuple-element.191), channel_id=1, source_target_pairs={{0,1},{1,0},{2,3},{3,2},{4,5},{5,4},{6,7},{7,6},{8,9},{9,8},{10,11... | collective-permute-start | bytes 122888 | tf_op jit(solution)/shard_map/ppermute | solution.py:703
  89.3 6.6 %collective-permute-start.22 = (f32[16,640]{1,0:T(8,128)}, f32[16,640]{1,0:T(8,128)S(1)}, u32[]{:S(2)}, u32[]{:S(2)}) collective-permute-start(f32[16,640]{1,0:T(8,128)} %get-tuple-element.192), channel_id=1, source_target_pairs={{0,2},{1,3},{2,0},{3,1},{4,6},{5,7},{6,4},{7,5},{8,10},{9,11},{10,... | collective-permute-start | bytes 122888 | tf_op jit(solution)/shard_map/ppermute | solution.py:703
  90.8 5.0 %collective-permute-start.23 = (f32[16,640]{1,0:T(8,128)}, f32[16,640]{1,0:T(8,128)S(1)}, u32[]{:S(2)}, u32[]{:S(2)}) collective-permute-start(f32[16,640]{1,0:T(8,128)} %get-tuple-element.193), channel_id=1, source_target_pairs={{0,16},{8,24},{16,0},{24,8},{1,17},{9,25},{17,1},{25,9},{2,18},{10... | collective-permute-start | bytes 122888 | tf_op jit(solution)/shard_map/ppermute | solution.py:703
  99.4 10.0 %all-to-all-start.6 = ((f32[32,4,128]{2,1,0:T(4,128)}), f32[32,4,128]{2,1,0:T(4,128)S(1)}, u32[]{:S(2)}, u32[]{:S(2)}) async-start(f32[32,4,128]{2,1,0:T(4,128)} %bitcast.74), calls=%async_computation.6 | async-start | bytes 131072 | tf_op jit(solution)/shard_map/all_to_all | solution.py:707
  102.0 9.6 %collective-permute-start.25 = (f32[16,640]{1,0:T(8,128)}, f32[16,640]{1,0:T(8,128)S(1)}, u32[]{:S(2)}, u32[]{:S(2)}) collective-permute-start(f32[16,640]{1,0:T(8,128)} %get-tuple-element.207), channel_id=1, source_target_pairs={{0,4},{1,5},{2,6},{3,7},{4,0},{5,1},{6,2},{7,3},{8,12},{9,13},{10,... | collective-permute-start | bytes 122888 | tf_op jit(solution)/shard_map/ppermute | solution.py:703
  104.8 6.9 %collective-permute-start.26 = (f32[16,640]{1,0:T(8,128)}, f32[16,640]{1,0:T(8,128)S(1)}, u32[]{:S(2)}, u32[]{:S(2)}) collective-permute-start(f32[16,640]{1,0:T(8,128)} %get-tuple-element.208), channel_id=1, source_target_pairs={{0,1},{1,0},{2,3},{3,2},{4,5},{5,4},{6,7},{7,6},{8,9},{9,8},{10,11... | collective-permute-start | bytes 122888 | tf_op jit(solution)/shard_map/ppermute | solution.py:703
  106.2 5.4 %collective-permute-start.27 = (f32[16,640]{1,0:T(8,128)}, f32[16,640]{1,0:T(8,128)S(1)}, u32[]{:S(2)}, u32[]{:S(2)}) collective-permute-start(f32[16,640]{1,0:T(8,128)} %get-tuple-element.209), channel_id=1, source_target_pairs={{0,2},{1,3},{2,0},{3,1},{4,6},{5,7},{6,4},{7,5},{8,10},{9,11},{10,... | collective-permute-start | bytes 122888 | tf_op jit(solution)/shard_map/ppermute | solution.py:703
  113.9 10.0 %all-to-all-start.7 = ((f32[32,4,128]{2,1,0:T(4,128)}), f32[32,4,128]{2,1,0:T(4,128)S(1)}, u32[]{:S(2)}, u32[]{:S(2)}) async-start(f32[32,4,128]{2,1,0:T(4,128)} %bitcast.70), calls=%async_computation.7 | async-start | bytes 131072 | tf_op jit(solution)/shard_map/all_to_all | solution.py:707
  116.5 11.1 %collective-permute-start.30 = (f32[16,640]{1,0:T(8,128)}, f32[16,640]{1,0:T(8,128)S(1)}, u32[]{:S(2)}, u32[]{:S(2)}) collective-permute-start(f32[16,640]{1,0:T(8,128)} %get-tuple-element.224), channel_id=1, source_target_pairs={{0,4},{1,5},{2,6},{3,7},{4,0},{5,1},{6,2},{7,3},{8,12},{9,13},{10,... | collective-permute-start | bytes 122888 | tf_op jit(solution)/shard_map/ppermute | solution.py:703
  119.2 8.4 %collective-permute-start.31 = (f32[16,640]{1,0:T(8,128)}, f32[16,640]{1,0:T(8,128)S(1)}, u32[]{:S(2)}, u32[]{:S(2)}) collective-permute-start(f32[16,640]{1,0:T(8,128)} %get-tuple-element.225), channel_id=1, source_target_pairs={{0,1},{1,0},{2,3},{3,2},{4,5},{5,4},{6,7},{7,6},{8,9},{9,8},{10,11... | collective-permute-start | bytes 122888 | tf_op jit(solution)/shard_map/ppermute | solution.py:703
  120.7 6.9 %collective-permute-start.32 = (f32[16,640]{1,0:T(8,128)}, f32[16,640]{1,0:T(8,128)S(1)}, u32[]{:S(2)}, u32[]{:S(2)}) collective-permute-start(f32[16,640]{1,0:T(8,128)} %get-tuple-element.226), channel_id=1, source_target_pairs={{0,2},{1,3},{2,0},{3,1},{4,6},{5,7},{6,4},{7,5},{8,10},{9,11},{10,... | collective-permute-start | bytes 122888 | tf_op jit(solution)/shard_map/ppermute | solution.py:703
  122.3 5.4 %collective-permute-start.33 = (f32[16,640]{1,0:T(8,128)}, f32[16,640]{1,0:T(8,128)S(1)}, u32[]{:S(2)}, u32[]{:S(2)}) collective-permute-start(f32[16,640]{1,0:T(8,128)} %get-tuple-element.227), channel_id=1, source_target_pairs={{0,16},{8,24},{16,0},{24,8},{1,17},{9,25},{17,1},{25,9},{2,18},{10... | collective-permute-start | bytes 122888 | tf_op jit(solution)/shard_map/ppermute | solution.py:703
  (12 other events, 43.6 us)

commit v7 on v6

--- a/solution.py
+++ b/solution.py
@@ -209,7 +209,7 @@
 
 def slots_kernel(
     devices, count, owner, active, mortar, start_rows, right_rows, basis, a_high, a_low, start,
-    right, products,
+    right, products, raw_out,
 ):
     owner, active = owner(), active()
     rows = owner.shape[1]
@@ -232,10 +232,18 @@
     extra = jnp.zeros((2 * 16 - directions - modes, length), F32)
     both = jnp.concatenate([start.ref[0]] + first + [extra], axis=0)
     products.ref[...] = times(both, a_high.ref[...], a_low.ref[...], turned_dot)
+    products.flush()
+    here = lax.rem(iota((directions, LANES), 1), directions) == iota((directions, LANES), 0)
+    raw_out.ref[...] = jnp.zeros(raw_out.ref.shape, F32)
+    for m in range(modes):
+        acc = sum(fold(right.ref[f] * basis[m * blocks + f]) for f in range(blocks))
+        column = jnp.sum(acc, axis=1, keepdims=True)
+        row = jnp.sum(jnp.where(here, column, 0.0), axis=0, keepdims=True)
+        raw_out.ref[m : m + 1, :] = row
 
 
 def first_kernel(
-    organs, arrived, matches, basis, start, products, right, message, unit, modes_out, *sends
+    organs, arrived, matches, basis, start, products, raw, message, unit, modes_out, *sends
 ):
     devices = arrived.shape[0]
     subs = devices // organs
@@ -301,7 +309,12 @@
     lines = pack(turned_modes, slave[rows], devices)
     half = LANES // 2
     put(message.ref, 4, 2, jnp.concatenate([line[:, :half] for line in lines], axis=1))
-    spread_rows(message.ref, 4, 3, coefficients_row(right(), modes_ref))
+    raw = raw()
+    row = jnp.zeros((1, LANES), F32)
+    for i in range(modes):
+        value = sum(inverse[i, j] * raw[j : j + 1, :] for j in range(i + 1))
+        row = jnp.where(lane // directions == i, value, row)
+    spread_rows(message.ref, 4, 3, row)
     message.flush()
 
 
@@ -757,9 +770,9 @@
         smem=1,
     )
     arrived = exchange(setup)
-    a_high, a_low, start, right, products = call(
+    a_high, a_low, start, right, products, raw = call(
         functools.partial(slots_kernel, devices),
-        [((width, length), BF16)] * 2 + [whole] * 2 + [((32, width), F32)],
+        [((width, length), BF16)] * 2 + [whole] * 2 + [((32, width), F32), ((8, LANES), F32)],
         (count,),
         (owner, active, mortar, start_rows, right_rows, basis),
         smem=1,
@@ -773,7 +786,7 @@
         ]
         + [((directions + 8, length), F32)] * blocks,
         (arrived,),
-        (matches, basis, start, products, right),
+        (matches, basis, start, products, raw),
         held=1,
     )
     maps = (a_high, a_low, unit)

time: 142 us -> 142 us (level)
  no operation moved by 1% of the time
where the time goes in v7:
time: 142 us; the launch traced here: 141 us
  starting transfers between devices  75.8 us (53%)
  Pallas kernels  47.6 us (34%)
  blocking collectives  9.6 us (7%)
  waiting for transfers between devices  6.93 us (5%)
    ppermute x35, starting transfers between devices, from_partner(): return lax.ppermute(value, axis, pairs)  50.4 us
    pallas_call x18, Pallas kernels, call(): pl.pallas_call(body, out_shape=[pltpu.HBM(shape, kind) for shape, kind in...  47.6 us
    all_to_all x8, starting transfers between devices, exchange(): lax.all_to_all(message, AXES, split_axis=0, concat_axis=0, tiled=True)  25.4 us
    all_to_all x1, blocking collectives, exchange(): lax.all_to_all(message, AXES, split_axis=0, concat_axis=0, tiled=True)  9.6 us
    all_to_all x8, waiting for transfers between devices, exchange(): lax.all_to_all(message, AXES, split_axis=0, concat_axis=0, tiled=True)  5.27 us
  transfers between devices with their start and end apart: 43, of which 10 were waited for; matrix products, arithmetic and copies ran while one was open for 0% of the time, Pallas kernels for 16%

profile of v7, /device:TPU:0, one launch (start us, length us, event | category | flops | bytes accessed | tf_op | source)
XLA Modules:
  0.0 141.2 jit_solution(13247111748568914288)
XLA Ops:
  0.7 1.9 %shard_map.100 = f32[32,128]{1,0:T(8,128)} custom-call(s32[1]{0:T(128)} %bitcast.35.refs_0_, s32[1,128]{1,0:T(1,128)} %bitcast.81, s32[1,128]{1,0:T(1,128)} %bitcast.85, s32[1,128]{1,0:T(1,128)} %bitcast.83, f32[30,1,640]{2,1,0:T(1,128)} %bitcast.66), custom_call_target="tpu_custom_call" | custom-call | flops 2000000 | bytes 2000000 | tf_op jit(solution)/shard_map/pallas_call | solution.py:701
  2.6 7.3 %all-to-all-start = ((f32[32,1,128]{2,1,0:T(1,128)}), f32[32,1,128]{2,1,0:T(1,128)S(1)}, u32[]{:S(2)}, u32[]{:S(2)}) async-start(f32[32,1,128]{2,1,0:T(1,128)} %bitcast.80), calls=%async_computation | async-start | bytes 32768 | tf_op jit(solution)/shard_map/all_to_all | solution.py:720
  9.9 2.8 %shard_map.101 = (bf16[256,640]{1,0:T(8,128)(2,1)}, bf16[256,640]{1,0:T(8,128)(2,1)}, f32[5,16,640]{2,1,0:T(8,128)}, f32[5,16,640]{2,1,0:T(8,128)}, f32[32,256]{1,0:T(8,128)}, /*index=5*/f32[8,128]{1,0:T(8,128)}) custom-call(s32[1]{0:T(128)} %bitcast.36.refs_0_, s32[1,128]{1,0:T(1,128)} %bitcast.82, s32[1,128]{1,0:T(1,128)} %bitcast.84, ...), custom_call_target="tpu_custom_call" | custom-call | flops 2000000 | bytes 2000000 | tf_op jit(solution)/shard_map/pallas_call | solution.py:701
  12.7 4.3 %all-to-all-done = f32[32,1,128]{2,1,0:T(1,128)S(1)} async-done(((f32[32,1,128]{2,1,0:T(1,128)}), f32[32,1,128]{2,1,0:T(1,128)S(1)}, u32[]{:S(2)}, u32[]{:S(2)}) %all-to-all-start) | async-done | bytes 16416 | tf_op jit(solution)/shard_map/all_to_all | solution.py:720
  17.0 2.5 %shard_map.102 = (f32[128,128]{1,0:T(8,128)}, bf16[256,640]{1,0:T(8,128)(2,1)}, f32[6,5,640]{2,1,0:T(8,128)}, f32[24,640]{1,0:T(8,128)}, f32[24,640]{1,0:T(8,128...) custom-call(f32[32,128]{1,0:T(8,128)S(1)} %bitcast.45, s32[5]{0:T(128)} %bitcast.46, ...), custom_call_target="tpu_custom_call" | custom-call | flops 2000000 | bytes 2000000 | tf_op jit(solution)/shard_map/pallas_call | solution.py:701
  19.5 2.6 %all-to-all-start.1 = ((f32[32,4,128]{2,1,0:T(4,128)}), f32[32,4,128]{2,1,0:T(4,128)S(1)}, u32[]{:S(2)}, u32[]{:S(2)}) async-start(f32[32,4,128]{2,1,0:T(4,128)} %bitcast.73), calls=%async_computation.1 | async-start | bytes 131072 | tf_op jit(solution)/shard_map/all_to_all | solution.py:720
  22.1 2.7 %collective-permute-start = (f32[24,640]{1,0:T(8,128)}, f32[24,640]{1,0:T(8,128)S(1)}, u32[]{:S(2)}, u32[]{:S(2)}) collective-permute-start(f32[24,640]{1,0:T(8,128)} %get-tuple-element.128), channel_id=1, source_target_pairs={{0,4},{1,5},{2,6},{3,7},{4,0},{5,1},{6,2},{7,3},{8,12},{9,13},{10,... | collective-permute-start | bytes 184328 | tf_op jit(solution)/shard_map/ppermute | solution.py:716
  29.5 3.2 %shard_map.103 = (f32[5,16,640]{2,1,0:T(8,128)}, f32[5,16,640]{2,1,0:T(8,128)S(1)}, f32[32,640]{1,0:T(8,128)S(1)}, bf16[256,640]{1,0:T(8,128)(2,1)S(1)}, bf16[25...) custom-call(f32[128,128]{1,0:T(8,128)S(1)} %bitcast.38, ...), custom_call_target="tpu_custom_call" | custom-call | flops 2000000 | bytes 2000000 | tf_op jit(solution)/shard_map/pallas_call | solution.py:701
  32.8 3.7 %shard_map.104 = (f32[64,128]{1,0:T(8,128)}, f32[5,16,640]{2,1,0:T(8,128)}, f32[5,32,640]{2,1,0:T(8,128)}, f32[16,640]{1,0:T(8,128)}, f32[16,640]{1,0:T(8,128)},...) custom-call(s32[5]{0:T(128)S(1)} %bitcast.47, f32[24,640]{1,0:T(8,128)S(1)} %collective-permute-done.refs_1_, ...), custom_call_target="tpu_custom_call" | custom-call | flops 2000000 | bytes 2000000 | tf_op jit(solution)/shard_map/pallas_call | solution.py:701
  36.4 2.5 %all-to-all-start.2 = ((f32[32,2,128]{2,1,0:T(2,128)}), f32[32,2,128]{2,1,0:T(2,128)S(1)}, u32[]{:S(2)}, u32[]{:S(2)}) async-start(f32[32,2,128]{2,1,0:T(2,128)} %bitcast.78), calls=%async_computation.2 | async-start | bytes 65536 | tf_op jit(solution)/shard_map/all_to_all | solution.py:720
  39.0 2.7 %collective-permute-start.5 = (f32[16,640]{1,0:T(8,128)}, f32[16,640]{1,0:T(8,128)S(1)}, u32[]{:S(2)}, u32[]{:S(2)}) collective-permute-start(f32[16,640]{1,0:T(8,128)} %get-tuple-element.148), channel_id=1, source_target_pairs={{0,4},{1,5},{2,6},{3,7},{4,0},{5,1},{6,2},{7,3},{8,12},{9,13},{10,... | collective-permute-start | bytes 122888 | tf_op jit(solution)/shard_map/ppermute | solution.py:716
  50.8 2.6 %all-to-all-start.3 = ((f32[32,4,128]{2,1,0:T(4,128)}), f32[32,4,128]{2,1,0:T(4,128)S(1)}, u32[]{:S(2)}, u32[]{:S(2)}) async-start(f32[32,4,128]{2,1,0:T(4,128)} %bitcast.72), calls=%async_computation.3 | async-start | bytes 131072 | tf_op jit(solution)/shard_map/all_to_all | solution.py:720
  53.4 2.7 %collective-permute-start.10 = (f32[16,640]{1,0:T(8,128)}, f32[16,640]{1,0:T(8,128)S(1)}, u32[]{:S(2)}, u32[]{:S(2)}) collective-permute-start(f32[16,640]{1,0:T(8,128)} %get-tuple-element.161), channel_id=1, source_target_pairs={{0,4},{1,5},{2,6},{3,7},{4,0},{5,1},{6,2},{7,3},{8,12},{9,13},{10,... | collective-permute-start | bytes 122888 | tf_op jit(solution)/shard_map/ppermute | solution.py:716
  60.8 3.3 %shard_map.107 = (f32[5,16,640]{2,1,0:T(8,128)}, f32[5,16,640]{2,1,0:T(8,128)S(1)}, f32[8,128]{1,0:T(8,128)S(1)}, bf16[256,640]{1,0:T(8,128)(2,1)S(1)}, bf16[256...) custom-call(f32[128,128]{1,0:T(8,128)S(1)} %bitcast.39, ...), custom_call_target="tpu_custom_call" | custom-call | flops 2000000 | bytes 2000000 | tf_op jit(solution)/shard_map/pallas_call | solution.py:701
  64.2 3.6 %shard_map.108 = (f32[128,128]{1,0:T(8,128)}, f32[5,16,640]{2,1,0:T(8,128)}, f32[5,16,640]{2,1,0:T(8,128)}, f32[16,640]{1,0:T(8,128)}, f32[16,640]{1,0:T(8,128)}...) custom-call(s32[5]{0:T(128)S(1)} %bitcast.49, f32[16,640]{1,0:T(8,128)S(1)} %collective-permute-done.10.refs_1_, ...), custom_call_target="tpu_custom_call" | custom-call | flops 2000000 | bytes 2000000 | tf_op jit(solution)/shard_map/pallas_call | solution.py:701
  67.8 2.5 %all-to-all-start.4 = ((f32[32,4,128]{2,1,0:T(4,128)}), f32[32,4,128]{2,1,0:T(4,128)S(1)}, u32[]{:S(2)}, u32[]{:S(2)}) async-start(f32[32,4,128]{2,1,0:T(4,128)} %bitcast.75), calls=%async_computation.4 | async-start | bytes 131072 | tf_op jit(solution)/shard_map/all_to_all | solution.py:720
  70.3 2.7 %collective-permute-start.15 = (f32[16,640]{1,0:T(8,128)}, f32[16,640]{1,0:T(8,128)S(1)}, u32[]{:S(2)}, u32[]{:S(2)}) collective-permute-start(f32[16,640]{1,0:T(8,128)} %get-tuple-element.177), channel_id=1, source_target_pairs={{0,4},{1,5},{2,6},{3,7},{4,0},{5,1},{6,2},{7,3},{8,12},{9,13},{10,... | collective-permute-start | bytes 122888 | tf_op jit(solution)/shard_map/ppermute | solution.py:716
  77.7 2.1 %shard_map.109 = (f32[4,16,128]{2,1,0:T(8,128)}, f32[5,16,640]{2,1,0:T(8,128)S(1)}, f32[16,128]{1,0:T(8,128)S(1)}, f32[5,16,640]{2,1,0:T(8,128)S(1)}, bf16[256,6...) custom-call(f32[128,128]{1,0:T(8,128)S(1)} %bitcast.42, ...), custom_call_target="tpu_custom_call" | custom-call | flops 2000000 | bytes 2000000 | tf_op jit(solution)/shard_map/pallas_call | solution.py:701
  80.3 2.0 %shard_map.110 = (f32[128,128]{1,0:T(8,128)}, f32[5,16,640]{2,1,0:T(8,128)}, f32[5,16,640]{2,1,0:T(8,128)}, f32[16,640]{1,0:T(8,128)}, f32[16,640]{1,0:T(8,128)}...) custom-call(s32[5]{0:T(128)S(1)} %bitcast.50, f32[16,640]{1,0:T(8,128)S(1)} %collective-permute-done.15.refs_1_, ...), custom_call_target="tpu_custom_call" | custom-call | flops 2000000 | bytes 2000000 | tf_op jit(solution)/shard_map/pallas_call | solution.py:701
  82.3 2.8 %all-to-all-start.5 = ((f32[32,4,128]{2,1,0:T(4,128)}), f32[32,4,128]{2,1,0:T(4,128)S(1)}, u32[]{:S(2)}, u32[]{:S(2)}) async-start(f32[32,4,128]{2,1,0:T(4,128)} %bitcast.71), calls=%async_computation.5 | async-start | bytes 131072 | tf_op jit(solution)/shard_map/all_to_all | solution.py:720
  85.1 2.5 %collective-permute-start.20 = (f32[16,640]{1,0:T(8,128)}, f32[16,640]{1,0:T(8,128)S(1)}, u32[]{:S(2)}, u32[]{:S(2)}) collective-permute-start(f32[16,640]{1,0:T(8,128)} %get-tuple-element.192), channel_id=1, source_target_pairs={{0,4},{1,5},{2,6},{3,7},{4,0},{5,1},{6,2},{7,3},{8,12},{9,13},{10,... | collective-permute-start | bytes 122888 | tf_op jit(solution)/shard_map/ppermute | solution.py:716
  92.3 3.4 %shard_map.111 = (f32[5,16,640]{2,1,0:T(8,128)}, f32[5,16,640]{2,1,0:T(8,128)S(1)}, f32[8,128]{1,0:T(8,128)S(1)}, bf16[256,640]{1,0:T(8,128)(2,1)S(1)}, bf16[256...) custom-call(f32[128,128]{1,0:T(8,128)S(1)} %bitcast.40, ...), custom_call_target="tpu_custom_call" | custom-call | flops 2000000 | bytes 2000000 | tf_op jit(solution)/shard_map/pallas_call | solution.py:701
  95.7 3.5 %shard_map.112 = (f32[128,128]{1,0:T(8,128)}, f32[5,16,640]{2,1,0:T(8,128)}, f32[5,16,640]{2,1,0:T(8,128)}, f32[16,640]{1,0:T(8,128)}, f32[16,640]{1,0:T(8,128)}...) custom-call(s32[5]{0:T(128)S(1)} %bitcast.51, f32[16,640]{1,0:T(8,128)S(1)} %collective-permute-done.20.refs_1_, ...), custom_call_target="tpu_custom_call" | custom-call | flops 2000000 | bytes 2000000 | tf_op jit(solution)/shard_map/pallas_call | solution.py:701
  99.2 2.6 %all-to-all-start.6 = ((f32[32,4,128]{2,1,0:T(4,128)}), f32[32,4,128]{2,1,0:T(4,128)S(1)}, u32[]{:S(2)}, u32[]{:S(2)}) async-start(f32[32,4,128]{2,1,0:T(4,128)} %bitcast.74), calls=%async_computation.6 | async-start | bytes 131072 | tf_op jit(solution)/shard_map/all_to_all | solution.py:720
  101.8 2.7 %collective-permute-start.25 = (f32[16,640]{1,0:T(8,128)}, f32[16,640]{1,0:T(8,128)S(1)}, u32[]{:S(2)}, u32[]{:S(2)}) collective-permute-start(f32[16,640]{1,0:T(8,128)} %get-tuple-element.209), channel_id=1, source_target_pairs={{0,4},{1,5},{2,6},{3,7},{4,0},{5,1},{6,2},{7,3},{8,12},{9,13},{10,... | collective-permute-start | bytes 122888 | tf_op jit(solution)/shard_map/ppermute | solution.py:716
  109.2 2.2 %shard_map.113 = (f32[4,16,128]{2,1,0:T(8,128)}, f32[5,16,640]{2,1,0:T(8,128)S(1)}, f32[16,128]{1,0:T(8,128)S(1)}, f32[5,16,640]{2,1,0:T(8,128)S(1)}, bf16[256,6...) custom-call(f32[128,128]{1,0:T(8,128)S(1)} %bitcast.41, ...), custom_call_target="tpu_custom_call" | custom-call | flops 2000000 | bytes 2000000 | tf_op jit(solution)/shard_map/pallas_call | solution.py:701
  111.8 1.9 %shard_map.114 = (f32[128,128]{1,0:T(8,128)}, f32[5,16,640]{2,1,0:T(8,128)}, f32[16,640]{1,0:T(8,128)}, f32[16,640]{1,0:T(8,128)}, f32[16,640]{1,0:T(8,128)}, /*index=5*/f32[16,640]{1,0:T(8,128)}, f32[16,640]{1,0:T(8,128)}) custom-call(s32[5]{0:T(128)S(1)} %bitcast.52, f32[16,640]{1,0:T(8,128)S(1)} %collective-permute-done.25.refs_1_, ...), custom_call_target="tpu_custom_call" | custom-call | flops 2000000 | bytes 2000000 | tf_op jit(solution)/shard_map/pallas_call | solution.py:701
  113.7 2.6 %all-to-all-start.7 = ((f32[32,4,128]{2,1,0:T(4,128)}), f32[32,4,128]{2,1,0:T(4,128)S(1)}, u32[]{:S(2)}, u32[]{:S(2)}) async-start(f32[32,4,128]{2,1,0:T(4,128)} %bitcast.70), calls=%async_computation.7 | async-start | bytes 131072 | tf_op jit(solution)/shard_map/all_to_all | solution.py:720
  116.3 2.7 %collective-permute-start.30 = (f32[16,640]{1,0:T(8,128)}, f32[16,640]{1,0:T(8,128)S(1)}, u32[]{:S(2)}, u32[]{:S(2)}) collective-permute-start(f32[16,640]{1,0:T(8,128)} %get-tuple-element.226), channel_id=1, source_target_pairs={{0,4},{1,5},{2,6},{3,7},{4,0},{5,1},{6,2},{7,3},{8,12},{9,13},{10,... | collective-permute-start | bytes 122888 | tf_op jit(solution)/shard_map/ppermute | solution.py:716
  123.7 3.7 %shard_map.115 = (f32[5,16,640]{2,1,0:T(8,128)S(1)}, f32[5,16,640]{2,1,0:T(8,128)S(1)}, f32[5,16,640]{2,1,0:T(8,128)S(1)}, f32[5,16,640]{2,1,0:T(8,128)S(1)}, f3...) custom-call(f32[128,128]{1,0:T(8,128)S(1)} %bitcast.37, ...), custom_call_target="tpu_custom_call" | custom-call | flops 2000000 | bytes 2000000 | tf_op jit(solution)/shard_map/pallas_call | solution.py:701
  127.5 3.0 %shard_map.116 = f32[32,128]{1,0:T(8,128)} custom-call(s32[5]{0:T(128)S(1)} %bitcast.53, f32[16,640]{1,0:T(8,128)S(1)} %collective-permute-done.30.refs_1_, f32[16,640]{1,0:T(8,128)S(1)} %collective-permute-done.31.refs_2_, f32[16,640]{1,0:T(8,128)S(1)} %collective-permute-done.32.refs_3_, f32[16,640]{1,0:T(8,128)S(1)} %collective-permute-done.33.refs_4_, ...), custom_call_target="tpu_custom_call" | custom-call | flops 2000000 | bytes 2000000 | tf_op jit(solution)/shard_map/pallas_call | solution.py:701
  130.5 9.6 %all_to_all.99 = f32[32,1,128]{2,1,0:T(1,128)S(1)} all-to-all(f32[32,1,128]{2,1,0:T(1,128)} %bitcast.79), channel_id=1, replica_groups=mesh['organ'=4,'sub'=8] {'organ','sub'}, dimensions={0} | all-to-all | bytes 32768 | tf_op jit(solution)/shard_map/all_to_all | solution.py:720
  (75 shorter events, 38.9 us)
Async XLA Ops:
  2.6 14.4 %all-to-all-start = ((f32[32,1,128]{2,1,0:T(1,128)}), f32[32,1,128]{2,1,0:T(1,128)S(1)}, u32[]{:S(2)}, u32[]{:S(2)}) async-start(f32[32,1,128]{2,1,0:T(1,128)} %bitcast.80), calls=%async_computation | async-start | bytes 32768 | tf_op jit(solution)/shard_map/all_to_all | solution.py:720
  19.5 10.0 %all-to-all-start.1 = ((f32[32,4,128]{2,1,0:T(4,128)}), f32[32,4,128]{2,1,0:T(4,128)S(1)}, u32[]{:S(2)}, u32[]{:S(2)}) async-start(f32[32,4,128]{2,1,0:T(4,128)} %bitcast.73), calls=%async_computation.1 | async-start | bytes 131072 | tf_op jit(solution)/shard_map/all_to_all | solution.py:720
  22.1 10.6 %collective-permute-start = (f32[24,640]{1,0:T(8,128)}, f32[24,640]{1,0:T(8,128)S(1)}, u32[]{:S(2)}, u32[]{:S(2)}) collective-permute-start(f32[24,640]{1,0:T(8,128)} %get-tuple-element.128), channel_id=1, source_target_pairs={{0,4},{1,5},{2,6},{3,7},{4,0},{5,1},{6,2},{7,3},{8,12},{9,13},{10,... | collective-permute-start | bytes 184328 | tf_op jit(solution)/shard_map/ppermute | solution.py:716
  24.8 7.9 %collective-permute-start.1 = (f32[24,640]{1,0:T(8,128)}, f32[24,640]{1,0:T(8,128)S(1)}, u32[]{:S(2)}, u32[]{:S(2)}) collective-permute-start(f32[24,640]{1,0:T(8,128)} %get-tuple-element.129), channel_id=1, source_target_pairs={{0,1},{1,0},{2,3},{3,2},{4,5},{5,4},{6,7},{7,6},{8,9},{9,8},{10,11... | collective-permute-start | bytes 184328 | tf_op jit(solution)/shard_map/ppermute | solution.py:716
  26.3 6.4 %collective-permute-start.2 = (f32[24,640]{1,0:T(8,128)}, f32[24,640]{1,0:T(8,128)S(1)}, u32[]{:S(2)}, u32[]{:S(2)}) collective-permute-start(f32[24,640]{1,0:T(8,128)} %get-tuple-element.130), channel_id=1, source_target_pairs={{0,2},{1,3},{2,0},{3,1},{4,6},{5,7},{6,4},{7,5},{8,10},{9,11},{10,... | collective-permute-start | bytes 184328 | tf_op jit(solution)/shard_map/ppermute | solution.py:716
  27.8 4.9 %collective-permute-start.3 = (f32[24,640]{1,0:T(8,128)}, f32[24,640]{1,0:T(8,128)S(1)}, u32[]{:S(2)}, u32[]{:S(2)}) collective-permute-start(f32[24,640]{1,0:T(8,128)} %get-tuple-element.131), channel_id=1, source_target_pairs={{0,16},{8,24},{16,0},{24,8},{1,17},{9,25},{17,1},{25,9},{2,18},{10... | collective-permute-start | bytes 184328 | tf_op jit(solution)/shard_map/ppermute | solution.py:716
  36.4 9.8 %all-to-all-start.2 = ((f32[32,2,128]{2,1,0:T(2,128)}), f32[32,2,128]{2,1,0:T(2,128)S(1)}, u32[]{:S(2)}, u32[]{:S(2)}) async-start(f32[32,2,128]{2,1,0:T(2,128)} %bitcast.78), calls=%async_computation.2 | async-start | bytes 65536 | tf_op jit(solution)/shard_map/all_to_all | solution.py:720
  39.0 9.1 %collective-permute-start.5 = (f32[16,640]{1,0:T(8,128)}, f32[16,640]{1,0:T(8,128)S(1)}, u32[]{:S(2)}, u32[]{:S(2)}) collective-permute-start(f32[16,640]{1,0:T(8,128)} %get-tuple-element.148), channel_id=1, source_target_pairs={{0,4},{1,5},{2,6},{3,7},{4,0},{5,1},{6,2},{7,3},{8,12},{9,13},{10,... | collective-permute-start | bytes 122888 | tf_op jit(solution)/shard_map/ppermute | solution.py:716
  41.7 6.4 %collective-permute-start.6 = (f32[16,640]{1,0:T(8,128)}, f32[16,640]{1,0:T(8,128)S(1)}, u32[]{:S(2)}, u32[]{:S(2)}) collective-permute-start(f32[16,640]{1,0:T(8,128)} %get-tuple-element.149), channel_id=1, source_target_pairs={{0,1},{1,0},{2,3},{3,2},{4,5},{5,4},{6,7},{7,6},{8,9},{9,8},{10,11... | collective-permute-start | bytes 122888 | tf_op jit(solution)/shard_map/ppermute | solution.py:716
  50.8 10.0 %all-to-all-start.3 = ((f32[32,4,128]{2,1,0:T(4,128)}), f32[32,4,128]{2,1,0:T(4,128)S(1)}, u32[]{:S(2)}, u32[]{:S(2)}) async-start(f32[32,4,128]{2,1,0:T(4,128)} %bitcast.72), calls=%async_computation.3 | async-start | bytes 131072 | tf_op jit(solution)/shard_map/all_to_all | solution.py:720
  53.4 10.7 %collective-permute-start.10 = (f32[16,640]{1,0:T(8,128)}, f32[16,640]{1,0:T(8,128)S(1)}, u32[]{:S(2)}, u32[]{:S(2)}) collective-permute-start(f32[16,640]{1,0:T(8,128)} %get-tuple-element.161), channel_id=1, source_target_pairs={{0,4},{1,5},{2,6},{3,7},{4,0},{5,1},{6,2},{7,3},{8,12},{9,13},{10,... | collective-permute-start | bytes 122888 | tf_op jit(solution)/shard_map/ppermute | solution.py:716
  56.1 8.0 %collective-permute-start.11 = (f32[16,640]{1,0:T(8,128)}, f32[16,640]{1,0:T(8,128)S(1)}, u32[]{:S(2)}, u32[]{:S(2)}) collective-permute-start(f32[16,640]{1,0:T(8,128)} %get-tuple-element.162), channel_id=1, source_target_pairs={{0,1},{1,0},{2,3},{3,2},{4,5},{5,4},{6,7},{7,6},{8,9},{9,8},{10,11... | collective-permute-start | bytes 122888 | tf_op jit(solution)/shard_map/ppermute | solution.py:716
  57.6 6.5 %collective-permute-start.12 = (f32[16,640]{1,0:T(8,128)}, f32[16,640]{1,0:T(8,128)S(1)}, u32[]{:S(2)}, u32[]{:S(2)}) collective-permute-start(f32[16,640]{1,0:T(8,128)} %get-tuple-element.163), channel_id=1, source_target_pairs={{0,2},{1,3},{2,0},{3,1},{4,6},{5,7},{6,4},{7,5},{8,10},{9,11},{10,... | collective-permute-start | bytes 122888 | tf_op jit(solution)/shard_map/ppermute | solution.py:716
  59.2 5.0 %collective-permute-start.13 = (f32[16,640]{1,0:T(8,128)}, f32[16,640]{1,0:T(8,128)S(1)}, u32[]{:S(2)}, u32[]{:S(2)}) collective-permute-start(f32[16,640]{1,0:T(8,128)} %get-tuple-element.164), channel_id=1, source_target_pairs={{0,16},{8,24},{16,0},{24,8},{1,17},{9,25},{17,1},{25,9},{2,18},{10... | collective-permute-start | bytes 122888 | tf_op jit(solution)/shard_map/ppermute | solution.py:716
  67.8 9.9 %all-to-all-start.4 = ((f32[32,4,128]{2,1,0:T(4,128)}), f32[32,4,128]{2,1,0:T(4,128)S(1)}, u32[]{:S(2)}, u32[]{:S(2)}) async-start(f32[32,4,128]{2,1,0:T(4,128)} %bitcast.75), calls=%async_computation.4 | async-start | bytes 131072 | tf_op jit(solution)/shard_map/all_to_all | solution.py:720
  70.3 9.5 %collective-permute-start.15 = (f32[16,640]{1,0:T(8,128)}, f32[16,640]{1,0:T(8,128)S(1)}, u32[]{:S(2)}, u32[]{:S(2)}) collective-permute-start(f32[16,640]{1,0:T(8,128)} %get-tuple-element.177), channel_id=1, source_target_pairs={{0,4},{1,5},{2,6},{3,7},{4,0},{5,1},{6,2},{7,3},{8,12},{9,13},{10,... | collective-permute-start | bytes 122888 | tf_op jit(solution)/shard_map/ppermute | solution.py:716
  73.0 6.8 %collective-permute-start.16 = (f32[16,640]{1,0:T(8,128)}, f32[16,640]{1,0:T(8,128)S(1)}, u32[]{:S(2)}, u32[]{:S(2)}) collective-permute-start(f32[16,640]{1,0:T(8,128)} %get-tuple-element.178), channel_id=1, source_target_pairs={{0,1},{1,0},{2,3},{3,2},{4,5},{5,4},{6,7},{7,6},{8,9},{9,8},{10,11... | collective-permute-start | bytes 122888 | tf_op jit(solution)/shard_map/ppermute | solution.py:716
  74.5 5.3 %collective-permute-start.17 = (f32[16,640]{1,0:T(8,128)}, f32[16,640]{1,0:T(8,128)S(1)}, u32[]{:S(2)}, u32[]{:S(2)}) collective-permute-start(f32[16,640]{1,0:T(8,128)} %get-tuple-element.179), channel_id=1, source_target_pairs={{0,2},{1,3},{2,0},{3,1},{4,6},{5,7},{6,4},{7,5},{8,10},{9,11},{10,... | collective-permute-start | bytes 122888 | tf_op jit(solution)/shard_map/ppermute | solution.py:716
  82.3 10.0 %all-to-all-start.5 = ((f32[32,4,128]{2,1,0:T(4,128)}), f32[32,4,128]{2,1,0:T(4,128)S(1)}, u32[]{:S(2)}, u32[]{:S(2)}) async-start(f32[32,4,128]{2,1,0:T(4,128)} %bitcast.71), calls=%async_computation.5 | async-start | bytes 131072 | tf_op jit(solution)/shard_map/all_to_all | solution.py:720
  85.1 10.6 %collective-permute-start.20 = (f32[16,640]{1,0:T(8,128)}, f32[16,640]{1,0:T(8,128)S(1)}, u32[]{:S(2)}, u32[]{:S(2)}) collective-permute-start(f32[16,640]{1,0:T(8,128)} %get-tuple-element.192), channel_id=1, source_target_pairs={{0,4},{1,5},{2,6},{3,7},{4,0},{5,1},{6,2},{7,3},{8,12},{9,13},{10,... | collective-permute-start | bytes 122888 | tf_op jit(solution)/shard_map/ppermute | solution.py:716
  87.6 8.1 %collective-permute-start.21 = (f32[16,640]{1,0:T(8,128)}, f32[16,640]{1,0:T(8,128)S(1)}, u32[]{:S(2)}, u32[]{:S(2)}) collective-permute-start(f32[16,640]{1,0:T(8,128)} %get-tuple-element.193), channel_id=1, source_target_pairs={{0,1},{1,0},{2,3},{3,2},{4,5},{5,4},{6,7},{7,6},{8,9},{9,8},{10,11... | collective-permute-start | bytes 122888 | tf_op jit(solution)/shard_map/ppermute | solution.py:716
  89.1 6.6 %collective-permute-start.22 = (f32[16,640]{1,0:T(8,128)}, f32[16,640]{1,0:T(8,128)S(1)}, u32[]{:S(2)}, u32[]{:S(2)}) collective-permute-start(f32[16,640]{1,0:T(8,128)} %get-tuple-element.194), channel_id=1, source_target_pairs={{0,2},{1,3},{2,0},{3,1},{4,6},{5,7},{6,4},{7,5},{8,10},{9,11},{10,... | collective-permute-start | bytes 122888 | tf_op jit(solution)/shard_map/ppermute | solution.py:716
  90.6 5.0 %collective-permute-start.23 = (f32[16,640]{1,0:T(8,128)}, f32[16,640]{1,0:T(8,128)S(1)}, u32[]{:S(2)}, u32[]{:S(2)}) collective-permute-start(f32[16,640]{1,0:T(8,128)} %get-tuple-element.195), channel_id=1, source_target_pairs={{0,16},{8,24},{16,0},{24,8},{1,17},{9,25},{17,1},{25,9},{2,18},{10... | collective-permute-start | bytes 122888 | tf_op jit(solution)/shard_map/ppermute | solution.py:716
  99.2 10.0 %all-to-all-start.6 = ((f32[32,4,128]{2,1,0:T(4,128)}), f32[32,4,128]{2,1,0:T(4,128)S(1)}, u32[]{:S(2)}, u32[]{:S(2)}) async-start(f32[32,4,128]{2,1,0:T(4,128)} %bitcast.74), calls=%async_computation.6 | async-start | bytes 131072 | tf_op jit(solution)/shard_map/all_to_all | solution.py:720
  101.8 9.6 %collective-permute-start.25 = (f32[16,640]{1,0:T(8,128)}, f32[16,640]{1,0:T(8,128)S(1)}, u32[]{:S(2)}, u32[]{:S(2)}) collective-permute-start(f32[16,640]{1,0:T(8,128)} %get-tuple-element.209), channel_id=1, source_target_pairs={{0,4},{1,5},{2,6},{3,7},{4,0},{5,1},{6,2},{7,3},{8,12},{9,13},{10,... | collective-permute-start | bytes 122888 | tf_op jit(solution)/shard_map/ppermute | solution.py:716
  104.5 6.9 %collective-permute-start.26 = (f32[16,640]{1,0:T(8,128)}, f32[16,640]{1,0:T(8,128)S(1)}, u32[]{:S(2)}, u32[]{:S(2)}) collective-permute-start(f32[16,640]{1,0:T(8,128)} %get-tuple-element.210), channel_id=1, source_target_pairs={{0,1},{1,0},{2,3},{3,2},{4,5},{5,4},{6,7},{7,6},{8,9},{9,8},{10,11... | collective-permute-start | bytes 122888 | tf_op jit(solution)/shard_map/ppermute | solution.py:716
  106.0 5.4 %collective-permute-start.27 = (f32[16,640]{1,0:T(8,128)}, f32[16,640]{1,0:T(8,128)S(1)}, u32[]{:S(2)}, u32[]{:S(2)}) collective-permute-start(f32[16,640]{1,0:T(8,128)} %get-tuple-element.211), channel_id=1, source_target_pairs={{0,2},{1,3},{2,0},{3,1},{4,6},{5,7},{6,4},{7,5},{8,10},{9,11},{10,... | collective-permute-start | bytes 122888 | tf_op jit(solution)/shard_map/ppermute | solution.py:716
  113.7 10.0 %all-to-all-start.7 = ((f32[32,4,128]{2,1,0:T(4,128)}), f32[32,4,128]{2,1,0:T(4,128)S(1)}, u32[]{:S(2)}, u32[]{:S(2)}) async-start(f32[32,4,128]{2,1,0:T(4,128)} %bitcast.70), calls=%async_computation.7 | async-start | bytes 131072 | tf_op jit(solution)/shard_map/all_to_all | solution.py:720
  116.3 11.1 %collective-permute-start.30 = (f32[16,640]{1,0:T(8,128)}, f32[16,640]{1,0:T(8,128)S(1)}, u32[]{:S(2)}, u32[]{:S(2)}) collective-permute-start(f32[16,640]{1,0:T(8,128)} %get-tuple-element.226), channel_id=1, source_target_pairs={{0,4},{1,5},{2,6},{3,7},{4,0},{5,1},{6,2},{7,3},{8,12},{9,13},{10,... | collective-permute-start | bytes 122888 | tf_op jit(solution)/shard_map/ppermute | solution.py:716
  119.0 8.4 %collective-permute-start.31 = (f32[16,640]{1,0:T(8,128)}, f32[16,640]{1,0:T(8,128)S(1)}, u32[]{:S(2)}, u32[]{:S(2)}) collective-permute-start(f32[16,640]{1,0:T(8,128)} %get-tuple-element.227), channel_id=1, source_target_pairs={{0,1},{1,0},{2,3},{3,2},{4,5},{5,4},{6,7},{7,6},{8,9},{9,8},{10,11... | collective-permute-start | bytes 122888 | tf_op jit(solution)/shard_map/ppermute | solution.py:716
  120.5 6.9 %collective-permute-start.32 = (f32[16,640]{1,0:T(8,128)}, f32[16,640]{1,0:T(8,128)S(1)}, u32[]{:S(2)}, u32[]{:S(2)}) collective-permute-start(f32[16,640]{1,0:T(8,128)} %get-tuple-element.228), channel_id=1, source_target_pairs={{0,2},{1,3},{2,0},{3,1},{4,6},{5,7},{6,4},{7,5},{8,10},{9,11},{10,... | collective-permute-start | bytes 122888 | tf_op jit(solution)/shard_map/ppermute | solution.py:716
  122.1 5.4 %collective-permute-start.33 = (f32[16,640]{1,0:T(8,128)}, f32[16,640]{1,0:T(8,128)S(1)}, u32[]{:S(2)}, u32[]{:S(2)}) collective-permute-start(f32[16,640]{1,0:T(8,128)} %get-tuple-element.229), channel_id=1, source_target_pairs={{0,16},{8,24},{16,0},{24,8},{1,17},{9,25},{17,1},{25,9},{2,18},{10... | collective-permute-start | bytes 122888 | tf_op jit(solution)/shard_map/ppermute | solution.py:716
  (12 other events, 43.5 us)
